TPU v7x, 32 devices: a whole 2x2x4 slice. The times are simulated.
32 devices in a mesh: grp: 4 (over z), gx: 2 (over y), gy: 4 (over x, core).
Axes of the slice: x: 2, y: 2, z: 4, core: 2. Of those that a mesh axis runs over, the one named last changes fastest.
Arguments:
- populations: float32 [27, 8, 32, 512], P(None, 'gx', 'gy', 'grp'), may hold values from 0 to 1, as said below
- thermal: float32 [7, 8, 32, 512], P(None, ('gx', 'grp'), 'gy'), may hold values from 0 to 1, as said below
- velocity_prev: float32 [3, 8, 32, 512], P(None, 'gx', 'gy', 'grp'), may hold values from -0.3 to 0.3
- solid: int32 [8, 32, 512], P('gx', 'gy', 'grp'), may hold values 0 or 1
- phase_ids: int32 [8, 32, 512], P(('gx', 'grp'), 'gy'), may hold values from 0 to 3
- conductivity: float32 [4], replicated, may hold values from 0.02 to 0.3
- rates: float32 [27], replicated, may hold values from 0.7 to 1.7
Outputs:
- populations_out: float32 [27, 8, 32, 512], P(None, 'gx', 'gy', 'grp')
- thermal_out: float32 [7, 8, 32, 512], P(None, ('gx', 'grp'), 'gy')
Inputs may be any that keep to these rules, and one draw needn't show every extreme that they name: `populations`: positive. `thermal`: positive.
All inputs are finite; a program needn't handle non-finite values. No bound on the sum of `solid` on one device may be relied on, other than what follows from the above.
Results may differ from a plain program's by a relative error of at most 0.0001.
Values sent between devices are 32-bit elements; how exact they have to be, the bound alone decides.
No kernel may reach another device: no remote copies, remote signals or barrier semaphores. Data moves between devices by JAX's collectives and lax.ppermute only.
A program may use at most 64 MiB of HBM per device.

v0:
```python
import jax
import jax.numpy as jnp
import numpy as np
from jax import lax
from jax.experimental import pallas as pl
from jax.experimental.pallas import tpu as pltpu
from jax.sharding import PartitionSpec as P

STEPS = 4
WINDOWS = 2


HIGHEST = lax.Precision.HIGHEST
BUOYANCY = 0.03
REFERENCE_HEAT = 1.0
OFFSET_TABLE = [(number // 9 - 1, number // 3 % 3 - 1, number % 3 - 1) for number in range(27)]
LATTICE_WEIGHTS = np.array(
    [
        np.prod([2.0 / 3.0 if component == 0 else 1.0 / 6.0 for component in triple])
        for triple in OFFSET_TABLE
    ]
)
VANDERMONDE = np.array([[1.0, 1.0, 1.0], [-1.0, 0.0, 1.0], [1.0, 0.0, 1.0]])
VANDER_INVERSE = np.array([[0.0, -0.5, 0.5], [1.0, 0.0, -1.0], [0.0, 0.5, 0.5]])
MOMENT_MATRIX = np.kron(np.kron(VANDERMONDE, VANDERMONDE), VANDERMONDE)
MOMENT_INVERSE = np.kron(np.kron(VANDER_INVERSE, VANDER_INVERSE), VANDER_INVERSE)
RELAXED = np.array([0.0 if number in (0, 1, 3, 9) else 1.0 for number in range(27)])
SUMMING = np.concatenate([np.ones((1, 27)), 1.0 * np.array(OFFSET_TABLE).T], axis=0)
HEAT_WEIGHTS = np.array([0.25] + [0.125] * 6)


def from_behind(value, axis, steps):
    count = lax.axis_size(axis)
    pairs = [(source, (source + steps) % count) for source in range(count)]
    return lax.ppermute(value, axis, pairs)


def extended(cells, sides, width):
    for axis, dim in sides:
        count = lax.axis_size(axis)
        head = lax.slice_in_dim(cells, 0, width, axis=dim)
        tail = lax.slice_in_dim(cells, cells.shape[dim] - width, cells.shape[dim], axis=dim)
        cells = jnp.concatenate(
            [
                lax.ppermute(tail, axis, [(i, (i + 1) % count) for i in range(count)]),
                cells,
                lax.ppermute(head, axis, [((i + 1) % count, i) for i in range(count)]),
            ],
            axis=dim,
        )
    return cells


def flow_state(flat, heat_flat):
    sums = jnp.dot(jnp.asarray(SUMMING, jnp.float32), flat, precision=HIGHEST)
    density = sums[0]
    force = BUOYANCY * (heat_flat - REFERENCE_HEAT)
    speed = jnp.stack([sums[1], sums[2], sums[3] + 0.5 * force]) / density
    return (density, force, speed)


def collide(popul, heat, rates):
    flat = popul.reshape(27, -1)
    density, force, speed = flow_state(flat, heat.reshape(-1))
    along = jnp.dot(jnp.asarray(SUMMING[1:].T, jnp.float32), speed, precision=HIGHEST)
    square = jnp.sum(speed * speed, axis=0)
    balance = (
        density
        * jnp.asarray(LATTICE_WEIGHTS, jnp.float32)[:, None]
        * (1.0 + 3.0 * along + 4.5 * along * along - 1.5 * square)
    )
    scaled = (
        jnp.asarray(MOMENT_INVERSE, jnp.float32)
        * (rates * jnp.asarray(RELAXED, jnp.float32))[None, :]
    )
    relax = jnp.dot(scaled, jnp.asarray(MOMENT_MATRIX, jnp.float32), precision=HIGHEST)
    post = (
        flat
        - jnp.dot(relax, flat - balance, precision=HIGHEST)
        + jnp.asarray(MOMENT_INVERSE[:, 1], jnp.float32)[:, None] * force[None, :]
    )
    return post.reshape(popul.shape)


def flow_speed(popul, heat, solid):
    density, force, speed = flow_state(popul.reshape(27, -1), heat.reshape(-1))
    return jnp.where(solid[None] == 0, speed.reshape((3,) + solid.shape), 0.0)


def heat_collide(heat_pops, speed, relax_time):
    total = jnp.sum(heat_pops, axis=0)
    still = jnp.zeros_like(speed[0])
    along = jnp.stack([still, speed[0], -speed[0], speed[1], -speed[1], speed[2], -speed[2]])
    balance = (
        jnp.asarray(HEAT_WEIGHTS, jnp.float32)[:, None, None, None]
        * total[None]
        * (1.0 + 4.0 * along)
    )
    return heat_pops - (heat_pops - balance) / relax_time[None]


def relaxation(phase_ids, conductivity):
    levels = jnp.arange(conductivity.shape[0], dtype=jnp.int32)
    chosen = jnp.sum(
        jnp.where(
            phase_ids[None] == levels[:, None, None, None], conductivity[:, None, None, None], 0.0
        ),
        axis=0,
    )
    return 0.5 + 4.0 * chosen


def inner_window(padded, triple, sizes):
    return padded[
        1 - triple[0] : 1 - triple[0] + sizes[0],
        1 - triple[1] : 1 - triple[1] + sizes[1],
        1 - triple[2] : 1 - triple[2] + sizes[2],
    ]


def advance(grid, axis_number, send_up, send_down):
    space = 3 + axis_number
    length = grid.shape[space]
    rising = lax.index_in_dim(grid, 2, axis_number, keepdims=True)
    resting = lax.index_in_dim(grid, 1, axis_number, keepdims=True)
    falling = lax.index_in_dim(grid, 0, axis_number, keepdims=True)
    from_below = send_up(lax.slice_in_dim(rising, length - 1, length, axis=space))
    from_above = send_down(lax.slice_in_dim(falling, 0, 1, axis=space))
    rising = jnp.concatenate(
        [from_below, lax.slice_in_dim(rising, 0, length - 1, axis=space)], axis=space
    )
    falling = jnp.concatenate(
        [lax.slice_in_dim(falling, 1, length, axis=space), from_above], axis=space
    )
    return jnp.concatenate([falling, resting, rising], axis=axis_number)


def flow_arrivals(post):
    sizes = post.shape[1:]
    grid = post.reshape((3, 3, 3) + sizes)
    grid = advance(
        grid,
        0,
        lambda plane: from_behind(plane, "gx", 1),
        lambda plane: from_behind(plane, "gx", -1),
    )
    grid = advance(
        grid,
        1,
        lambda plane: from_behind(plane, "gy", 1),
        lambda plane: from_behind(plane, "gy", -1),
    )
    grid = advance(
        grid,
        2,
        lambda plane: from_behind(plane, "grp", 1),
        lambda plane: from_behind(plane, "grp", -1),
    )
    return grid.reshape(post.shape)


def stream_heat(post, grp_index, last_grp):
    length = post.shape[1]
    size_y = post.shape[2]
    eastward = post[1]
    westward = post[2]
    lower_first = from_behind(eastward, "grp", 1)
    lower_second = from_behind(lower_first, "gx", 1)
    entering = jnp.where(grp_index == 0, lower_second, lower_first)
    eastward = jnp.concatenate([entering, eastward[: length - 1]], axis=0)
    upper_first = from_behind(westward, "grp", -1)
    upper_second = from_behind(upper_first, "gx", -1)
    entering = jnp.where(grp_index == last_grp, upper_second, upper_first)
    westward = jnp.concatenate([westward[1:], entering], axis=0)
    sides = extended(post[3:5], (("gy", 2),), 1)
    northward = sides[0, :, 0:size_y]
    southward = sides[1, :, 2 : size_y + 2]
    upward = jnp.roll(post[5], 1, axis=2)
    downward = jnp.roll(post[6], -1, axis=2)
    return jnp.stack([post[0], eastward, westward, northward, southward, upward, downward])


def on_device(populations, thermal, velocity_prev, solid, phase_ids, conductivity, rates):
    padded_solid = extended(solid, (("grp", 2), ("gx", 0), ("gy", 1)), 1)
    sizes = solid.shape
    blocked = jnp.stack(
        [inner_window(padded_solid, OFFSET_TABLE[number], sizes) != 0 for number in range(27)]
    )
    fluid_cells = (solid == 0)[None]
    grp_index = lax.axis_index("grp")
    last_grp = lax.axis_size("grp") - 1
    relax_time = relaxation(phase_ids, conductivity)
    speed_brick = velocity_prev
    popul = populations
    heat_pops = thermal
    for window_number in range(WINDOWS):
        heat_brick = lax.all_to_all(
            jnp.sum(heat_pops, axis=0), "grp", split_axis=2, concat_axis=0, tiled=True
        )
        speed_column = lax.all_to_all(speed_brick, "grp", split_axis=1, concat_axis=3, tiled=True)
        for step_number in range(STEPS):
            post = collide(popul, heat_brick, rates)
            arrived = flow_arrivals(post)
            popul = jnp.where(fluid_cells, jnp.where(blocked, post[::-1], arrived), popul)
        for step_number in range(STEPS):
            heat_pops = stream_heat(
                heat_collide(heat_pops, speed_column, relax_time), grp_index, last_grp
            )
        if window_number + 1 < WINDOWS:
            speed_brick = flow_speed(popul, heat_brick, solid)
    return (popul, heat_pops)


SUBLANES = 8
LANES = 128
F32 = jnp.float32


class Slab:
    def __init__(self, mesh_shape, flow_block, heat_block):
        self.grp, self.gx, self.gy = (mesh_shape[name] for name in ("grp", "gx", "gy"))
        self.block_x, self.block_y, self.block_z = flow_block
        self.sub = self.gx * self.gy
        self.planes = self.block_z // self.sub
        self.halo = self.planes // 2
        self.fits = (
            self.block_y == SUBLANES
            and self.block_z == LANES
            and self.planes * self.sub == LANES
            and self.halo * 2 == self.planes
            and self.halo == STEPS * WINDOWS
            and 2 * self.block_x == self.sub
            and self.block_x == self.grp
            and heat_block == (1, SUBLANES, self.grp * LANES)
            and self.sub & (self.sub - 1) == 0
            and self.grp & (self.grp - 1) == 0
            and self.gy % 2 == 0
        )
        if self.fits:
            self.snake = [
                x * self.gy + (y if x % 2 == 0 else self.gy - 1 - y)
                for x in range(self.gx)
                for y in range(self.gy)
            ]
            self.ring = [
                part * self.sub + self.snake[place if part % 2 == 0 else self.sub - 1 - place]
                for part in range(self.grp)
                for place in range(self.sub)
            ]

    def holders(self):
        even = lax.axis_index("grp") % 2 == 0
        return [jnp.where(even, *pair) for pair in zip(self.snake, self.snake[::-1])]


def lane_index():
    return lax.broadcasted_iota(jnp.int32, (SUBLANES, LANES), 1)


def row_index():
    return lax.broadcasted_iota(jnp.int32, (SUBLANES, LANES), 0)


def lane_roll(value, amount):
    amount = amount % LANES
    return value if amount == 0 else pltpu.roll(value, amount, 1)


def swap_groups(values, group):
    count = len(values)
    lane = lane_index()
    values = list(values)
    bit = 1
    while bit < count:
        low = (lane // (group * bit)) % 2 == 0
        for first in range(count):
            if first & bit == 0:
                a, b = values[first], values[first | bit]
                values[first] = jnp.where(low, a, lane_roll(b, group * bit))
                values[first | bit] = jnp.where(low, lane_roll(a, -group * bit), b)
        bit *= 2
    return values


SPEED_AT, SOLID_AT, HEAT_AT, RATE_AT, ROWS = 27, 30, 31, 38, 40
MOVING = 34


def moving_row(number):
    return number + (HEAT_AT - SPEED_AT) * (number >= SPEED_AT)


def offer_heat(slab, levels_hbm, heat_hbm, phase_hbm, *refs):
    outs, (levels_ref, heat_ref, phase_ref, sems) = refs[: slab.grp], refs[slab.grp :]
    copies = [
        pltpu.make_async_copy(heat_hbm, heat_ref, sems.at[0]),
        pltpu.make_async_copy(phase_hbm, phase_ref, sems.at[1]),
        pltpu.make_async_copy(levels_hbm, levels_ref, sems.at[2]),
    ]
    for copy in copies:
        copy.start()
    for copy in copies:
        copy.wait()
    mine = lax.axis_index("grp")
    for step in range(slab.grp):
        part = jnp.bitwise_xor(mine, step)
        span = pl.ds(pl.multiple_of(part * LANES, LANES), LANES)
        phase = phase_ref[0, :, span]
        chosen = jnp.zeros((SUBLANES, LANES), F32)
        for level in range(levels_ref.shape[0]):
            chosen = jnp.where(phase == level, levels_ref[level], chosen)
        for k in range(7):
            outs[step][k] = heat_ref[k, 0, :, span]
        outs[step][7] = 1.0 / (0.5 + 4.0 * chosen)


def for_each(count, body):
    for number in range(count):
        body(number)


def pack_flow(slab, popul_hbm, speed_hbm, solid_hbm, sent, flags, fields, solid_ref, sems):
    copies = [
        pltpu.make_async_copy(popul_hbm, fields.at[pl.ds(0, SPEED_AT)], sems.at[0]),
        pltpu.make_async_copy(speed_hbm, fields.at[pl.ds(SPEED_AT, 3)], sems.at[1]),
        pltpu.make_async_copy(solid_hbm, solid_ref, sems.at[2]),
    ]
    for copy in copies:
        copy.start()
    for copy in copies:
        copy.wait()
    holders = slab.holders()

    def one(pair):
        pack_pair(slab, fields, pair, sent, pair, holders)

    for_each(SOLID_AT // 2, one)
    flags[...] = solid_ref[...].astype(F32)


def pack_pair(slab, fields, source, sent, target, holders):
    sources = [fields[2 * source + h, x] for x in range(slab.block_x) for h in range(2)]
    for place, value in enumerate(swap_groups(sources, slab.planes)):
        sent[holders[place], target] = value


def pack_heat(slab, sent_in, flags, *refs):
    parts, (sent, held, packed, sem) = refs[: slab.grp], refs[slab.grp :]
    mine = lax.axis_index("grp")
    holders = slab.holders()
    held[0] = flags[...]
    held[9] = jnp.zeros(flags.shape, F32)
    for step in range(slab.grp):
        held[pl.ds(1, 8), jnp.bitwise_xor(mine, step)] = parts[step][...]
    first, count = SOLID_AT // 2, (ROWS - SOLID_AT) // 2

    def one(pair):
        pack_pair(slab, held, pair, packed, pair, holders)

    for_each(count, one)
    copy = pltpu.make_async_copy(packed, sent.at[:, pl.ds(first, count)], sem)
    copy.start()
    copy.wait()


def in_first_half(slab):
    return lane_index() % slab.planes < slab.halo


def offer_halo(slab, came, low_out, high_out):
    def one(number, _):
        tile = 2 * number
        first = in_first_half(slab)
        for pair in range(ROWS // 2):
            a, b = came[tile, pair], came[tile + 1, pair]
            low_out[number, pair] = jnp.where(first, a, lane_roll(b, slab.halo))
            high_out[number, pair] = jnp.where(first, lane_roll(b, -slab.halo), a)
        return 0

    lax.fori_loop(0, slab.sub // 2, one, 0)


def make_tiles(slab, came, below_ref, above_ref, state):
    def one(number, _):
        first = in_first_half(slab)
        even = (lane_index() // slab.planes) % 2 == 0
        back = 2 * slab.planes
        for pair in range(ROWS // 2):
            below, above = below_ref[number, pair], above_ref[number, pair]
            beside = (
                jnp.where(first, above, lane_roll(below, -back)),
                jnp.where(first, lane_roll(above, -slab.halo), lane_roll(below, slab.halo - back)),
            )
            for which in range(2):
                tile = 2 * number + which
                own, halo = came[tile, pair], beside[which]
                state[2 * pair, tile] = jnp.where(even, own, lane_roll(halo, slab.planes))
                state[2 * pair + 1, tile] = jnp.where(even, lane_roll(own, -slab.planes), halo)
        return 0

    lax.fori_loop(0, slab.sub // 2, one, 0)


def pack_out(slab, came, state, sent):
    def one(tile, _):
        even = (lane_index() // slab.planes) % 2 == 0
        flags = came[tile, SOLID_AT // 2]
        solid = jnp.where(even, flags, lane_roll(flags, slab.planes)) != 0.0
        for pair in range(MOVING // 2):
            first, second = (state[moving_row(2 * pair + h), tile] for h in range(2))
            value = jnp.where(even, first, lane_roll(second, slab.planes))
            if 2 * pair + 1 < SPEED_AT:
                value = jnp.where(solid, came[tile, pair], value)
            elif 2 * pair < SPEED_AT:
                value = jnp.where(jnp.logical_and(solid, even), came[tile, pair], value)
            sent[tile, pair] = value
        return 0

    lax.fori_loop(0, slab.sub, one, 0)


def unpack_pair(slab, came, pair, holders):
    sources = [came[holders[place], pair] for place in range(slab.sub)]
    values = swap_groups(sources, slab.planes)
    return [values[0::2], values[1::2]]


def return_heat(slab, came, *refs):
    outs, held = refs[: slab.grp], refs[slab.grp]
    holders = slab.holders()
    _, values = unpack_pair(slab, came, SPEED_AT // 2, holders)
    for x in range(slab.block_x):
        held[x, 0] = values[x]

    def one(pair):
        for h, values in enumerate(unpack_pair(slab, came, SPEED_AT // 2 + 1 + pair, holders)):
            for x in range(slab.block_x):
                held[x, 2 * pair + 1 + h] = values[x]

    for_each(3, one)
    mine = lax.axis_index("grp")
    for step in range(slab.grp):
        outs[step][...] = held[jnp.bitwise_xor(mine, step)]


def unpack_flow(slab, came, popul_out):
    holders = slab.holders()

    def one(pair):
        for h, values in enumerate(unpack_pair(slab, came, pair, holders)):
            for x in range(slab.block_x):
                popul_out[2 * pair + h, x] = values[x]

    for_each(SPEED_AT // 2, one)
    values, _ = unpack_pair(slab, came, SPEED_AT // 2, holders)
    for x in range(slab.block_x):
        popul_out[SPEED_AT - 1, x] = values[x]


def join_heat(slab, *refs):
    parts, thermal_out = refs[: slab.grp], refs[slab.grp]
    mine = lax.axis_index("grp")
    for step in range(slab.grp):
        part = jnp.bitwise_xor(mine, step)
        span = pl.ds(pl.multiple_of(part * LANES, LANES), LANES)
        for k in range(7):
            thermal_out[k, 0, :, span] = parts[step][k]


def forward3(values):
    for stride in (9, 3, 1):
        out = [None] * 27
        for n in range(27):
            if n // stride % 3 == 0:
                a, b, c = values[n], values[n + stride], values[n + 2 * stride]
                both = a + c
                out[n], out[n + stride], out[n + 2 * stride] = both + b, c - a, both
        values = out
    return values


def backward3(values):
    for stride in (9, 3, 1):
        out = [None] * 27
        for n in range(27):
            if n // stride % 3 == 0:
                a, b, c = values[n], values[n + stride], values[n + 2 * stride]
                even, odd = 0.5 * c, 0.5 * b
                out[n], out[n + stride], out[n + 2 * stride] = even - odd, a - c, even + odd
        values = out
    return values


def collide_tile(values, force, rate):
    moments = forward3(values)
    density = moments[0]
    jx, jy, jz = moments[9], moments[3], moments[1] + 0.5 * force
    inverse = 1.0 / density
    flux = (jx, jy, jz)
    u = tuple(j * inverse for j in flux)
    third = 1.0 / 3.0
    base = {0: density}
    for k in (1, 2, 3):
        base[k] = density * third**k
    squares = [flux[d] * u[d] for d in range(3)]
    square_at = {}
    scaled = {}

    def scale(key, value, count):
        if count == 0:
            return value
        if (key, count) not in scaled:
            scaled[key, count] = value * third**count
        return scaled[key, count]

    cross = {(0, 1): jx * u[1], (0, 2): jx * u[2], (1, 2): jy * u[2]}
    out = [None] * 27
    for n in range(27):
        powers = (n // 9, n // 3 % 3, n % 3)
        if n in (0, 3, 9):
            out[n] = moments[n]
            continue
        if n == 1:
            out[n] = moments[n] + force
            continue
        odd = tuple(d for d in range(3) if powers[d] == 1)
        even = tuple(d for d in range(3) if powers[d] == 2)
        count = len(even)
        if len(odd) == 3:
            out[n] = moments[n] - rate(n) * moments[n]
            continue
        if len(odd) == 0:
            if even not in square_at:
                total = squares[even[0]]
                for d in even[1:]:
                    total = total + squares[d]
                square_at[even] = base[count] + (total * (3.0 * third**count) if count > 1 else total)
            level = square_at[even]
        elif len(odd) == 1:
            level = scale(odd, flux[odd[0]], count)
        else:
            level = scale(odd, cross[odd], count)
        out[n] = moments[n] - rate(n) * (moments[n] - level)
    return backward3(out)


HEAT_OFFSETS = [(0, 0, 0), (1, 0, 0), (-1, 0, 0), (0, 1, 0), (0, -1, 0), (0, 0, 1), (0, 0, -1)]


def run_steps(slab, rates_ref, state, post, force_ref):
    def collide_one(tile, _):
        values = [state[n, tile] for n in range(27)]
        solid = state[SOLID_AT, tile] != 0.0
        moved = collide_tile(values, force_ref[tile], lambda n: rates_ref[n])
        for n in range(27):
            post[n, tile] = jnp.where(solid, jnp.nan, moved[n])
        heat = [state[HEAT_AT + k, tile] for k in range(7)]
        total = heat[0]
        for k in range(1, 7):
            total = total + heat[k]
        omega = state[RATE_AT, tile]
        side = 0.125 * total
        half = 0.5 * total
        for k in range(7):
            if k == 0:
                level = 0.25 * total
            else:
                drift = half * state[SPEED_AT + (k - 1) // 2, tile]
                level = side + drift if k % 2 == 1 else side - drift
            post[SPEED_AT + k, tile] = heat[k] - (heat[k] - level) * omega
        return 0

    def stream_one(tile, _):
        block_x, block_y = tile // slab.gy, tile % slab.gy
        x_of = {a: lax.rem(block_x + slab.gx - a, slab.gx) for a in (-1, 0, 1)}
        y_of = {b: lax.rem(block_y + slab.gy - b, slab.gy) for b in (-1, 0, 1)}
        row = row_index()
        per_x = 2 * slab.planes
        in_x = (lane_index() + slab.halo) % LANES // per_x
        last_x = {1: in_x == slab.block_x - 1, -1: in_x == 0}
        last_y = {1: row == SUBLANES - 1, -1: row == 0}

        def arrive(number, offset):
            a, b, c = offset

            def take(x):
                value = post[number, x_of[x] * slab.gy + block_y]
                if b != 0:
                    other = post[number, x_of[x] * slab.gy + y_of[b]]
                    value = jnp.where(last_y[b], other, value)
                return value

            value = take(0)
            if a != 0:
                value = jnp.where(last_x[a], take(a), value)
            if b != 0:
                value = pltpu.roll(value, b % SUBLANES, 0)
            return lane_roll(value, a * per_x + c)

        for n in range(27):
            value = arrive(n, OFFSET_TABLE[n])
            state[n, tile] = jnp.where(value != value, post[26 - n, tile], value)
        for k in range(7):
            state[HEAT_AT + k, tile] = arrive(SPEED_AT + k, HEAT_OFFSETS[k])
        return 0

    def step(number, _):
        lax.fori_loop(0, slab.sub, collide_one, 0)
        lax.fori_loop(0, slab.sub, stream_one, 0)
        return 0

    lax.fori_loop(0, STEPS, step, 0)


def heat_force(state, tile):
    total = state[HEAT_AT, tile]
    for k in range(1, 7):
        total = total + state[HEAT_AT + k, tile]
    return BUOYANCY * (total - REFERENCE_HEAT)


def flow_speed_tile(state, tile, force):
    values = [state[n, tile] for n in range(27)]
    total = values[0]
    for n in range(1, 27):
        total = total + values[n]
    sums = []
    for d in range(3):
        plus, minus = None, None
        for n in range(27):
            part = OFFSET_TABLE[n][d]
            if part == 1:
                plus = values[n] if plus is None else plus + values[n]
            if part == -1:
                minus = values[n] if minus is None else minus + values[n]
        sums.append(plus - minus)
    sums[2] = sums[2] + 0.5 * force
    return [each / total for each in sums]


def both_windows(slab, rates_hbm, came, below_ref, above_ref, *refs):
    sent, rates_ref, sem, state, post, force = refs
    rates_copy = pltpu.make_async_copy(rates_hbm, rates_ref, sem)
    rates_copy.start()
    make_tiles(slab, came, below_ref, above_ref, state)

    def first_force(tile, _):
        force[tile] = heat_force(state, tile)
        return 0

    lax.fori_loop(0, slab.sub, first_force, 0)
    rates_copy.wait()

    def next_speed(tile, _):
        solid = state[SOLID_AT, tile] != 0.0
        for d, each in enumerate(flow_speed_tile(state, tile, force[tile])):
            state[SPEED_AT + d, tile] = jnp.where(solid, 0.0, each)
        force[tile] = heat_force(state, tile)
        return 0

    def one_window(window, _):
        run_steps(slab, rates_ref, state, post, force)

        @pl.when(window + 1 < WINDOWS)
        def _():
            lax.fori_loop(0, slab.sub, next_speed, 0)

        return 0

    lax.fori_loop(0, WINDOWS, one_window, 0)
    pack_out(slab, came, state, sent)


def local_call(body, slab, arrays, outs, scratch=(), in_hbm=0, carried=False):
    def kernel(*refs):
        body(slab, *refs)

    return pl.pallas_call(
        kernel,
        out_shape=[jax.ShapeDtypeStruct(shape, F32) for shape in outs],
        in_specs=[
            pl.BlockSpec(
                memory_space=pltpu.HBM if i < in_hbm else pl.ANY if carried and i == 0 else pltpu.VMEM
            )
            for i in range(len(arrays))
        ],
        out_specs=[pl.BlockSpec(memory_space=pl.ANY if carried else pltpu.VMEM)] * len(outs),
        input_output_aliases={0: 0} if carried else {},
        scratch_shapes=[pltpu.VMEM(s, F32) if isinstance(s, tuple) else s for s in scratch],
        compiler_params=pltpu.CompilerParams(vmem_limit_bytes=24 * 1024 * 1024),
    )(
        *(
            pltpu.with_memory_space_constraint(array, pltpu.HBM) if i < in_hbm else array
            for i, array in enumerate(arrays)
        )
    )


RING = ("grp", "gx", "gy")


def exchange(slab, low, high):
    ring = slab.ring
    upward = [(ring[i - 1], ring[i]) for i in range(len(ring))]
    from_below = lax.ppermute(high, RING, upward)
    from_above = lax.ppermute(low, RING, [(b, a) for a, b in upward])
    return from_below, from_above


def across_planes(slab, parts):
    return [parts[0]] + [
        lax.ppermute(parts[step], "grp", [(i, i ^ step) for i in range(slab.grp)])
        for step in range(1, slab.grp)
    ]


def on_slabs(slab, populations, thermal, velocity_prev, solid, phase_ids, conductivity, rates):
    tile = (SUBLANES, LANES)

    def vmem_like(array):
        return pltpu.VMEM(array.shape, array.dtype)

    parts = local_call(
        offer_heat,
        slab,
        [conductivity, thermal, phase_ids],
        [(8,) + tile] * slab.grp,
        [
            pltpu.SMEM(conductivity.shape, F32),
            vmem_like(thermal),
            vmem_like(phase_ids),
            pltpu.SemaphoreType.DMA((3,)),
        ],
        in_hbm=3,
    )
    parts = across_planes(slab, parts)
    sent_shape = (slab.sub, ROWS // 2) + tile
    sent, flags = local_call(
        pack_flow,
        slab,
        [populations, velocity_prev, solid],
        [sent_shape, solid.shape],
        [
            (SOLID_AT,) + solid.shape,
            pltpu.VMEM(solid.shape, solid.dtype),
            pltpu.SemaphoreType.DMA((3,)),
        ],
        in_hbm=3,
    )
    (sent,) = local_call(
        pack_heat,
        slab,
        [sent, flags] + parts,
        [sent_shape],
        [
            (ROWS - SOLID_AT,) + solid.shape,
            (slab.sub, (ROWS - SOLID_AT) // 2) + tile,
            pltpu.SemaphoreType.DMA,
        ],
        carried=True,
    )
    came = lax.all_to_all(sent, ("gx", "gy"), split_axis=0, concat_axis=0, tiled=True)
    halo_shape = (slab.sub // 2, ROWS // 2) + tile
    low, high = local_call(offer_halo, slab, [came], [halo_shape, halo_shape])
    below, above = exchange(slab, low, high)
    (sent,) = local_call(
        both_windows,
        slab,
        [rates, came, below, above],
        [(slab.sub, MOVING // 2) + tile],
        [
            pltpu.SMEM(rates.shape, F32),
            pltpu.SemaphoreType.DMA,
            (ROWS, slab.sub) + tile,
            (MOVING, slab.sub) + tile,
            (slab.sub,) + tile,
        ],
        in_hbm=1,
    )
    came = lax.all_to_all(sent, ("gx", "gy"), split_axis=0, concat_axis=0, tiled=True)
    parts = local_call(
        return_heat, slab, [came], [(7,) + tile] * slab.grp, [(slab.grp, 7) + tile]
    )
    parts = across_planes(slab, parts)
    (populations_out,) = local_call(unpack_flow, slab, [came], [populations.shape])
    (thermal_out,) = local_call(join_heat, slab, parts, [thermal.shape])
    return populations_out, thermal_out


def solution(mesh):
    in_specs = (
        P(None, "gx", "gy", "grp"),
        P(None, ("gx", "grp"), "gy", None),
        P(None, "gx", "gy", "grp"),
        P("gx", "gy", "grp"),
        P(("gx", "grp"), "gy", None),
        P(),
        P(),
    )
    out_specs = (P(None, "gx", "gy", "grp"), P(None, ("gx", "grp"), "gy", None))

    def per_device(populations, thermal, *others):
        slab = Slab(mesh.shape, populations.shape[1:], thermal.shape[1:])
        plan = (lambda *arrays: on_slabs(slab, *arrays)) if slab.fits else on_device
        return plan(populations, thermal, *others)

    return jax.shard_map(
        per_device, mesh=mesh, in_specs=in_specs, out_specs=out_specs, check_vma=False
    )
```

profile of v0, /device:TPU:0, one launch (start us, length us, event | category | flops | bytes accessed | tf_op | source)
XLA Modules:
  0.0 76.3 jit_solution(14179895145046997967)
XLA Ops:
  0.6 1.0 %shard_map.87 = (f32[8,8,128]{2,1,0:T(8,128)S(1)}, f32[8,8,128]{2,1,0:T(8,128)S(1)}, f32[8,8,128]{2,1,0:T(8,128)S(1)}, f32[8,8,128]{2,1,0:T(8,128)S(1)}) custom-call(f32[4]{0:T(128)} %refs_0_.4, f32[7,1,8,512]{3,2,1,0:T(8,128)} %refs_1_.3, s32[1,8,512]{2,1,0:T(8,128)} %refs_2_.3), custom_call_target="tpu_custom_call" | custom-call | tf_op jit(solution)/shard_map/pallas_call | solution.py:678
  1.6 3.1 %collective-permute-start = (f32[8,8,128]{2,1,0:T(8,128)S(1)}, f32[8,8,128]{2,1,0:T(8,128)S(1)}, u32[]{:S(2)}, u32[]{:S(2)}) collective-permute-start(f32[8,8,128]{2,1,0:T(8,128)S(1)} %get-tuple-element.17), channel_id=1, source_target_pairs={{0,8},{8,0},{16,24},{24,16},{1,9},{9,1},{17,25},{25,17},{2,10},{10... | collective-permute-start | bytes 98312 | tf_op jit(solution)/shard_map/ppermute | solution.py:712
  4.7 2.6 %collective-permute-start.1 = (f32[8,8,128]{2,1,0:T(8,128)S(1)}, f32[8,8,128]{2,1,0:T(8,128)S(1)}, u32[]{:S(2)}, u32[]{:S(2)}) collective-permute-start(f32[8,8,128]{2,1,0:T(8,128)S(1)} %get-tuple-element.18), channel_id=1, source_target_pairs={{0,16},{8,24},{16,0},{24,8},{1,17},{9,25},{17,1},{25,9},{2,18},{10... | collective-permute-start | bytes 98312 | tf_op jit(solution)/shard_map/ppermute | solution.py:712
  7.3 0.0 collective-permute-start.2
  7.3 2.4 %shard_map.86 = (f32[8,20,8,128]{3,2,1,0:T(8,128)S(1)}, f32[4,8,128]{2,1,0:T(8,128)S(1)}) custom-call(f32[27,4,8,128]{3,2,1,0:T(8,128)} %refs_0_.3, f32[3,4,8,128]{3,2,1,0:T(8,128)} %refs_1_.2, s32[4,8,128]{2,1,0:T(8,128)} %refs_2_.2), custom_call_target="tpu_custom_call" | custom-call | tf_op jit(solution)/shard_map/pallas_call | solution.py:678
  9.7 0.0 collective-permute-done.refs_3_
  9.7 0.4 collective-permute-done.1.refs_4_
  10.1 2.9 %collective-permute-done.2.refs_5_ = f32[8,8,128]{2,1,0:T(8,128)S(1)} collective-permute-done((f32[8,8,128]{2,1,0:T(8,128)S(1)}, f32[8,8,128]{2,1,0:T(8,128)S(1)}, u32[]{:S(2)}, u32[]{:S(2)}) %collective-permute-start.2) | collective-permute-done | bytes 32800 | tf_op jit(solution)/shard_map/ppermute | solution.py:712
  13.0 0.3 shard_map.88
  13.3 14.7 %all_to_all.10.refs_0_.refs_1_ = f32[8,20,8,128]{3,2,1,0:T(8,128)S(1)} all-to-all(f32[8,20,8,128]{3,2,1,0:T(8,128)S(1)} %shard_map.88), channel_id=1, replica_groups=mesh['grp'=4,'gx'=2,'gy'=4] {'gx','gy'}, dimensions={0} | all-to-all | bytes 1310720 | tf_op jit(solution)/shard_map/all_to_all | solution.py:762
  28.0 0.4 shard_map.89
  28.4 0.1 collective-permute-start.3
  28.5 3.8 %collective-permute-start.4 = (f32[4,20,8,128]{3,2,1,0:T(8,128)S(1)}, f32[4,20,8,128]{3,2,1,0:T(8,128)S(1)}, u32[]{:S(2)}, u32[]{:S(2)}) collective-permute-start(f32[4,20,8,128]{3,2,1,0:T(8,128)S(1)} %get-tuple-element.21), channel_id=1, source_target_pairs={{0,24},{1,0},{2,1},{3,2},{7,3},{6,7},{5,6},{4,5},{12,4},{13,12},{1... | collective-permute-start | bytes 983048 | tf_op jit(solution)/shard_map/ppermute | solution.py:706
  32.3 5.2 %collective-permute-done.3.refs_2_ = f32[4,20,8,128]{3,2,1,0:T(8,128)S(1)} collective-permute-done((f32[4,20,8,128]{3,2,1,0:T(8,128)S(1)}, f32[4,20,8,128]{3,2,1,0:T(8,128)S(1)}, u32[]{:S(2)}, u32[]{:S(2)}) %collective-permute-start.3) | collective-permute-done | bytes 327712 | tf_op jit(solution)/shard_map/ppermute | solution.py:705
  37.5 0.0 collective-permute-done.4.refs_3_
  37.5 15.4 %shard_map.90 = f32[8,17,8,128]{3,2,1,0:T(8,128)S(1)} custom-call(f32[27]{0:T(128)} %refs_0_.5, f32[8,20,8,128]{3,2,1,0:T(8,128)S(1)} %all_to_all.10.refs_0_.refs_1_, f32[4,20,8,128]{3,2,1,0:T(8,128)S(1)} %collective-permute-done.3.refs_2_, f32[4,20,8,128]{3,2,1,0:T(8,128)S(1)} %collective-permute-done.4.refs_3_), custom_call_target="tpu_custom_call" | custom-call | tf_op jit(solution)/shard_map/pallas_call | solution.py:678
  52.9 12.5 %all_to_all.11.refs_0_ = f32[8,17,8,128]{3,2,1,0:T(8,128)S(1)} all-to-all(f32[8,17,8,128]{3,2,1,0:T(8,128)S(1)} %shard_map.90), channel_id=1, replica_groups=mesh['grp'=4,'gx'=2,'gy'=4] {'gx','gy'}, dimensions={0} | all-to-all | bytes 1114112 | tf_op jit(solution)/shard_map/all_to_all | solution.py:780
  65.4 0.3 shard_map.92
  65.7 1.3 %collective-permute-start.5 = (f32[7,8,128]{2,1,0:T(8,128)S(1)}, f32[7,8,128]{2,1,0:T(8,128)S(1)}, u32[]{:S(2)}, u32[]{:S(2)}) collective-permute-start(f32[7,8,128]{2,1,0:T(8,128)S(1)} %get-tuple-element.23), channel_id=1, source_target_pairs={{0,8},{8,0},{16,24},{24,16},{1,9},{9,1},{17,25},{25,17},{2,10},{10... | collective-permute-start | bytes 86024 | tf_op jit(solution)/shard_map/ppermute | solution.py:712
  67.0 3.0 %collective-permute-start.6 = (f32[7,8,128]{2,1,0:T(8,128)S(1)}, f32[7,8,128]{2,1,0:T(8,128)S(1)}, u32[]{:S(2)}, u32[]{:S(2)}) collective-permute-start(f32[7,8,128]{2,1,0:T(8,128)S(1)} %get-tuple-element.24), channel_id=1, source_target_pairs={{0,16},{8,24},{16,0},{24,8},{1,17},{9,25},{17,1},{25,9},{2,18},{10... | collective-permute-start | bytes 86024 | tf_op jit(solution)/shard_map/ppermute | solution.py:712
  70.0 0.1 collective-permute-start.7
  70.1 1.8 %shard_map.91 = f32[27,4,8,128]{3,2,1,0:T(8,128)} custom-call(f32[8,17,8,128]{3,2,1,0:T(8,128)S(1)} %all_to_all.11.refs_0_), custom_call_target="tpu_custom_call" | custom-call | tf_op jit(solution)/shard_map/pallas_call | solution.py:678
  71.9 0.0 collective-permute-done.5.refs_1_
  71.9 0.4 collective-permute-done.6.refs_2_
  72.2 3.4 %collective-permute-done.7.refs_3_ = f32[7,8,128]{2,1,0:T(8,128)S(1)} collective-permute-done((f32[7,8,128]{2,1,0:T(8,128)S(1)}, f32[7,8,128]{2,1,0:T(8,128)S(1)}, u32[]{:S(2)}, u32[]{:S(2)}) %collective-permute-start.7) | collective-permute-done | bytes 28704 | tf_op jit(solution)/shard_map/ppermute | solution.py:712
  75.7 0.7 shard_map.93
Async XLA Ops:
  1.6 8.1 %collective-permute-start = (f32[8,8,128]{2,1,0:T(8,128)S(1)}, f32[8,8,128]{2,1,0:T(8,128)S(1)}, u32[]{:S(2)}, u32[]{:S(2)}) collective-permute-start(f32[8,8,128]{2,1,0:T(8,128)S(1)} %get-tuple-element.17), channel_id=1, source_target_pairs={{0,8},{8,0},{16,24},{24,16},{1,9},{9,1},{17,25},{25,17},{2,10},{10... | collective-permute-start | bytes 98312 | tf_op jit(solution)/shard_map/ppermute | solution.py:712
  4.7 5.4 %collective-permute-start.1 = (f32[8,8,128]{2,1,0:T(8,128)S(1)}, f32[8,8,128]{2,1,0:T(8,128)S(1)}, u32[]{:S(2)}, u32[]{:S(2)}) collective-permute-start(f32[8,8,128]{2,1,0:T(8,128)S(1)} %get-tuple-element.18), channel_id=1, source_target_pairs={{0,16},{8,24},{16,0},{24,8},{1,17},{9,25},{17,1},{25,9},{2,18},{10... | collective-permute-start | bytes 98312 | tf_op jit(solution)/shard_map/ppermute | solution.py:712
  7.3 5.7 %collective-permute-start.2 = (f32[8,8,128]{2,1,0:T(8,128)S(1)}, f32[8,8,128]{2,1,0:T(8,128)S(1)}, u32[]{:S(2)}, u32[]{:S(2)}) collective-permute-start(f32[8,8,128]{2,1,0:T(8,128)S(1)} %get-tuple-element.19), channel_id=1, source_target_pairs={{0,24},{8,16},{16,8},{24,0},{1,25},{9,17},{17,9},{25,1},{2,26},{10... | collective-permute-start | bytes 98312 | tf_op jit(solution)/shard_map/ppermute | solution.py:712
  28.4 9.0 %collective-permute-start.3 = (f32[4,20,8,128]{3,2,1,0:T(8,128)S(1)}, f32[4,20,8,128]{3,2,1,0:T(8,128)S(1)}, u32[]{:S(2)}, u32[]{:S(2)}) collective-permute-start(f32[4,20,8,128]{3,2,1,0:T(8,128)S(1)} %get-tuple-element.20), channel_id=1, source_target_pairs={{24,0},{0,1},{1,2},{2,3},{3,7},{7,6},{6,5},{5,4},{4,12},{12,13},{1... | collective-permute-start | bytes 983048 | tf_op jit(solution)/shard_map/ppermute | solution.py:705
  28.5 9.0 %collective-permute-start.4 = (f32[4,20,8,128]{3,2,1,0:T(8,128)S(1)}, f32[4,20,8,128]{3,2,1,0:T(8,128)S(1)}, u32[]{:S(2)}, u32[]{:S(2)}) collective-permute-start(f32[4,20,8,128]{3,2,1,0:T(8,128)S(1)} %get-tuple-element.21), channel_id=1, source_target_pairs={{0,24},{1,0},{2,1},{3,2},{7,3},{6,7},{5,6},{4,5},{12,4},{13,12},{1... | collective-permute-start | bytes 983048 | tf_op jit(solution)/shard_map/ppermute | solution.py:706
  65.7 6.2 %collective-permute-start.5 = (f32[7,8,128]{2,1,0:T(8,128)S(1)}, f32[7,8,128]{2,1,0:T(8,128)S(1)}, u32[]{:S(2)}, u32[]{:S(2)}) collective-permute-start(f32[7,8,128]{2,1,0:T(8,128)S(1)} %get-tuple-element.23), channel_id=1, source_target_pairs={{0,8},{8,0},{16,24},{24,16},{1,9},{9,1},{17,25},{25,17},{2,10},{10... | collective-permute-start | bytes 86024 | tf_op jit(solution)/shard_map/ppermute | solution.py:712
  67.0 5.3 %collective-permute-start.6 = (f32[7,8,128]{2,1,0:T(8,128)S(1)}, f32[7,8,128]{2,1,0:T(8,128)S(1)}, u32[]{:S(2)}, u32[]{:S(2)}) collective-permute-start(f32[7,8,128]{2,1,0:T(8,128)S(1)} %get-tuple-element.24), channel_id=1, source_target_pairs={{0,16},{8,24},{16,0},{24,8},{1,17},{9,25},{17,1},{25,9},{2,18},{10... | collective-permute-start | bytes 86024 | tf_op jit(solution)/shard_map/ppermute | solution.py:712
  70.0 5.7 %collective-permute-start.7 = (f32[7,8,128]{2,1,0:T(8,128)S(1)}, f32[7,8,128]{2,1,0:T(8,128)S(1)}, u32[]{:S(2)}, u32[]{:S(2)}) collective-permute-start(f32[7,8,128]{2,1,0:T(8,128)S(1)} %get-tuple-element.25), channel_id=1, source_target_pairs={{0,24},{8,16},{16,8},{24,0},{1,25},{9,17},{17,9},{25,1},{2,26},{10... | collective-permute-start | bytes 86024 | tf_op jit(solution)/shard_map/ppermute | solution.py:712
where the time goes:
time: 76.6 us; the launch traced here: 76.3 us
  blocking collectives  27.1 us (35%)
  Pallas kernels  22.2 us (29%)
  starting transfers between devices  14 us (18%)
  waiting for transfers between devices  12.2 us (16%)
    all_to_all x2, blocking collectives, on_slabs(): lax.all_to_all(sent, ('gx', 'gy'), split_axis=0, concat_axis=0, tiled=True)  27.1 us
    pallas_call x8, Pallas kernels, local_call(): pl.pallas_call(kernel, out_shape=[jax.ShapeDtypeStruct(shape, F32) for sh...  22.2 us
    ppermute x6, starting transfers between devices, across_planes(): lax.ppermute(parts[step], 'grp', [(i, i ^ step) for i in range(slab.grp)])  10.1 us
    ppermute x6, waiting for transfers between devices, across_planes(): lax.ppermute(parts[step], 'grp', [(i, i ^ step) for i in range(slab.grp)])  7.06 us
    ppermute x1, waiting for transfers between devices, exchange(): from_below = lax.ppermute(high, RING, upward)  5.15 us
    ppermute x1, starting transfers between devices, exchange(): from_above = lax.ppermute(low, RING, [(b, a) for a, b in upward])  3.81 us
  transfers between devices with their start and end apart: 8, of which 5 were waited for; matrix products, arithmetic and copies ran while one was open for 0% of the time, Pallas kernels for 5%

commit v1 on v0

--- a/solution.py
+++ b/solution.py
@@ -250,7 +250,14 @@
 
     def holders(self):
         even = lax.axis_index("grp") % 2 == 0
-        return [jnp.where(even, *pair) for pair in zip(self.snake, self.snake[::-1])]
+        mine = self.place_in_plane()
+        return [
+            jnp.bitwise_xor(jnp.where(even, *pair), mine)
+            for pair in zip(self.snake, self.snake[::-1])
+        ]
+
+    def place_in_plane(self):
+        return lax.axis_index("gx") * self.gy + lax.axis_index("gy")
 
 
 def lane_index():
@@ -367,7 +374,16 @@
     return lane_index() % slab.planes < slab.halo
 
 
-def offer_halo(slab, came, low_out, high_out):
+def collect(slab, parts, came):
+    mine = slab.place_in_plane()
+    for step in range(slab.sub):
+        came[jnp.bitwise_xor(mine, step)] = parts[step][...]
+
+
+def offer_halo(slab, *refs):
+    parts, (came, low_out, high_out) = refs[: slab.sub], refs[slab.sub :]
+    collect(slab, parts, came)
+
     def one(number, _):
         tile = 2 * number
         first = in_first_half(slab)
@@ -404,6 +420,7 @@
 def pack_out(slab, came, state, sent):
     def one(tile, _):
         even = (lane_index() // slab.planes) % 2 == 0
+        partner = jnp.bitwise_xor(tile, slab.place_in_plane())
         flags = came[tile, SOLID_AT // 2]
         solid = jnp.where(even, flags, lane_roll(flags, slab.planes)) != 0.0
         for pair in range(MOVING // 2):
@@ -413,7 +430,7 @@
                 value = jnp.where(solid, came[tile, pair], value)
             elif 2 * pair < SPEED_AT:
                 value = jnp.where(jnp.logical_and(solid, even), came[tile, pair], value)
-            sent[tile, pair] = value
+            sent[partner, pair] = value
         return 0
 
     lax.fori_loop(0, slab.sub, one, 0)
@@ -425,8 +442,15 @@
     return [values[0::2], values[1::2]]
 
 
-def return_heat(slab, came, *refs):
-    outs, held = refs[: slab.grp], refs[slab.grp]
+def return_heat(slab, *refs):
+    parts, came, outs, held = (
+        refs[: slab.sub],
+        refs[slab.sub],
+        refs[slab.sub + 1 : slab.sub + 1 + slab.grp],
+        refs[-1],
+    )
+    for step in range(slab.sub):
+        came[step] = parts[step][...]
     holders = slab.holders()
     _, values = unpack_pair(slab, came, SPEED_AT // 2, holders)
     for x in range(slab.block_x):
@@ -707,6 +731,14 @@
     return from_below, from_above
 
 
+def across_plane(slab, sent):
+    came = {0: sent[0]}
+    for step in sorted(range(1, slab.sub), key=lambda step: -bin(step >> 1).count("1")):
+        pairs = [(i, i ^ step) for i in range(slab.sub)]
+        came[step] = lax.ppermute(sent[step], ("gx", "gy"), pairs)
+    return [came[step] for step in range(slab.sub)]
+
+
 def across_planes(slab, parts):
     return [parts[0]] + [
         lax.ppermute(parts[step], "grp", [(i, i ^ step) for i in range(slab.grp)])
@@ -759,9 +791,10 @@
         ],
         carried=True,
     )
-    came = lax.all_to_all(sent, ("gx", "gy"), split_axis=0, concat_axis=0, tiled=True)
     halo_shape = (slab.sub // 2, ROWS // 2) + tile
-    low, high = local_call(offer_halo, slab, [came], [halo_shape, halo_shape])
+    came, low, high = local_call(
+        offer_halo, slab, across_plane(slab, sent), [sent_shape, halo_shape, halo_shape]
+    )
     below, above = exchange(slab, low, high)
     (sent,) = local_call(
         both_windows,
@@ -777,9 +810,12 @@
         ],
         in_hbm=1,
     )
-    came = lax.all_to_all(sent, ("gx", "gy"), split_axis=0, concat_axis=0, tiled=True)
-    parts = local_call(
-        return_heat, slab, [came], [(7,) + tile] * slab.grp, [(slab.grp, 7) + tile]
+    came, *parts = local_call(
+        return_heat,
+        slab,
+        across_plane(slab, sent),
+        [sent.shape] + [(7,) + tile] * slab.grp,
+        [(slab.grp, 7) + tile],
     )
     parts = across_planes(slab, parts)
     (populations_out,) = local_call(unpack_flow, slab, [came], [populations.shape])

time: 76.6 us -> 70.2 us (0.916)
  blocking collectives: 27.1 us -> 0 us
  starting transfers between devices: 14 us -> 25.5 us
  waiting for transfers between devices: 12.2 us -> 21.6 us
    all_to_all x2 -> x0, blocking collectives: 27.1 us -> none  [on_slabs(): lax.all_to_all(sent, ('gx', 'gy'), split_axis=0, concat_axis=0, tiled=True)]
    ppermute x0 -> x14, starting transfers between devices: none -> 11.4 us  [across_plane(): came[step] = lax.ppermute(sent[step], ('gx', 'gy'), pairs)]
    ppermute x0 -> x14, waiting for transfers between devices: none -> 9.22 us  [across_plane(): came[step] = lax.ppermute(sent[step], ('gx', 'gy'), pairs)]
  transfers between devices with their start and end apart: 8 -> 22, of which waited for: 5 -> 14; matrix products, arithmetic and copies ran while one was open for 0% -> 0% of each run, Pallas kernels for 5% -> 6%
where the time goes in v1:
time: 70.2 us; the launch traced here: 70 us
  starting transfers between devices  25.5 us (36%)
  Pallas kernels  22.2 us (32%)
  waiting for transfers between devices  21.6 us (31%)
  between operations  0.73 us (1%)
    pallas_call x8, Pallas kernels, local_call(): pl.pallas_call(kernel, out_shape=[jax.ShapeDtypeStruct(shape, F32) for sh...  22.2 us
    ppermute x14, starting transfers between devices, across_plane(): came[step] = lax.ppermute(sent[step], ('gx', 'gy'), pairs)  11.4 us
    ppermute x6, starting transfers between devices, across_planes(): lax.ppermute(parts[step], 'grp', [(i, i ^ step) for i in range(slab.grp)])  10.1 us
    ppermute x14, waiting for transfers between devices, across_plane(): came[step] = lax.ppermute(sent[step], ('gx', 'gy'), pairs)  9.22 us
    ppermute x6, waiting for transfers between devices, across_planes(): lax.ppermute(parts[step], 'grp', [(i, i ^ step) for i in range(slab.grp)])  7.2 us
    ppermute x1, waiting for transfers between devices, exchange(): from_below = lax.ppermute(high, RING, upward)  5.15 us
    ppermute x1, starting transfers between devices, exchange(): from_above = lax.ppermute(low, RING, [(b, a) for a, b in upward])  3.75 us
  transfers between devices with their start and end apart: 22, of which 14 were waited for; matrix products, arithmetic and copies ran while one was open for 0% of the time, Pallas kernels for 6%

profile of v1, /device:TPU:0, one launch (start us, length us, event | category | flops | bytes accessed | tf_op | source)
XLA Modules:
  0.0 70.0 jit_solution(6877231291182970603)
XLA Ops:
  0.6 1.0 %shard_map.87 = (f32[8,8,128]{2,1,0:T(8,128)S(1)}, f32[8,8,128]{2,1,0:T(8,128)S(1)}, f32[8,8,128]{2,1,0:T(8,128)S(1)}, f32[8,8,128]{2,1,0:T(8,128)S(1)}) custom-call(f32[4]{0:T(128)} %refs_0_.4, f32[7,1,8,512]{3,2,1,0:T(8,128)} %refs_1_.3, s32[1,8,512]{2,1,0:T(8,128)} %refs_2_.3), custom_call_target="tpu_custom_call" | custom-call | tf_op jit(solution)/shard_map/pallas_call | solution.py:702
  1.6 3.1 %collective-permute-start = (f32[8,8,128]{2,1,0:T(8,128)S(1)}, f32[8,8,128]{2,1,0:T(8,128)S(1)}, u32[]{:S(2)}, u32[]{:S(2)}) collective-permute-start(f32[8,8,128]{2,1,0:T(8,128)S(1)} %get-tuple-element.19), channel_id=1, source_target_pairs={{0,8},{8,0},{16,24},{24,16},{1,9},{9,1},{17,25},{25,17},{2,10},{10... | collective-permute-start | bytes 98312 | tf_op jit(solution)/shard_map/ppermute | solution.py:744
  4.7 2.6 %collective-permute-start.1 = (f32[8,8,128]{2,1,0:T(8,128)S(1)}, f32[8,8,128]{2,1,0:T(8,128)S(1)}, u32[]{:S(2)}, u32[]{:S(2)}) collective-permute-start(f32[8,8,128]{2,1,0:T(8,128)S(1)} %get-tuple-element.20), channel_id=1, source_target_pairs={{0,16},{8,24},{16,0},{24,8},{1,17},{9,25},{17,1},{25,9},{2,18},{10... | collective-permute-start | bytes 98312 | tf_op jit(solution)/shard_map/ppermute | solution.py:744
  7.3 0.0 collective-permute-start.2
  7.3 2.3 %shard_map.86 = (f32[8,20,8,128]{3,2,1,0:T(8,128)S(1)}, f32[4,8,128]{2,1,0:T(8,128)S(1)}) custom-call(f32[27,4,8,128]{3,2,1,0:T(8,128)} %refs_0_.3, f32[3,4,8,128]{3,2,1,0:T(8,128)} %refs_1_.2, s32[4,8,128]{2,1,0:T(8,128)} %refs_2_.2), custom_call_target="tpu_custom_call" | custom-call | tf_op jit(solution)/shard_map/pallas_call | solution.py:702
  9.6 0.0 collective-permute-done.refs_3_
  9.6 0.5 collective-permute-done.1.refs_4_
  10.1 2.9 %collective-permute-done.2.refs_5_ = f32[8,8,128]{2,1,0:T(8,128)S(1)} collective-permute-done((f32[8,8,128]{2,1,0:T(8,128)S(1)}, f32[8,8,128]{2,1,0:T(8,128)S(1)}, u32[]{:S(2)}, u32[]{:S(2)}) %collective-permute-start.2) | collective-permute-done | bytes 32800 | tf_op jit(solution)/shard_map/ppermute | solution.py:744
  13.0 0.3 shard_map.88
  13.4 0.3 collective-permute-start.9
  13.7 2.2 %collective-permute-start.8 = (f32[20,8,128]{2,1,0:T(8,128)S(1)}, f32[20,8,128]{2,1,0:T(8,128)S(1)}, u32[]{:S(2)}, u32[]{:S(2)}) collective-permute-start(f32[20,8,128]{2,1,0:T(8,128)S(1)} %get-tuple-element.31), channel_id=1, source_target_pairs={{0,6},{1,7},{2,4},{3,5},{4,2},{5,3},{6,0},{7,1},{8,14},{9,15},{10,... | collective-permute-start | bytes 245768 | tf_op jit(solution)/shard_map/ppermute | solution.py:738
  16.0 1.4 %collective-permute-start.7 = (f32[20,8,128]{2,1,0:T(8,128)S(1)}, f32[20,8,128]{2,1,0:T(8,128)S(1)}, u32[]{:S(2)}, u32[]{:S(2)}) collective-permute-start(f32[20,8,128]{2,1,0:T(8,128)S(1)} %get-tuple-element.32), channel_id=1, source_target_pairs={{0,5},{1,4},{2,7},{3,6},{4,1},{5,0},{6,3},{7,2},{8,13},{9,12},{10,... | collective-permute-start | bytes 245768 | tf_op jit(solution)/shard_map/ppermute | solution.py:738
  17.3 0.5 collective-permute-start.6
  17.8 0.7 %collective-permute-start.5 = (f32[20,8,128]{2,1,0:T(8,128)S(1)}, f32[20,8,128]{2,1,0:T(8,128)S(1)}, u32[]{:S(2)}, u32[]{:S(2)}) collective-permute-start(f32[20,8,128]{2,1,0:T(8,128)S(1)} %get-tuple-element.34), channel_id=1, source_target_pairs={{0,3},{1,2},{2,1},{3,0},{4,7},{5,6},{6,5},{7,4},{8,11},{9,10},{10,... | collective-permute-start | bytes 245768 | tf_op jit(solution)/shard_map/ppermute | solution.py:738
  18.6 0.4 collective-permute-done.9.refs_7_
  19.0 1.0 %collective-permute-start.4 = (f32[20,8,128]{2,1,0:T(8,128)S(1)}, f32[20,8,128]{2,1,0:T(8,128)S(1)}, u32[]{:S(2)}, u32[]{:S(2)}) collective-permute-start(f32[20,8,128]{2,1,0:T(8,128)S(1)} %get-tuple-element.35), channel_id=1, source_target_pairs={{0,2},{1,3},{2,0},{3,1},{4,6},{5,7},{6,4},{7,5},{8,10},{9,11},{10,... | collective-permute-start | bytes 245768 | tf_op jit(solution)/shard_map/ppermute | solution.py:738
  20.0 0.4 collective-permute-done.8.refs_6_
  20.5 0.3 collective-permute-start.3
  20.8 1.8 %collective-permute-done.7.refs_5_ = f32[20,8,128]{2,1,0:T(8,128)S(1)} collective-permute-done((f32[20,8,128]{2,1,0:T(8,128)S(1)}, f32[20,8,128]{2,1,0:T(8,128)S(1)}, u32[]{:S(2)}, u32[]{:S(2)}) %collective-permute-start.7) | collective-permute-done | bytes 81952 | tf_op jit(solution)/shard_map/ppermute | solution.py:738
  22.6 1.8 %collective-permute-done.6.refs_4_ = f32[20,8,128]{2,1,0:T(8,128)S(1)} collective-permute-done((f32[20,8,128]{2,1,0:T(8,128)S(1)}, f32[20,8,128]{2,1,0:T(8,128)S(1)}, u32[]{:S(2)}, u32[]{:S(2)}) %collective-permute-start.6) | collective-permute-done | bytes 81952 | tf_op jit(solution)/shard_map/ppermute | solution.py:738
  24.3 0.0 collective-permute-done.5.refs_3_
  24.4 0.0 collective-permute-done.4.refs_2_
  24.4 0.0 collective-permute-done.3.refs_1_
  24.4 0.5 shard_map.89
  24.9 0.1 collective-permute-start.10
  25.0 3.7 %collective-permute-start.11 = (f32[4,20,8,128]{3,2,1,0:T(8,128)S(1)}, f32[4,20,8,128]{3,2,1,0:T(8,128)S(1)}, u32[]{:S(2)}, u32[]{:S(2)}) collective-permute-start(f32[4,20,8,128]{3,2,1,0:T(8,128)S(1)} %get-tuple-element.24), channel_id=1, source_target_pairs={{0,24},{1,0},{2,1},{3,2},{7,3},{6,7},{5,6},{4,5},{12,4},{13,12},{1... | collective-permute-start | bytes 983048 | tf_op jit(solution)/shard_map/ppermute | solution.py:730
  28.8 5.2 %collective-permute-done.10.refs_2_ = f32[4,20,8,128]{3,2,1,0:T(8,128)S(1)} collective-permute-done((f32[4,20,8,128]{3,2,1,0:T(8,128)S(1)}, f32[4,20,8,128]{3,2,1,0:T(8,128)S(1)}, u32[]{:S(2)}, u32[]{:S(2)}) %collective-permute-start.10) | collective-permute-done | bytes 327712 | tf_op jit(solution)/shard_map/ppermute | solution.py:729
  33.9 0.0 collective-permute-done.11.refs_3_
  33.9 15.4 %shard_map.90 = f32[8,17,8,128]{3,2,1,0:T(8,128)S(1)} custom-call(f32[27]{0:T(128)} %refs_0_.5, f32[8,20,8,128]{3,2,1,0:T(8,128)S(1)} %get-tuple-element.22.refs_1_, f32[4,20,8,128]{3,2,1,0:T(8,128)S(1)} %collective-permute-done.10.refs_2_, f32[4,20,8,128]{3,2,1,0:T(8,128)S(1)} %collective-permute-done.11.refs_3_), custom_call_target="tpu_custom_call" | custom-call | tf_op jit(solution)/shard_map/pallas_call | solution.py:702
  49.4 0.1 collective-permute-start.18
  49.5 1.5 %collective-permute-start.17 = (f32[17,8,128]{2,1,0:T(8,128)S(1)}, f32[17,8,128]{2,1,0:T(8,128)S(1)}, u32[]{:S(2)}, u32[]{:S(2)}) collective-permute-start(f32[17,8,128]{2,1,0:T(8,128)S(1)} %get-tuple-element.39), channel_id=1, source_target_pairs={{0,6},{1,7},{2,4},{3,5},{4,2},{5,3},{6,0},{7,1},{8,14},{9,15},{10,... | collective-permute-start | bytes 208904 | tf_op jit(solution)/shard_map/ppermute | solution.py:738
  51.0 0.5 collective-permute-start.16
  51.5 2.4 %collective-permute-start.15 = (f32[17,8,128]{2,1,0:T(8,128)S(1)}, f32[17,8,128]{2,1,0:T(8,128)S(1)}, u32[]{:S(2)}, u32[]{:S(2)}) collective-permute-start(f32[17,8,128]{2,1,0:T(8,128)S(1)} %get-tuple-element.41), channel_id=1, source_target_pairs={{0,4},{1,5},{2,6},{3,7},{4,0},{5,1},{6,2},{7,3},{8,12},{9,13},{10,... | collective-permute-start | bytes 208904 | tf_op jit(solution)/shard_map/ppermute | solution.py:738
  53.9 0.0 collective-permute-start.14
  53.9 0.4 collective-permute-done.18.refs_7_
  54.3 0.3 collective-permute-start.13
  54.5 1.0 %collective-permute-done.17.refs_6_ = f32[17,8,128]{2,1,0:T(8,128)S(1)} collective-permute-done((f32[17,8,128]{2,1,0:T(8,128)S(1)}, f32[17,8,128]{2,1,0:T(8,128)S(1)}, u32[]{:S(2)}, u32[]{:S(2)}) %collective-permute-start.17) | collective-permute-done | bytes 69664 | tf_op jit(solution)/shard_map/ppermute | solution.py:738
  55.5 0.2 collective-permute-start.12
  55.7 1.3 %collective-permute-done.16.refs_5_ = f32[17,8,128]{2,1,0:T(8,128)S(1)} collective-permute-done((f32[17,8,128]{2,1,0:T(8,128)S(1)}, f32[17,8,128]{2,1,0:T(8,128)S(1)}, u32[]{:S(2)}, u32[]{:S(2)}) %collective-permute-start.16) | collective-permute-done | bytes 69664 | tf_op jit(solution)/shard_map/ppermute | solution.py:738
  57.0 1.6 %collective-permute-done.15.refs_4_ = f32[17,8,128]{2,1,0:T(8,128)S(1)} collective-permute-done((f32[17,8,128]{2,1,0:T(8,128)S(1)}, f32[17,8,128]{2,1,0:T(8,128)S(1)}, u32[]{:S(2)}, u32[]{:S(2)}) %collective-permute-start.15) | collective-permute-done | bytes 69664 | tf_op jit(solution)/shard_map/ppermute | solution.py:738
  58.6 0.0 collective-permute-done.14.refs_3_
  58.6 0.5 collective-permute-done.13.refs_2_
  59.1 0.0 collective-permute-done.12.refs_1_
  59.1 0.3 shard_map.91
  59.4 1.3 %collective-permute-start.19 = (f32[7,8,128]{2,1,0:T(8,128)S(1)}, f32[7,8,128]{2,1,0:T(8,128)S(1)}, u32[]{:S(2)}, u32[]{:S(2)}) collective-permute-start(f32[7,8,128]{2,1,0:T(8,128)S(1)} %get-tuple-element.27), channel_id=1, source_target_pairs={{0,8},{8,0},{16,24},{24,16},{1,9},{9,1},{17,25},{25,17},{2,10},{10... | collective-permute-start | bytes 86024 | tf_op jit(solution)/shard_map/ppermute | solution.py:744
  60.7 3.0 %collective-permute-start.20 = (f32[7,8,128]{2,1,0:T(8,128)S(1)}, f32[7,8,128]{2,1,0:T(8,128)S(1)}, u32[]{:S(2)}, u32[]{:S(2)}) collective-permute-start(f32[7,8,128]{2,1,0:T(8,128)S(1)} %get-tuple-element.28), channel_id=1, source_target_pairs={{0,16},{8,24},{16,0},{24,8},{1,17},{9,25},{17,1},{25,9},{2,18},{10... | collective-permute-start | bytes 86024 | tf_op jit(solution)/shard_map/ppermute | solution.py:744
  63.7 0.1 collective-permute-start.21
  63.8 1.8 %shard_map.92 = f32[27,4,8,128]{3,2,1,0:T(8,128)} custom-call(f32[8,17,8,128]{3,2,1,0:T(8,128)S(1)} %get-tuple-element.25.refs_0_), custom_call_target="tpu_custom_call" | custom-call | tf_op jit(solution)/shard_map/pallas_call | solution.py:702
  65.6 0.0 collective-permute-done.19.refs_1_
  65.6 0.4 collective-permute-done.20.refs_2_
  66.0 3.4 %collective-permute-done.21.refs_3_ = f32[7,8,128]{2,1,0:T(8,128)S(1)} collective-permute-done((f32[7,8,128]{2,1,0:T(8,128)S(1)}, f32[7,8,128]{2,1,0:T(8,128)S(1)}, u32[]{:S(2)}, u32[]{:S(2)}) %collective-permute-start.21) | collective-permute-done | bytes 28704 | tf_op jit(solution)/shard_map/ppermute | solution.py:744
  69.4 0.7 shard_map.93
  (2 shorter events, 0.1 us)
Async XLA Ops:
  1.6 8.0 %collective-permute-start = (f32[8,8,128]{2,1,0:T(8,128)S(1)}, f32[8,8,128]{2,1,0:T(8,128)S(1)}, u32[]{:S(2)}, u32[]{:S(2)}) collective-permute-start(f32[8,8,128]{2,1,0:T(8,128)S(1)} %get-tuple-element.19), channel_id=1, source_target_pairs={{0,8},{8,0},{16,24},{24,16},{1,9},{9,1},{17,25},{25,17},{2,10},{10... | collective-permute-start | bytes 98312 | tf_op jit(solution)/shard_map/ppermute | solution.py:744
  4.7 5.4 %collective-permute-start.1 = (f32[8,8,128]{2,1,0:T(8,128)S(1)}, f32[8,8,128]{2,1,0:T(8,128)S(1)}, u32[]{:S(2)}, u32[]{:S(2)}) collective-permute-start(f32[8,8,128]{2,1,0:T(8,128)S(1)} %get-tuple-element.20), channel_id=1, source_target_pairs={{0,16},{8,24},{16,0},{24,8},{1,17},{9,25},{17,1},{25,9},{2,18},{10... | collective-permute-start | bytes 98312 | tf_op jit(solution)/shard_map/ppermute | solution.py:744
  7.3 5.7 %collective-permute-start.2 = (f32[8,8,128]{2,1,0:T(8,128)S(1)}, f32[8,8,128]{2,1,0:T(8,128)S(1)}, u32[]{:S(2)}, u32[]{:S(2)}) collective-permute-start(f32[8,8,128]{2,1,0:T(8,128)S(1)} %get-tuple-element.21), channel_id=1, source_target_pairs={{0,24},{8,16},{16,8},{24,0},{1,25},{9,17},{17,9},{25,1},{2,26},{10... | collective-permute-start | bytes 98312 | tf_op jit(solution)/shard_map/ppermute | solution.py:744
  13.4 5.6 %collective-permute-start.9 = (f32[20,8,128]{2,1,0:T(8,128)S(1)}, f32[20,8,128]{2,1,0:T(8,128)S(1)}, u32[]{:S(2)}, u32[]{:S(2)}) collective-permute-start(f32[20,8,128]{2,1,0:T(8,128)S(1)} %get-tuple-element.30), channel_id=1, source_target_pairs={{0,7},{1,6},{2,5},{3,4},{4,3},{5,2},{6,1},{7,0},{8,15},{9,14},{10,... | collective-permute-start | bytes 245768 | tf_op jit(solution)/shard_map/ppermute | solution.py:738
  13.7 6.7 %collective-permute-start.8 = (f32[20,8,128]{2,1,0:T(8,128)S(1)}, f32[20,8,128]{2,1,0:T(8,128)S(1)}, u32[]{:S(2)}, u32[]{:S(2)}) collective-permute-start(f32[20,8,128]{2,1,0:T(8,128)S(1)} %get-tuple-element.31), channel_id=1, source_target_pairs={{0,6},{1,7},{2,4},{3,5},{4,2},{5,3},{6,0},{7,1},{8,14},{9,15},{10,... | collective-permute-start | bytes 245768 | tf_op jit(solution)/shard_map/ppermute | solution.py:738
  16.0 6.6 %collective-permute-start.7 = (f32[20,8,128]{2,1,0:T(8,128)S(1)}, f32[20,8,128]{2,1,0:T(8,128)S(1)}, u32[]{:S(2)}, u32[]{:S(2)}) collective-permute-start(f32[20,8,128]{2,1,0:T(8,128)S(1)} %get-tuple-element.32), channel_id=1, source_target_pairs={{0,5},{1,4},{2,7},{3,6},{4,1},{5,0},{6,3},{7,2},{8,13},{9,12},{10,... | collective-permute-start | bytes 245768 | tf_op jit(solution)/shard_map/ppermute | solution.py:738
  17.3 7.0 %collective-permute-start.6 = (f32[20,8,128]{2,1,0:T(8,128)S(1)}, f32[20,8,128]{2,1,0:T(8,128)S(1)}, u32[]{:S(2)}, u32[]{:S(2)}) collective-permute-start(f32[20,8,128]{2,1,0:T(8,128)S(1)} %get-tuple-element.33), channel_id=1, source_target_pairs={{0,4},{1,5},{2,6},{3,7},{4,0},{5,1},{6,2},{7,3},{8,12},{9,13},{10,... | collective-permute-start | bytes 245768 | tf_op jit(solution)/shard_map/ppermute | solution.py:738
  17.8 6.5 %collective-permute-start.5 = (f32[20,8,128]{2,1,0:T(8,128)S(1)}, f32[20,8,128]{2,1,0:T(8,128)S(1)}, u32[]{:S(2)}, u32[]{:S(2)}) collective-permute-start(f32[20,8,128]{2,1,0:T(8,128)S(1)} %get-tuple-element.34), channel_id=1, source_target_pairs={{0,3},{1,2},{2,1},{3,0},{4,7},{5,6},{6,5},{7,4},{8,11},{9,10},{10,... | collective-permute-start | bytes 245768 | tf_op jit(solution)/shard_map/ppermute | solution.py:738
  19.0 5.4 %collective-permute-start.4 = (f32[20,8,128]{2,1,0:T(8,128)S(1)}, f32[20,8,128]{2,1,0:T(8,128)S(1)}, u32[]{:S(2)}, u32[]{:S(2)}) collective-permute-start(f32[20,8,128]{2,1,0:T(8,128)S(1)} %get-tuple-element.35), channel_id=1, source_target_pairs={{0,2},{1,3},{2,0},{3,1},{4,6},{5,7},{6,4},{7,5},{8,10},{9,11},{10,... | collective-permute-start | bytes 245768 | tf_op jit(solution)/shard_map/ppermute | solution.py:738
  20.5 3.9 %collective-permute-start.3 = (f32[20,8,128]{2,1,0:T(8,128)S(1)}, f32[20,8,128]{2,1,0:T(8,128)S(1)}, u32[]{:S(2)}, u32[]{:S(2)}) collective-permute-start(f32[20,8,128]{2,1,0:T(8,128)S(1)} %get-tuple-element.36), channel_id=1, source_target_pairs={{0,1},{1,0},{2,3},{3,2},{4,5},{5,4},{6,7},{7,6},{8,9},{9,8},{10,11... | collective-permute-start | bytes 245768 | tf_op jit(solution)/shard_map/ppermute | solution.py:738
  24.9 9.0 %collective-permute-start.10 = (f32[4,20,8,128]{3,2,1,0:T(8,128)S(1)}, f32[4,20,8,128]{3,2,1,0:T(8,128)S(1)}, u32[]{:S(2)}, u32[]{:S(2)}) collective-permute-start(f32[4,20,8,128]{3,2,1,0:T(8,128)S(1)} %get-tuple-element.23), channel_id=1, source_target_pairs={{24,0},{0,1},{1,2},{2,3},{3,7},{7,6},{6,5},{5,4},{4,12},{12,13},{1... | collective-permute-start | bytes 983048 | tf_op jit(solution)/shard_map/ppermute | solution.py:729
  25.0 8.9 %collective-permute-start.11 = (f32[4,20,8,128]{3,2,1,0:T(8,128)S(1)}, f32[4,20,8,128]{3,2,1,0:T(8,128)S(1)}, u32[]{:S(2)}, u32[]{:S(2)}) collective-permute-start(f32[4,20,8,128]{3,2,1,0:T(8,128)S(1)} %get-tuple-element.24), channel_id=1, source_target_pairs={{0,24},{1,0},{2,1},{3,2},{7,3},{6,7},{5,6},{4,5},{12,4},{13,12},{1... | collective-permute-start | bytes 983048 | tf_op jit(solution)/shard_map/ppermute | solution.py:730
  49.4 4.9 %collective-permute-start.18 = (f32[17,8,128]{2,1,0:T(8,128)S(1)}, f32[17,8,128]{2,1,0:T(8,128)S(1)}, u32[]{:S(2)}, u32[]{:S(2)}) collective-permute-start(f32[17,8,128]{2,1,0:T(8,128)S(1)} %get-tuple-element.38), channel_id=1, source_target_pairs={{0,7},{1,6},{2,5},{3,4},{4,3},{5,2},{6,1},{7,0},{8,15},{9,14},{10,... | collective-permute-start | bytes 208904 | tf_op jit(solution)/shard_map/ppermute | solution.py:738
  49.5 6.1 %collective-permute-start.17 = (f32[17,8,128]{2,1,0:T(8,128)S(1)}, f32[17,8,128]{2,1,0:T(8,128)S(1)}, u32[]{:S(2)}, u32[]{:S(2)}) collective-permute-start(f32[17,8,128]{2,1,0:T(8,128)S(1)} %get-tuple-element.39), channel_id=1, source_target_pairs={{0,6},{1,7},{2,4},{3,5},{4,2},{5,3},{6,0},{7,1},{8,14},{9,15},{10,... | collective-permute-start | bytes 208904 | tf_op jit(solution)/shard_map/ppermute | solution.py:738
  51.0 6.0 %collective-permute-start.16 = (f32[17,8,128]{2,1,0:T(8,128)S(1)}, f32[17,8,128]{2,1,0:T(8,128)S(1)}, u32[]{:S(2)}, u32[]{:S(2)}) collective-permute-start(f32[17,8,128]{2,1,0:T(8,128)S(1)} %get-tuple-element.40), channel_id=1, source_target_pairs={{0,5},{1,4},{2,7},{3,6},{4,1},{5,0},{6,3},{7,2},{8,13},{9,12},{10,... | collective-permute-start | bytes 208904 | tf_op jit(solution)/shard_map/ppermute | solution.py:738
  51.5 7.1 %collective-permute-start.15 = (f32[17,8,128]{2,1,0:T(8,128)S(1)}, f32[17,8,128]{2,1,0:T(8,128)S(1)}, u32[]{:S(2)}, u32[]{:S(2)}) collective-permute-start(f32[17,8,128]{2,1,0:T(8,128)S(1)} %get-tuple-element.41), channel_id=1, source_target_pairs={{0,4},{1,5},{2,6},{3,7},{4,0},{5,1},{6,2},{7,3},{8,12},{9,13},{10,... | collective-permute-start | bytes 208904 | tf_op jit(solution)/shard_map/ppermute | solution.py:738
  53.9 4.7 %collective-permute-start.14 = (f32[17,8,128]{2,1,0:T(8,128)S(1)}, f32[17,8,128]{2,1,0:T(8,128)S(1)}, u32[]{:S(2)}, u32[]{:S(2)}) collective-permute-start(f32[17,8,128]{2,1,0:T(8,128)S(1)} %get-tuple-element.42), channel_id=1, source_target_pairs={{0,3},{1,2},{2,1},{3,0},{4,7},{5,6},{6,5},{7,4},{8,11},{9,10},{10,... | collective-permute-start | bytes 208904 | tf_op jit(solution)/shard_map/ppermute | solution.py:738
  54.3 4.8 %collective-permute-start.13 = (f32[17,8,128]{2,1,0:T(8,128)S(1)}, f32[17,8,128]{2,1,0:T(8,128)S(1)}, u32[]{:S(2)}, u32[]{:S(2)}) collective-permute-start(f32[17,8,128]{2,1,0:T(8,128)S(1)} %get-tuple-element.43), channel_id=1, source_target_pairs={{0,2},{1,3},{2,0},{3,1},{4,6},{5,7},{6,4},{7,5},{8,10},{9,11},{10,... | collective-permute-start | bytes 208904 | tf_op jit(solution)/shard_map/ppermute | solution.py:738
  55.5 3.5 %collective-permute-start.12 = (f32[17,8,128]{2,1,0:T(8,128)S(1)}, f32[17,8,128]{2,1,0:T(8,128)S(1)}, u32[]{:S(2)}, u32[]{:S(2)}) collective-permute-start(f32[17,8,128]{2,1,0:T(8,128)S(1)} %get-tuple-element.44), channel_id=1, source_target_pairs={{0,1},{1,0},{2,3},{3,2},{4,5},{5,4},{6,7},{7,6},{8,9},{9,8},{10,11... | collective-permute-start | bytes 208904 | tf_op jit(solution)/shard_map/ppermute | solution.py:738
  59.4 6.2 %collective-permute-start.19 = (f32[7,8,128]{2,1,0:T(8,128)S(1)}, f32[7,8,128]{2,1,0:T(8,128)S(1)}, u32[]{:S(2)}, u32[]{:S(2)}) collective-permute-start(f32[7,8,128]{2,1,0:T(8,128)S(1)} %get-tuple-element.27), channel_id=1, source_target_pairs={{0,8},{8,0},{16,24},{24,16},{1,9},{9,1},{17,25},{25,17},{2,10},{10... | collective-permute-start | bytes 86024 | tf_op jit(solution)/shard_map/ppermute | solution.py:744
  60.7 5.3 %collective-permute-start.20 = (f32[7,8,128]{2,1,0:T(8,128)S(1)}, f32[7,8,128]{2,1,0:T(8,128)S(1)}, u32[]{:S(2)}, u32[]{:S(2)}) collective-permute-start(f32[7,8,128]{2,1,0:T(8,128)S(1)} %get-tuple-element.28), channel_id=1, source_target_pairs={{0,16},{8,24},{16,0},{24,8},{1,17},{9,25},{17,1},{25,9},{2,18},{10... | collective-permute-start | bytes 86024 | tf_op jit(solution)/shard_map/ppermute | solution.py:744
  63.7 5.7 %collective-permute-start.21 = (f32[7,8,128]{2,1,0:T(8,128)S(1)}, f32[7,8,128]{2,1,0:T(8,128)S(1)}, u32[]{:S(2)}, u32[]{:S(2)}) collective-permute-start(f32[7,8,128]{2,1,0:T(8,128)S(1)} %get-tuple-element.29), channel_id=1, source_target_pairs={{0,24},{8,16},{16,8},{24,0},{1,25},{9,17},{17,9},{25,1},{2,26},{10... | collective-permute-start | bytes 86024 | tf_op jit(solution)/shard_map/ppermute | solution.py:744

commit v2 on v1

--- a/solution.py
+++ b/solution.py
@@ -235,25 +235,27 @@
             and self.sub & (self.sub - 1) == 0
             and self.grp & (self.grp - 1) == 0
             and self.gy % 2 == 0
+            and self.sub % self.grp == 0
         )
         if self.fits:
-            self.snake = [
-                x * self.gy + (y if x % 2 == 0 else self.gy - 1 - y)
-                for x in range(self.gx)
-                for y in range(self.gy)
-            ]
+            self.turn = self.sub // self.grp
             self.ring = [
-                part * self.sub + self.snake[place if part % 2 == 0 else self.sub - 1 - place]
+                part * self.sub + self.round_plane((place - self.turn * part) % self.sub)
                 for part in range(self.grp)
                 for place in range(self.sub)
             ]
 
+    def round_plane(self, number):
+        x, y = number // self.gy, number % self.gy
+        back = x % 2
+        return x * self.gy + y + back * (self.gy - 1 - 2 * y)
+
     def holders(self):
-        even = lax.axis_index("grp") % 2 == 0
+        begin = self.sub * self.grp - self.turn * lax.axis_index("grp")
         mine = self.place_in_plane()
         return [
-            jnp.bitwise_xor(jnp.where(even, *pair), mine)
-            for pair in zip(self.snake, self.snake[::-1])
+            jnp.bitwise_xor(self.round_plane(lax.rem(begin + place, self.sub)), mine)
+            for place in range(self.sub)
         ]
 
     def place_in_plane(self):
@@ -571,14 +573,24 @@
 HEAT_OFFSETS = [(0, 0, 0), (1, 0, 0), (-1, 0, 0), (0, 1, 0), (0, -1, 0), (0, 0, 1), (0, 0, -1)]
 
 
-def run_steps(slab, rates_ref, state, post, force_ref):
-    def collide_one(tile, _):
-        values = [state[n, tile] for n in range(27)]
+class Lattices:
+    def __init__(self, slab, rates_ref, state, post, force_ref):
+        self.slab, self.rates_ref = slab, rates_ref
+        self.state, self.post, self.force_ref = state, post, force_ref
+
+    def speeds(self, tile):
+        return [self.state[SPEED_AT + d, tile] for d in range(3)]
+
+    def held(self, tile):
+        flow = [self.state[n, tile] for n in range(27)]
+        return flow, [self.state[HEAT_AT + k, tile] for k in range(7)]
+
+    def collide(self, tile, flow, heat, force, speeds, target):
+        state, post = self.state, self.post
         solid = state[SOLID_AT, tile] != 0.0
-        moved = collide_tile(values, force_ref[tile], lambda n: rates_ref[n])
+        moved = collide_tile(flow, force, lambda n: self.rates_ref[n])
         for n in range(27):
-            post[n, tile] = jnp.where(solid, jnp.nan, moved[n])
-        heat = [state[HEAT_AT + k, tile] for k in range(7)]
+            post[target, n, tile] = jnp.where(solid, jnp.nan, moved[n])
         total = heat[0]
         for k in range(1, 7):
             total = total + heat[k]
@@ -589,12 +601,12 @@
             if k == 0:
                 level = 0.25 * total
             else:
-                drift = half * state[SPEED_AT + (k - 1) // 2, tile]
+                drift = half * speeds[(k - 1) // 2]
                 level = side + drift if k % 2 == 1 else side - drift
-            post[SPEED_AT + k, tile] = heat[k] - (heat[k] - level) * omega
-        return 0
-
-    def stream_one(tile, _):
+            post[target, SPEED_AT + k, tile] = heat[k] - (heat[k] - level) * omega
+
+    def stream(self, tile, source):
+        slab, post = self.slab, self.post
         block_x, block_y = tile // slab.gy, tile % slab.gy
         x_of = {a: lax.rem(block_x + slab.gx - a, slab.gx) for a in (-1, 0, 1)}
         y_of = {b: lax.rem(block_y + slab.gy - b, slab.gy) for b in (-1, 0, 1)}
@@ -608,9 +620,9 @@
             a, b, c = offset
 
             def take(x):
-                value = post[number, x_of[x] * slab.gy + block_y]
+                value = post[source, number, x_of[x] * slab.gy + block_y]
                 if b != 0:
-                    other = post[number, x_of[x] * slab.gy + y_of[b]]
+                    other = post[source, number, x_of[x] * slab.gy + y_of[b]]
                     value = jnp.where(last_y[b], other, value)
                 return value
 
@@ -621,30 +633,87 @@
                 value = pltpu.roll(value, b % SUBLANES, 0)
             return lane_roll(value, a * per_x + c)
 
+        flow = []
         for n in range(27):
             value = arrive(n, OFFSET_TABLE[n])
-            state[n, tile] = jnp.where(value != value, post[26 - n, tile], value)
-        for k in range(7):
-            state[HEAT_AT + k, tile] = arrive(SPEED_AT + k, HEAT_OFFSETS[k])
+            flow.append(jnp.where(value != value, post[source, 26 - n, tile], value))
+        return flow, [arrive(SPEED_AT + k, HEAT_OFFSETS[k]) for k in range(7)]
+
+
+def run_windows(slab, rates_ref, state, post, force_ref):
+    lattices = Lattices(slab, rates_ref, state, post, force_ref)
+
+    def over_tiles(body):
+        def one(tile, _):
+            body(tile)
+            return 0
+
+        lax.fori_loop(0, slab.sub, one, 0)
+
+    def begin(tile):
+        flow, heat = lattices.held(tile)
+        force = heat_force(heat)
+        force_ref[tile] = force
+        lattices.collide(tile, flow, heat, force, lattices.speeds(tile), 0)
+
+    over_tiles(begin)
+
+    def one_window(window, _):
+        def step(number, _):
+            source = lax.rem(window * STEPS + number, 2)
+
+            def go_on(tile):
+                flow, heat = lattices.stream(tile, source)
+                lattices.collide(
+                    tile, flow, heat, force_ref[tile], lattices.speeds(tile), 1 - source
+                )
+
+            over_tiles(go_on)
+            return 0
+
+        lax.fori_loop(0, STEPS - 1, step, 0)
+        source = lax.rem(window * STEPS + STEPS - 1, 2)
+
+        @pl.when(window + 1 < WINDOWS)
+        def _():
+            def next_window(tile):
+                flow, heat = lattices.stream(tile, source)
+                solid = state[SOLID_AT, tile] != 0.0
+                speeds = [
+                    jnp.where(solid, 0.0, each) for each in flow_speed_tile(flow, force_ref[tile])
+                ]
+                for d in range(3):
+                    state[SPEED_AT + d, tile] = speeds[d]
+                force = heat_force(heat)
+                force_ref[tile] = force
+                lattices.collide(tile, flow, heat, force, speeds, 1 - source)
+
+            over_tiles(next_window)
+
+        @pl.when(window + 1 == WINDOWS)
+        def _():
+            def end(tile):
+                flow, heat = lattices.stream(tile, source)
+                for n in range(27):
+                    state[n, tile] = flow[n]
+                for k in range(7):
+                    state[HEAT_AT + k, tile] = heat[k]
+
+            over_tiles(end)
+
         return 0
 
-    def step(number, _):
-        lax.fori_loop(0, slab.sub, collide_one, 0)
-        lax.fori_loop(0, slab.sub, stream_one, 0)
-        return 0
-
-    lax.fori_loop(0, STEPS, step, 0)
-
-
-def heat_force(state, tile):
-    total = state[HEAT_AT, tile]
+    lax.fori_loop(0, WINDOWS, one_window, 0)
+
+
+def heat_force(heat):
+    total = heat[0]
     for k in range(1, 7):
-        total = total + state[HEAT_AT + k, tile]
+        total = total + heat[k]
     return BUOYANCY * (total - REFERENCE_HEAT)
 
 
-def flow_speed_tile(state, tile, force):
-    values = [state[n, tile] for n in range(27)]
+def flow_speed_tile(values, force):
     total = values[0]
     for n in range(1, 27):
         total = total + values[n]
@@ -667,31 +736,8 @@
     rates_copy = pltpu.make_async_copy(rates_hbm, rates_ref, sem)
     rates_copy.start()
     make_tiles(slab, came, below_ref, above_ref, state)
-
-    def first_force(tile, _):
-        force[tile] = heat_force(state, tile)
-        return 0
-
-    lax.fori_loop(0, slab.sub, first_force, 0)
     rates_copy.wait()
-
-    def next_speed(tile, _):
-        solid = state[SOLID_AT, tile] != 0.0
-        for d, each in enumerate(flow_speed_tile(state, tile, force[tile])):
-            state[SPEED_AT + d, tile] = jnp.where(solid, 0.0, each)
-        force[tile] = heat_force(state, tile)
-        return 0
-
-    def one_window(window, _):
-        run_steps(slab, rates_ref, state, post, force)
-
-        @pl.when(window + 1 < WINDOWS)
-        def _():
-            lax.fori_loop(0, slab.sub, next_speed, 0)
-
-        return 0
-
-    lax.fori_loop(0, WINDOWS, one_window, 0)
+    run_windows(slab, rates_ref, state, post, force)
     pack_out(slab, came, state, sent)
 
 
@@ -733,7 +779,9 @@
 
 def across_plane(slab, sent):
     came = {0: sent[0]}
-    for step in sorted(range(1, slab.sub), key=lambda step: -bin(step >> 1).count("1")):
+    far_first = [step for k in range(2) for step in range(2 + k, slab.sub, 2)] + [1]
+    far_first.sort(key=lambda step: -bin(step >> 1).count("1"))
+    for step in far_first:
         pairs = [(i, i ^ step) for i in range(slab.sub)]
         came[step] = lax.ppermute(sent[step], ("gx", "gy"), pairs)
     return [came[step] for step in range(slab.sub)]
@@ -805,7 +853,7 @@
             pltpu.SMEM(rates.shape, F32),
             pltpu.SemaphoreType.DMA,
             (ROWS, slab.sub) + tile,
-            (MOVING, slab.sub) + tile,
+            (2, MOVING, slab.sub) + tile,
             (slab.sub,) + tile,
         ],
         in_hbm=1,

time: 70.2 us -> 68 us (0.969)
  Pallas kernels: 22.2 us -> 20.2 us
    pallas_call x8, Pallas kernels: 22.2 us -> 20.2 us  [local_call(): pl.pallas_call(kernel, out_shape=[jax.ShapeDtypeStruct(shape, F32) for sh...]
    ppermute x14, waiting for transfers between devices: 9.22 us -> 9.93 us  [across_plane(): came[step] = lax.ppermute(sent[step], ('gx', 'gy'), pairs)]
  transfers between devices with their start and end apart: 22 -> 22, of which waited for: 14 -> 13; matrix products, arithmetic and copies ran while one was open for 0% -> 0% of each run, Pallas kernels for 6% -> 6%
where the time goes in v2:
time: 68 us; the launch traced here: 67.9 us
  starting transfers between devices  25.1 us (37%)
  waiting for transfers between devices  21.7 us (32%)
  Pallas kernels  20.2 us (30%)
  between operations  0.74 us (1%)
    pallas_call x8, Pallas kernels, local_call(): pl.pallas_call(kernel, out_shape=[jax.ShapeDtypeStruct(shape, F32) for sh...  20.2 us
    ppermute x14, starting transfers between devices, across_plane(): came[step] = lax.ppermute(sent[step], ('gx', 'gy'), pairs)  11.4 us
    ppermute x6, starting transfers between devices, across_planes(): lax.ppermute(parts[step], 'grp', [(i, i ^ step) for i in range(slab.grp)])  10.1 us
    ppermute x14, waiting for transfers between devices, across_plane(): came[step] = lax.ppermute(sent[step], ('gx', 'gy'), pairs)  9.93 us
    ppermute x6, waiting for transfers between devices, across_planes(): lax.ppermute(parts[step], 'grp', [(i, i ^ step) for i in range(slab.grp)])  7.02 us
    ppermute x1, waiting for transfers between devices, exchange(): from_below = lax.ppermute(high, RING, upward)  4.75 us
    ppermute x1, starting transfers between devices, exchange(): from_above = lax.ppermute(low, RING, [(b, a) for a, b in upward])  3.47 us
  transfers between devices with their start and end apart: 22, of which 13 were waited for; matrix products, arithmetic and copies ran while one was open for 0% of the time, Pallas kernels for 6%

profile of v2, /device:TPU:0, one launch (start us, length us, event | category | flops | bytes accessed | tf_op | source)
XLA Modules:
  0.0 67.9 jit_solution(5062871618471606073)
XLA Ops:
  0.6 1.0 %shard_map.87 = (f32[8,8,128]{2,1,0:T(8,128)S(1)}, f32[8,8,128]{2,1,0:T(8,128)S(1)}, f32[8,8,128]{2,1,0:T(8,128)S(1)}, f32[8,8,128]{2,1,0:T(8,128)S(1)}) custom-call(f32[4]{0:T(128)} %refs_0_.4, f32[7,1,8,512]{3,2,1,0:T(8,128)} %refs_1_.3, s32[1,8,512]{2,1,0:T(8,128)} %refs_2_.3), custom_call_target="tpu_custom_call" | custom-call | tf_op jit(solution)/shard_map/pallas_call | solution.py:748
  1.6 3.1 %collective-permute-start = (f32[8,8,128]{2,1,0:T(8,128)S(1)}, f32[8,8,128]{2,1,0:T(8,128)S(1)}, u32[]{:S(2)}, u32[]{:S(2)}) collective-permute-start(f32[8,8,128]{2,1,0:T(8,128)S(1)} %get-tuple-element.19), channel_id=1, source_target_pairs={{0,8},{8,0},{16,24},{24,16},{1,9},{9,1},{17,25},{25,17},{2,10},{10... | collective-permute-start | bytes 98312 | tf_op jit(solution)/shard_map/ppermute | solution.py:792
  4.7 2.6 %collective-permute-start.1 = (f32[8,8,128]{2,1,0:T(8,128)S(1)}, f32[8,8,128]{2,1,0:T(8,128)S(1)}, u32[]{:S(2)}, u32[]{:S(2)}) collective-permute-start(f32[8,8,128]{2,1,0:T(8,128)S(1)} %get-tuple-element.20), channel_id=1, source_target_pairs={{0,16},{8,24},{16,0},{24,8},{1,17},{9,25},{17,1},{25,9},{2,18},{10... | collective-permute-start | bytes 98312 | tf_op jit(solution)/shard_map/ppermute | solution.py:792
  7.3 0.0 collective-permute-start.2
  7.3 2.3 %shard_map.86 = (f32[8,20,8,128]{3,2,1,0:T(8,128)S(1)}, f32[4,8,128]{2,1,0:T(8,128)S(1)}) custom-call(f32[27,4,8,128]{3,2,1,0:T(8,128)} %refs_0_.3, f32[3,4,8,128]{3,2,1,0:T(8,128)} %refs_1_.2, s32[4,8,128]{2,1,0:T(8,128)} %refs_2_.2), custom_call_target="tpu_custom_call" | custom-call | tf_op jit(solution)/shard_map/pallas_call | solution.py:748
  9.6 0.0 collective-permute-done.refs_3_
  9.6 0.5 collective-permute-done.1.refs_4_
  10.1 2.9 %collective-permute-done.2.refs_5_ = f32[8,8,128]{2,1,0:T(8,128)S(1)} collective-permute-done((f32[8,8,128]{2,1,0:T(8,128)S(1)}, f32[8,8,128]{2,1,0:T(8,128)S(1)}, u32[]{:S(2)}, u32[]{:S(2)}) %collective-permute-start.2) | collective-permute-done | bytes 32800 | tf_op jit(solution)/shard_map/ppermute | solution.py:792
  13.0 0.3 shard_map.88
  13.4 0.3 collective-permute-start.9
  13.7 2.2 %collective-permute-start.8 = (f32[20,8,128]{2,1,0:T(8,128)S(1)}, f32[20,8,128]{2,1,0:T(8,128)S(1)}, u32[]{:S(2)}, u32[]{:S(2)}) collective-permute-start(f32[20,8,128]{2,1,0:T(8,128)S(1)} %get-tuple-element.31), channel_id=1, source_target_pairs={{0,6},{1,7},{2,4},{3,5},{4,2},{5,3},{6,0},{7,1},{8,14},{9,15},{10,... | collective-permute-start | bytes 245768 | tf_op jit(solution)/shard_map/ppermute | solution.py:786
  16.0 1.4 %collective-permute-start.7 = (f32[20,8,128]{2,1,0:T(8,128)S(1)}, f32[20,8,128]{2,1,0:T(8,128)S(1)}, u32[]{:S(2)}, u32[]{:S(2)}) collective-permute-start(f32[20,8,128]{2,1,0:T(8,128)S(1)} %get-tuple-element.32), channel_id=1, source_target_pairs={{0,5},{1,4},{2,7},{3,6},{4,1},{5,0},{6,3},{7,2},{8,13},{9,12},{10,... | collective-permute-start | bytes 245768 | tf_op jit(solution)/shard_map/ppermute | solution.py:786
  17.3 0.5 collective-permute-start.6
  17.8 0.7 %collective-permute-start.5 = (f32[20,8,128]{2,1,0:T(8,128)S(1)}, f32[20,8,128]{2,1,0:T(8,128)S(1)}, u32[]{:S(2)}, u32[]{:S(2)}) collective-permute-start(f32[20,8,128]{2,1,0:T(8,128)S(1)} %get-tuple-element.34), channel_id=1, source_target_pairs={{0,3},{1,2},{2,1},{3,0},{4,7},{5,6},{6,5},{7,4},{8,11},{9,10},{10,... | collective-permute-start | bytes 245768 | tf_op jit(solution)/shard_map/ppermute | solution.py:786
  18.6 0.4 collective-permute-done.9.refs_7_
  19.0 1.0 %collective-permute-start.4 = (f32[20,8,128]{2,1,0:T(8,128)S(1)}, f32[20,8,128]{2,1,0:T(8,128)S(1)}, u32[]{:S(2)}, u32[]{:S(2)}) collective-permute-start(f32[20,8,128]{2,1,0:T(8,128)S(1)} %get-tuple-element.35), channel_id=1, source_target_pairs={{0,2},{1,3},{2,0},{3,1},{4,6},{5,7},{6,4},{7,5},{8,10},{9,11},{10,... | collective-permute-start | bytes 245768 | tf_op jit(solution)/shard_map/ppermute | solution.py:786
  20.0 0.4 collective-permute-done.8.refs_6_
  20.5 0.3 collective-permute-start.3
  20.8 1.8 %collective-permute-done.7.refs_5_ = f32[20,8,128]{2,1,0:T(8,128)S(1)} collective-permute-done((f32[20,8,128]{2,1,0:T(8,128)S(1)}, f32[20,8,128]{2,1,0:T(8,128)S(1)}, u32[]{:S(2)}, u32[]{:S(2)}) %collective-permute-start.7) | collective-permute-done | bytes 81952 | tf_op jit(solution)/shard_map/ppermute | solution.py:786
  22.6 1.8 %collective-permute-done.6.refs_4_ = f32[20,8,128]{2,1,0:T(8,128)S(1)} collective-permute-done((f32[20,8,128]{2,1,0:T(8,128)S(1)}, f32[20,8,128]{2,1,0:T(8,128)S(1)}, u32[]{:S(2)}, u32[]{:S(2)}) %collective-permute-start.6) | collective-permute-done | bytes 81952 | tf_op jit(solution)/shard_map/ppermute | solution.py:786
  24.3 0.0 collective-permute-done.5.refs_3_
  24.4 0.0 collective-permute-done.4.refs_2_
  24.4 0.0 collective-permute-done.3.refs_1_
  24.4 0.5 shard_map.89
  24.9 0.1 collective-permute-start.10
  25.0 3.5 %collective-permute-start.11 = (f32[4,20,8,128]{3,2,1,0:T(8,128)S(1)}, f32[4,20,8,128]{3,2,1,0:T(8,128)S(1)}, u32[]{:S(2)}, u32[]{:S(2)}) collective-permute-start(f32[4,20,8,128]{3,2,1,0:T(8,128)S(1)} %get-tuple-element.24), channel_id=1, source_target_pairs={{0,25},{1,0},{2,1},{3,2},{7,3},{6,7},{5,6},{4,5},{13,4},{12,13},{8... | collective-permute-start | bytes 983048 | tf_op jit(solution)/shard_map/ppermute | solution.py:776
  28.5 4.8 %collective-permute-done.10.refs_2_ = f32[4,20,8,128]{3,2,1,0:T(8,128)S(1)} collective-permute-done((f32[4,20,8,128]{3,2,1,0:T(8,128)S(1)}, f32[4,20,8,128]{3,2,1,0:T(8,128)S(1)}, u32[]{:S(2)}, u32[]{:S(2)}) %collective-permute-start.10) | collective-permute-done | bytes 327712 | tf_op jit(solution)/shard_map/ppermute | solution.py:775
  33.2 0.0 collective-permute-done.11.refs_3_
  33.2 13.5 %shard_map.90 = f32[8,17,8,128]{3,2,1,0:T(8,128)S(1)} custom-call(f32[27]{0:T(128)} %refs_0_.5, f32[8,20,8,128]{3,2,1,0:T(8,128)S(1)} %get-tuple-element.22.refs_1_, f32[4,20,8,128]{3,2,1,0:T(8,128)S(1)} %collective-permute-done.10.refs_2_, f32[4,20,8,128]{3,2,1,0:T(8,128)S(1)} %collective-permute-done.11.refs_3_), custom_call_target="tpu_custom_call" | custom-call | tf_op jit(solution)/shard_map/pallas_call | solution.py:748
  46.8 0.1 collective-permute-start.18
  46.8 2.2 %collective-permute-start.17 = (f32[17,8,128]{2,1,0:T(8,128)S(1)}, f32[17,8,128]{2,1,0:T(8,128)S(1)}, u32[]{:S(2)}, u32[]{:S(2)}) collective-permute-start(f32[17,8,128]{2,1,0:T(8,128)S(1)} %get-tuple-element.39), channel_id=1, source_target_pairs={{0,6},{1,7},{2,4},{3,5},{4,2},{5,3},{6,0},{7,1},{8,14},{9,15},{10,... | collective-permute-start | bytes 208904 | tf_op jit(solution)/shard_map/ppermute | solution.py:786
  49.1 0.0 collective-permute-start.16
  49.1 2.1 %collective-permute-start.15 = (f32[17,8,128]{2,1,0:T(8,128)S(1)}, f32[17,8,128]{2,1,0:T(8,128)S(1)}, u32[]{:S(2)}, u32[]{:S(2)}) collective-permute-start(f32[17,8,128]{2,1,0:T(8,128)S(1)} %get-tuple-element.41), channel_id=1, source_target_pairs={{0,4},{1,5},{2,6},{3,7},{4,0},{5,1},{6,2},{7,3},{8,12},{9,13},{10,... | collective-permute-start | bytes 208904 | tf_op jit(solution)/shard_map/ppermute | solution.py:786
  51.2 0.0 collective-permute-start.14
  51.2 1.0 %collective-permute-done.18.refs_7_ = f32[17,8,128]{2,1,0:T(8,128)S(1)} collective-permute-done((f32[17,8,128]{2,1,0:T(8,128)S(1)}, f32[17,8,128]{2,1,0:T(8,128)S(1)}, u32[]{:S(2)}, u32[]{:S(2)}) %collective-permute-start.18) | collective-permute-done | bytes 69664 | tf_op jit(solution)/shard_map/ppermute | solution.py:786
  52.2 0.3 collective-permute-start.13
  52.6 1.0 %collective-permute-done.17.refs_6_ = f32[17,8,128]{2,1,0:T(8,128)S(1)} collective-permute-done((f32[17,8,128]{2,1,0:T(8,128)S(1)}, f32[17,8,128]{2,1,0:T(8,128)S(1)}, u32[]{:S(2)}, u32[]{:S(2)}) %collective-permute-start.17) | collective-permute-done | bytes 69664 | tf_op jit(solution)/shard_map/ppermute | solution.py:786
  53.6 0.0 collective-permute-start.12
  53.6 1.4 %collective-permute-done.16.refs_5_ = f32[17,8,128]{2,1,0:T(8,128)S(1)} collective-permute-done((f32[17,8,128]{2,1,0:T(8,128)S(1)}, f32[17,8,128]{2,1,0:T(8,128)S(1)}, u32[]{:S(2)}, u32[]{:S(2)}) %collective-permute-start.16) | collective-permute-done | bytes 69664 | tf_op jit(solution)/shard_map/ppermute | solution.py:786
  55.0 1.6 %collective-permute-done.15.refs_4_ = f32[17,8,128]{2,1,0:T(8,128)S(1)} collective-permute-done((f32[17,8,128]{2,1,0:T(8,128)S(1)}, f32[17,8,128]{2,1,0:T(8,128)S(1)}, u32[]{:S(2)}, u32[]{:S(2)}) %collective-permute-start.15) | collective-permute-done | bytes 69664 | tf_op jit(solution)/shard_map/ppermute | solution.py:786
  56.6 0.0 collective-permute-done.14.refs_3_
  56.6 0.5 collective-permute-done.13.refs_2_
  57.1 0.0 collective-permute-done.12.refs_1_
  57.1 0.3 shard_map.91
  57.4 0.1 collective-permute-start.19
  57.5 4.0 %collective-permute-start.20 = (f32[7,8,128]{2,1,0:T(8,128)S(1)}, f32[7,8,128]{2,1,0:T(8,128)S(1)}, u32[]{:S(2)}, u32[]{:S(2)}) collective-permute-start(f32[7,8,128]{2,1,0:T(8,128)S(1)} %get-tuple-element.28), channel_id=1, source_target_pairs={{0,16},{8,24},{16,0},{24,8},{1,17},{9,25},{17,1},{25,9},{2,18},{10... | collective-permute-start | bytes 86024 | tf_op jit(solution)/shard_map/ppermute | solution.py:792
  61.5 0.3 collective-permute-start.21
  61.9 1.7 %shard_map.92 = f32[27,4,8,128]{3,2,1,0:T(8,128)} custom-call(f32[8,17,8,128]{3,2,1,0:T(8,128)S(1)} %get-tuple-element.25.refs_0_), custom_call_target="tpu_custom_call" | custom-call | tf_op jit(solution)/shard_map/pallas_call | solution.py:748
  63.6 0.0 collective-permute-done.19.refs_1_
  63.6 0.0 collective-permute-done.20.refs_2_
  63.6 3.6 %collective-permute-done.21.refs_3_ = f32[7,8,128]{2,1,0:T(8,128)S(1)} collective-permute-done((f32[7,8,128]{2,1,0:T(8,128)S(1)}, f32[7,8,128]{2,1,0:T(8,128)S(1)}, u32[]{:S(2)}, u32[]{:S(2)}) %collective-permute-start.21) | collective-permute-done | bytes 28704 | tf_op jit(solution)/shard_map/ppermute | solution.py:792
  67.2 0.7 shard_map.93
  (2 shorter events, 0.1 us)
Async XLA Ops:
  1.6 8.0 %collective-permute-start = (f32[8,8,128]{2,1,0:T(8,128)S(1)}, f32[8,8,128]{2,1,0:T(8,128)S(1)}, u32[]{:S(2)}, u32[]{:S(2)}) collective-permute-start(f32[8,8,128]{2,1,0:T(8,128)S(1)} %get-tuple-element.19), channel_id=1, source_target_pairs={{0,8},{8,0},{16,24},{24,16},{1,9},{9,1},{17,25},{25,17},{2,10},{10... | collective-permute-start | bytes 98312 | tf_op jit(solution)/shard_map/ppermute | solution.py:792
  4.7 5.4 %collective-permute-start.1 = (f32[8,8,128]{2,1,0:T(8,128)S(1)}, f32[8,8,128]{2,1,0:T(8,128)S(1)}, u32[]{:S(2)}, u32[]{:S(2)}) collective-permute-start(f32[8,8,128]{2,1,0:T(8,128)S(1)} %get-tuple-element.20), channel_id=1, source_target_pairs={{0,16},{8,24},{16,0},{24,8},{1,17},{9,25},{17,1},{25,9},{2,18},{10... | collective-permute-start | bytes 98312 | tf_op jit(solution)/shard_map/ppermute | solution.py:792
  7.3 5.7 %collective-permute-start.2 = (f32[8,8,128]{2,1,0:T(8,128)S(1)}, f32[8,8,128]{2,1,0:T(8,128)S(1)}, u32[]{:S(2)}, u32[]{:S(2)}) collective-permute-start(f32[8,8,128]{2,1,0:T(8,128)S(1)} %get-tuple-element.21), channel_id=1, source_target_pairs={{0,24},{8,16},{16,8},{24,0},{1,25},{9,17},{17,9},{25,1},{2,26},{10... | collective-permute-start | bytes 98312 | tf_op jit(solution)/shard_map/ppermute | solution.py:792
  13.4 5.6 %collective-permute-start.9 = (f32[20,8,128]{2,1,0:T(8,128)S(1)}, f32[20,8,128]{2,1,0:T(8,128)S(1)}, u32[]{:S(2)}, u32[]{:S(2)}) collective-permute-start(f32[20,8,128]{2,1,0:T(8,128)S(1)} %get-tuple-element.30), channel_id=1, source_target_pairs={{0,7},{1,6},{2,5},{3,4},{4,3},{5,2},{6,1},{7,0},{8,15},{9,14},{10,... | collective-permute-start | bytes 245768 | tf_op jit(solution)/shard_map/ppermute | solution.py:786
  13.7 6.7 %collective-permute-start.8 = (f32[20,8,128]{2,1,0:T(8,128)S(1)}, f32[20,8,128]{2,1,0:T(8,128)S(1)}, u32[]{:S(2)}, u32[]{:S(2)}) collective-permute-start(f32[20,8,128]{2,1,0:T(8,128)S(1)} %get-tuple-element.31), channel_id=1, source_target_pairs={{0,6},{1,7},{2,4},{3,5},{4,2},{5,3},{6,0},{7,1},{8,14},{9,15},{10,... | collective-permute-start | bytes 245768 | tf_op jit(solution)/shard_map/ppermute | solution.py:786
  16.0 6.6 %collective-permute-start.7 = (f32[20,8,128]{2,1,0:T(8,128)S(1)}, f32[20,8,128]{2,1,0:T(8,128)S(1)}, u32[]{:S(2)}, u32[]{:S(2)}) collective-permute-start(f32[20,8,128]{2,1,0:T(8,128)S(1)} %get-tuple-element.32), channel_id=1, source_target_pairs={{0,5},{1,4},{2,7},{3,6},{4,1},{5,0},{6,3},{7,2},{8,13},{9,12},{10,... | collective-permute-start | bytes 245768 | tf_op jit(solution)/shard_map/ppermute | solution.py:786
  17.3 7.0 %collective-permute-start.6 = (f32[20,8,128]{2,1,0:T(8,128)S(1)}, f32[20,8,128]{2,1,0:T(8,128)S(1)}, u32[]{:S(2)}, u32[]{:S(2)}) collective-permute-start(f32[20,8,128]{2,1,0:T(8,128)S(1)} %get-tuple-element.33), channel_id=1, source_target_pairs={{0,4},{1,5},{2,6},{3,7},{4,0},{5,1},{6,2},{7,3},{8,12},{9,13},{10,... | collective-permute-start | bytes 245768 | tf_op jit(solution)/shard_map/ppermute | solution.py:786
  17.8 6.5 %collective-permute-start.5 = (f32[20,8,128]{2,1,0:T(8,128)S(1)}, f32[20,8,128]{2,1,0:T(8,128)S(1)}, u32[]{:S(2)}, u32[]{:S(2)}) collective-permute-start(f32[20,8,128]{2,1,0:T(8,128)S(1)} %get-tuple-element.34), channel_id=1, source_target_pairs={{0,3},{1,2},{2,1},{3,0},{4,7},{5,6},{6,5},{7,4},{8,11},{9,10},{10,... | collective-permute-start | bytes 245768 | tf_op jit(solution)/shard_map/ppermute | solution.py:786
  19.0 5.4 %collective-permute-start.4 = (f32[20,8,128]{2,1,0:T(8,128)S(1)}, f32[20,8,128]{2,1,0:T(8,128)S(1)}, u32[]{:S(2)}, u32[]{:S(2)}) collective-permute-start(f32[20,8,128]{2,1,0:T(8,128)S(1)} %get-tuple-element.35), channel_id=1, source_target_pairs={{0,2},{1,3},{2,0},{3,1},{4,6},{5,7},{6,4},{7,5},{8,10},{9,11},{10,... | collective-permute-start | bytes 245768 | tf_op jit(solution)/shard_map/ppermute | solution.py:786
  20.5 3.9 %collective-permute-start.3 = (f32[20,8,128]{2,1,0:T(8,128)S(1)}, f32[20,8,128]{2,1,0:T(8,128)S(1)}, u32[]{:S(2)}, u32[]{:S(2)}) collective-permute-start(f32[20,8,128]{2,1,0:T(8,128)S(1)} %get-tuple-element.36), channel_id=1, source_target_pairs={{0,1},{1,0},{2,3},{3,2},{4,5},{5,4},{6,7},{7,6},{8,9},{9,8},{10,11... | collective-permute-start | bytes 245768 | tf_op jit(solution)/shard_map/ppermute | solution.py:786
  24.9 8.4 %collective-permute-start.10 = (f32[4,20,8,128]{3,2,1,0:T(8,128)S(1)}, f32[4,20,8,128]{3,2,1,0:T(8,128)S(1)}, u32[]{:S(2)}, u32[]{:S(2)}) collective-permute-start(f32[4,20,8,128]{3,2,1,0:T(8,128)S(1)} %get-tuple-element.23), channel_id=1, source_target_pairs={{25,0},{0,1},{1,2},{2,3},{3,7},{7,6},{6,5},{5,4},{4,13},{13,12},{1... | collective-permute-start | bytes 983048 | tf_op jit(solution)/shard_map/ppermute | solution.py:775
  25.0 8.2 %collective-permute-start.11 = (f32[4,20,8,128]{3,2,1,0:T(8,128)S(1)}, f32[4,20,8,128]{3,2,1,0:T(8,128)S(1)}, u32[]{:S(2)}, u32[]{:S(2)}) collective-permute-start(f32[4,20,8,128]{3,2,1,0:T(8,128)S(1)} %get-tuple-element.24), channel_id=1, source_target_pairs={{0,25},{1,0},{2,1},{3,2},{7,3},{6,7},{5,6},{4,5},{13,4},{12,13},{8... | collective-permute-start | bytes 983048 | tf_op jit(solution)/shard_map/ppermute | solution.py:776
  46.8 5.5 %collective-permute-start.18 = (f32[17,8,128]{2,1,0:T(8,128)S(1)}, f32[17,8,128]{2,1,0:T(8,128)S(1)}, u32[]{:S(2)}, u32[]{:S(2)}) collective-permute-start(f32[17,8,128]{2,1,0:T(8,128)S(1)} %get-tuple-element.38), channel_id=1, source_target_pairs={{0,7},{1,6},{2,5},{3,4},{4,3},{5,2},{6,1},{7,0},{8,15},{9,14},{10,... | collective-permute-start | bytes 208904 | tf_op jit(solution)/shard_map/ppermute | solution.py:786
  46.8 6.7 %collective-permute-start.17 = (f32[17,8,128]{2,1,0:T(8,128)S(1)}, f32[17,8,128]{2,1,0:T(8,128)S(1)}, u32[]{:S(2)}, u32[]{:S(2)}) collective-permute-start(f32[17,8,128]{2,1,0:T(8,128)S(1)} %get-tuple-element.39), channel_id=1, source_target_pairs={{0,6},{1,7},{2,4},{3,5},{4,2},{5,3},{6,0},{7,1},{8,14},{9,15},{10,... | collective-permute-start | bytes 208904 | tf_op jit(solution)/shard_map/ppermute | solution.py:786
  49.1 5.9 %collective-permute-start.16 = (f32[17,8,128]{2,1,0:T(8,128)S(1)}, f32[17,8,128]{2,1,0:T(8,128)S(1)}, u32[]{:S(2)}, u32[]{:S(2)}) collective-permute-start(f32[17,8,128]{2,1,0:T(8,128)S(1)} %get-tuple-element.40), channel_id=1, source_target_pairs={{0,5},{1,4},{2,7},{3,6},{4,1},{5,0},{6,3},{7,2},{8,13},{9,12},{10,... | collective-permute-start | bytes 208904 | tf_op jit(solution)/shard_map/ppermute | solution.py:786
  49.1 7.5 %collective-permute-start.15 = (f32[17,8,128]{2,1,0:T(8,128)S(1)}, f32[17,8,128]{2,1,0:T(8,128)S(1)}, u32[]{:S(2)}, u32[]{:S(2)}) collective-permute-start(f32[17,8,128]{2,1,0:T(8,128)S(1)} %get-tuple-element.41), channel_id=1, source_target_pairs={{0,4},{1,5},{2,6},{3,7},{4,0},{5,1},{6,2},{7,3},{8,12},{9,13},{10,... | collective-permute-start | bytes 208904 | tf_op jit(solution)/shard_map/ppermute | solution.py:786
  51.2 5.4 %collective-permute-start.14 = (f32[17,8,128]{2,1,0:T(8,128)S(1)}, f32[17,8,128]{2,1,0:T(8,128)S(1)}, u32[]{:S(2)}, u32[]{:S(2)}) collective-permute-start(f32[17,8,128]{2,1,0:T(8,128)S(1)} %get-tuple-element.42), channel_id=1, source_target_pairs={{0,3},{1,2},{2,1},{3,0},{4,7},{5,6},{6,5},{7,4},{8,11},{9,10},{10,... | collective-permute-start | bytes 208904 | tf_op jit(solution)/shard_map/ppermute | solution.py:786
  52.2 4.9 %collective-permute-start.13 = (f32[17,8,128]{2,1,0:T(8,128)S(1)}, f32[17,8,128]{2,1,0:T(8,128)S(1)}, u32[]{:S(2)}, u32[]{:S(2)}) collective-permute-start(f32[17,8,128]{2,1,0:T(8,128)S(1)} %get-tuple-element.43), channel_id=1, source_target_pairs={{0,2},{1,3},{2,0},{3,1},{4,6},{5,7},{6,4},{7,5},{8,10},{9,11},{10,... | collective-permute-start | bytes 208904 | tf_op jit(solution)/shard_map/ppermute | solution.py:786
  53.6 3.5 %collective-permute-start.12 = (f32[17,8,128]{2,1,0:T(8,128)S(1)}, f32[17,8,128]{2,1,0:T(8,128)S(1)}, u32[]{:S(2)}, u32[]{:S(2)}) collective-permute-start(f32[17,8,128]{2,1,0:T(8,128)S(1)} %get-tuple-element.44), channel_id=1, source_target_pairs={{0,1},{1,0},{2,3},{3,2},{4,5},{5,4},{6,7},{7,6},{8,9},{9,8},{10,11... | collective-permute-start | bytes 208904 | tf_op jit(solution)/shard_map/ppermute | solution.py:786
  57.4 6.2 %collective-permute-start.19 = (f32[7,8,128]{2,1,0:T(8,128)S(1)}, f32[7,8,128]{2,1,0:T(8,128)S(1)}, u32[]{:S(2)}, u32[]{:S(2)}) collective-permute-start(f32[7,8,128]{2,1,0:T(8,128)S(1)} %get-tuple-element.27), channel_id=1, source_target_pairs={{0,8},{8,0},{16,24},{24,16},{1,9},{9,1},{17,25},{25,17},{2,10},{10... | collective-permute-start | bytes 86024 | tf_op jit(solution)/shard_map/ppermute | solution.py:792
  57.5 6.1 %collective-permute-start.20 = (f32[7,8,128]{2,1,0:T(8,128)S(1)}, f32[7,8,128]{2,1,0:T(8,128)S(1)}, u32[]{:S(2)}, u32[]{:S(2)}) collective-permute-start(f32[7,8,128]{2,1,0:T(8,128)S(1)} %get-tuple-element.28), channel_id=1, source_target_pairs={{0,16},{8,24},{16,0},{24,8},{1,17},{9,25},{17,1},{25,9},{2,18},{10... | collective-permute-start | bytes 86024 | tf_op jit(solution)/shard_map/ppermute | solution.py:792
  61.5 5.7 %collective-permute-start.21 = (f32[7,8,128]{2,1,0:T(8,128)S(1)}, f32[7,8,128]{2,1,0:T(8,128)S(1)}, u32[]{:S(2)}, u32[]{:S(2)}) collective-permute-start(f32[7,8,128]{2,1,0:T(8,128)S(1)} %get-tuple-element.29), channel_id=1, source_target_pairs={{0,24},{8,16},{16,8},{24,0},{1,25},{9,17},{17,9},{25,1},{2,26},{10... | collective-permute-start | bytes 86024 | tf_op jit(solution)/shard_map/ppermute | solution.py:792

commit v3 on v1

--- a/solution.py
+++ b/solution.py
@@ -228,32 +228,36 @@
             and self.block_z == LANES
             and self.planes * self.sub == LANES
             and self.halo * 2 == self.planes
+            and WINDOWS == 2
             and self.halo == STEPS * WINDOWS
+            and self.sub >= 8
             and 2 * self.block_x == self.sub
             and self.block_x == self.grp
             and heat_block == (1, SUBLANES, self.grp * LANES)
             and self.sub & (self.sub - 1) == 0
             and self.grp & (self.grp - 1) == 0
             and self.gy % 2 == 0
+            and self.sub % self.grp == 0
         )
         if self.fits:
-            self.snake = [
-                x * self.gy + (y if x % 2 == 0 else self.gy - 1 - y)
-                for x in range(self.gx)
-                for y in range(self.gy)
-            ]
+            self.turn = self.sub // self.grp
             self.ring = [
-                part * self.sub + self.snake[place if part % 2 == 0 else self.sub - 1 - place]
+                part * self.sub + self.round_plane((place - self.turn * part) % self.sub)
                 for part in range(self.grp)
                 for place in range(self.sub)
             ]
 
-    def holders(self):
-        even = lax.axis_index("grp") % 2 == 0
+    def round_plane(self, number):
+        x, y = number // self.gy, number % self.gy
+        back = x % 2
+        return x * self.gy + y + back * (self.gy - 1 - 2 * y)
+
+    def holders(self, part):
+        begin = self.sub * self.grp - self.turn * part
         mine = self.place_in_plane()
         return [
-            jnp.bitwise_xor(jnp.where(even, *pair), mine)
-            for pair in zip(self.snake, self.snake[::-1])
+            jnp.bitwise_xor(self.round_plane(lax.rem(begin + place, self.sub)), mine)
+            for place in range(self.sub)
         ]
 
     def place_in_plane(self):
@@ -290,11 +294,7 @@
 
 
 SPEED_AT, SOLID_AT, HEAT_AT, RATE_AT, ROWS = 27, 30, 31, 38, 40
-MOVING = 34
-
-
-def moving_row(number):
-    return number + (HEAT_AT - SPEED_AT) * (number >= SPEED_AT)
+FLOW_PAIRS = 14
 
 
 def offer_heat(slab, levels_hbm, heat_hbm, phase_hbm, *refs):
@@ -336,7 +336,7 @@
         copy.start()
     for copy in copies:
         copy.wait()
-    holders = slab.holders()
+    holders = slab.holders(lax.axis_index("grp"))
 
     def one(pair):
         pack_pair(slab, fields, pair, sent, pair, holders)
@@ -354,7 +354,7 @@
 def pack_heat(slab, sent_in, flags, *refs):
     parts, (sent, held, packed, sem) = refs[: slab.grp], refs[slab.grp :]
     mine = lax.axis_index("grp")
-    holders = slab.holders()
+    holders = slab.holders(lax.axis_index("grp"))
     held[0] = flags[...]
     held[9] = jnp.zeros(flags.shape, F32)
     for step in range(slab.grp):
@@ -417,78 +417,47 @@
     lax.fori_loop(0, slab.sub // 2, one, 0)
 
 
-def pack_out(slab, came, state, sent):
-    def one(tile, _):
-        even = (lane_index() // slab.planes) % 2 == 0
-        partner = jnp.bitwise_xor(tile, slab.place_in_plane())
-        flags = came[tile, SOLID_AT // 2]
-        solid = jnp.where(even, flags, lane_roll(flags, slab.planes)) != 0.0
-        for pair in range(MOVING // 2):
-            first, second = (state[moving_row(2 * pair + h), tile] for h in range(2))
-            value = jnp.where(even, first, lane_roll(second, slab.planes))
-            if 2 * pair + 1 < SPEED_AT:
-                value = jnp.where(solid, came[tile, pair], value)
-            elif 2 * pair < SPEED_AT:
-                value = jnp.where(jnp.logical_and(solid, even), came[tile, pair], value)
-            sent[partner, pair] = value
-        return 0
-
-    lax.fori_loop(0, slab.sub, one, 0)
-
-
-def unpack_pair(slab, came, pair, holders):
-    sources = [came[holders[place], pair] for place in range(slab.sub)]
-    values = swap_groups(sources, slab.planes)
-    return [values[0::2], values[1::2]]
-
-
-def return_heat(slab, *refs):
-    parts, came, outs, held = (
-        refs[: slab.sub],
-        refs[slab.sub],
-        refs[slab.sub + 1 : slab.sub + 1 + slab.grp],
-        refs[-1],
-    )
+def pack_out(slab, flow, came, tile, sent):
+    even = (lane_index() // slab.planes) % 2 == 0
+    flags = came[tile, SOLID_AT // 2]
+    solid = jnp.where(even, flags, lane_roll(flags, slab.planes)) != 0.0
+    partner = jnp.bitwise_xor(tile, slab.place_in_plane())
+    for pair in range(FLOW_PAIRS):
+        value = flow[2 * pair]
+        if 2 * pair + 1 < len(flow):
+            value = jnp.where(even, value, lane_roll(flow[2 * pair + 1], slab.planes))
+        sent[partner, pair] = jnp.where(solid, came[tile, pair], value)
+
+
+def add_heat(slab, sent_in, *refs):
+    parts, (sent, packed, sem) = refs[: slab.grp], refs[slab.grp :]
+    mine = slab.place_in_plane()
+    for tile in range(slab.sub):
+        for step in range(slab.grp):
+            packed[jnp.bitwise_xor(mine, tile), step] = parts[step][tile]
+    copy = pltpu.make_async_copy(packed, sent.at[:, pl.ds(FLOW_PAIRS, slab.grp)], sem)
+    copy.start()
+    copy.wait()
+
+
+def unpack_out(slab, *refs):
+    parts, (popul_out, thermal_out, came) = refs[: slab.sub], refs[slab.sub :]
     for step in range(slab.sub):
         came[step] = parts[step][...]
-    holders = slab.holders()
-    _, values = unpack_pair(slab, came, SPEED_AT // 2, holders)
-    for x in range(slab.block_x):
-        held[x, 0] = values[x]
-
-    def one(pair):
-        for h, values in enumerate(unpack_pair(slab, came, SPEED_AT // 2 + 1 + pair, holders)):
-            for x in range(slab.block_x):
-                held[x, 2 * pair + 1 + h] = values[x]
-
-    for_each(3, one)
     mine = lax.axis_index("grp")
-    for step in range(slab.grp):
-        outs[step][...] = held[jnp.bitwise_xor(mine, step)]
-
-
-def unpack_flow(slab, came, popul_out):
-    holders = slab.holders()
-
-    def one(pair):
-        for h, values in enumerate(unpack_pair(slab, came, pair, holders)):
-            for x in range(slab.block_x):
-                popul_out[2 * pair + h, x] = values[x]
-
-    for_each(SPEED_AT // 2, one)
-    values, _ = unpack_pair(slab, came, SPEED_AT // 2, holders)
-    for x in range(slab.block_x):
-        popul_out[SPEED_AT - 1, x] = values[x]
-
-
-def join_heat(slab, *refs):
-    parts, thermal_out = refs[: slab.grp], refs[slab.grp]
-    mine = lax.axis_index("grp")
+    holders = slab.holders(mine)
+    for pair in range(FLOW_PAIRS):
+        sources = [came[holders[place], pair] for place in range(slab.sub)]
+        for number, value in enumerate(swap_groups(sources, slab.planes)):
+            if 2 * pair + number % 2 < 27:
+                popul_out[2 * pair + number % 2, number // 2] = value
     for step in range(slab.grp):
         part = jnp.bitwise_xor(mine, step)
+        holders = slab.holders(part)
         span = pl.ds(pl.multiple_of(part * LANES, LANES), LANES)
-        for k in range(7):
-            thermal_out[k, 0, :, span] = parts[step][k]
+        sources = [came[holders[place], FLOW_PAIRS + step] for place in range(slab.sub)]
+        for k, value in enumerate(swap_groups(sources, slab.planes)[:7]):
+            thermal_out[k, 0, :, span] = value
 
 
 def forward3(values):
@@ -515,7 +484,7 @@
     return values
 
 
-def collide_tile(values, force, rate):
+def collide_tile(values, force, rate, solid):
     moments = forward3(values)
     density = moments[0]
     jx, jy, jz = moments[9], moments[3], moments[1] + 0.5 * force
@@ -565,86 +534,204 @@
         else:
             level = scale(odd, cross[odd], count)
         out[n] = moments[n] - rate(n) * (moments[n] - level)
+    out[26] = jnp.where(solid, jnp.nan, out[26])
     return backward3(out)
 
 
 HEAT_OFFSETS = [(0, 0, 0), (1, 0, 0), (-1, 0, 0), (0, 1, 0), (0, -1, 0), (0, 0, 1), (0, 0, -1)]
 
 
-def run_steps(slab, rates_ref, state, post, force_ref):
-    def collide_one(tile, _):
-        values = [state[n, tile] for n in range(27)]
+def collide_flow(rates_ref, flow, force, solid, target, tile):
+    for n, value in enumerate(collide_tile(flow, force, lambda n: rates_ref[n], solid)):
+        target[n, tile] = value
+
+
+def collide_heat(heat, omega, speeds, target, tile):
+    total = heat[0]
+    for k in range(1, 7):
+        total = total + heat[k]
+    side = 0.125 * total
+    half = 0.5 * total
+    for k in range(7):
+        if k == 0:
+            level = 0.25 * total
+        else:
+            drift = half * speeds[(k - 1) // 2]
+            level = side + drift if k % 2 == 1 else side - drift
+        target[k, tile] = heat[k] - (heat[k] - level) * omega
+
+
+def stream(slab, post, tile, offsets):
+    block_x, block_y = tile // slab.gy, tile % slab.gy
+    x_of = {a: lax.rem(block_x + slab.gx - a, slab.gx) for a in (-1, 0, 1)}
+    y_of = {b: lax.rem(block_y + slab.gy - b, slab.gy) for b in (-1, 0, 1)}
+    row = row_index()
+    per_x = 2 * slab.planes
+    in_x = (lane_index() + slab.halo) % LANES // per_x
+    last_x = {1: in_x == slab.block_x - 1, -1: in_x == 0}
+    last_y = {1: row == SUBLANES - 1, -1: row == 0}
+
+    def arrive(number, offset):
+        a, b, c = offset
+
+        def take(x):
+            value = post[number, x_of[x] * slab.gy + block_y]
+            if b != 0:
+                other = post[number, x_of[x] * slab.gy + y_of[b]]
+                value = jnp.where(last_y[b], other, value)
+            return value
+
+        value = take(0)
+        if a != 0:
+            value = jnp.where(last_x[a], take(a), value)
+        if b != 0:
+            value = pltpu.roll(value, b % SUBLANES, 0)
+        return lane_roll(value, a * per_x + c)
+
+    return [arrive(number, offset) for number, offset in enumerate(offsets)]
+
+
+def stream_flow(slab, post, tile):
+    return [
+        jnp.where(value != value, post[26 - n, tile], value)
+        for n, value in enumerate(stream(slab, post, tile, OFFSET_TABLE))
+    ]
+
+
+def over_tiles(slab, body, unroll=1):
+    def one(tile, _):
+        body(tile)
+        return 0
+
+    lax.fori_loop(0, slab.sub, one, 0, unroll=unroll)
+
+
+def over_steps(count, body):
+    def one(number, _):
+        body(number)
+        return 0
+
+    lax.fori_loop(0, count, one, 0)
+
+
+def first_window(slab, rates_hbm, came, below_ref, above_ref, *refs):
+    flow_out, keep_out, heat_outs = refs[0], refs[1], refs[2 : 2 + slab.grp]
+    rates_ref, sem, state, flow_post, heat_post, held = refs[2 + slab.grp :]
+    rates_copy = pltpu.make_async_copy(rates_hbm, rates_ref, sem)
+    rates_copy.start()
+    make_tiles(slab, came, below_ref, above_ref, state)
+    rates_copy.wait()
+
+    def speeds_of(tile):
+        return [state[SPEED_AT + d, tile] for d in range(3)]
+
+    def begin(tile):
+        solid = state[SOLID_AT, tile]
+        heat = [state[HEAT_AT + k, tile] for k in range(7)]
+        force = heat_force(heat)
+        keep_out[0, tile] = force
+        keep_out[1, tile] = solid
+        flow = [state[n, tile] for n in range(27)]
+        collide_flow(rates_ref, flow, force, solid != 0.0, flow_post.at[0], tile)
+        collide_heat(heat, state[RATE_AT, tile], speeds_of(tile), heat_post.at[0], tile)
+
+    over_tiles(slab, begin)
+
+    def step(number):
+        source = lax.rem(number, 2)
+
+        def go_on(tile):
+            flow = stream_flow(slab, flow_post.at[source], tile)
+            solid = state[SOLID_AT, tile] != 0.0
+            collide_flow(rates_ref, flow, keep_out[0, tile], solid, flow_post.at[1 - source], tile)
+            heat = stream(slab, heat_post.at[source], tile, HEAT_OFFSETS)
+            omega = state[RATE_AT, tile]
+            collide_heat(heat, omega, speeds_of(tile), heat_post.at[1 - source], tile)
+
+        over_tiles(slab, go_on)
+
+    over_steps(STEPS - 1, step)
+    source = (STEPS - 1) % 2
+
+    def next_window(tile):
+        flow = stream_flow(slab, flow_post.at[source], tile)
+        heat = stream(slab, heat_post.at[source], tile, HEAT_OFFSETS)
         solid = state[SOLID_AT, tile] != 0.0
-        moved = collide_tile(values, force_ref[tile], lambda n: rates_ref[n])
-        for n in range(27):
-            post[n, tile] = jnp.where(solid, jnp.nan, moved[n])
-        heat = [state[HEAT_AT + k, tile] for k in range(7)]
-        total = heat[0]
-        for k in range(1, 7):
-            total = total + heat[k]
-        omega = state[RATE_AT, tile]
-        side = 0.125 * total
-        half = 0.5 * total
-        for k in range(7):
-            if k == 0:
-                level = 0.25 * total
-            else:
-                drift = half * state[SPEED_AT + (k - 1) // 2, tile]
-                level = side + drift if k % 2 == 1 else side - drift
-            post[SPEED_AT + k, tile] = heat[k] - (heat[k] - level) * omega
+        speeds = [
+            jnp.where(solid, 0.0, each) for each in flow_speed_tile(flow, keep_out[0, tile])
+        ]
+        for d in range(3):
+            state[SPEED_AT + d, tile] = speeds[d]
+        force = heat_force(heat)
+        keep_out[0, tile] = force
+        collide_flow(rates_ref, flow, force, solid, flow_out, tile)
+        collide_heat(heat, state[RATE_AT, tile], speeds, heat_post.at[1 - source], tile)
+
+    over_tiles(slab, next_window)
+
+    def heat_step(number):
+        source = lax.rem(number + STEPS, 2)
+
+        def go_on(tile):
+            heat = stream(slab, heat_post.at[source], tile, HEAT_OFFSETS)
+            omega = state[RATE_AT, tile]
+            collide_heat(heat, omega, speeds_of(tile), heat_post.at[1 - source], tile)
+
+        over_tiles(slab, go_on, unroll=2)
+
+    over_steps(STEPS - 1, heat_step)
+    zero = jnp.zeros((SUBLANES, LANES), F32)
+
+    def end_heat(tile):
+        heat = stream(slab, heat_post.at[(2 * STEPS - 1) % 2], tile, HEAT_OFFSETS)
+        heat += [zero] * (slab.sub - 7)
+        for x, value in enumerate(swap_groups(heat, slab.planes)[0::2]):
+            held[x, tile] = value
+
+    over_tiles(slab, end_heat, unroll=2)
+    mine = lax.axis_index("grp")
+    for step_number in range(slab.grp):
+        heat_outs[step_number][...] = held[jnp.bitwise_xor(mine, step_number)]
+
+
+def last_window(slab, rates_hbm, came, flow_in, keep_ref, sent, rates_ref, sem, flow_post):
+    rates_copy = pltpu.make_async_copy(rates_hbm, rates_ref, sem)
+    rates_copy.start()
+
+    def copy(n, _):
+        flow_post[0, n] = flow_in[n]
         return 0
 
-    def stream_one(tile, _):
-        block_x, block_y = tile // slab.gy, tile % slab.gy
-        x_of = {a: lax.rem(block_x + slab.gx - a, slab.gx) for a in (-1, 0, 1)}
-        y_of = {b: lax.rem(block_y + slab.gy - b, slab.gy) for b in (-1, 0, 1)}
-        row = row_index()
-        per_x = 2 * slab.planes
-        in_x = (lane_index() + slab.halo) % LANES // per_x
-        last_x = {1: in_x == slab.block_x - 1, -1: in_x == 0}
-        last_y = {1: row == SUBLANES - 1, -1: row == 0}
-
-        def arrive(number, offset):
-            a, b, c = offset
-
-            def take(x):
-                value = post[number, x_of[x] * slab.gy + block_y]
-                if b != 0:
-                    other = post[number, x_of[x] * slab.gy + y_of[b]]
-                    value = jnp.where(last_y[b], other, value)
-                return value
-
-            value = take(0)
-            if a != 0:
-                value = jnp.where(last_x[a], take(a), value)
-            if b != 0:
-                value = pltpu.roll(value, b % SUBLANES, 0)
-            return lane_roll(value, a * per_x + c)
-
-        for n in range(27):
-            value = arrive(n, OFFSET_TABLE[n])
-            state[n, tile] = jnp.where(value != value, post[26 - n, tile], value)
-        for k in range(7):
-            state[HEAT_AT + k, tile] = arrive(SPEED_AT + k, HEAT_OFFSETS[k])
-        return 0
-
-    def step(number, _):
-        lax.fori_loop(0, slab.sub, collide_one, 0)
-        lax.fori_loop(0, slab.sub, stream_one, 0)
-        return 0
-
-    lax.fori_loop(0, STEPS, step, 0)
-
-
-def heat_force(state, tile):
-    total = state[HEAT_AT, tile]
+    lax.fori_loop(0, 27, copy, 0, unroll=3)
+    rates_copy.wait()
+
+    def step(number):
+        source = lax.rem(number, 2)
+
+        def go_on(tile):
+            flow = stream_flow(slab, flow_post.at[source], tile)
+            solid = keep_ref[1, tile] != 0.0
+            collide_flow(rates_ref, flow, keep_ref[0, tile], solid, flow_post.at[1 - source], tile)
+
+        over_tiles(slab, go_on)
+
+    over_steps(STEPS - 1, step)
+
+    def end(tile):
+        flow = stream_flow(slab, flow_post.at[(STEPS - 1) % 2], tile)
+        pack_out(slab, flow, came, tile, sent)
+
+    over_tiles(slab, end)
+
+
+def heat_force(heat):
+    total = heat[0]
     for k in range(1, 7):
-        total = total + state[HEAT_AT + k, tile]
+        total = total + heat[k]
     return BUOYANCY * (total - REFERENCE_HEAT)
 
 
-def flow_speed_tile(state, tile, force):
-    values = [state[n, tile] for n in range(27)]
+def flow_speed_tile(values, force):
     total = values[0]
     for n in range(1, 27):
         total = total + values[n]
@@ -660,39 +747,6 @@
         sums.append(plus - minus)
     sums[2] = sums[2] + 0.5 * force
     return [each / total for each in sums]
-
-
-def both_windows(slab, rates_hbm, came, below_ref, above_ref, *refs):
-    sent, rates_ref, sem, state, post, force = refs
-    rates_copy = pltpu.make_async_copy(rates_hbm, rates_ref, sem)
-    rates_copy.start()
-    make_tiles(slab, came, below_ref, above_ref, state)
-
-    def first_force(tile, _):
-        force[tile] = heat_force(state, tile)
-        return 0
-
-    lax.fori_loop(0, slab.sub, first_force, 0)
-    rates_copy.wait()
-
-    def next_speed(tile, _):
-        solid = state[SOLID_AT, tile] != 0.0
-        for d, each in enumerate(flow_speed_tile(state, tile, force[tile])):
-            state[SPEED_AT + d, tile] = jnp.where(solid, 0.0, each)
-        force[tile] = heat_force(state, tile)
-        return 0
-
-    def one_window(window, _):
-        run_steps(slab, rates_ref, state, post, force)
-
-        @pl.when(window + 1 < WINDOWS)
-        def _():
-            lax.fori_loop(0, slab.sub, next_speed, 0)
-
-        return 0
-
-    lax.fori_loop(0, WINDOWS, one_window, 0)
-    pack_out(slab, came, state, sent)
 
 
 def local_call(body, slab, arrays, outs, scratch=(), in_hbm=0, carried=False):
@@ -733,7 +787,9 @@
 
 def across_plane(slab, sent):
     came = {0: sent[0]}
-    for step in sorted(range(1, slab.sub), key=lambda step: -bin(step >> 1).count("1")):
+    far_first = [step for k in range(2) for step in range(2 + k, slab.sub, 2)] + [1]
+    far_first.sort(key=lambda step: -bin(step >> 1).count("1"))
+    for step in far_first:
         pairs = [(i, i ^ step) for i in range(slab.sub)]
         came[step] = lax.ppermute(sent[step], ("gx", "gy"), pairs)
     return [came[step] for step in range(slab.sub)]
@@ -796,31 +852,43 @@
         offer_halo, slab, across_plane(slab, sent), [sent_shape, halo_shape, halo_shape]
     )
     below, above = exchange(slab, low, high)
-    (sent,) = local_call(
-        both_windows,
+    plane = (slab.sub,) + tile
+    scalars = [pltpu.SMEM(rates.shape, F32), pltpu.SemaphoreType.DMA]
+    flow, keep, *parts = local_call(
+        first_window,
         slab,
         [rates, came, below, above],
-        [(slab.sub, MOVING // 2) + tile],
-        [
-            pltpu.SMEM(rates.shape, F32),
-            pltpu.SemaphoreType.DMA,
-            (ROWS, slab.sub) + tile,
-            (MOVING, slab.sub) + tile,
-            (slab.sub,) + tile,
-        ],
+        [(27,) + plane, (2,) + plane] + [plane] * slab.grp,
+        scalars + [(ROWS,) + plane, (2, 27) + plane, (2, 7) + plane, (slab.grp,) + plane],
         in_hbm=1,
     )
-    came, *parts = local_call(
-        return_heat,
+    parts = across_planes(slab, parts)
+    last_shape = (slab.sub, FLOW_PAIRS + slab.grp) + tile
+    (sent,) = local_call(
+        last_window,
         slab,
-        across_plane(slab, sent),
-        [sent.shape] + [(7,) + tile] * slab.grp,
-        [(slab.grp, 7) + tile],
-    )
-    parts = across_planes(slab, parts)
-    (populations_out,) = local_call(unpack_flow, slab, [came], [populations.shape])
-    (thermal_out,) = local_call(join_heat, slab, parts, [thermal.shape])
-    return populations_out, thermal_out
+        [rates, came, flow, keep],
+        [last_shape],
+        scalars + [(2, 27) + plane],
+        in_hbm=1,
+    )
+    (sent,) = local_call(
+        add_heat,
+        slab,
+        [sent] + parts,
+        [last_shape],
+        [(slab.sub, slab.grp) + tile, pltpu.SemaphoreType.DMA],
+        carried=True,
+    )
+    return tuple(
+        local_call(
+            unpack_out,
+            slab,
+            across_plane(slab, sent),
+            [populations.shape, thermal.shape],
+            [last_shape],
+        )
+    )
 
 
 def solution(mesh):

time: 70.2 us -> 67.4 us (0.960)
  waiting for transfers between devices: 21.6 us -> 18.3 us
  Pallas kernels: 22.2 us -> 23.2 us
    ppermute x6, waiting for transfers between devices: 7.2 us -> 3.44 us  [across_planes(): lax.ppermute(parts[step], 'grp', [(i, i ^ step) for i in range(slab.grp)])]
    pallas_call x8, Pallas kernels: 22.2 us -> 23.2 us  [local_call(): pl.pallas_call(kernel, out_shape=[jax.ShapeDtypeStruct(shape, F32) for sh...]
    ppermute x14, waiting for transfers between devices: 9.22 us -> 10.1 us  [across_plane(): came[step] = lax.ppermute(sent[step], ('gx', 'gy'), pairs)]
  transfers between devices with their start and end apart: 22 -> 22, of which waited for: 14 -> 12; matrix products, arithmetic and copies ran while one was open for 0% -> 0% of each run, Pallas kernels for 6% -> 12%
where the time goes in v3:
time: 67.4 us; the launch traced here: 67.3 us
  starting transfers between devices  24.9 us (37%)
  Pallas kernels  23.2 us (34%)
  waiting for transfers between devices  18.3 us (27%)
  between operations  0.78 us (1%)
    pallas_call x8, Pallas kernels, local_call(): pl.pallas_call(kernel, out_shape=[jax.ShapeDtypeStruct(shape, F32) for sh...  23.2 us
    ppermute x14, starting transfers between devices, across_plane(): came[step] = lax.ppermute(sent[step], ('gx', 'gy'), pairs)  11.2 us
    ppermute x14, waiting for transfers between devices, across_plane(): came[step] = lax.ppermute(sent[step], ('gx', 'gy'), pairs)  10.1 us
    ppermute x6, starting transfers between devices, across_planes(): lax.ppermute(parts[step], 'grp', [(i, i ^ step) for i in range(slab.grp)])  10.1 us
    ppermute x1, waiting for transfers between devices, exchange(): from_below = lax.ppermute(high, RING, upward)  4.75 us
    ppermute x1, starting transfers between devices, exchange(): from_above = lax.ppermute(low, RING, [(b, a) for a, b in upward])  3.47 us
    ppermute x6, waiting for transfers between devices, across_planes(): lax.ppermute(parts[step], 'grp', [(i, i ^ step) for i in range(slab.grp)])  3.44 us
  transfers between devices with their start and end apart: 22, of which 12 were waited for; matrix products, arithmetic and copies ran while one was open for 0% of the time, Pallas kernels for 12%

profile of v3, /device:TPU:0, one launch (start us, length us, event | category | flops | bytes accessed | tf_op | source)
XLA Modules:
  0.0 67.3 jit_solution(15320179488422539866)
XLA Ops:
  0.6 1.0 %shard_map.87 = (f32[8,8,128]{2,1,0:T(8,128)S(1)}, f32[8,8,128]{2,1,0:T(8,128)S(1)}, f32[8,8,128]{2,1,0:T(8,128)S(1)}, f32[8,8,128]{2,1,0:T(8,128)S(1)}) custom-call(f32[4]{0:T(128)} %refs_0_.5, f32[7,1,8,512]{3,2,1,0:T(8,128)} %refs_1_.3, s32[1,8,512]{2,1,0:T(8,128)} %refs_2_.3), custom_call_target="tpu_custom_call" | custom-call | tf_op jit(solution)/shard_map/pallas_call | solution.py:756
  1.6 3.1 %collective-permute-start = (f32[8,8,128]{2,1,0:T(8,128)S(1)}, f32[8,8,128]{2,1,0:T(8,128)S(1)}, u32[]{:S(2)}, u32[]{:S(2)}) collective-permute-start(f32[8,8,128]{2,1,0:T(8,128)S(1)} %get-tuple-element.20), channel_id=1, source_target_pairs={{0,8},{8,0},{16,24},{24,16},{1,9},{9,1},{17,25},{25,17},{2,10},{10... | collective-permute-start | bytes 98312 | tf_op jit(solution)/shard_map/ppermute | solution.py:800
  4.7 2.6 %collective-permute-start.1 = (f32[8,8,128]{2,1,0:T(8,128)S(1)}, f32[8,8,128]{2,1,0:T(8,128)S(1)}, u32[]{:S(2)}, u32[]{:S(2)}) collective-permute-start(f32[8,8,128]{2,1,0:T(8,128)S(1)} %get-tuple-element.21), channel_id=1, source_target_pairs={{0,16},{8,24},{16,0},{24,8},{1,17},{9,25},{17,1},{25,9},{2,18},{10... | collective-permute-start | bytes 98312 | tf_op jit(solution)/shard_map/ppermute | solution.py:800
  7.3 0.0 collective-permute-start.2
  7.3 2.3 %shard_map.86 = (f32[8,20,8,128]{3,2,1,0:T(8,128)S(1)}, f32[4,8,128]{2,1,0:T(8,128)S(1)}) custom-call(f32[27,4,8,128]{3,2,1,0:T(8,128)} %refs_0_.4, f32[3,4,8,128]{3,2,1,0:T(8,128)} %refs_1_.2, s32[4,8,128]{2,1,0:T(8,128)} %refs_2_.2), custom_call_target="tpu_custom_call" | custom-call | tf_op jit(solution)/shard_map/pallas_call | solution.py:756
  9.6 0.0 collective-permute-done.refs_3_
  9.6 0.5 collective-permute-done.1.refs_4_
  10.1 2.9 %collective-permute-done.2.refs_5_ = f32[8,8,128]{2,1,0:T(8,128)S(1)} collective-permute-done((f32[8,8,128]{2,1,0:T(8,128)S(1)}, f32[8,8,128]{2,1,0:T(8,128)S(1)}, u32[]{:S(2)}, u32[]{:S(2)}) %collective-permute-start.2) | collective-permute-done | bytes 32800 | tf_op jit(solution)/shard_map/ppermute | solution.py:800
  13.0 0.3 shard_map.88
  13.4 0.3 collective-permute-start.9
  13.7 2.2 %collective-permute-start.8 = (f32[20,8,128]{2,1,0:T(8,128)S(1)}, f32[20,8,128]{2,1,0:T(8,128)S(1)}, u32[]{:S(2)}, u32[]{:S(2)}) collective-permute-start(f32[20,8,128]{2,1,0:T(8,128)S(1)} %get-tuple-element.33), channel_id=1, source_target_pairs={{0,6},{1,7},{2,4},{3,5},{4,2},{5,3},{6,0},{7,1},{8,14},{9,15},{10,... | collective-permute-start | bytes 245768 | tf_op jit(solution)/shard_map/ppermute | solution.py:794
  16.0 1.4 %collective-permute-start.7 = (f32[20,8,128]{2,1,0:T(8,128)S(1)}, f32[20,8,128]{2,1,0:T(8,128)S(1)}, u32[]{:S(2)}, u32[]{:S(2)}) collective-permute-start(f32[20,8,128]{2,1,0:T(8,128)S(1)} %get-tuple-element.34), channel_id=1, source_target_pairs={{0,5},{1,4},{2,7},{3,6},{4,1},{5,0},{6,3},{7,2},{8,13},{9,12},{10,... | collective-permute-start | bytes 245768 | tf_op jit(solution)/shard_map/ppermute | solution.py:794
  17.3 0.5 collective-permute-start.6
  17.8 0.7 %collective-permute-start.5 = (f32[20,8,128]{2,1,0:T(8,128)S(1)}, f32[20,8,128]{2,1,0:T(8,128)S(1)}, u32[]{:S(2)}, u32[]{:S(2)}) collective-permute-start(f32[20,8,128]{2,1,0:T(8,128)S(1)} %get-tuple-element.36), channel_id=1, source_target_pairs={{0,3},{1,2},{2,1},{3,0},{4,7},{5,6},{6,5},{7,4},{8,11},{9,10},{10,... | collective-permute-start | bytes 245768 | tf_op jit(solution)/shard_map/ppermute | solution.py:794
  18.6 0.4 collective-permute-done.9.refs_7_
  19.0 1.0 %collective-permute-start.4 = (f32[20,8,128]{2,1,0:T(8,128)S(1)}, f32[20,8,128]{2,1,0:T(8,128)S(1)}, u32[]{:S(2)}, u32[]{:S(2)}) collective-permute-start(f32[20,8,128]{2,1,0:T(8,128)S(1)} %get-tuple-element.37), channel_id=1, source_target_pairs={{0,2},{1,3},{2,0},{3,1},{4,6},{5,7},{6,4},{7,5},{8,10},{9,11},{10,... | collective-permute-start | bytes 245768 | tf_op jit(solution)/shard_map/ppermute | solution.py:794
  20.0 0.4 collective-permute-done.8.refs_6_
  20.5 0.3 collective-permute-start.3
  20.8 1.8 %collective-permute-done.7.refs_5_ = f32[20,8,128]{2,1,0:T(8,128)S(1)} collective-permute-done((f32[20,8,128]{2,1,0:T(8,128)S(1)}, f32[20,8,128]{2,1,0:T(8,128)S(1)}, u32[]{:S(2)}, u32[]{:S(2)}) %collective-permute-start.7) | collective-permute-done | bytes 81952 | tf_op jit(solution)/shard_map/ppermute | solution.py:794
  22.6 1.8 %collective-permute-done.6.refs_4_ = f32[20,8,128]{2,1,0:T(8,128)S(1)} collective-permute-done((f32[20,8,128]{2,1,0:T(8,128)S(1)}, f32[20,8,128]{2,1,0:T(8,128)S(1)}, u32[]{:S(2)}, u32[]{:S(2)}) %collective-permute-start.6) | collective-permute-done | bytes 81952 | tf_op jit(solution)/shard_map/ppermute | solution.py:794
  24.3 0.0 collective-permute-done.5.refs_3_
  24.4 0.0 collective-permute-done.4.refs_2_
  24.4 0.0 collective-permute-done.3.refs_1_
  24.4 0.5 shard_map.89
  24.9 0.1 collective-permute-start.10
  25.0 3.5 %collective-permute-start.11 = (f32[4,20,8,128]{3,2,1,0:T(8,128)S(1)}, f32[4,20,8,128]{3,2,1,0:T(8,128)S(1)}, u32[]{:S(2)}, u32[]{:S(2)}) collective-permute-start(f32[4,20,8,128]{3,2,1,0:T(8,128)S(1)} %get-tuple-element.25), channel_id=1, source_target_pairs={{0,25},{1,0},{2,1},{3,2},{7,3},{6,7},{5,6},{4,5},{13,4},{12,13},{8... | collective-permute-start | bytes 983048 | tf_op jit(solution)/shard_map/ppermute | solution.py:784
  28.5 4.8 %collective-permute-done.10.refs_2_ = f32[4,20,8,128]{3,2,1,0:T(8,128)S(1)} collective-permute-done((f32[4,20,8,128]{3,2,1,0:T(8,128)S(1)}, f32[4,20,8,128]{3,2,1,0:T(8,128)S(1)}, u32[]{:S(2)}, u32[]{:S(2)}) %collective-permute-start.10) | collective-permute-done | bytes 327712 | tf_op jit(solution)/shard_map/ppermute | solution.py:783
  33.2 0.0 collective-permute-done.11.refs_3_
  33.2 10.7 %shard_map.90 = (f32[27,8,8,128]{3,2,1,0:T(8,128)S(1)}, f32[2,8,8,128]{3,2,1,0:T(8,128)S(1)}, f32[8,8,128]{2,1,0:T(8,128)S(1)}, f32[8,8,128]{2,1,0:T(8,128)S(1)}...) custom-call(f32[27]{0:T(128)} %refs_0_.7, f32[8,20,8,128]{3,2,1,0:T(8,128)S(1)} %get-tuple-element.23.refs_1_, ...), custom_call_target="tpu_custom_call" | custom-call | tf_op jit(solution)/shard_map/pallas_call | solution.py:756
  44.0 0.1 collective-permute-start.12
  44.1 0.1 collective-permute-start.13
  44.1 4.3 %collective-permute-start.14 = (f32[8,8,128]{2,1,0:T(8,128)S(1)}, f32[8,8,128]{2,1,0:T(8,128)S(1)}, u32[]{:S(2)}, u32[]{:S(2)}) collective-permute-start(f32[8,8,128]{2,1,0:T(8,128)S(1)} %get-tuple-element.31), channel_id=1, source_target_pairs={{0,24},{8,16},{16,8},{24,0},{1,25},{9,17},{17,9},{25,1},{2,26},{10... | collective-permute-start | bytes 98312 | tf_op jit(solution)/shard_map/ppermute | solution.py:800
  48.4 5.9 %shard_map.91.refs_0_ = f32[8,18,8,128]{3,2,1,0:T(8,128)S(1)} custom-call(f32[27]{0:T(128)} %refs_0_.7, f32[8,20,8,128]{3,2,1,0:T(8,128)S(1)} %get-tuple-element.23.refs_1_, f32[27,8,8,128]{3,2,1,0:T(8,128)S(1)} %get-tuple-element.26.refs_2_, f32[2,8,8,128]{3,2,1,0:T(8,128)S(1)} %get-tuple-element.27.refs_3_), custom_call_target="tpu_custom_call" | custom-call | tf_op jit(solution)/shard_map/pallas_call | solution.py:756
  54.3 0.0 collective-permute-done.12.refs_2_
  54.3 0.0 collective-permute-done.13.refs_3_
  54.4 0.0 collective-permute-done.14.refs_4_
  54.4 0.1 shard_map.92
  54.5 0.1 collective-permute-start.21
  54.6 2.1 %collective-permute-start.20 = (f32[18,8,128]{2,1,0:T(8,128)S(1)}, f32[18,8,128]{2,1,0:T(8,128)S(1)}, u32[]{:S(2)}, u32[]{:S(2)}) collective-permute-start(f32[18,8,128]{2,1,0:T(8,128)S(1)} %get-tuple-element.41), channel_id=1, source_target_pairs={{0,6},{1,7},{2,4},{3,5},{4,2},{5,3},{6,0},{7,1},{8,14},{9,15},{10,... | collective-permute-start | bytes 221192 | tf_op jit(solution)/shard_map/ppermute | solution.py:794
  56.6 0.0 collective-permute-start.19
  56.7 2.3 %collective-permute-start.18 = (f32[18,8,128]{2,1,0:T(8,128)S(1)}, f32[18,8,128]{2,1,0:T(8,128)S(1)}, u32[]{:S(2)}, u32[]{:S(2)}) collective-permute-start(f32[18,8,128]{2,1,0:T(8,128)S(1)} %get-tuple-element.43), channel_id=1, source_target_pairs={{0,4},{1,5},{2,6},{3,7},{4,0},{5,1},{6,2},{7,3},{8,12},{9,13},{10,... | collective-permute-start | bytes 221192 | tf_op jit(solution)/shard_map/ppermute | solution.py:794
  59.0 0.0 collective-permute-start.17
  59.0 1.1 %collective-permute-done.21.refs_7_ = f32[18,8,128]{2,1,0:T(8,128)S(1)} collective-permute-done((f32[18,8,128]{2,1,0:T(8,128)S(1)}, f32[18,8,128]{2,1,0:T(8,128)S(1)}, u32[]{:S(2)}, u32[]{:S(2)}) %collective-permute-start.21) | collective-permute-done | bytes 73760 | tf_op jit(solution)/shard_map/ppermute | solution.py:794
  60.1 0.1 collective-permute-start.16
  60.1 1.0 %collective-permute-done.20.refs_6_ = f32[18,8,128]{2,1,0:T(8,128)S(1)} collective-permute-done((f32[18,8,128]{2,1,0:T(8,128)S(1)}, f32[18,8,128]{2,1,0:T(8,128)S(1)}, u32[]{:S(2)}, u32[]{:S(2)}) %collective-permute-start.20) | collective-permute-done | bytes 73760 | tf_op jit(solution)/shard_map/ppermute | solution.py:794
  61.2 0.1 collective-permute-start.15
  61.3 1.6 %collective-permute-done.19.refs_5_ = f32[18,8,128]{2,1,0:T(8,128)S(1)} collective-permute-done((f32[18,8,128]{2,1,0:T(8,128)S(1)}, f32[18,8,128]{2,1,0:T(8,128)S(1)}, u32[]{:S(2)}, u32[]{:S(2)}) %collective-permute-start.19) | collective-permute-done | bytes 73760 | tf_op jit(solution)/shard_map/ppermute | solution.py:794
  62.8 1.7 %collective-permute-done.18.refs_4_ = f32[18,8,128]{2,1,0:T(8,128)S(1)} collective-permute-done((f32[18,8,128]{2,1,0:T(8,128)S(1)}, f32[18,8,128]{2,1,0:T(8,128)S(1)}, u32[]{:S(2)}, u32[]{:S(2)}) %collective-permute-start.18) | collective-permute-done | bytes 73760 | tf_op jit(solution)/shard_map/ppermute | solution.py:794
  64.5 0.0 collective-permute-done.17.refs_3_
  64.5 0.3 collective-permute-done.16.refs_2_
  64.8 0.0 collective-permute-done.15.refs_1_
  64.8 2.4 %shard_map.93 = (f32[27,4,8,128]{3,2,1,0:T(8,128)}, f32[7,1,8,512]{3,2,1,0:T(8,128)}) custom-call(f32[18,8,128]{2,1,0:T(8,128)S(1)} %get-tuple-element.47.refs_0_, f32[18,8,128]{2,1,0:T(8,128)S(1)} %collective-permute-done.15.refs_1_, f32[18,8,128]{2,1,0:T(8,128)S(1)} %collective-permute-done.16.refs_2_, f32[18,8,128]{2,1,0:T(8,128)S(1)} %collective-permute-done.17.refs_3_, ...), custom_call_target="tpu_custom_call" | custom-call | tf_op jit(solution)/shard_map/pallas_call | solution.py:756
  (2 shorter events, 0.1 us)
Async XLA Ops:
  1.6 8.0 %collective-permute-start = (f32[8,8,128]{2,1,0:T(8,128)S(1)}, f32[8,8,128]{2,1,0:T(8,128)S(1)}, u32[]{:S(2)}, u32[]{:S(2)}) collective-permute-start(f32[8,8,128]{2,1,0:T(8,128)S(1)} %get-tuple-element.20), channel_id=1, source_target_pairs={{0,8},{8,0},{16,24},{24,16},{1,9},{9,1},{17,25},{25,17},{2,10},{10... | collective-permute-start | bytes 98312 | tf_op jit(solution)/shard_map/ppermute | solution.py:800
  4.7 5.4 %collective-permute-start.1 = (f32[8,8,128]{2,1,0:T(8,128)S(1)}, f32[8,8,128]{2,1,0:T(8,128)S(1)}, u32[]{:S(2)}, u32[]{:S(2)}) collective-permute-start(f32[8,8,128]{2,1,0:T(8,128)S(1)} %get-tuple-element.21), channel_id=1, source_target_pairs={{0,16},{8,24},{16,0},{24,8},{1,17},{9,25},{17,1},{25,9},{2,18},{10... | collective-permute-start | bytes 98312 | tf_op jit(solution)/shard_map/ppermute | solution.py:800
  7.3 5.7 %collective-permute-start.2 = (f32[8,8,128]{2,1,0:T(8,128)S(1)}, f32[8,8,128]{2,1,0:T(8,128)S(1)}, u32[]{:S(2)}, u32[]{:S(2)}) collective-permute-start(f32[8,8,128]{2,1,0:T(8,128)S(1)} %get-tuple-element.22), channel_id=1, source_target_pairs={{0,24},{8,16},{16,8},{24,0},{1,25},{9,17},{17,9},{25,1},{2,26},{10... | collective-permute-start | bytes 98312 | tf_op jit(solution)/shard_map/ppermute | solution.py:800
  13.4 5.6 %collective-permute-start.9 = (f32[20,8,128]{2,1,0:T(8,128)S(1)}, f32[20,8,128]{2,1,0:T(8,128)S(1)}, u32[]{:S(2)}, u32[]{:S(2)}) collective-permute-start(f32[20,8,128]{2,1,0:T(8,128)S(1)} %get-tuple-element.32), channel_id=1, source_target_pairs={{0,7},{1,6},{2,5},{3,4},{4,3},{5,2},{6,1},{7,0},{8,15},{9,14},{10,... | collective-permute-start | bytes 245768 | tf_op jit(solution)/shard_map/ppermute | solution.py:794
  13.7 6.7 %collective-permute-start.8 = (f32[20,8,128]{2,1,0:T(8,128)S(1)}, f32[20,8,128]{2,1,0:T(8,128)S(1)}, u32[]{:S(2)}, u32[]{:S(2)}) collective-permute-start(f32[20,8,128]{2,1,0:T(8,128)S(1)} %get-tuple-element.33), channel_id=1, source_target_pairs={{0,6},{1,7},{2,4},{3,5},{4,2},{5,3},{6,0},{7,1},{8,14},{9,15},{10,... | collective-permute-start | bytes 245768 | tf_op jit(solution)/shard_map/ppermute | solution.py:794
  16.0 6.6 %collective-permute-start.7 = (f32[20,8,128]{2,1,0:T(8,128)S(1)}, f32[20,8,128]{2,1,0:T(8,128)S(1)}, u32[]{:S(2)}, u32[]{:S(2)}) collective-permute-start(f32[20,8,128]{2,1,0:T(8,128)S(1)} %get-tuple-element.34), channel_id=1, source_target_pairs={{0,5},{1,4},{2,7},{3,6},{4,1},{5,0},{6,3},{7,2},{8,13},{9,12},{10,... | collective-permute-start | bytes 245768 | tf_op jit(solution)/shard_map/ppermute | solution.py:794
  17.3 7.0 %collective-permute-start.6 = (f32[20,8,128]{2,1,0:T(8,128)S(1)}, f32[20,8,128]{2,1,0:T(8,128)S(1)}, u32[]{:S(2)}, u32[]{:S(2)}) collective-permute-start(f32[20,8,128]{2,1,0:T(8,128)S(1)} %get-tuple-element.35), channel_id=1, source_target_pairs={{0,4},{1,5},{2,6},{3,7},{4,0},{5,1},{6,2},{7,3},{8,12},{9,13},{10,... | collective-permute-start | bytes 245768 | tf_op jit(solution)/shard_map/ppermute | solution.py:794
  17.8 6.5 %collective-permute-start.5 = (f32[20,8,128]{2,1,0:T(8,128)S(1)}, f32[20,8,128]{2,1,0:T(8,128)S(1)}, u32[]{:S(2)}, u32[]{:S(2)}) collective-permute-start(f32[20,8,128]{2,1,0:T(8,128)S(1)} %get-tuple-element.36), channel_id=1, source_target_pairs={{0,3},{1,2},{2,1},{3,0},{4,7},{5,6},{6,5},{7,4},{8,11},{9,10},{10,... | collective-permute-start | bytes 245768 | tf_op jit(solution)/shard_map/ppermute | solution.py:794
  19.0 5.4 %collective-permute-start.4 = (f32[20,8,128]{2,1,0:T(8,128)S(1)}, f32[20,8,128]{2,1,0:T(8,128)S(1)}, u32[]{:S(2)}, u32[]{:S(2)}) collective-permute-start(f32[20,8,128]{2,1,0:T(8,128)S(1)} %get-tuple-element.37), channel_id=1, source_target_pairs={{0,2},{1,3},{2,0},{3,1},{4,6},{5,7},{6,4},{7,5},{8,10},{9,11},{10,... | collective-permute-start | bytes 245768 | tf_op jit(solution)/shard_map/ppermute | solution.py:794
  20.5 3.9 %collective-permute-start.3 = (f32[20,8,128]{2,1,0:T(8,128)S(1)}, f32[20,8,128]{2,1,0:T(8,128)S(1)}, u32[]{:S(2)}, u32[]{:S(2)}) collective-permute-start(f32[20,8,128]{2,1,0:T(8,128)S(1)} %get-tuple-element.38), channel_id=1, source_target_pairs={{0,1},{1,0},{2,3},{3,2},{4,5},{5,4},{6,7},{7,6},{8,9},{9,8},{10,11... | collective-permute-start | bytes 245768 | tf_op jit(solution)/shard_map/ppermute | solution.py:794
  24.9 8.4 %collective-permute-start.10 = (f32[4,20,8,128]{3,2,1,0:T(8,128)S(1)}, f32[4,20,8,128]{3,2,1,0:T(8,128)S(1)}, u32[]{:S(2)}, u32[]{:S(2)}) collective-permute-start(f32[4,20,8,128]{3,2,1,0:T(8,128)S(1)} %get-tuple-element.24), channel_id=1, source_target_pairs={{25,0},{0,1},{1,2},{2,3},{3,7},{7,6},{6,5},{5,4},{4,13},{13,12},{1... | collective-permute-start | bytes 983048 | tf_op jit(solution)/shard_map/ppermute | solution.py:783
  25.0 8.2 %collective-permute-start.11 = (f32[4,20,8,128]{3,2,1,0:T(8,128)S(1)}, f32[4,20,8,128]{3,2,1,0:T(8,128)S(1)}, u32[]{:S(2)}, u32[]{:S(2)}) collective-permute-start(f32[4,20,8,128]{3,2,1,0:T(8,128)S(1)} %get-tuple-element.25), channel_id=1, source_target_pairs={{0,25},{1,0},{2,1},{3,2},{7,3},{6,7},{5,6},{4,5},{13,4},{12,13},{8... | collective-permute-start | bytes 983048 | tf_op jit(solution)/shard_map/ppermute | solution.py:784
  44.0 10.3 %collective-permute-start.12 = (f32[8,8,128]{2,1,0:T(8,128)S(1)}, f32[8,8,128]{2,1,0:T(8,128)S(1)}, u32[]{:S(2)}, u32[]{:S(2)}) collective-permute-start(f32[8,8,128]{2,1,0:T(8,128)S(1)} %get-tuple-element.29), channel_id=1, source_target_pairs={{0,8},{8,0},{16,24},{24,16},{1,9},{9,1},{17,25},{25,17},{2,10},{10... | collective-permute-start | bytes 98312 | tf_op jit(solution)/shard_map/ppermute | solution.py:800
  44.1 10.3 %collective-permute-start.13 = (f32[8,8,128]{2,1,0:T(8,128)S(1)}, f32[8,8,128]{2,1,0:T(8,128)S(1)}, u32[]{:S(2)}, u32[]{:S(2)}) collective-permute-start(f32[8,8,128]{2,1,0:T(8,128)S(1)} %get-tuple-element.30), channel_id=1, source_target_pairs={{0,16},{8,24},{16,0},{24,8},{1,17},{9,25},{17,1},{25,9},{2,18},{10... | collective-permute-start | bytes 98312 | tf_op jit(solution)/shard_map/ppermute | solution.py:800
  44.1 10.2 %collective-permute-start.14 = (f32[8,8,128]{2,1,0:T(8,128)S(1)}, f32[8,8,128]{2,1,0:T(8,128)S(1)}, u32[]{:S(2)}, u32[]{:S(2)}) collective-permute-start(f32[8,8,128]{2,1,0:T(8,128)S(1)} %get-tuple-element.31), channel_id=1, source_target_pairs={{0,24},{8,16},{16,8},{24,0},{1,25},{9,17},{17,9},{25,1},{2,26},{10... | collective-permute-start | bytes 98312 | tf_op jit(solution)/shard_map/ppermute | solution.py:800
  54.5 5.6 %collective-permute-start.21 = (f32[18,8,128]{2,1,0:T(8,128)S(1)}, f32[18,8,128]{2,1,0:T(8,128)S(1)}, u32[]{:S(2)}, u32[]{:S(2)}) collective-permute-start(f32[18,8,128]{2,1,0:T(8,128)S(1)} %get-tuple-element.40), channel_id=1, source_target_pairs={{0,7},{1,6},{2,5},{3,4},{4,3},{5,2},{6,1},{7,0},{8,15},{9,14},{10,... | collective-permute-start | bytes 221192 | tf_op jit(solution)/shard_map/ppermute | solution.py:794
  54.6 6.6 %collective-permute-start.20 = (f32[18,8,128]{2,1,0:T(8,128)S(1)}, f32[18,8,128]{2,1,0:T(8,128)S(1)}, u32[]{:S(2)}, u32[]{:S(2)}) collective-permute-start(f32[18,8,128]{2,1,0:T(8,128)S(1)} %get-tuple-element.41), channel_id=1, source_target_pairs={{0,6},{1,7},{2,4},{3,5},{4,2},{5,3},{6,0},{7,1},{8,14},{9,15},{10,... | collective-permute-start | bytes 221192 | tf_op jit(solution)/shard_map/ppermute | solution.py:794
  56.6 6.2 %collective-permute-start.19 = (f32[18,8,128]{2,1,0:T(8,128)S(1)}, f32[18,8,128]{2,1,0:T(8,128)S(1)}, u32[]{:S(2)}, u32[]{:S(2)}) collective-permute-start(f32[18,8,128]{2,1,0:T(8,128)S(1)} %get-tuple-element.42), channel_id=1, source_target_pairs={{0,5},{1,4},{2,7},{3,6},{4,1},{5,0},{6,3},{7,2},{8,13},{9,12},{10,... | collective-permute-start | bytes 221192 | tf_op jit(solution)/shard_map/ppermute | solution.py:794
  56.7 7.8 %collective-permute-start.18 = (f32[18,8,128]{2,1,0:T(8,128)S(1)}, f32[18,8,128]{2,1,0:T(8,128)S(1)}, u32[]{:S(2)}, u32[]{:S(2)}) collective-permute-start(f32[18,8,128]{2,1,0:T(8,128)S(1)} %get-tuple-element.43), channel_id=1, source_target_pairs={{0,4},{1,5},{2,6},{3,7},{4,0},{5,1},{6,2},{7,3},{8,12},{9,13},{10,... | collective-permute-start | bytes 221192 | tf_op jit(solution)/shard_map/ppermute | solution.py:794
  59.0 5.6 %collective-permute-start.17 = (f32[18,8,128]{2,1,0:T(8,128)S(1)}, f32[18,8,128]{2,1,0:T(8,128)S(1)}, u32[]{:S(2)}, u32[]{:S(2)}) collective-permute-start(f32[18,8,128]{2,1,0:T(8,128)S(1)} %get-tuple-element.44), channel_id=1, source_target_pairs={{0,3},{1,2},{2,1},{3,0},{4,7},{5,6},{6,5},{7,4},{8,11},{9,10},{10,... | collective-permute-start | bytes 221192 | tf_op jit(solution)/shard_map/ppermute | solution.py:794
  60.1 4.8 %collective-permute-start.16 = (f32[18,8,128]{2,1,0:T(8,128)S(1)}, f32[18,8,128]{2,1,0:T(8,128)S(1)}, u32[]{:S(2)}, u32[]{:S(2)}) collective-permute-start(f32[18,8,128]{2,1,0:T(8,128)S(1)} %get-tuple-element.45), channel_id=1, source_target_pairs={{0,2},{1,3},{2,0},{3,1},{4,6},{5,7},{6,4},{7,5},{8,10},{9,11},{10,... | collective-permute-start | bytes 221192 | tf_op jit(solution)/shard_map/ppermute | solution.py:794
  61.2 3.7 %collective-permute-start.15 = (f32[18,8,128]{2,1,0:T(8,128)S(1)}, f32[18,8,128]{2,1,0:T(8,128)S(1)}, u32[]{:S(2)}, u32[]{:S(2)}) collective-permute-start(f32[18,8,128]{2,1,0:T(8,128)S(1)} %get-tuple-element.46), channel_id=1, source_target_pairs={{0,1},{1,0},{2,3},{3,2},{4,5},{5,4},{6,7},{7,6},{8,9},{9,8},{10,11... | collective-permute-start | bytes 221192 | tf_op jit(solution)/shard_map/ppermute | solution.py:794

commit v4 on v3

--- a/solution.py
+++ b/solution.py
@@ -241,6 +241,9 @@
         )
         if self.fits:
             self.turn = self.sub // self.grp
+            partners = [step for k in (1, 0) for step in range(self.sub - 2 + k, 1, -2)]
+            partners.sort(key=lambda step: bin(step >> 1).count("1"))
+            self.steps = [0, 1] + partners
             self.ring = [
                 part * self.sub + self.round_plane((place - self.turn * part) % self.sub)
                 for part in range(self.grp)
@@ -376,8 +379,8 @@
 
 def collect(slab, parts, came):
     mine = slab.place_in_plane()
-    for step in range(slab.sub):
-        came[jnp.bitwise_xor(mine, step)] = parts[step][...]
+    for part, step in zip(parts, slab.steps):
+        came[jnp.bitwise_xor(mine, step)] = part[...]
 
 
 def offer_halo(slab, *refs):
@@ -441,23 +444,35 @@
 
 
 def unpack_out(slab, *refs):
-    parts, (popul_out, thermal_out, came) = refs[: slab.sub], refs[slab.sub :]
-    for step in range(slab.sub):
-        came[step] = parts[step][...]
+    parts, (popul_hbm, thermal_hbm, came, popul, thermal, sems) = refs[: slab.sub], refs[slab.sub :]
+    for part, step in zip(parts, slab.steps):
+        came[step] = part[...]
     mine = lax.axis_index("grp")
-    holders = slab.holders(mine)
-    for pair in range(FLOW_PAIRS):
-        sources = [came[holders[place], pair] for place in range(slab.sub)]
-        for number, value in enumerate(swap_groups(sources, slab.planes)):
-            if 2 * pair + number % 2 < 27:
-                popul_out[2 * pair + number % 2, number // 2] = value
     for step in range(slab.grp):
         part = jnp.bitwise_xor(mine, step)
         holders = slab.holders(part)
         span = pl.ds(pl.multiple_of(part * LANES, LANES), LANES)
         sources = [came[holders[place], FLOW_PAIRS + step] for place in range(slab.sub)]
         for k, value in enumerate(swap_groups(sources, slab.planes)[:7]):
-            thermal_out[k, 0, :, span] = value
+            thermal[k, 0, :, span] = value
+    copies = [pltpu.make_async_copy(thermal, thermal_hbm, sems.at[0])]
+    copies[0].start()
+    holders = slab.holders(mine)
+    begin = 0
+    for pair in range(FLOW_PAIRS):
+        sources = [came[holders[place], pair] for place in range(slab.sub)]
+        for number, value in enumerate(swap_groups(sources, slab.planes)):
+            if 2 * pair + number % 2 < 27:
+                popul[2 * pair + number % 2, number // 2] = value
+        end = min(2 * pair + 2, 27)
+        if pair % 4 == 3 or end == 27:
+            rows = pl.ds(begin, end - begin)
+            sem = sems.at[len(copies)]
+            copies.append(pltpu.make_async_copy(popul.at[rows], popul_hbm.at[rows], sem))
+            copies[-1].start()
+            begin = end
+    for copy in copies:
+        copy.wait()
 
 
 def forward3(values):
@@ -562,7 +577,7 @@
 
 
 def stream(slab, post, tile, offsets):
-    block_x, block_y = tile // slab.gy, tile % slab.gy
+    block_x, block_y = lax.div(tile, slab.gy), lax.rem(tile, slab.gy)
     x_of = {a: lax.rem(block_x + slab.gx - a, slab.gx) for a in (-1, 0, 1)}
     y_of = {b: lax.rem(block_y + slab.gy - b, slab.gy) for b in (-1, 0, 1)}
     row = row_index()
@@ -616,7 +631,7 @@
 
 def first_window(slab, rates_hbm, came, below_ref, above_ref, *refs):
     flow_out, keep_out, heat_outs = refs[0], refs[1], refs[2 : 2 + slab.grp]
-    rates_ref, sem, state, flow_post, heat_post, held = refs[2 + slab.grp :]
+    rates_ref, sem, state, flow_post, heat_post, heat_a, heat_b, held = refs[2 + slab.grp :]
     rates_copy = pltpu.make_async_copy(rates_hbm, rates_ref, sem)
     rates_copy.start()
     make_tiles(slab, came, below_ref, above_ref, state)
@@ -665,25 +680,22 @@
         force = heat_force(heat)
         keep_out[0, tile] = force
         collide_flow(rates_ref, flow, force, solid, flow_out, tile)
-        collide_heat(heat, state[RATE_AT, tile], speeds, heat_post.at[1 - source], tile)
+        collide_heat(heat, state[RATE_AT, tile], speeds, heat_a, tile)
 
     over_tiles(slab, next_window)
-
-    def heat_step(number):
-        source = lax.rem(number + STEPS, 2)
-
-        def go_on(tile):
-            heat = stream(slab, heat_post.at[source], tile, HEAT_OFFSETS)
-            omega = state[RATE_AT, tile]
-            collide_heat(heat, omega, speeds_of(tile), heat_post.at[1 - source], tile)
-
-        over_tiles(slab, go_on, unroll=2)
-
-    over_steps(STEPS - 1, heat_step)
+    here, there = heat_a, heat_b
+    for _ in range(STEPS - 1):
+
+        def heat_alone(tile, here=here, there=there):
+            heat = stream(slab, here, tile, HEAT_OFFSETS)
+            collide_heat(heat, state[RATE_AT, tile], speeds_of(tile), there, tile)
+
+        over_tiles(slab, heat_alone, unroll=4)
+        here, there = there, here
     zero = jnp.zeros((SUBLANES, LANES), F32)
 
     def end_heat(tile):
-        heat = stream(slab, heat_post.at[(2 * STEPS - 1) % 2], tile, HEAT_OFFSETS)
+        heat = stream(slab, here, tile, HEAT_OFFSETS)
         heat += [zero] * (slab.sub - 7)
         for x, value in enumerate(swap_groups(heat, slab.planes)[0::2]):
             held[x, tile] = value
@@ -749,7 +761,7 @@
     return [each / total for each in sums]
 
 
-def local_call(body, slab, arrays, outs, scratch=(), in_hbm=0, carried=False):
+def local_call(body, slab, arrays, outs, scratch=(), in_hbm=0, carried=False, outs_in_hbm=False):
     def kernel(*refs):
         body(slab, *refs)
 
@@ -762,7 +774,10 @@
             )
             for i in range(len(arrays))
         ],
-        out_specs=[pl.BlockSpec(memory_space=pl.ANY if carried else pltpu.VMEM)] * len(outs),
+        out_specs=[
+            pl.BlockSpec(memory_space=pl.ANY if carried or outs_in_hbm else pltpu.VMEM)
+        ]
+        * len(outs),
         input_output_aliases={0: 0} if carried else {},
         scratch_shapes=[pltpu.VMEM(s, F32) if isinstance(s, tuple) else s for s in scratch],
         compiler_params=pltpu.CompilerParams(vmem_limit_bytes=24 * 1024 * 1024),
@@ -787,12 +802,10 @@
 
 def across_plane(slab, sent):
     came = {0: sent[0]}
-    far_first = [step for k in range(2) for step in range(2 + k, slab.sub, 2)] + [1]
-    far_first.sort(key=lambda step: -bin(step >> 1).count("1"))
-    for step in far_first:
+    for step in slab.steps[1:]:
         pairs = [(i, i ^ step) for i in range(slab.sub)]
         came[step] = lax.ppermute(sent[step], ("gx", "gy"), pairs)
-    return [came[step] for step in range(slab.sub)]
+    return [came[step] for step in slab.steps]
 
 
 def across_planes(slab, parts):
@@ -859,7 +872,7 @@
         slab,
         [rates, came, below, above],
         [(27,) + plane, (2,) + plane] + [plane] * slab.grp,
-        scalars + [(ROWS,) + plane, (2, 27) + plane, (2, 7) + plane, (slab.grp,) + plane],
+        scalars + [(ROWS,) + plane, (2, 27) + plane, (2, 7) + plane] + [(7,) + plane] * 2 + [(slab.grp,) + plane],
         in_hbm=1,
     )
     parts = across_planes(slab, parts)
@@ -886,7 +899,13 @@
             slab,
             across_plane(slab, sent),
             [populations.shape, thermal.shape],
-            [last_shape],
+            [
+                last_shape,
+                populations.shape,
+                thermal.shape,
+                pltpu.SemaphoreType.DMA((1 + -(-FLOW_PAIRS // 4),)),
+            ],
+            outs_in_hbm=True,
         )
     )
 

time: 67.4 us -> 65.8 us (0.976)
  Pallas kernels: 23.2 us -> 21.9 us
  waiting for transfers between devices: 18.3 us -> 17 us
  starting transfers between devices: 24.9 us -> 25.8 us
    ppermute x14, waiting for transfers between devices: 10.1 us -> 8.84 us  [across_plane(): came[step] = lax.ppermute(sent[step], ('gx', 'gy'), pairs)]
    pallas_call x8, Pallas kernels: 23.2 us -> 21.9 us  [local_call(): pl.pallas_call(kernel, out_shape=[jax.ShapeDtypeStruct(shape, F32) for sh...]
    ppermute x14, starting transfers between devices: 11.2 us -> 12.1 us  [across_plane(): came[step] = lax.ppermute(sent[step], ('gx', 'gy'), pairs)]
  transfers between devices with their start and end apart: 22 -> 22, of which waited for: 12 -> 11; matrix products, arithmetic and copies ran while one was open for 0% -> 0% of each run, Pallas kernels for 12% -> 12%
where the time goes in v4:
time: 65.8 us; the launch traced here: 65.6 us
  starting transfers between devices  25.8 us (39%)
  Pallas kernels  21.9 us (33%)
  waiting for transfers between devices  17 us (26%)
  between operations  0.78 us (1%)
    pallas_call x8, Pallas kernels, local_call(): pl.pallas_call(kernel, out_shape=[jax.ShapeDtypeStruct(shape, F32) for sh...  21.9 us
    ppermute x14, starting transfers between devices, across_plane(): came[step] = lax.ppermute(sent[step], ('gx', 'gy'), pairs)  12.1 us
    ppermute x6, starting transfers between devices, across_planes(): lax.ppermute(parts[step], 'grp', [(i, i ^ step) for i in range(slab.grp)])  10.1 us
    ppermute x14, waiting for transfers between devices, across_plane(): came[step] = lax.ppermute(sent[step], ('gx', 'gy'), pairs)  8.84 us
    ppermute x1, waiting for transfers between devices, exchange(): from_below = lax.ppermute(high, RING, upward)  4.75 us
    ppermute x1, starting transfers between devices, exchange(): from_above = lax.ppermute(low, RING, [(b, a) for a, b in upward])  3.53 us
    ppermute x6, waiting for transfers between devices, across_planes(): lax.ppermute(parts[step], 'grp', [(i, i ^ step) for i in range(slab.grp)])  3.44 us
  transfers between devices with their start and end apart: 22, of which 11 were waited for; matrix products, arithmetic and copies ran while one was open for 0% of the time, Pallas kernels for 12%

profile of v4, /device:TPU:0, one launch (start us, length us, event | category | flops | bytes accessed | tf_op | source)
XLA Modules:
  0.0 65.6 jit_solution(10927055776741326598)
XLA Ops:
  0.6 1.0 %shard_map.87 = (f32[8,8,128]{2,1,0:T(8,128)S(1)}, f32[8,8,128]{2,1,0:T(8,128)S(1)}, f32[8,8,128]{2,1,0:T(8,128)S(1)}, f32[8,8,128]{2,1,0:T(8,128)S(1)}) custom-call(f32[4]{0:T(128)} %refs_0_.5, f32[7,1,8,512]{3,2,1,0:T(8,128)} %refs_1_.3, s32[1,8,512]{2,1,0:T(8,128)} %refs_2_.3), custom_call_target="tpu_custom_call" | custom-call | tf_op jit(solution)/shard_map/pallas_call | solution.py:768
  1.6 3.1 %collective-permute-start = (f32[8,8,128]{2,1,0:T(8,128)S(1)}, f32[8,8,128]{2,1,0:T(8,128)S(1)}, u32[]{:S(2)}, u32[]{:S(2)}) collective-permute-start(f32[8,8,128]{2,1,0:T(8,128)S(1)} %get-tuple-element.20), channel_id=1, source_target_pairs={{0,8},{8,0},{16,24},{24,16},{1,9},{9,1},{17,25},{25,17},{2,10},{10... | collective-permute-start | bytes 98312 | tf_op jit(solution)/shard_map/ppermute | solution.py:813
  4.7 2.6 %collective-permute-start.1 = (f32[8,8,128]{2,1,0:T(8,128)S(1)}, f32[8,8,128]{2,1,0:T(8,128)S(1)}, u32[]{:S(2)}, u32[]{:S(2)}) collective-permute-start(f32[8,8,128]{2,1,0:T(8,128)S(1)} %get-tuple-element.21), channel_id=1, source_target_pairs={{0,16},{8,24},{16,0},{24,8},{1,17},{9,25},{17,1},{25,9},{2,18},{10... | collective-permute-start | bytes 98312 | tf_op jit(solution)/shard_map/ppermute | solution.py:813
  7.3 0.0 collective-permute-start.2
  7.3 2.3 %shard_map.86 = (f32[8,20,8,128]{3,2,1,0:T(8,128)S(1)}, f32[4,8,128]{2,1,0:T(8,128)S(1)}) custom-call(f32[27,4,8,128]{3,2,1,0:T(8,128)} %refs_0_.4, f32[3,4,8,128]{3,2,1,0:T(8,128)} %refs_1_.2, s32[4,8,128]{2,1,0:T(8,128)} %refs_2_.2), custom_call_target="tpu_custom_call" | custom-call | tf_op jit(solution)/shard_map/pallas_call | solution.py:768
  9.6 0.0 collective-permute-done.refs_3_
  9.6 0.5 collective-permute-done.1.refs_4_
  10.1 2.9 %collective-permute-done.2.refs_5_ = f32[8,8,128]{2,1,0:T(8,128)S(1)} collective-permute-done((f32[8,8,128]{2,1,0:T(8,128)S(1)}, f32[8,8,128]{2,1,0:T(8,128)S(1)}, u32[]{:S(2)}, u32[]{:S(2)}) %collective-permute-start.2) | collective-permute-done | bytes 32800 | tf_op jit(solution)/shard_map/ppermute | solution.py:813
  13.0 0.3 shard_map.88
  13.4 2.5 %collective-permute-start.9 = (f32[20,8,128]{2,1,0:T(8,128)S(1)}, f32[20,8,128]{2,1,0:T(8,128)S(1)}, u32[]{:S(2)}, u32[]{:S(2)}) collective-permute-start(f32[20,8,128]{2,1,0:T(8,128)S(1)} %get-tuple-element.32), channel_id=1, source_target_pairs={{0,6},{1,7},{2,4},{3,5},{4,2},{5,3},{6,0},{7,1},{8,14},{9,15},{10,... | collective-permute-start | bytes 245768 | tf_op jit(solution)/shard_map/ppermute | solution.py:807
  15.9 0.0 collective-permute-start.8
  15.9 0.5 collective-permute-start.7
  16.4 0.5 collective-permute-start.6
  17.0 2.1 %collective-permute-start.5 = (f32[20,8,128]{2,1,0:T(8,128)S(1)}, f32[20,8,128]{2,1,0:T(8,128)S(1)}, u32[]{:S(2)}, u32[]{:S(2)}) collective-permute-start(f32[20,8,128]{2,1,0:T(8,128)S(1)} %get-tuple-element.36), channel_id=1, source_target_pairs={{0,3},{1,2},{2,1},{3,0},{4,7},{5,6},{6,5},{7,4},{8,11},{9,10},{10,... | collective-permute-start | bytes 245768 | tf_op jit(solution)/shard_map/ppermute | solution.py:807
  19.1 0.0 collective-permute-done.9.refs_7_
  19.1 0.6 collective-permute-start.4
  19.7 1.9 %collective-permute-done.8.refs_6_ = f32[20,8,128]{2,1,0:T(8,128)S(1)} collective-permute-done((f32[20,8,128]{2,1,0:T(8,128)S(1)}, f32[20,8,128]{2,1,0:T(8,128)S(1)}, u32[]{:S(2)}, u32[]{:S(2)}) %collective-permute-start.8) | collective-permute-done | bytes 81952 | tf_op jit(solution)/shard_map/ppermute | solution.py:807
  21.5 0.0 collective-permute-start.3
  21.5 0.9 %collective-permute-done.7.refs_5_ = f32[20,8,128]{2,1,0:T(8,128)S(1)} collective-permute-done((f32[20,8,128]{2,1,0:T(8,128)S(1)}, f32[20,8,128]{2,1,0:T(8,128)S(1)}, u32[]{:S(2)}, u32[]{:S(2)}) %collective-permute-start.7) | collective-permute-done | bytes 81952 | tf_op jit(solution)/shard_map/ppermute | solution.py:807
  22.4 0.0 collective-permute-done.6.refs_4_
  22.4 1.7 %collective-permute-done.5.refs_3_ = f32[20,8,128]{2,1,0:T(8,128)S(1)} collective-permute-done((f32[20,8,128]{2,1,0:T(8,128)S(1)}, f32[20,8,128]{2,1,0:T(8,128)S(1)}, u32[]{:S(2)}, u32[]{:S(2)}) %collective-permute-start.5) | collective-permute-done | bytes 81952 | tf_op jit(solution)/shard_map/ppermute | solution.py:807
  24.1 0.2 collective-permute-done.4.refs_2_
  24.3 0.0 collective-permute-done.3.refs_1_
  24.3 0.5 shard_map.89
  24.8 0.1 collective-permute-start.10
  24.9 3.5 %collective-permute-start.11 = (f32[4,20,8,128]{3,2,1,0:T(8,128)S(1)}, f32[4,20,8,128]{3,2,1,0:T(8,128)S(1)}, u32[]{:S(2)}, u32[]{:S(2)}) collective-permute-start(f32[4,20,8,128]{3,2,1,0:T(8,128)S(1)} %get-tuple-element.25), channel_id=1, source_target_pairs={{0,25},{1,0},{2,1},{3,2},{7,3},{6,7},{5,6},{4,5},{13,4},{12,13},{8... | collective-permute-start | bytes 983048 | tf_op jit(solution)/shard_map/ppermute | solution.py:799
  28.4 4.8 %collective-permute-done.10.refs_2_ = f32[4,20,8,128]{3,2,1,0:T(8,128)S(1)} collective-permute-done((f32[4,20,8,128]{3,2,1,0:T(8,128)S(1)}, f32[4,20,8,128]{3,2,1,0:T(8,128)S(1)}, u32[]{:S(2)}, u32[]{:S(2)}) %collective-permute-start.10) | collective-permute-done | bytes 327712 | tf_op jit(solution)/shard_map/ppermute | solution.py:798
  33.2 0.0 collective-permute-done.11.refs_3_
  33.2 9.4 %shard_map.90 = (f32[27,8,8,128]{3,2,1,0:T(8,128)S(1)}, f32[2,8,8,128]{3,2,1,0:T(8,128)S(1)}, f32[8,8,128]{2,1,0:T(8,128)S(1)}, f32[8,8,128]{2,1,0:T(8,128)S(1)}...) custom-call(f32[27]{0:T(128)} %refs_0_.7, f32[8,20,8,128]{3,2,1,0:T(8,128)S(1)} %get-tuple-element.23.refs_1_, ...), custom_call_target="tpu_custom_call" | custom-call | tf_op jit(solution)/shard_map/pallas_call | solution.py:768
  42.6 0.1 collective-permute-start.12
  42.7 0.1 collective-permute-start.13
  42.8 4.3 %collective-permute-start.14 = (f32[8,8,128]{2,1,0:T(8,128)S(1)}, f32[8,8,128]{2,1,0:T(8,128)S(1)}, u32[]{:S(2)}, u32[]{:S(2)}) collective-permute-start(f32[8,8,128]{2,1,0:T(8,128)S(1)} %get-tuple-element.31), channel_id=1, source_target_pairs={{0,24},{8,16},{16,8},{24,0},{1,25},{9,17},{17,9},{25,1},{2,26},{10... | collective-permute-start | bytes 98312 | tf_op jit(solution)/shard_map/ppermute | solution.py:813
  47.1 5.8 %shard_map.91.refs_0_ = f32[8,18,8,128]{3,2,1,0:T(8,128)S(1)} custom-call(f32[27]{0:T(128)} %refs_0_.7, f32[8,20,8,128]{3,2,1,0:T(8,128)S(1)} %get-tuple-element.23.refs_1_, f32[27,8,8,128]{3,2,1,0:T(8,128)S(1)} %get-tuple-element.26.refs_2_, f32[2,8,8,128]{3,2,1,0:T(8,128)S(1)} %get-tuple-element.27.refs_3_), custom_call_target="tpu_custom_call" | custom-call | tf_op jit(solution)/shard_map/pallas_call | solution.py:768
  52.9 0.0 collective-permute-done.12.refs_2_
  52.9 0.0 collective-permute-done.13.refs_3_
  52.9 0.0 collective-permute-done.14.refs_4_
  52.9 0.1 shard_map.92
  53.1 0.6 collective-permute-start.21
  53.7 1.3 %collective-permute-start.20 = (f32[18,8,128]{2,1,0:T(8,128)S(1)}, f32[18,8,128]{2,1,0:T(8,128)S(1)}, u32[]{:S(2)}, u32[]{:S(2)}) collective-permute-start(f32[18,8,128]{2,1,0:T(8,128)S(1)} %get-tuple-element.41), channel_id=1, source_target_pairs={{0,7},{1,6},{2,5},{3,4},{4,3},{5,2},{6,1},{7,0},{8,15},{9,14},{10,... | collective-permute-start | bytes 221192 | tf_op jit(solution)/shard_map/ppermute | solution.py:807
  54.9 0.0 collective-permute-start.19
  54.9 1.7 %collective-permute-start.18 = (f32[18,8,128]{2,1,0:T(8,128)S(1)}, f32[18,8,128]{2,1,0:T(8,128)S(1)}, u32[]{:S(2)}, u32[]{:S(2)}) collective-permute-start(f32[18,8,128]{2,1,0:T(8,128)S(1)} %get-tuple-element.43), channel_id=1, source_target_pairs={{0,4},{1,5},{2,6},{3,7},{4,0},{5,1},{6,2},{7,3},{8,12},{9,13},{10,... | collective-permute-start | bytes 221192 | tf_op jit(solution)/shard_map/ppermute | solution.py:807
  56.6 0.9 %collective-permute-start.17 = (f32[18,8,128]{2,1,0:T(8,128)S(1)}, f32[18,8,128]{2,1,0:T(8,128)S(1)}, u32[]{:S(2)}, u32[]{:S(2)}) collective-permute-start(f32[18,8,128]{2,1,0:T(8,128)S(1)} %get-tuple-element.44), channel_id=1, source_target_pairs={{0,3},{1,2},{2,1},{3,0},{4,7},{5,6},{6,5},{7,4},{8,11},{9,10},{10,... | collective-permute-start | bytes 221192 | tf_op jit(solution)/shard_map/ppermute | solution.py:807
  57.5 1.7 %collective-permute-done.21.refs_7_ = f32[18,8,128]{2,1,0:T(8,128)S(1)} collective-permute-done((f32[18,8,128]{2,1,0:T(8,128)S(1)}, f32[18,8,128]{2,1,0:T(8,128)S(1)}, u32[]{:S(2)}, u32[]{:S(2)}) %collective-permute-start.21) | collective-permute-done | bytes 73760 | tf_op jit(solution)/shard_map/ppermute | solution.py:807
  59.2 0.0 collective-permute-start.16
  59.2 0.0 collective-permute-done.20.refs_6_
  59.2 1.4 %collective-permute-start.15 = (f32[18,8,128]{2,1,0:T(8,128)S(1)}, f32[18,8,128]{2,1,0:T(8,128)S(1)}, u32[]{:S(2)}, u32[]{:S(2)}) collective-permute-start(f32[18,8,128]{2,1,0:T(8,128)S(1)} %get-tuple-element.46), channel_id=1, source_target_pairs={{0,1},{1,0},{2,3},{3,2},{4,5},{5,4},{6,7},{7,6},{8,9},{9,8},{10,11... | collective-permute-start | bytes 221192 | tf_op jit(solution)/shard_map/ppermute | solution.py:807
  60.6 0.0 collective-permute-done.19.refs_5_
  60.6 0.9 %collective-permute-done.18.refs_4_ = f32[18,8,128]{2,1,0:T(8,128)S(1)} collective-permute-done((f32[18,8,128]{2,1,0:T(8,128)S(1)}, f32[18,8,128]{2,1,0:T(8,128)S(1)}, u32[]{:S(2)}, u32[]{:S(2)}) %collective-permute-start.18) | collective-permute-done | bytes 73760 | tf_op jit(solution)/shard_map/ppermute | solution.py:807
  61.5 0.2 collective-permute-done.17.refs_3_
  61.7 1.4 %collective-permute-done.16.refs_2_ = f32[18,8,128]{2,1,0:T(8,128)S(1)} collective-permute-done((f32[18,8,128]{2,1,0:T(8,128)S(1)}, f32[18,8,128]{2,1,0:T(8,128)S(1)}, u32[]{:S(2)}, u32[]{:S(2)}) %collective-permute-start.16) | collective-permute-done | bytes 73760 | tf_op jit(solution)/shard_map/ppermute | solution.py:807
  63.1 0.0 collective-permute-done.15.refs_1_
  63.1 2.5 %shard_map.93 = (f32[27,4,8,128]{3,2,1,0:T(8,128)}, f32[7,1,8,512]{3,2,1,0:T(8,128)}) custom-call(f32[18,8,128]{2,1,0:T(8,128)S(1)} %get-tuple-element.47.refs_0_, f32[18,8,128]{2,1,0:T(8,128)S(1)} %collective-permute-done.15.refs_1_, f32[18,8,128]{2,1,0:T(8,128)S(1)} %collective-permute-done.16.refs_2_, f32[18,8,128]{2,1,0:T(8,128)S(1)} %collective-permute-done.17.refs_3_, ...), custom_call_target="tpu_custom_call" | custom-call | tf_op jit(solution)/shard_map/pallas_call | solution.py:768
  (2 shorter events, 0.1 us)
Async XLA Ops:
  1.6 8.0 %collective-permute-start = (f32[8,8,128]{2,1,0:T(8,128)S(1)}, f32[8,8,128]{2,1,0:T(8,128)S(1)}, u32[]{:S(2)}, u32[]{:S(2)}) collective-permute-start(f32[8,8,128]{2,1,0:T(8,128)S(1)} %get-tuple-element.20), channel_id=1, source_target_pairs={{0,8},{8,0},{16,24},{24,16},{1,9},{9,1},{17,25},{25,17},{2,10},{10... | collective-permute-start | bytes 98312 | tf_op jit(solution)/shard_map/ppermute | solution.py:813
  4.7 5.4 %collective-permute-start.1 = (f32[8,8,128]{2,1,0:T(8,128)S(1)}, f32[8,8,128]{2,1,0:T(8,128)S(1)}, u32[]{:S(2)}, u32[]{:S(2)}) collective-permute-start(f32[8,8,128]{2,1,0:T(8,128)S(1)} %get-tuple-element.21), channel_id=1, source_target_pairs={{0,16},{8,24},{16,0},{24,8},{1,17},{9,25},{17,1},{25,9},{2,18},{10... | collective-permute-start | bytes 98312 | tf_op jit(solution)/shard_map/ppermute | solution.py:813
  7.3 5.7 %collective-permute-start.2 = (f32[8,8,128]{2,1,0:T(8,128)S(1)}, f32[8,8,128]{2,1,0:T(8,128)S(1)}, u32[]{:S(2)}, u32[]{:S(2)}) collective-permute-start(f32[8,8,128]{2,1,0:T(8,128)S(1)} %get-tuple-element.22), channel_id=1, source_target_pairs={{0,24},{8,16},{16,8},{24,0},{1,25},{9,17},{17,9},{25,1},{2,26},{10... | collective-permute-start | bytes 98312 | tf_op jit(solution)/shard_map/ppermute | solution.py:813
  13.4 5.7 %collective-permute-start.9 = (f32[20,8,128]{2,1,0:T(8,128)S(1)}, f32[20,8,128]{2,1,0:T(8,128)S(1)}, u32[]{:S(2)}, u32[]{:S(2)}) collective-permute-start(f32[20,8,128]{2,1,0:T(8,128)S(1)} %get-tuple-element.32), channel_id=1, source_target_pairs={{0,6},{1,7},{2,4},{3,5},{4,2},{5,3},{6,0},{7,1},{8,14},{9,15},{10,... | collective-permute-start | bytes 245768 | tf_op jit(solution)/shard_map/ppermute | solution.py:807
  15.9 5.6 %collective-permute-start.8 = (f32[20,8,128]{2,1,0:T(8,128)S(1)}, f32[20,8,128]{2,1,0:T(8,128)S(1)}, u32[]{:S(2)}, u32[]{:S(2)}) collective-permute-start(f32[20,8,128]{2,1,0:T(8,128)S(1)} %get-tuple-element.33), channel_id=1, source_target_pairs={{0,7},{1,6},{2,5},{3,4},{4,3},{5,2},{6,1},{7,0},{8,15},{9,14},{10,... | collective-permute-start | bytes 245768 | tf_op jit(solution)/shard_map/ppermute | solution.py:807
  15.9 6.5 %collective-permute-start.7 = (f32[20,8,128]{2,1,0:T(8,128)S(1)}, f32[20,8,128]{2,1,0:T(8,128)S(1)}, u32[]{:S(2)}, u32[]{:S(2)}) collective-permute-start(f32[20,8,128]{2,1,0:T(8,128)S(1)} %get-tuple-element.34), channel_id=1, source_target_pairs={{0,2},{1,3},{2,0},{3,1},{4,6},{5,7},{6,4},{7,5},{8,10},{9,11},{10,... | collective-permute-start | bytes 245768 | tf_op jit(solution)/shard_map/ppermute | solution.py:807
  16.4 6.0 %collective-permute-start.6 = (f32[20,8,128]{2,1,0:T(8,128)S(1)}, f32[20,8,128]{2,1,0:T(8,128)S(1)}, u32[]{:S(2)}, u32[]{:S(2)}) collective-permute-start(f32[20,8,128]{2,1,0:T(8,128)S(1)} %get-tuple-element.35), channel_id=1, source_target_pairs={{0,4},{1,5},{2,6},{3,7},{4,0},{5,1},{6,2},{7,3},{8,12},{9,13},{10,... | collective-permute-start | bytes 245768 | tf_op jit(solution)/shard_map/ppermute | solution.py:807
  17.0 7.1 %collective-permute-start.5 = (f32[20,8,128]{2,1,0:T(8,128)S(1)}, f32[20,8,128]{2,1,0:T(8,128)S(1)}, u32[]{:S(2)}, u32[]{:S(2)}) collective-permute-start(f32[20,8,128]{2,1,0:T(8,128)S(1)} %get-tuple-element.36), channel_id=1, source_target_pairs={{0,3},{1,2},{2,1},{3,0},{4,7},{5,6},{6,5},{7,4},{8,11},{9,10},{10,... | collective-permute-start | bytes 245768 | tf_op jit(solution)/shard_map/ppermute | solution.py:807
  19.1 5.2 %collective-permute-start.4 = (f32[20,8,128]{2,1,0:T(8,128)S(1)}, f32[20,8,128]{2,1,0:T(8,128)S(1)}, u32[]{:S(2)}, u32[]{:S(2)}) collective-permute-start(f32[20,8,128]{2,1,0:T(8,128)S(1)} %get-tuple-element.37), channel_id=1, source_target_pairs={{0,5},{1,4},{2,7},{3,6},{4,1},{5,0},{6,3},{7,2},{8,13},{9,12},{10,... | collective-permute-start | bytes 245768 | tf_op jit(solution)/shard_map/ppermute | solution.py:807
  21.5 2.8 %collective-permute-start.3 = (f32[20,8,128]{2,1,0:T(8,128)S(1)}, f32[20,8,128]{2,1,0:T(8,128)S(1)}, u32[]{:S(2)}, u32[]{:S(2)}) collective-permute-start(f32[20,8,128]{2,1,0:T(8,128)S(1)} %get-tuple-element.38), channel_id=1, source_target_pairs={{0,1},{1,0},{2,3},{3,2},{4,5},{5,4},{6,7},{7,6},{8,9},{9,8},{10,11... | collective-permute-start | bytes 245768 | tf_op jit(solution)/shard_map/ppermute | solution.py:807
  24.8 8.4 %collective-permute-start.10 = (f32[4,20,8,128]{3,2,1,0:T(8,128)S(1)}, f32[4,20,8,128]{3,2,1,0:T(8,128)S(1)}, u32[]{:S(2)}, u32[]{:S(2)}) collective-permute-start(f32[4,20,8,128]{3,2,1,0:T(8,128)S(1)} %get-tuple-element.24), channel_id=1, source_target_pairs={{25,0},{0,1},{1,2},{2,3},{3,7},{7,6},{6,5},{5,4},{4,13},{13,12},{1... | collective-permute-start | bytes 983048 | tf_op jit(solution)/shard_map/ppermute | solution.py:798
  24.9 8.3 %collective-permute-start.11 = (f32[4,20,8,128]{3,2,1,0:T(8,128)S(1)}, f32[4,20,8,128]{3,2,1,0:T(8,128)S(1)}, u32[]{:S(2)}, u32[]{:S(2)}) collective-permute-start(f32[4,20,8,128]{3,2,1,0:T(8,128)S(1)} %get-tuple-element.25), channel_id=1, source_target_pairs={{0,25},{1,0},{2,1},{3,2},{7,3},{6,7},{5,6},{4,5},{13,4},{12,13},{8... | collective-permute-start | bytes 983048 | tf_op jit(solution)/shard_map/ppermute | solution.py:799
  42.6 10.3 %collective-permute-start.12 = (f32[8,8,128]{2,1,0:T(8,128)S(1)}, f32[8,8,128]{2,1,0:T(8,128)S(1)}, u32[]{:S(2)}, u32[]{:S(2)}) collective-permute-start(f32[8,8,128]{2,1,0:T(8,128)S(1)} %get-tuple-element.29), channel_id=1, source_target_pairs={{0,8},{8,0},{16,24},{24,16},{1,9},{9,1},{17,25},{25,17},{2,10},{10... | collective-permute-start | bytes 98312 | tf_op jit(solution)/shard_map/ppermute | solution.py:813
  42.7 10.2 %collective-permute-start.13 = (f32[8,8,128]{2,1,0:T(8,128)S(1)}, f32[8,8,128]{2,1,0:T(8,128)S(1)}, u32[]{:S(2)}, u32[]{:S(2)}) collective-permute-start(f32[8,8,128]{2,1,0:T(8,128)S(1)} %get-tuple-element.30), channel_id=1, source_target_pairs={{0,16},{8,24},{16,0},{24,8},{1,17},{9,25},{17,1},{25,9},{2,18},{10... | collective-permute-start | bytes 98312 | tf_op jit(solution)/shard_map/ppermute | solution.py:813
  42.8 10.2 %collective-permute-start.14 = (f32[8,8,128]{2,1,0:T(8,128)S(1)}, f32[8,8,128]{2,1,0:T(8,128)S(1)}, u32[]{:S(2)}, u32[]{:S(2)}) collective-permute-start(f32[8,8,128]{2,1,0:T(8,128)S(1)} %get-tuple-element.31), channel_id=1, source_target_pairs={{0,24},{8,16},{16,8},{24,0},{1,25},{9,17},{17,9},{25,1},{2,26},{10... | collective-permute-start | bytes 98312 | tf_op jit(solution)/shard_map/ppermute | solution.py:813
  53.1 6.1 %collective-permute-start.21 = (f32[18,8,128]{2,1,0:T(8,128)S(1)}, f32[18,8,128]{2,1,0:T(8,128)S(1)}, u32[]{:S(2)}, u32[]{:S(2)}) collective-permute-start(f32[18,8,128]{2,1,0:T(8,128)S(1)} %get-tuple-element.40), channel_id=1, source_target_pairs={{0,6},{1,7},{2,4},{3,5},{4,2},{5,3},{6,0},{7,1},{8,14},{9,15},{10,... | collective-permute-start | bytes 221192 | tf_op jit(solution)/shard_map/ppermute | solution.py:807
  53.7 5.5 %collective-permute-start.20 = (f32[18,8,128]{2,1,0:T(8,128)S(1)}, f32[18,8,128]{2,1,0:T(8,128)S(1)}, u32[]{:S(2)}, u32[]{:S(2)}) collective-permute-start(f32[18,8,128]{2,1,0:T(8,128)S(1)} %get-tuple-element.41), channel_id=1, source_target_pairs={{0,7},{1,6},{2,5},{3,4},{4,3},{5,2},{6,1},{7,0},{8,15},{9,14},{10,... | collective-permute-start | bytes 221192 | tf_op jit(solution)/shard_map/ppermute | solution.py:807
  54.9 5.6 %collective-permute-start.19 = (f32[18,8,128]{2,1,0:T(8,128)S(1)}, f32[18,8,128]{2,1,0:T(8,128)S(1)}, u32[]{:S(2)}, u32[]{:S(2)}) collective-permute-start(f32[18,8,128]{2,1,0:T(8,128)S(1)} %get-tuple-element.42), channel_id=1, source_target_pairs={{0,2},{1,3},{2,0},{3,1},{4,6},{5,7},{6,4},{7,5},{8,10},{9,11},{10,... | collective-permute-start | bytes 221192 | tf_op jit(solution)/shard_map/ppermute | solution.py:807
  54.9 6.6 %collective-permute-start.18 = (f32[18,8,128]{2,1,0:T(8,128)S(1)}, f32[18,8,128]{2,1,0:T(8,128)S(1)}, u32[]{:S(2)}, u32[]{:S(2)}) collective-permute-start(f32[18,8,128]{2,1,0:T(8,128)S(1)} %get-tuple-element.43), channel_id=1, source_target_pairs={{0,4},{1,5},{2,6},{3,7},{4,0},{5,1},{6,2},{7,3},{8,12},{9,13},{10,... | collective-permute-start | bytes 221192 | tf_op jit(solution)/shard_map/ppermute | solution.py:807
  56.6 5.0 %collective-permute-start.17 = (f32[18,8,128]{2,1,0:T(8,128)S(1)}, f32[18,8,128]{2,1,0:T(8,128)S(1)}, u32[]{:S(2)}, u32[]{:S(2)}) collective-permute-start(f32[18,8,128]{2,1,0:T(8,128)S(1)} %get-tuple-element.44), channel_id=1, source_target_pairs={{0,3},{1,2},{2,1},{3,0},{4,7},{5,6},{6,5},{7,4},{8,11},{9,10},{10,... | collective-permute-start | bytes 221192 | tf_op jit(solution)/shard_map/ppermute | solution.py:807
  59.2 3.9 %collective-permute-start.16 = (f32[18,8,128]{2,1,0:T(8,128)S(1)}, f32[18,8,128]{2,1,0:T(8,128)S(1)}, u32[]{:S(2)}, u32[]{:S(2)}) collective-permute-start(f32[18,8,128]{2,1,0:T(8,128)S(1)} %get-tuple-element.45), channel_id=1, source_target_pairs={{0,5},{1,4},{2,7},{3,6},{4,1},{5,0},{6,3},{7,2},{8,13},{9,12},{10,... | collective-permute-start | bytes 221192 | tf_op jit(solution)/shard_map/ppermute | solution.py:807
  59.2 3.9 %collective-permute-start.15 = (f32[18,8,128]{2,1,0:T(8,128)S(1)}, f32[18,8,128]{2,1,0:T(8,128)S(1)}, u32[]{:S(2)}, u32[]{:S(2)}) collective-permute-start(f32[18,8,128]{2,1,0:T(8,128)S(1)} %get-tuple-element.46), channel_id=1, source_target_pairs={{0,1},{1,0},{2,3},{3,2},{4,5},{5,4},{6,7},{7,6},{8,9},{9,8},{10,11... | collective-permute-start | bytes 221192 | tf_op jit(solution)/shard_map/ppermute | solution.py:807

commit v5 on v4

--- a/solution.py
+++ b/solution.py
@@ -296,81 +296,65 @@
     return values
 
 
-SPEED_AT, SOLID_AT, HEAT_AT, RATE_AT, ROWS = 27, 30, 31, 38, 40
+SPEED_AT, SOLID_AT, HEAT_AT, RATE_AT, ROWS = 27, 30, 32, 39, 40
+IN_PAIRS = 16
 FLOW_PAIRS = 14
 
 
-def offer_heat(slab, levels_hbm, heat_hbm, phase_hbm, *refs):
-    outs, (levels_ref, heat_ref, phase_ref, sems) = refs[: slab.grp], refs[slab.grp :]
+def pack_in(
+    slab, levels_hbm, popul_hbm, speed_hbm, solid_hbm, heat_hbm, phase_hbm, sent, *scratch
+):
+    levels_ref, fields, solid_ref, heat_ref, phase_ref, sems = scratch
     copies = [
-        pltpu.make_async_copy(heat_hbm, heat_ref, sems.at[0]),
-        pltpu.make_async_copy(phase_hbm, phase_ref, sems.at[1]),
-        pltpu.make_async_copy(levels_hbm, levels_ref, sems.at[2]),
+        pltpu.make_async_copy(source, target, sems.at[number])
+        for number, (source, target) in enumerate(
+            [
+                (heat_hbm, heat_ref),
+                (phase_hbm, phase_ref),
+                (levels_hbm, levels_ref),
+                (speed_hbm, fields.at[pl.ds(SPEED_AT, 3)]),
+                (solid_hbm, solid_ref),
+                (popul_hbm, fields.at[pl.ds(0, SPEED_AT)]),
+            ]
+        )
     ]
     for copy in copies:
         copy.start()
-    for copy in copies:
+    for copy in copies[:3]:
         copy.wait()
-    mine = lax.axis_index("grp")
-    for step in range(slab.grp):
-        part = jnp.bitwise_xor(mine, step)
-        span = pl.ds(pl.multiple_of(part * LANES, LANES), LANES)
+    lane = lane_index()
+    first = in_first_half(slab)
+    columns = []
+    for part in range(slab.grp):
+        span = pl.ds(part * LANES, LANES)
         phase = phase_ref[0, :, span]
         chosen = jnp.zeros((SUBLANES, LANES), F32)
         for level in range(levels_ref.shape[0]):
             chosen = jnp.where(phase == level, levels_ref[level], chosen)
-        for k in range(7):
-            outs[step][k] = heat_ref[k, 0, :, span]
-        outs[step][7] = 1.0 / (0.5 + 4.0 * chosen)
-
-
-def for_each(count, body):
-    for number in range(count):
-        body(number)
-
-
-def pack_flow(slab, popul_hbm, speed_hbm, solid_hbm, sent, flags, fields, solid_ref, sems):
-    copies = [
-        pltpu.make_async_copy(popul_hbm, fields.at[pl.ds(0, SPEED_AT)], sems.at[0]),
-        pltpu.make_async_copy(speed_hbm, fields.at[pl.ds(SPEED_AT, 3)], sems.at[1]),
-        pltpu.make_async_copy(solid_hbm, solid_ref, sems.at[2]),
-    ]
-    for copy in copies:
-        copy.start()
-    for copy in copies:
+        columns.append([heat_ref[k, 0, :, span] for k in range(7)] + [1.0 / (0.5 + 4.0 * chosen)])
+    for part in range(slab.grp):
+        own, after = columns[part], columns[(part + 1) % slab.grp]
+        before = columns[part - 1]
+        beside = []
+        for k in range(8):
+            above = jnp.where(lane < slab.planes, after[k], own[k])
+            below = jnp.where(lane >= LANES - slab.planes, before[k], own[k])
+            beside.append(
+                jnp.where(first, lane_roll(above, -slab.planes), lane_roll(below, slab.planes))
+            )
+        holders = slab.holders(part)
+        for which, sources in enumerate((own, beside)):
+            for place, value in enumerate(swap_groups(sources, slab.planes)):
+                sent[holders[place], IN_PAIRS + 2 * part + which] = value
+    for copy in copies[3:]:
         copy.wait()
+    fields[SOLID_AT] = solid_ref[...].astype(F32)
+    fields[SOLID_AT + 1] = jnp.zeros(solid_ref.shape, F32)
     holders = slab.holders(lax.axis_index("grp"))
-
-    def one(pair):
-        pack_pair(slab, fields, pair, sent, pair, holders)
-
-    for_each(SOLID_AT // 2, one)
-    flags[...] = solid_ref[...].astype(F32)
-
-
-def pack_pair(slab, fields, source, sent, target, holders):
-    sources = [fields[2 * source + h, x] for x in range(slab.block_x) for h in range(2)]
-    for place, value in enumerate(swap_groups(sources, slab.planes)):
-        sent[holders[place], target] = value
-
-
-def pack_heat(slab, sent_in, flags, *refs):
-    parts, (sent, held, packed, sem) = refs[: slab.grp], refs[slab.grp :]
-    mine = lax.axis_index("grp")
-    holders = slab.holders(lax.axis_index("grp"))
-    held[0] = flags[...]
-    held[9] = jnp.zeros(flags.shape, F32)
-    for step in range(slab.grp):
-        held[pl.ds(1, 8), jnp.bitwise_xor(mine, step)] = parts[step][...]
-    first, count = SOLID_AT // 2, (ROWS - SOLID_AT) // 2
-
-    def one(pair):
-        pack_pair(slab, held, pair, packed, pair, holders)
-
-    for_each(count, one)
-    copy = pltpu.make_async_copy(packed, sent.at[:, pl.ds(first, count)], sem)
-    copy.start()
-    copy.wait()
+    for pair in range(IN_PAIRS):
+        sources = [fields[2 * pair + h, x] for x in range(slab.block_x) for h in range(2)]
+        for place, value in enumerate(swap_groups(sources, slab.planes)):
+            sent[holders[place], pair] = value
 
 
 def in_first_half(slab):
@@ -384,19 +368,38 @@
 
 
 def offer_halo(slab, *refs):
-    parts, (came, low_out, high_out) = refs[: slab.sub], refs[slab.sub :]
+    parts, (came, low_out, high_out, *heat_outs) = refs[: slab.sub], refs[slab.sub :]
     collect(slab, parts, came)
+    mine = lax.axis_index("grp")
+    for step, heat_out in enumerate(heat_outs):
+        slots = pl.ds(IN_PAIRS + 2 * jnp.bitwise_xor(mine, step), 2)
+        for tile in range(slab.sub):
+            heat_out[tile] = came[tile, slots]
 
     def one(number, _):
         tile = 2 * number
         first = in_first_half(slab)
-        for pair in range(ROWS // 2):
+        for pair in range(IN_PAIRS):
             a, b = came[tile, pair], came[tile + 1, pair]
             low_out[number, pair] = jnp.where(first, a, lane_roll(b, slab.halo))
             high_out[number, pair] = jnp.where(first, lane_roll(b, -slab.halo), a)
         return 0
 
     lax.fori_loop(0, slab.sub // 2, one, 0)
+
+
+def make_heat_tiles(slab, parts, held, state):
+    mine = lax.axis_index("grp")
+    for step, part in enumerate(parts):
+        held[jnp.bitwise_xor(mine, step)] = part[...]
+    first = in_first_half(slab)
+    for tile in range(slab.sub):
+        sources = []
+        for x in range(slab.block_x):
+            after = held[(x + 1) % slab.block_x, tile, 1]
+            sources += [held[x, tile, 0], jnp.where(first, held[x, tile, 1], after)]
+        for k, value in enumerate(swap_groups(sources, slab.planes)):
+            state[HEAT_AT + k, tile] = value
 
 
 def make_tiles(slab, came, below_ref, above_ref, state):
@@ -404,7 +407,7 @@
         first = in_first_half(slab)
         even = (lane_index() // slab.planes) % 2 == 0
         back = 2 * slab.planes
-        for pair in range(ROWS // 2):
+        for pair in range(IN_PAIRS):
             below, above = below_ref[number, pair], above_ref[number, pair]
             beside = (
                 jnp.where(first, above, lane_roll(below, -back)),
@@ -630,11 +633,15 @@
 
 
 def first_window(slab, rates_hbm, came, below_ref, above_ref, *refs):
+    heat_parts, refs = refs[: slab.grp], refs[slab.grp :]
     flow_out, keep_out, heat_outs = refs[0], refs[1], refs[2 : 2 + slab.grp]
-    rates_ref, sem, state, flow_post, heat_post, heat_a, heat_b, held = refs[2 + slab.grp :]
+    rates_ref, sem, state, flow_post, heat_post, heat_a, heat_b, held, came_heat = refs[
+        2 + slab.grp :
+    ]
     rates_copy = pltpu.make_async_copy(rates_hbm, rates_ref, sem)
     rates_copy.start()
     make_tiles(slab, came, below_ref, above_ref, state)
+    make_heat_tiles(slab, heat_parts, came_heat, state)
     rates_copy.wait()
 
     def speeds_of(tile):
@@ -821,58 +828,43 @@
     def vmem_like(array):
         return pltpu.VMEM(array.shape, array.dtype)
 
-    parts = local_call(
-        offer_heat,
+    sent_shape = (slab.sub, IN_PAIRS + 2 * slab.grp) + tile
+    (sent,) = local_call(
+        pack_in,
         slab,
-        [conductivity, thermal, phase_ids],
-        [(8,) + tile] * slab.grp,
+        [conductivity, populations, velocity_prev, solid, thermal, phase_ids],
+        [sent_shape],
         [
             pltpu.SMEM(conductivity.shape, F32),
+            (2 * IN_PAIRS,) + solid.shape,
+            vmem_like(solid),
             vmem_like(thermal),
             vmem_like(phase_ids),
-            pltpu.SemaphoreType.DMA((3,)),
+            pltpu.SemaphoreType.DMA((6,)),
         ],
-        in_hbm=3,
-    )
+        in_hbm=6,
+    )
+    plane = (slab.sub,) + tile
+    halo_shape = (slab.sub // 2, IN_PAIRS) + tile
+    heat_shape = (slab.sub, 2) + tile
+    came, low, high, *parts = local_call(
+        offer_halo,
+        slab,
+        across_plane(slab, sent),
+        [sent_shape, halo_shape, halo_shape] + [heat_shape] * slab.grp,
+    )
+    below, above = exchange(slab, low, high)
     parts = across_planes(slab, parts)
-    sent_shape = (slab.sub, ROWS // 2) + tile
-    sent, flags = local_call(
-        pack_flow,
-        slab,
-        [populations, velocity_prev, solid],
-        [sent_shape, solid.shape],
-        [
-            (SOLID_AT,) + solid.shape,
-            pltpu.VMEM(solid.shape, solid.dtype),
-            pltpu.SemaphoreType.DMA((3,)),
-        ],
-        in_hbm=3,
-    )
-    (sent,) = local_call(
-        pack_heat,
-        slab,
-        [sent, flags] + parts,
-        [sent_shape],
-        [
-            (ROWS - SOLID_AT,) + solid.shape,
-            (slab.sub, (ROWS - SOLID_AT) // 2) + tile,
-            pltpu.SemaphoreType.DMA,
-        ],
-        carried=True,
-    )
-    halo_shape = (slab.sub // 2, ROWS // 2) + tile
-    came, low, high = local_call(
-        offer_halo, slab, across_plane(slab, sent), [sent_shape, halo_shape, halo_shape]
-    )
-    below, above = exchange(slab, low, high)
-    plane = (slab.sub,) + tile
     scalars = [pltpu.SMEM(rates.shape, F32), pltpu.SemaphoreType.DMA]
     flow, keep, *parts = local_call(
         first_window,
         slab,
-        [rates, came, below, above],
+        [rates, came, below, above] + parts,
         [(27,) + plane, (2,) + plane] + [plane] * slab.grp,
-        scalars + [(ROWS,) + plane, (2, 27) + plane, (2, 7) + plane] + [(7,) + plane] * 2 + [(slab.grp,) + plane],
+        scalars
+        + [(ROWS,) + plane, (2, 27) + plane, (2, 7) + plane]
+        + [(7,) + plane] * 2
+        + [(slab.grp,) + plane, (slab.grp,) + heat_shape],
         in_hbm=1,
     )
     parts = across_planes(slab, parts)

time: 65.8 us -> 63.3 us (0.962)
  waiting for transfers between devices: 17 us -> 14.7 us
  starting transfers between devices: 25.8 us -> 26.6 us
  Pallas kernels: 21.9 us -> 21.1 us
    ppermute x1, waiting for transfers between devices: 4.75 us -> 0.01 us  [exchange(): from_below = lax.ppermute(high, RING, upward)]
    ppermute x14, starting transfers between devices: 12.1 us -> 13.6 us  [across_plane(): came[step] = lax.ppermute(sent[step], ('gx', 'gy'), pairs)]
    ppermute x14, waiting for transfers between devices: 8.84 us -> 10.3 us  [across_plane(): came[step] = lax.ppermute(sent[step], ('gx', 'gy'), pairs)]
    ppermute x6, waiting for transfers between devices: 3.44 us -> 4.42 us  [across_planes(): lax.ppermute(parts[step], 'grp', [(i, i ^ step) for i in range(slab.grp)])]
    pallas_call x8 -> x6, Pallas kernels: 21.9 us -> 21.1 us  [local_call(): pl.pallas_call(kernel, out_shape=[jax.ShapeDtypeStruct(shape, F32) for sh...]
    ppermute x6, starting transfers between devices: 10.1 us -> 9.38 us  [across_planes(): lax.ppermute(parts[step], 'grp', [(i, i ^ step) for i in range(slab.grp)])]
  transfers between devices with their start and end apart: 22 -> 22, of which waited for: 11 -> 11; matrix products, arithmetic and copies ran while one was open for 0% -> 0% of each run, Pallas kernels for 12% -> 9%
where the time goes in v5:
time: 63.3 us; the launch traced here: 63.1 us
  starting transfers between devices  26.6 us (42%)
  Pallas kernels  21.1 us (33%)
  waiting for transfers between devices  14.7 us (23%)
  between operations  0.74 us (1%)
    pallas_call x6, Pallas kernels, local_call(): pl.pallas_call(kernel, out_shape=[jax.ShapeDtypeStruct(shape, F32) for sh...  21.1 us
    ppermute x14, starting transfers between devices, across_plane(): came[step] = lax.ppermute(sent[step], ('gx', 'gy'), pairs)  13.6 us
    ppermute x14, waiting for transfers between devices, across_plane(): came[step] = lax.ppermute(sent[step], ('gx', 'gy'), pairs)  10.3 us
    ppermute x6, starting transfers between devices, across_planes(): lax.ppermute(parts[step], 'grp', [(i, i ^ step) for i in range(slab.grp)])  9.38 us
    ppermute x6, waiting for transfers between devices, across_planes(): lax.ppermute(parts[step], 'grp', [(i, i ^ step) for i in range(slab.grp)])  4.42 us
    ppermute x1, starting transfers between devices, exchange(): from_above = lax.ppermute(low, RING, [(b, a) for a, b in upward])  3.43 us
  transfers between devices with their start and end apart: 22, of which 11 were waited for; matrix products, arithmetic and copies ran while one was open for 0% of the time, Pallas kernels for 9%

profile of v5, /device:TPU:0, one launch (start us, length us, event | category | flops | bytes accessed | tf_op | source)
XLA Modules:
  0.0 63.1 jit_solution(10247430690337564072)
XLA Ops:
  0.6 2.8 %shard_map.86 = f32[8,24,8,128]{3,2,1,0:T(8,128)S(1)} custom-call(f32[4]{0:T(128)} %refs_0_.3, f32[27,4,8,128]{3,2,1,0:T(8,128)} %refs_1_.1, f32[3,4,8,128]{3,2,1,0:T(8,128)} %refs_2_.1, s32[4,8,128]{2,1,0:T(8,128)} %refs_3_.1, f32[7,1,8,512]{3,2,1,0:T(8,128)} %refs_4_.1, s32[1,8,512]{2,1,0:T(8,128)} %refs_5_.1), custom_call_target="tpu_custom_call" | custom-call | tf_op jit(solution)/shard_map/pallas_call | solution.py:775
  3.5 0.1 slice_bitcast_fusion
  3.5 4.0 %collective-permute-start.6 = (f32[24,8,128]{2,1,0:T(8,128)S(1)}, f32[24,8,128]{2,1,0:T(8,128)S(1)}, u32[]{:S(2)}, u32[]{:S(2)}) collective-permute-start(f32[24,8,128]{2,1,0:T(8,128)S(1)} %get-tuple-element.28), channel_id=1, source_target_pairs={{0,6},{1,7},{2,4},{3,5},{4,2},{5,3},{6,0},{7,1},{8,14},{9,15},{10,... | collective-permute-start | bytes 294920 | tf_op jit(solution)/shard_map/ppermute | solution.py:814
  7.5 0.0 collective-permute-start.5
  7.5 1.1 %collective-permute-start.4 = (f32[24,8,128]{2,1,0:T(8,128)S(1)}, f32[24,8,128]{2,1,0:T(8,128)S(1)}, u32[]{:S(2)}, u32[]{:S(2)}) collective-permute-start(f32[24,8,128]{2,1,0:T(8,128)S(1)} %get-tuple-element.30), channel_id=1, source_target_pairs={{0,2},{1,3},{2,0},{3,1},{4,6},{5,7},{6,4},{7,5},{8,10},{9,11},{10,... | collective-permute-start | bytes 294920 | tf_op jit(solution)/shard_map/ppermute | solution.py:814
  8.6 1.5 %collective-permute-start.3 = (f32[24,8,128]{2,1,0:T(8,128)S(1)}, f32[24,8,128]{2,1,0:T(8,128)S(1)}, u32[]{:S(2)}, u32[]{:S(2)}) collective-permute-start(f32[24,8,128]{2,1,0:T(8,128)S(1)} %get-tuple-element.31), channel_id=1, source_target_pairs={{0,4},{1,5},{2,6},{3,7},{4,0},{5,1},{6,2},{7,3},{8,12},{9,13},{10,... | collective-permute-start | bytes 294920 | tf_op jit(solution)/shard_map/ppermute | solution.py:814
  10.1 0.6 collective-permute-start.2
  10.7 0.0 collective-permute-done.6.refs_7_
  10.7 0.6 collective-permute-start.1
  11.3 2.2 %collective-permute-done.5.refs_6_ = f32[24,8,128]{2,1,0:T(8,128)S(1)} collective-permute-done((f32[24,8,128]{2,1,0:T(8,128)S(1)}, f32[24,8,128]{2,1,0:T(8,128)S(1)}, u32[]{:S(2)}, u32[]{:S(2)}) %collective-permute-start.5) | collective-permute-done | bytes 98336 | tf_op jit(solution)/shard_map/ppermute | solution.py:814
  13.5 0.0 collective-permute-start
  13.5 1.6 %collective-permute-done.4.refs_5_ = f32[24,8,128]{2,1,0:T(8,128)S(1)} collective-permute-done((f32[24,8,128]{2,1,0:T(8,128)S(1)}, f32[24,8,128]{2,1,0:T(8,128)S(1)}, u32[]{:S(2)}, u32[]{:S(2)}) %collective-permute-start.4) | collective-permute-done | bytes 98336 | tf_op jit(solution)/shard_map/ppermute | solution.py:814
  15.0 0.3 collective-permute-done.3.refs_4_
  15.3 1.4 %collective-permute-done.2.refs_3_ = f32[24,8,128]{2,1,0:T(8,128)S(1)} collective-permute-done((f32[24,8,128]{2,1,0:T(8,128)S(1)}, f32[24,8,128]{2,1,0:T(8,128)S(1)}, u32[]{:S(2)}, u32[]{:S(2)}) %collective-permute-start.2) | collective-permute-done | bytes 98336 | tf_op jit(solution)/shard_map/ppermute | solution.py:814
  16.7 0.7 %collective-permute-done.1.refs_2_ = f32[24,8,128]{2,1,0:T(8,128)S(1)} collective-permute-done((f32[24,8,128]{2,1,0:T(8,128)S(1)}, f32[24,8,128]{2,1,0:T(8,128)S(1)}, u32[]{:S(2)}, u32[]{:S(2)}) %collective-permute-start.1) | collective-permute-done | bytes 98336 | tf_op jit(solution)/shard_map/ppermute | solution.py:814
  17.4 0.0 collective-permute-done.refs_1_
  17.4 0.5 shard_map.87
  17.9 0.2 collective-permute-start.7
  18.1 3.4 %collective-permute-start.8 = (f32[4,16,8,128]{3,2,1,0:T(8,128)S(1)}, f32[4,16,8,128]{3,2,1,0:T(8,128)S(1)}, u32[]{:S(2)}, u32[]{:S(2)}) collective-permute-start(f32[4,16,8,128]{3,2,1,0:T(8,128)S(1)} %get-tuple-element.17), channel_id=1, source_target_pairs={{0,25},{1,0},{2,1},{3,2},{7,3},{6,7},{5,6},{4,5},{13,4},{12,13},{8... | collective-permute-start | bytes 786440 | tf_op jit(solution)/shard_map/ppermute | solution.py:806
  21.5 0.1 collective-permute-start.9
  21.6 2.6 %collective-permute-start.10 = (f32[8,2,8,128]{3,2,1,0:T(8,128)S(1)}, f32[8,2,8,128]{3,2,1,0:T(8,128)S(1)}, u32[]{:S(2)}, u32[]{:S(2)}) collective-permute-start(f32[8,2,8,128]{3,2,1,0:T(8,128)S(1)} %get-tuple-element.20), channel_id=1, source_target_pairs={{0,16},{8,24},{16,0},{24,8},{1,17},{9,25},{17,1},{25,9},{2,18},{10... | collective-permute-start | bytes 196616 | tf_op jit(solution)/shard_map/ppermute | solution.py:820
  24.1 1.7 %collective-permute-start.11 = (f32[8,2,8,128]{3,2,1,0:T(8,128)S(1)}, f32[8,2,8,128]{3,2,1,0:T(8,128)S(1)}, u32[]{:S(2)}, u32[]{:S(2)}) collective-permute-start(f32[8,2,8,128]{3,2,1,0:T(8,128)S(1)} %get-tuple-element.21), channel_id=1, source_target_pairs={{0,24},{8,16},{16,8},{24,0},{1,25},{9,17},{17,9},{25,1},{2,26},{10... | collective-permute-start | bytes 196616 | tf_op jit(solution)/shard_map/ppermute | solution.py:820
  25.9 1.7 %collective-permute-done.9.refs_5_ = f32[8,2,8,128]{3,2,1,0:T(8,128)S(1)} collective-permute-done((f32[8,2,8,128]{3,2,1,0:T(8,128)S(1)}, f32[8,2,8,128]{3,2,1,0:T(8,128)S(1)}, u32[]{:S(2)}, u32[]{:S(2)}) %collective-permute-start.9) | collective-permute-done | bytes 65568 | tf_op jit(solution)/shard_map/ppermute | solution.py:820
  27.6 2.7 %collective-permute-done.10.refs_6_ = f32[8,2,8,128]{3,2,1,0:T(8,128)S(1)} collective-permute-done((f32[8,2,8,128]{3,2,1,0:T(8,128)S(1)}, f32[8,2,8,128]{3,2,1,0:T(8,128)S(1)}, u32[]{:S(2)}, u32[]{:S(2)}) %collective-permute-start.10) | collective-permute-done | bytes 65568 | tf_op jit(solution)/shard_map/ppermute | solution.py:820
  30.3 0.0 collective-permute-done.11.refs_7_
  30.3 0.0 collective-permute-done.7.refs_2_
  30.3 0.0 collective-permute-done.8.refs_3_
  30.3 9.3 %shard_map.88 = (f32[27,8,8,128]{3,2,1,0:T(8,128)S(1)}, f32[2,8,8,128]{3,2,1,0:T(8,128)S(1)}, f32[8,8,128]{2,1,0:T(8,128)S(1)}, f32[8,8,128]{2,1,0:T(8,128)S(1)}...) custom-call(f32[27]{0:T(128)} %refs_0_.5, f32[8,24,8,128]{3,2,1,0:T(8,128)S(1)} %get-tuple-element.15.refs_1_, ...), custom_call_target="tpu_custom_call" | custom-call | tf_op jit(solution)/shard_map/pallas_call | solution.py:775
  39.6 1.6 %collective-permute-start.12 = (f32[8,8,128]{2,1,0:T(8,128)S(1)}, f32[8,8,128]{2,1,0:T(8,128)S(1)}, u32[]{:S(2)}, u32[]{:S(2)}) collective-permute-start(f32[8,8,128]{2,1,0:T(8,128)S(1)} %get-tuple-element.25), channel_id=1, source_target_pairs={{0,8},{8,0},{16,24},{24,16},{1,9},{9,1},{17,25},{25,17},{2,10},{10... | collective-permute-start | bytes 98312 | tf_op jit(solution)/shard_map/ppermute | solution.py:820
  41.3 2.7 %collective-permute-start.13 = (f32[8,8,128]{2,1,0:T(8,128)S(1)}, f32[8,8,128]{2,1,0:T(8,128)S(1)}, u32[]{:S(2)}, u32[]{:S(2)}) collective-permute-start(f32[8,8,128]{2,1,0:T(8,128)S(1)} %get-tuple-element.26), channel_id=1, source_target_pairs={{0,16},{8,24},{16,0},{24,8},{1,17},{9,25},{17,1},{25,9},{2,18},{10... | collective-permute-start | bytes 98312 | tf_op jit(solution)/shard_map/ppermute | solution.py:820
  44.0 0.7 %collective-permute-start.14 = (f32[8,8,128]{2,1,0:T(8,128)S(1)}, f32[8,8,128]{2,1,0:T(8,128)S(1)}, u32[]{:S(2)}, u32[]{:S(2)}) collective-permute-start(f32[8,8,128]{2,1,0:T(8,128)S(1)} %get-tuple-element.27), channel_id=1, source_target_pairs={{0,24},{8,16},{16,8},{24,0},{1,25},{9,17},{17,9},{25,1},{2,26},{10... | collective-permute-start | bytes 98312 | tf_op jit(solution)/shard_map/ppermute | solution.py:820
  44.6 5.8 %shard_map.89.refs_0_ = f32[8,18,8,128]{3,2,1,0:T(8,128)S(1)} custom-call(f32[27]{0:T(128)} %refs_0_.5, f32[8,24,8,128]{3,2,1,0:T(8,128)S(1)} %get-tuple-element.15.refs_1_, f32[27,8,8,128]{3,2,1,0:T(8,128)S(1)} %get-tuple-element.22.refs_2_, f32[2,8,8,128]{3,2,1,0:T(8,128)S(1)} %get-tuple-element.23.refs_3_), custom_call_target="tpu_custom_call" | custom-call | tf_op jit(solution)/shard_map/pallas_call | solution.py:775
  50.5 0.0 collective-permute-done.12.refs_2_
  50.5 0.0 collective-permute-done.13.refs_3_
  50.5 0.0 collective-permute-done.14.refs_4_
  50.5 0.1 shard_map.90
  50.6 0.6 collective-permute-start.21
  51.2 0.2 collective-permute-start.20
  51.4 0.8 %collective-permute-start.19 = (f32[18,8,128]{2,1,0:T(8,128)S(1)}, f32[18,8,128]{2,1,0:T(8,128)S(1)}, u32[]{:S(2)}, u32[]{:S(2)}) collective-permute-start(f32[18,8,128]{2,1,0:T(8,128)S(1)} %get-tuple-element.38), channel_id=1, source_target_pairs={{0,2},{1,3},{2,0},{3,1},{4,6},{5,7},{6,4},{7,5},{8,10},{9,11},{10,... | collective-permute-start | bytes 221192 | tf_op jit(solution)/shard_map/ppermute | solution.py:814
  52.2 2.2 %collective-permute-start.18 = (f32[18,8,128]{2,1,0:T(8,128)S(1)}, f32[18,8,128]{2,1,0:T(8,128)S(1)}, u32[]{:S(2)}, u32[]{:S(2)}) collective-permute-start(f32[18,8,128]{2,1,0:T(8,128)S(1)} %get-tuple-element.39), channel_id=1, source_target_pairs={{0,4},{1,5},{2,6},{3,7},{4,0},{5,1},{6,2},{7,3},{8,12},{9,13},{10,... | collective-permute-start | bytes 221192 | tf_op jit(solution)/shard_map/ppermute | solution.py:814
  54.4 0.6 %collective-permute-start.17 = (f32[18,8,128]{2,1,0:T(8,128)S(1)}, f32[18,8,128]{2,1,0:T(8,128)S(1)}, u32[]{:S(2)}, u32[]{:S(2)}) collective-permute-start(f32[18,8,128]{2,1,0:T(8,128)S(1)} %get-tuple-element.40), channel_id=1, source_target_pairs={{0,3},{1,2},{2,1},{3,0},{4,7},{5,6},{6,5},{7,4},{8,11},{9,10},{10,... | collective-permute-start | bytes 221192 | tf_op jit(solution)/shard_map/ppermute | solution.py:814
  55.1 1.6 %collective-permute-done.21.refs_7_ = f32[18,8,128]{2,1,0:T(8,128)S(1)} collective-permute-done((f32[18,8,128]{2,1,0:T(8,128)S(1)}, f32[18,8,128]{2,1,0:T(8,128)S(1)}, u32[]{:S(2)}, u32[]{:S(2)}) %collective-permute-start.21) | collective-permute-done | bytes 73760 | tf_op jit(solution)/shard_map/ppermute | solution.py:814
  56.7 0.0 collective-permute-start.16
  56.7 0.0 collective-permute-done.20.refs_6_
  56.7 1.4 %collective-permute-start.15 = (f32[18,8,128]{2,1,0:T(8,128)S(1)}, f32[18,8,128]{2,1,0:T(8,128)S(1)}, u32[]{:S(2)}, u32[]{:S(2)}) collective-permute-start(f32[18,8,128]{2,1,0:T(8,128)S(1)} %get-tuple-element.42), channel_id=1, source_target_pairs={{0,1},{1,0},{2,3},{3,2},{4,5},{5,4},{6,7},{7,6},{8,9},{9,8},{10,11... | collective-permute-start | bytes 221192 | tf_op jit(solution)/shard_map/ppermute | solution.py:814
  58.1 0.0 collective-permute-done.19.refs_5_
  58.1 0.4 collective-permute-done.18.refs_4_
  58.5 0.1 collective-permute-done.17.refs_3_
  58.6 2.0 %collective-permute-done.16.refs_2_ = f32[18,8,128]{2,1,0:T(8,128)S(1)} collective-permute-done((f32[18,8,128]{2,1,0:T(8,128)S(1)}, f32[18,8,128]{2,1,0:T(8,128)S(1)}, u32[]{:S(2)}, u32[]{:S(2)}) %collective-permute-start.16) | collective-permute-done | bytes 73760 | tf_op jit(solution)/shard_map/ppermute | solution.py:814
  60.6 0.0 collective-permute-done.15.refs_1_
  60.6 2.5 %shard_map.91 = (f32[27,4,8,128]{3,2,1,0:T(8,128)}, f32[7,1,8,512]{3,2,1,0:T(8,128)}) custom-call(f32[18,8,128]{2,1,0:T(8,128)S(1)} %get-tuple-element.43.refs_0_, f32[18,8,128]{2,1,0:T(8,128)S(1)} %collective-permute-done.15.refs_1_, f32[18,8,128]{2,1,0:T(8,128)S(1)} %collective-permute-done.16.refs_2_, f32[18,8,128]{2,1,0:T(8,128)S(1)} %collective-permute-done.17.refs_3_, ...), custom_call_target="tpu_custom_call" | custom-call | tf_op jit(solution)/shard_map/pallas_call | solution.py:775
  (1 shorter events, 0.0 us)
Async XLA Ops:
  3.5 7.2 %collective-permute-start.6 = (f32[24,8,128]{2,1,0:T(8,128)S(1)}, f32[24,8,128]{2,1,0:T(8,128)S(1)}, u32[]{:S(2)}, u32[]{:S(2)}) collective-permute-start(f32[24,8,128]{2,1,0:T(8,128)S(1)} %get-tuple-element.28), channel_id=1, source_target_pairs={{0,6},{1,7},{2,4},{3,5},{4,2},{5,3},{6,0},{7,1},{8,14},{9,15},{10,... | collective-permute-start | bytes 294920 | tf_op jit(solution)/shard_map/ppermute | solution.py:814
  7.5 6.0 %collective-permute-start.5 = (f32[24,8,128]{2,1,0:T(8,128)S(1)}, f32[24,8,128]{2,1,0:T(8,128)S(1)}, u32[]{:S(2)}, u32[]{:S(2)}) collective-permute-start(f32[24,8,128]{2,1,0:T(8,128)S(1)} %get-tuple-element.29), channel_id=1, source_target_pairs={{0,7},{1,6},{2,5},{3,4},{4,3},{5,2},{6,1},{7,0},{8,15},{9,14},{10,... | collective-permute-start | bytes 294920 | tf_op jit(solution)/shard_map/ppermute | solution.py:814
  7.5 7.5 %collective-permute-start.4 = (f32[24,8,128]{2,1,0:T(8,128)S(1)}, f32[24,8,128]{2,1,0:T(8,128)S(1)}, u32[]{:S(2)}, u32[]{:S(2)}) collective-permute-start(f32[24,8,128]{2,1,0:T(8,128)S(1)} %get-tuple-element.30), channel_id=1, source_target_pairs={{0,2},{1,3},{2,0},{3,1},{4,6},{5,7},{6,4},{7,5},{8,10},{9,11},{10,... | collective-permute-start | bytes 294920 | tf_op jit(solution)/shard_map/ppermute | solution.py:814
  8.6 6.7 %collective-permute-start.3 = (f32[24,8,128]{2,1,0:T(8,128)S(1)}, f32[24,8,128]{2,1,0:T(8,128)S(1)}, u32[]{:S(2)}, u32[]{:S(2)}) collective-permute-start(f32[24,8,128]{2,1,0:T(8,128)S(1)} %get-tuple-element.31), channel_id=1, source_target_pairs={{0,4},{1,5},{2,6},{3,7},{4,0},{5,1},{6,2},{7,3},{8,12},{9,13},{10,... | collective-permute-start | bytes 294920 | tf_op jit(solution)/shard_map/ppermute | solution.py:814
  10.1 6.6 %collective-permute-start.2 = (f32[24,8,128]{2,1,0:T(8,128)S(1)}, f32[24,8,128]{2,1,0:T(8,128)S(1)}, u32[]{:S(2)}, u32[]{:S(2)}) collective-permute-start(f32[24,8,128]{2,1,0:T(8,128)S(1)} %get-tuple-element.32), channel_id=1, source_target_pairs={{0,3},{1,2},{2,1},{3,0},{4,7},{5,6},{6,5},{7,4},{8,11},{9,10},{10,... | collective-permute-start | bytes 294920 | tf_op jit(solution)/shard_map/ppermute | solution.py:814
  10.7 6.7 %collective-permute-start.1 = (f32[24,8,128]{2,1,0:T(8,128)S(1)}, f32[24,8,128]{2,1,0:T(8,128)S(1)}, u32[]{:S(2)}, u32[]{:S(2)}) collective-permute-start(f32[24,8,128]{2,1,0:T(8,128)S(1)} %get-tuple-element.33), channel_id=1, source_target_pairs={{0,5},{1,4},{2,7},{3,6},{4,1},{5,0},{6,3},{7,2},{8,13},{9,12},{10,... | collective-permute-start | bytes 294920 | tf_op jit(solution)/shard_map/ppermute | solution.py:814
  13.5 3.9 %collective-permute-start = (f32[24,8,128]{2,1,0:T(8,128)S(1)}, f32[24,8,128]{2,1,0:T(8,128)S(1)}, u32[]{:S(2)}, u32[]{:S(2)}) collective-permute-start(f32[24,8,128]{2,1,0:T(8,128)S(1)} %get-tuple-element.34), channel_id=1, source_target_pairs={{0,1},{1,0},{2,3},{3,2},{4,5},{5,4},{6,7},{7,6},{8,9},{9,8},{10,11... | collective-permute-start | bytes 294920 | tf_op jit(solution)/shard_map/ppermute | solution.py:814
  17.9 12.4 %collective-permute-start.7 = (f32[4,16,8,128]{3,2,1,0:T(8,128)S(1)}, f32[4,16,8,128]{3,2,1,0:T(8,128)S(1)}, u32[]{:S(2)}, u32[]{:S(2)}) collective-permute-start(f32[4,16,8,128]{3,2,1,0:T(8,128)S(1)} %get-tuple-element.16), channel_id=1, source_target_pairs={{25,0},{0,1},{1,2},{2,3},{3,7},{7,6},{6,5},{5,4},{4,13},{13,12},{1... | collective-permute-start | bytes 786440 | tf_op jit(solution)/shard_map/ppermute | solution.py:805
  18.1 12.2 %collective-permute-start.8 = (f32[4,16,8,128]{3,2,1,0:T(8,128)S(1)}, f32[4,16,8,128]{3,2,1,0:T(8,128)S(1)}, u32[]{:S(2)}, u32[]{:S(2)}) collective-permute-start(f32[4,16,8,128]{3,2,1,0:T(8,128)S(1)} %get-tuple-element.17), channel_id=1, source_target_pairs={{0,25},{1,0},{2,1},{3,2},{7,3},{6,7},{5,6},{4,5},{13,4},{12,13},{8... | collective-permute-start | bytes 786440 | tf_op jit(solution)/shard_map/ppermute | solution.py:806
  21.5 6.1 %collective-permute-start.9 = (f32[8,2,8,128]{3,2,1,0:T(8,128)S(1)}, f32[8,2,8,128]{3,2,1,0:T(8,128)S(1)}, u32[]{:S(2)}, u32[]{:S(2)}) collective-permute-start(f32[8,2,8,128]{3,2,1,0:T(8,128)S(1)} %get-tuple-element.19), channel_id=1, source_target_pairs={{0,8},{8,0},{16,24},{24,16},{1,9},{9,1},{17,25},{25,17},{2,10},{10... | collective-permute-start | bytes 196616 | tf_op jit(solution)/shard_map/ppermute | solution.py:820
  21.6 8.7 %collective-permute-start.10 = (f32[8,2,8,128]{3,2,1,0:T(8,128)S(1)}, f32[8,2,8,128]{3,2,1,0:T(8,128)S(1)}, u32[]{:S(2)}, u32[]{:S(2)}) collective-permute-start(f32[8,2,8,128]{3,2,1,0:T(8,128)S(1)} %get-tuple-element.20), channel_id=1, source_target_pairs={{0,16},{8,24},{16,0},{24,8},{1,17},{9,25},{17,1},{25,9},{2,18},{10... | collective-permute-start | bytes 196616 | tf_op jit(solution)/shard_map/ppermute | solution.py:820
  24.1 6.1 %collective-permute-start.11 = (f32[8,2,8,128]{3,2,1,0:T(8,128)S(1)}, f32[8,2,8,128]{3,2,1,0:T(8,128)S(1)}, u32[]{:S(2)}, u32[]{:S(2)}) collective-permute-start(f32[8,2,8,128]{3,2,1,0:T(8,128)S(1)} %get-tuple-element.21), channel_id=1, source_target_pairs={{0,24},{8,16},{16,8},{24,0},{1,25},{9,17},{17,9},{25,1},{2,26},{10... | collective-permute-start | bytes 196616 | tf_op jit(solution)/shard_map/ppermute | solution.py:820
  39.6 10.8 %collective-permute-start.12 = (f32[8,8,128]{2,1,0:T(8,128)S(1)}, f32[8,8,128]{2,1,0:T(8,128)S(1)}, u32[]{:S(2)}, u32[]{:S(2)}) collective-permute-start(f32[8,8,128]{2,1,0:T(8,128)S(1)} %get-tuple-element.25), channel_id=1, source_target_pairs={{0,8},{8,0},{16,24},{24,16},{1,9},{9,1},{17,25},{25,17},{2,10},{10... | collective-permute-start | bytes 98312 | tf_op jit(solution)/shard_map/ppermute | solution.py:820
  41.3 9.2 %collective-permute-start.13 = (f32[8,8,128]{2,1,0:T(8,128)S(1)}, f32[8,8,128]{2,1,0:T(8,128)S(1)}, u32[]{:S(2)}, u32[]{:S(2)}) collective-permute-start(f32[8,8,128]{2,1,0:T(8,128)S(1)} %get-tuple-element.26), channel_id=1, source_target_pairs={{0,16},{8,24},{16,0},{24,8},{1,17},{9,25},{17,1},{25,9},{2,18},{10... | collective-permute-start | bytes 98312 | tf_op jit(solution)/shard_map/ppermute | solution.py:820
  44.0 6.5 %collective-permute-start.14 = (f32[8,8,128]{2,1,0:T(8,128)S(1)}, f32[8,8,128]{2,1,0:T(8,128)S(1)}, u32[]{:S(2)}, u32[]{:S(2)}) collective-permute-start(f32[8,8,128]{2,1,0:T(8,128)S(1)} %get-tuple-element.27), channel_id=1, source_target_pairs={{0,24},{8,16},{16,8},{24,0},{1,25},{9,17},{17,9},{25,1},{2,26},{10... | collective-permute-start | bytes 98312 | tf_op jit(solution)/shard_map/ppermute | solution.py:820
  50.6 6.1 %collective-permute-start.21 = (f32[18,8,128]{2,1,0:T(8,128)S(1)}, f32[18,8,128]{2,1,0:T(8,128)S(1)}, u32[]{:S(2)}, u32[]{:S(2)}) collective-permute-start(f32[18,8,128]{2,1,0:T(8,128)S(1)} %get-tuple-element.36), channel_id=1, source_target_pairs={{0,6},{1,7},{2,4},{3,5},{4,2},{5,3},{6,0},{7,1},{8,14},{9,15},{10,... | collective-permute-start | bytes 221192 | tf_op jit(solution)/shard_map/ppermute | solution.py:814
  51.2 5.6 %collective-permute-start.20 = (f32[18,8,128]{2,1,0:T(8,128)S(1)}, f32[18,8,128]{2,1,0:T(8,128)S(1)}, u32[]{:S(2)}, u32[]{:S(2)}) collective-permute-start(f32[18,8,128]{2,1,0:T(8,128)S(1)} %get-tuple-element.37), channel_id=1, source_target_pairs={{0,7},{1,6},{2,5},{3,4},{4,3},{5,2},{6,1},{7,0},{8,15},{9,14},{10,... | collective-permute-start | bytes 221192 | tf_op jit(solution)/shard_map/ppermute | solution.py:814
  51.4 6.7 %collective-permute-start.19 = (f32[18,8,128]{2,1,0:T(8,128)S(1)}, f32[18,8,128]{2,1,0:T(8,128)S(1)}, u32[]{:S(2)}, u32[]{:S(2)}) collective-permute-start(f32[18,8,128]{2,1,0:T(8,128)S(1)} %get-tuple-element.38), channel_id=1, source_target_pairs={{0,2},{1,3},{2,0},{3,1},{4,6},{5,7},{6,4},{7,5},{8,10},{9,11},{10,... | collective-permute-start | bytes 221192 | tf_op jit(solution)/shard_map/ppermute | solution.py:814
  52.2 6.3 %collective-permute-start.18 = (f32[18,8,128]{2,1,0:T(8,128)S(1)}, f32[18,8,128]{2,1,0:T(8,128)S(1)}, u32[]{:S(2)}, u32[]{:S(2)}) collective-permute-start(f32[18,8,128]{2,1,0:T(8,128)S(1)} %get-tuple-element.39), channel_id=1, source_target_pairs={{0,4},{1,5},{2,6},{3,7},{4,0},{5,1},{6,2},{7,3},{8,12},{9,13},{10,... | collective-permute-start | bytes 221192 | tf_op jit(solution)/shard_map/ppermute | solution.py:814
  54.4 4.2 %collective-permute-start.17 = (f32[18,8,128]{2,1,0:T(8,128)S(1)}, f32[18,8,128]{2,1,0:T(8,128)S(1)}, u32[]{:S(2)}, u32[]{:S(2)}) collective-permute-start(f32[18,8,128]{2,1,0:T(8,128)S(1)} %get-tuple-element.40), channel_id=1, source_target_pairs={{0,3},{1,2},{2,1},{3,0},{4,7},{5,6},{6,5},{7,4},{8,11},{9,10},{10,... | collective-permute-start | bytes 221192 | tf_op jit(solution)/shard_map/ppermute | solution.py:814
  56.7 3.9 %collective-permute-start.16 = (f32[18,8,128]{2,1,0:T(8,128)S(1)}, f32[18,8,128]{2,1,0:T(8,128)S(1)}, u32[]{:S(2)}, u32[]{:S(2)}) collective-permute-start(f32[18,8,128]{2,1,0:T(8,128)S(1)} %get-tuple-element.41), channel_id=1, source_target_pairs={{0,5},{1,4},{2,7},{3,6},{4,1},{5,0},{6,3},{7,2},{8,13},{9,12},{10,... | collective-permute-start | bytes 221192 | tf_op jit(solution)/shard_map/ppermute | solution.py:814
  56.7 3.9 %collective-permute-start.15 = (f32[18,8,128]{2,1,0:T(8,128)S(1)}, f32[18,8,128]{2,1,0:T(8,128)S(1)}, u32[]{:S(2)}, u32[]{:S(2)}) collective-permute-start(f32[18,8,128]{2,1,0:T(8,128)S(1)} %get-tuple-element.42), channel_id=1, source_target_pairs={{0,1},{1,0},{2,3},{3,2},{4,5},{5,4},{6,7},{7,6},{8,9},{9,8},{10,11... | collective-permute-start | bytes 221192 | tf_op jit(solution)/shard_map/ppermute | solution.py:814

commit v6 on v5

--- a/solution.py
+++ b/solution.py
@@ -290,13 +290,18 @@
         for first in range(count):
             if first & bit == 0:
                 a, b = values[first], values[first | bit]
+                if 2 * group * bit == LANES:
+                    crossed = lane_roll(jnp.where(low, b, a), group * bit)
+                    values[first] = jnp.where(low, a, crossed)
+                    values[first | bit] = jnp.where(low, crossed, b)
+                    continue
                 values[first] = jnp.where(low, a, lane_roll(b, group * bit))
                 values[first | bit] = jnp.where(low, lane_roll(a, -group * bit), b)
         bit *= 2
     return values
 
 
-SPEED_AT, SOLID_AT, HEAT_AT, RATE_AT, ROWS = 27, 30, 32, 39, 40
+SPEED_AT, SOLID_AT = 27, 30
 IN_PAIRS = 16
 FLOW_PAIRS = 14
 
@@ -388,7 +393,7 @@
     lax.fori_loop(0, slab.sub // 2, one, 0)
 
 
-def make_heat_tiles(slab, parts, held, state):
+def make_heat_tiles(slab, parts, held, heat_tiles):
     mine = lax.axis_index("grp")
     for step, part in enumerate(parts):
         held[jnp.bitwise_xor(mine, step)] = part[...]
@@ -399,7 +404,7 @@
             after = held[(x + 1) % slab.block_x, tile, 1]
             sources += [held[x, tile, 0], jnp.where(first, held[x, tile, 1], after)]
         for k, value in enumerate(swap_groups(sources, slab.planes)):
-            state[HEAT_AT + k, tile] = value
+            heat_tiles[k, tile] = value
 
 
 def make_tiles(slab, came, below_ref, above_ref, state):
@@ -632,30 +637,31 @@
     lax.fori_loop(0, count, one, 0)
 
 
-def first_window(slab, rates_hbm, came, below_ref, above_ref, *refs):
+def first_window(slab, rates_hbm, state, *refs):
     heat_parts, refs = refs[: slab.grp], refs[slab.grp :]
     flow_out, keep_out, heat_outs = refs[0], refs[1], refs[2 : 2 + slab.grp]
-    rates_ref, sem, state, flow_post, heat_post, heat_a, heat_b, held, came_heat = refs[
+    (rates_ref, sem, speed, heat_tiles, flow_post, heat_post, heat_a, heat_b, held, came_heat) = refs[
         2 + slab.grp :
     ]
     rates_copy = pltpu.make_async_copy(rates_hbm, rates_ref, sem)
     rates_copy.start()
-    make_tiles(slab, came, below_ref, above_ref, state)
-    make_heat_tiles(slab, heat_parts, came_heat, state)
+    make_heat_tiles(slab, heat_parts, came_heat, heat_tiles)
     rates_copy.wait()
 
     def speeds_of(tile):
-        return [state[SPEED_AT + d, tile] for d in range(3)]
+        return [speed[d, tile] for d in range(3)]
 
     def begin(tile):
         solid = state[SOLID_AT, tile]
-        heat = [state[HEAT_AT + k, tile] for k in range(7)]
+        heat = [heat_tiles[k, tile] for k in range(7)]
+        for d in range(3):
+            speed[d, tile] = state[SPEED_AT + d, tile]
         force = heat_force(heat)
         keep_out[0, tile] = force
         keep_out[1, tile] = solid
         flow = [state[n, tile] for n in range(27)]
         collide_flow(rates_ref, flow, force, solid != 0.0, flow_post.at[0], tile)
-        collide_heat(heat, state[RATE_AT, tile], speeds_of(tile), heat_post.at[0], tile)
+        collide_heat(heat, heat_tiles[7, tile], speeds_of(tile), heat_post.at[0], tile)
 
     over_tiles(slab, begin)
 
@@ -667,7 +673,7 @@
             solid = state[SOLID_AT, tile] != 0.0
             collide_flow(rates_ref, flow, keep_out[0, tile], solid, flow_post.at[1 - source], tile)
             heat = stream(slab, heat_post.at[source], tile, HEAT_OFFSETS)
-            omega = state[RATE_AT, tile]
+            omega = heat_tiles[7, tile]
             collide_heat(heat, omega, speeds_of(tile), heat_post.at[1 - source], tile)
 
         over_tiles(slab, go_on)
@@ -683,11 +689,11 @@
             jnp.where(solid, 0.0, each) for each in flow_speed_tile(flow, keep_out[0, tile])
         ]
         for d in range(3):
-            state[SPEED_AT + d, tile] = speeds[d]
+            speed[d, tile] = speeds[d]
         force = heat_force(heat)
         keep_out[0, tile] = force
         collide_flow(rates_ref, flow, force, solid, flow_out, tile)
-        collide_heat(heat, state[RATE_AT, tile], speeds, heat_a, tile)
+        collide_heat(heat, heat_tiles[7, tile], speeds, heat_a, tile)
 
     over_tiles(slab, next_window)
     here, there = heat_a, heat_b
@@ -695,7 +701,7 @@
 
         def heat_alone(tile, here=here, there=there):
             heat = stream(slab, here, tile, HEAT_OFFSETS)
-            collide_heat(heat, state[RATE_AT, tile], speeds_of(tile), there, tile)
+            collide_heat(heat, heat_tiles[7, tile], speeds_of(tile), there, tile)
 
         over_tiles(slab, heat_alone, unroll=4)
         here, there = there, here
@@ -855,14 +861,15 @@
     )
     below, above = exchange(slab, low, high)
     parts = across_planes(slab, parts)
+    (state,) = local_call(make_tiles, slab, [came, below, above], [(2 * IN_PAIRS,) + plane])
     scalars = [pltpu.SMEM(rates.shape, F32), pltpu.SemaphoreType.DMA]
     flow, keep, *parts = local_call(
         first_window,
         slab,
-        [rates, came, below, above] + parts,
+        [rates, state] + parts,
         [(27,) + plane, (2,) + plane] + [plane] * slab.grp,
         scalars
-        + [(ROWS,) + plane, (2, 27) + plane, (2, 7) + plane]
+        + [(3,) + plane, (8,) + plane, (2, 27) + plane, (2, 7) + plane]
         + [(7,) + plane] * 2
         + [(slab.grp,) + plane, (slab.grp,) + heat_shape],
         in_hbm=1,

time: 63.3 us -> 62.1 us (0.981)
  waiting for transfers between devices: 14.7 us -> 13.7 us
    ppermute x6, waiting for transfers between devices: 4.42 us -> 2.46 us  [across_planes(): lax.ppermute(parts[step], 'grp', [(i, i ^ step) for i in range(slab.grp)])]
    ppermute x1, waiting for transfers between devices: 0.01 us -> 0.99 us  [exchange(): from_above = lax.ppermute(low, RING, [(b, a) for a, b in upward])]
    pallas_call x6 -> x7, Pallas kernels: 21.1 us -> 20.8 us  [local_call(): pl.pallas_call(kernel, out_shape=[jax.ShapeDtypeStruct(shape, F32) for sh...]
  transfers between devices with their start and end apart: 22 -> 22, of which waited for: 11 -> 11; matrix products, arithmetic and copies ran while one was open for 0% -> 0% of each run, Pallas kernels for 9% -> 11%
where the time goes in v6:
time: 62.1 us; the launch traced here: 61.9 us
  starting transfers between devices  26.6 us (43%)
  Pallas kernels  20.8 us (33%)
  waiting for transfers between devices  13.7 us (22%)
  between operations  0.73 us (1%)
    pallas_call x7, Pallas kernels, local_call(): pl.pallas_call(kernel, out_shape=[jax.ShapeDtypeStruct(shape, F32) for sh...  20.8 us
    ppermute x14, starting transfers between devices, across_plane(): came[step] = lax.ppermute(sent[step], ('gx', 'gy'), pairs)  13.6 us
    ppermute x14, waiting for transfers between devices, across_plane(): came[step] = lax.ppermute(sent[step], ('gx', 'gy'), pairs)  10.3 us
    ppermute x6, starting transfers between devices, across_planes(): lax.ppermute(parts[step], 'grp', [(i, i ^ step) for i in range(slab.grp)])  9.39 us
    ppermute x1, starting transfers between devices, exchange(): from_above = lax.ppermute(low, RING, [(b, a) for a, b in upward])  3.43 us
    ppermute x6, waiting for transfers between devices, across_planes(): lax.ppermute(parts[step], 'grp', [(i, i ^ step) for i in range(slab.grp)])  2.46 us
  transfers between devices with their start and end apart: 22, of which 11 were waited for; matrix products, arithmetic and copies ran while one was open for 0% of the time, Pallas kernels for 11%

profile of v6, /device:TPU:0, one launch (start us, length us, event | category | flops | bytes accessed | tf_op | source)
XLA Modules:
  0.0 61.9 jit_solution(7309613129446841077)
XLA Ops:
  0.6 2.5 %shard_map.86 = f32[8,24,8,128]{3,2,1,0:T(8,128)S(1)} custom-call(f32[4]{0:T(128)} %refs_0_.3, f32[27,4,8,128]{3,2,1,0:T(8,128)} %refs_1_.1, f32[3,4,8,128]{3,2,1,0:T(8,128)} %refs_2_.1, s32[4,8,128]{2,1,0:T(8,128)} %refs_3_.1, f32[7,1,8,512]{3,2,1,0:T(8,128)} %refs_4_.1, s32[1,8,512]{2,1,0:T(8,128)} %refs_5_.1), custom_call_target="tpu_custom_call" | custom-call | tf_op jit(solution)/shard_map/pallas_call | solution.py:781
  3.2 0.1 slice_bitcast_fusion
  3.2 4.0 %collective-permute-start.6 = (f32[24,8,128]{2,1,0:T(8,128)S(1)}, f32[24,8,128]{2,1,0:T(8,128)S(1)}, u32[]{:S(2)}, u32[]{:S(2)}) collective-permute-start(f32[24,8,128]{2,1,0:T(8,128)S(1)} %get-tuple-element.28), channel_id=1, source_target_pairs={{0,6},{1,7},{2,4},{3,5},{4,2},{5,3},{6,0},{7,1},{8,14},{9,15},{10,... | collective-permute-start | bytes 294920 | tf_op jit(solution)/shard_map/ppermute | solution.py:820
  7.2 0.0 collective-permute-start.5
  7.2 1.1 %collective-permute-start.4 = (f32[24,8,128]{2,1,0:T(8,128)S(1)}, f32[24,8,128]{2,1,0:T(8,128)S(1)}, u32[]{:S(2)}, u32[]{:S(2)}) collective-permute-start(f32[24,8,128]{2,1,0:T(8,128)S(1)} %get-tuple-element.30), channel_id=1, source_target_pairs={{0,2},{1,3},{2,0},{3,1},{4,6},{5,7},{6,4},{7,5},{8,10},{9,11},{10,... | collective-permute-start | bytes 294920 | tf_op jit(solution)/shard_map/ppermute | solution.py:820
  8.3 1.5 %collective-permute-start.3 = (f32[24,8,128]{2,1,0:T(8,128)S(1)}, f32[24,8,128]{2,1,0:T(8,128)S(1)}, u32[]{:S(2)}, u32[]{:S(2)}) collective-permute-start(f32[24,8,128]{2,1,0:T(8,128)S(1)} %get-tuple-element.31), channel_id=1, source_target_pairs={{0,4},{1,5},{2,6},{3,7},{4,0},{5,1},{6,2},{7,3},{8,12},{9,13},{10,... | collective-permute-start | bytes 294920 | tf_op jit(solution)/shard_map/ppermute | solution.py:820
  9.8 0.6 collective-permute-start.2
  10.4 0.0 collective-permute-done.6.refs_7_
  10.4 0.6 collective-permute-start.1
  11.0 2.2 %collective-permute-done.5.refs_6_ = f32[24,8,128]{2,1,0:T(8,128)S(1)} collective-permute-done((f32[24,8,128]{2,1,0:T(8,128)S(1)}, f32[24,8,128]{2,1,0:T(8,128)S(1)}, u32[]{:S(2)}, u32[]{:S(2)}) %collective-permute-start.5) | collective-permute-done | bytes 98336 | tf_op jit(solution)/shard_map/ppermute | solution.py:820
  13.2 0.0 collective-permute-start
  13.2 1.6 %collective-permute-done.4.refs_5_ = f32[24,8,128]{2,1,0:T(8,128)S(1)} collective-permute-done((f32[24,8,128]{2,1,0:T(8,128)S(1)}, f32[24,8,128]{2,1,0:T(8,128)S(1)}, u32[]{:S(2)}, u32[]{:S(2)}) %collective-permute-start.4) | collective-permute-done | bytes 98336 | tf_op jit(solution)/shard_map/ppermute | solution.py:820
  14.7 0.3 collective-permute-done.3.refs_4_
  15.0 1.4 %collective-permute-done.2.refs_3_ = f32[24,8,128]{2,1,0:T(8,128)S(1)} collective-permute-done((f32[24,8,128]{2,1,0:T(8,128)S(1)}, f32[24,8,128]{2,1,0:T(8,128)S(1)}, u32[]{:S(2)}, u32[]{:S(2)}) %collective-permute-start.2) | collective-permute-done | bytes 98336 | tf_op jit(solution)/shard_map/ppermute | solution.py:820
  16.4 0.7 %collective-permute-done.1.refs_2_ = f32[24,8,128]{2,1,0:T(8,128)S(1)} collective-permute-done((f32[24,8,128]{2,1,0:T(8,128)S(1)}, f32[24,8,128]{2,1,0:T(8,128)S(1)}, u32[]{:S(2)}, u32[]{:S(2)}) %collective-permute-start.1) | collective-permute-done | bytes 98336 | tf_op jit(solution)/shard_map/ppermute | solution.py:820
  17.1 0.0 collective-permute-done.refs_1_
  17.1 0.5 shard_map.87
  17.6 0.2 collective-permute-start.7
  17.8 3.4 %collective-permute-start.8 = (f32[4,16,8,128]{3,2,1,0:T(8,128)S(1)}, f32[4,16,8,128]{3,2,1,0:T(8,128)S(1)}, u32[]{:S(2)}, u32[]{:S(2)}) collective-permute-start(f32[4,16,8,128]{3,2,1,0:T(8,128)S(1)} %get-tuple-element.17), channel_id=1, source_target_pairs={{0,25},{1,0},{2,1},{3,2},{7,3},{6,7},{5,6},{4,5},{13,4},{12,13},{8... | collective-permute-start | bytes 786440 | tf_op jit(solution)/shard_map/ppermute | solution.py:812
  21.2 0.1 collective-permute-start.9
  21.3 2.6 %collective-permute-start.10 = (f32[8,2,8,128]{3,2,1,0:T(8,128)S(1)}, f32[8,2,8,128]{3,2,1,0:T(8,128)S(1)}, u32[]{:S(2)}, u32[]{:S(2)}) collective-permute-start(f32[8,2,8,128]{3,2,1,0:T(8,128)S(1)} %get-tuple-element.20), channel_id=1, source_target_pairs={{0,16},{8,24},{16,0},{24,8},{1,17},{9,25},{17,1},{25,9},{2,18},{10... | collective-permute-start | bytes 196616 | tf_op jit(solution)/shard_map/ppermute | solution.py:826
  23.8 1.7 %collective-permute-start.11 = (f32[8,2,8,128]{3,2,1,0:T(8,128)S(1)}, f32[8,2,8,128]{3,2,1,0:T(8,128)S(1)}, u32[]{:S(2)}, u32[]{:S(2)}) collective-permute-start(f32[8,2,8,128]{3,2,1,0:T(8,128)S(1)} %get-tuple-element.21), channel_id=1, source_target_pairs={{0,24},{8,16},{16,8},{24,0},{1,25},{9,17},{17,9},{25,1},{2,26},{10... | collective-permute-start | bytes 196616 | tf_op jit(solution)/shard_map/ppermute | solution.py:826
  25.6 0.0 collective-permute-done.7.refs_1_
  25.6 1.0 %collective-permute-done.8.refs_2_ = f32[4,16,8,128]{3,2,1,0:T(8,128)S(1)} collective-permute-done((f32[4,16,8,128]{3,2,1,0:T(8,128)S(1)}, f32[4,16,8,128]{3,2,1,0:T(8,128)S(1)}, u32[]{:S(2)}, u32[]{:S(2)}) %collective-permute-start.8) | collective-permute-done | bytes 262176 | tf_op jit(solution)/shard_map/ppermute | solution.py:812
  26.6 1.0 %shard_map.88.refs_1_ = f32[32,8,8,128]{3,2,1,0:T(8,128)S(1)} custom-call(f32[8,24,8,128]{3,2,1,0:T(8,128)S(1)} %get-tuple-element.15.refs_0_.refs_1_, f32[4,16,8,128]{3,2,1,0:T(8,128)S(1)} %collective-permute-done.7.refs_1_, f32[4,16,8,128]{3,2,1,0:T(8,128)S(1)} %collective-permute-done.8.refs_2_), custom_call_target="tpu_custom_call" | custom-call | tf_op jit(solution)/shard_map/pallas_call | solution.py:781
  27.5 0.0 collective-permute-done.9.refs_3_
  27.5 2.4 %collective-permute-done.10.refs_4_ = f32[8,2,8,128]{3,2,1,0:T(8,128)S(1)} collective-permute-done((f32[8,2,8,128]{3,2,1,0:T(8,128)S(1)}, f32[8,2,8,128]{3,2,1,0:T(8,128)S(1)}, u32[]{:S(2)}, u32[]{:S(2)}) %collective-permute-start.10) | collective-permute-done | bytes 65568 | tf_op jit(solution)/shard_map/ppermute | solution.py:826
  30.0 0.0 collective-permute-done.11.refs_5_
  30.0 8.6 %shard_map.89 = (f32[27,8,8,128]{3,2,1,0:T(8,128)S(1)}, f32[2,8,8,128]{3,2,1,0:T(8,128)S(1)}, f32[8,8,128]{2,1,0:T(8,128)S(1)}, f32[8,8,128]{2,1,0:T(8,128)S(1)}...) custom-call(f32[27]{0:T(128)} %refs_0_.5, f32[32,8,8,128]{3,2,1,0:T(8,128)S(1)} %shard_map.88.refs_1_, ...), custom_call_target="tpu_custom_call" | custom-call | tf_op jit(solution)/shard_map/pallas_call | solution.py:781
  38.6 1.6 %collective-permute-start.12 = (f32[8,8,128]{2,1,0:T(8,128)S(1)}, f32[8,8,128]{2,1,0:T(8,128)S(1)}, u32[]{:S(2)}, u32[]{:S(2)}) collective-permute-start(f32[8,8,128]{2,1,0:T(8,128)S(1)} %get-tuple-element.25), channel_id=1, source_target_pairs={{0,8},{8,0},{16,24},{24,16},{1,9},{9,1},{17,25},{25,17},{2,10},{10... | collective-permute-start | bytes 98312 | tf_op jit(solution)/shard_map/ppermute | solution.py:826
  40.2 2.7 %collective-permute-start.13 = (f32[8,8,128]{2,1,0:T(8,128)S(1)}, f32[8,8,128]{2,1,0:T(8,128)S(1)}, u32[]{:S(2)}, u32[]{:S(2)}) collective-permute-start(f32[8,8,128]{2,1,0:T(8,128)S(1)} %get-tuple-element.26), channel_id=1, source_target_pairs={{0,16},{8,24},{16,0},{24,8},{1,17},{9,25},{17,1},{25,9},{2,18},{10... | collective-permute-start | bytes 98312 | tf_op jit(solution)/shard_map/ppermute | solution.py:826
  42.9 0.7 %collective-permute-start.14 = (f32[8,8,128]{2,1,0:T(8,128)S(1)}, f32[8,8,128]{2,1,0:T(8,128)S(1)}, u32[]{:S(2)}, u32[]{:S(2)}) collective-permute-start(f32[8,8,128]{2,1,0:T(8,128)S(1)} %get-tuple-element.27), channel_id=1, source_target_pairs={{0,24},{8,16},{16,8},{24,0},{1,25},{9,17},{17,9},{25,1},{2,26},{10... | collective-permute-start | bytes 98312 | tf_op jit(solution)/shard_map/ppermute | solution.py:826
  43.6 5.8 %shard_map.90.refs_0_ = f32[8,18,8,128]{3,2,1,0:T(8,128)S(1)} custom-call(f32[27]{0:T(128)} %refs_0_.5, f32[8,24,8,128]{3,2,1,0:T(8,128)S(1)} %get-tuple-element.15.refs_0_.refs_1_, f32[27,8,8,128]{3,2,1,0:T(8,128)S(1)} %get-tuple-element.22.refs_2_, f32[2,8,8,128]{3,2,1,0:T(8,128)S(1)} %get-tuple-element.23.refs_3_), custom_call_target="tpu_custom_call" | custom-call | tf_op jit(solution)/shard_map/pallas_call | solution.py:781
  49.4 0.0 collective-permute-done.12.refs_2_
  49.5 0.0 collective-permute-done.13.refs_3_
  49.5 0.0 collective-permute-done.14.refs_4_
  49.5 0.1 shard_map.91
  49.6 0.6 collective-permute-start.21
  50.2 0.2 collective-permute-start.20
  50.4 0.8 %collective-permute-start.19 = (f32[18,8,128]{2,1,0:T(8,128)S(1)}, f32[18,8,128]{2,1,0:T(8,128)S(1)}, u32[]{:S(2)}, u32[]{:S(2)}) collective-permute-start(f32[18,8,128]{2,1,0:T(8,128)S(1)} %get-tuple-element.38), channel_id=1, source_target_pairs={{0,2},{1,3},{2,0},{3,1},{4,6},{5,7},{6,4},{7,5},{8,10},{9,11},{10,... | collective-permute-start | bytes 221192 | tf_op jit(solution)/shard_map/ppermute | solution.py:820
  51.2 2.2 %collective-permute-start.18 = (f32[18,8,128]{2,1,0:T(8,128)S(1)}, f32[18,8,128]{2,1,0:T(8,128)S(1)}, u32[]{:S(2)}, u32[]{:S(2)}) collective-permute-start(f32[18,8,128]{2,1,0:T(8,128)S(1)} %get-tuple-element.39), channel_id=1, source_target_pairs={{0,4},{1,5},{2,6},{3,7},{4,0},{5,1},{6,2},{7,3},{8,12},{9,13},{10,... | collective-permute-start | bytes 221192 | tf_op jit(solution)/shard_map/ppermute | solution.py:820
  53.4 0.6 %collective-permute-start.17 = (f32[18,8,128]{2,1,0:T(8,128)S(1)}, f32[18,8,128]{2,1,0:T(8,128)S(1)}, u32[]{:S(2)}, u32[]{:S(2)}) collective-permute-start(f32[18,8,128]{2,1,0:T(8,128)S(1)} %get-tuple-element.40), channel_id=1, source_target_pairs={{0,3},{1,2},{2,1},{3,0},{4,7},{5,6},{6,5},{7,4},{8,11},{9,10},{10,... | collective-permute-start | bytes 221192 | tf_op jit(solution)/shard_map/ppermute | solution.py:820
  54.1 1.6 %collective-permute-done.21.refs_7_ = f32[18,8,128]{2,1,0:T(8,128)S(1)} collective-permute-done((f32[18,8,128]{2,1,0:T(8,128)S(1)}, f32[18,8,128]{2,1,0:T(8,128)S(1)}, u32[]{:S(2)}, u32[]{:S(2)}) %collective-permute-start.21) | collective-permute-done | bytes 73760 | tf_op jit(solution)/shard_map/ppermute | solution.py:820
  55.7 0.0 collective-permute-start.16
  55.7 0.0 collective-permute-done.20.refs_6_
  55.7 1.4 %collective-permute-start.15 = (f32[18,8,128]{2,1,0:T(8,128)S(1)}, f32[18,8,128]{2,1,0:T(8,128)S(1)}, u32[]{:S(2)}, u32[]{:S(2)}) collective-permute-start(f32[18,8,128]{2,1,0:T(8,128)S(1)} %get-tuple-element.42), channel_id=1, source_target_pairs={{0,1},{1,0},{2,3},{3,2},{4,5},{5,4},{6,7},{7,6},{8,9},{9,8},{10,11... | collective-permute-start | bytes 221192 | tf_op jit(solution)/shard_map/ppermute | solution.py:820
  57.1 0.0 collective-permute-done.19.refs_5_
  57.1 0.4 collective-permute-done.18.refs_4_
  57.5 0.1 collective-permute-done.17.refs_3_
  57.6 2.0 %collective-permute-done.16.refs_2_ = f32[18,8,128]{2,1,0:T(8,128)S(1)} collective-permute-done((f32[18,8,128]{2,1,0:T(8,128)S(1)}, f32[18,8,128]{2,1,0:T(8,128)S(1)}, u32[]{:S(2)}, u32[]{:S(2)}) %collective-permute-start.16) | collective-permute-done | bytes 73760 | tf_op jit(solution)/shard_map/ppermute | solution.py:820
  59.6 0.0 collective-permute-done.15.refs_1_
  59.6 2.3 %shard_map.92 = (f32[27,4,8,128]{3,2,1,0:T(8,128)}, f32[7,1,8,512]{3,2,1,0:T(8,128)}) custom-call(f32[18,8,128]{2,1,0:T(8,128)S(1)} %get-tuple-element.43.refs_0_, f32[18,8,128]{2,1,0:T(8,128)S(1)} %collective-permute-done.15.refs_1_, f32[18,8,128]{2,1,0:T(8,128)S(1)} %collective-permute-done.16.refs_2_, f32[18,8,128]{2,1,0:T(8,128)S(1)} %collective-permute-done.17.refs_3_, ...), custom_call_target="tpu_custom_call" | custom-call | tf_op jit(solution)/shard_map/pallas_call | solution.py:781
  (1 shorter events, 0.0 us)
Async XLA Ops:
  3.2 7.2 %collective-permute-start.6 = (f32[24,8,128]{2,1,0:T(8,128)S(1)}, f32[24,8,128]{2,1,0:T(8,128)S(1)}, u32[]{:S(2)}, u32[]{:S(2)}) collective-permute-start(f32[24,8,128]{2,1,0:T(8,128)S(1)} %get-tuple-element.28), channel_id=1, source_target_pairs={{0,6},{1,7},{2,4},{3,5},{4,2},{5,3},{6,0},{7,1},{8,14},{9,15},{10,... | collective-permute-start | bytes 294920 | tf_op jit(solution)/shard_map/ppermute | solution.py:820
  7.2 6.0 %collective-permute-start.5 = (f32[24,8,128]{2,1,0:T(8,128)S(1)}, f32[24,8,128]{2,1,0:T(8,128)S(1)}, u32[]{:S(2)}, u32[]{:S(2)}) collective-permute-start(f32[24,8,128]{2,1,0:T(8,128)S(1)} %get-tuple-element.29), channel_id=1, source_target_pairs={{0,7},{1,6},{2,5},{3,4},{4,3},{5,2},{6,1},{7,0},{8,15},{9,14},{10,... | collective-permute-start | bytes 294920 | tf_op jit(solution)/shard_map/ppermute | solution.py:820
  7.2 7.5 %collective-permute-start.4 = (f32[24,8,128]{2,1,0:T(8,128)S(1)}, f32[24,8,128]{2,1,0:T(8,128)S(1)}, u32[]{:S(2)}, u32[]{:S(2)}) collective-permute-start(f32[24,8,128]{2,1,0:T(8,128)S(1)} %get-tuple-element.30), channel_id=1, source_target_pairs={{0,2},{1,3},{2,0},{3,1},{4,6},{5,7},{6,4},{7,5},{8,10},{9,11},{10,... | collective-permute-start | bytes 294920 | tf_op jit(solution)/shard_map/ppermute | solution.py:820
  8.3 6.7 %collective-permute-start.3 = (f32[24,8,128]{2,1,0:T(8,128)S(1)}, f32[24,8,128]{2,1,0:T(8,128)S(1)}, u32[]{:S(2)}, u32[]{:S(2)}) collective-permute-start(f32[24,8,128]{2,1,0:T(8,128)S(1)} %get-tuple-element.31), channel_id=1, source_target_pairs={{0,4},{1,5},{2,6},{3,7},{4,0},{5,1},{6,2},{7,3},{8,12},{9,13},{10,... | collective-permute-start | bytes 294920 | tf_op jit(solution)/shard_map/ppermute | solution.py:820
  9.8 6.6 %collective-permute-start.2 = (f32[24,8,128]{2,1,0:T(8,128)S(1)}, f32[24,8,128]{2,1,0:T(8,128)S(1)}, u32[]{:S(2)}, u32[]{:S(2)}) collective-permute-start(f32[24,8,128]{2,1,0:T(8,128)S(1)} %get-tuple-element.32), channel_id=1, source_target_pairs={{0,3},{1,2},{2,1},{3,0},{4,7},{5,6},{6,5},{7,4},{8,11},{9,10},{10,... | collective-permute-start | bytes 294920 | tf_op jit(solution)/shard_map/ppermute | solution.py:820
  10.4 6.7 %collective-permute-start.1 = (f32[24,8,128]{2,1,0:T(8,128)S(1)}, f32[24,8,128]{2,1,0:T(8,128)S(1)}, u32[]{:S(2)}, u32[]{:S(2)}) collective-permute-start(f32[24,8,128]{2,1,0:T(8,128)S(1)} %get-tuple-element.33), channel_id=1, source_target_pairs={{0,5},{1,4},{2,7},{3,6},{4,1},{5,0},{6,3},{7,2},{8,13},{9,12},{10,... | collective-permute-start | bytes 294920 | tf_op jit(solution)/shard_map/ppermute | solution.py:820
  13.2 3.9 %collective-permute-start = (f32[24,8,128]{2,1,0:T(8,128)S(1)}, f32[24,8,128]{2,1,0:T(8,128)S(1)}, u32[]{:S(2)}, u32[]{:S(2)}) collective-permute-start(f32[24,8,128]{2,1,0:T(8,128)S(1)} %get-tuple-element.34), channel_id=1, source_target_pairs={{0,1},{1,0},{2,3},{3,2},{4,5},{5,4},{6,7},{7,6},{8,9},{9,8},{10,11... | collective-permute-start | bytes 294920 | tf_op jit(solution)/shard_map/ppermute | solution.py:820
  17.6 8.0 %collective-permute-start.7 = (f32[4,16,8,128]{3,2,1,0:T(8,128)S(1)}, f32[4,16,8,128]{3,2,1,0:T(8,128)S(1)}, u32[]{:S(2)}, u32[]{:S(2)}) collective-permute-start(f32[4,16,8,128]{3,2,1,0:T(8,128)S(1)} %get-tuple-element.16), channel_id=1, source_target_pairs={{25,0},{0,1},{1,2},{2,3},{3,7},{7,6},{6,5},{5,4},{4,13},{13,12},{1... | collective-permute-start | bytes 786440 | tf_op jit(solution)/shard_map/ppermute | solution.py:811
  17.8 8.8 %collective-permute-start.8 = (f32[4,16,8,128]{3,2,1,0:T(8,128)S(1)}, f32[4,16,8,128]{3,2,1,0:T(8,128)S(1)}, u32[]{:S(2)}, u32[]{:S(2)}) collective-permute-start(f32[4,16,8,128]{3,2,1,0:T(8,128)S(1)} %get-tuple-element.17), channel_id=1, source_target_pairs={{0,25},{1,0},{2,1},{3,2},{7,3},{6,7},{5,6},{4,5},{13,4},{12,13},{8... | collective-permute-start | bytes 786440 | tf_op jit(solution)/shard_map/ppermute | solution.py:812
  21.2 6.4 %collective-permute-start.9 = (f32[8,2,8,128]{3,2,1,0:T(8,128)S(1)}, f32[8,2,8,128]{3,2,1,0:T(8,128)S(1)}, u32[]{:S(2)}, u32[]{:S(2)}) collective-permute-start(f32[8,2,8,128]{3,2,1,0:T(8,128)S(1)} %get-tuple-element.19), channel_id=1, source_target_pairs={{0,8},{8,0},{16,24},{24,16},{1,9},{9,1},{17,25},{25,17},{2,10},{10... | collective-permute-start | bytes 196616 | tf_op jit(solution)/shard_map/ppermute | solution.py:826
  21.3 8.7 %collective-permute-start.10 = (f32[8,2,8,128]{3,2,1,0:T(8,128)S(1)}, f32[8,2,8,128]{3,2,1,0:T(8,128)S(1)}, u32[]{:S(2)}, u32[]{:S(2)}) collective-permute-start(f32[8,2,8,128]{3,2,1,0:T(8,128)S(1)} %get-tuple-element.20), channel_id=1, source_target_pairs={{0,16},{8,24},{16,0},{24,8},{1,17},{9,25},{17,1},{25,9},{2,18},{10... | collective-permute-start | bytes 196616 | tf_op jit(solution)/shard_map/ppermute | solution.py:826
  23.8 6.1 %collective-permute-start.11 = (f32[8,2,8,128]{3,2,1,0:T(8,128)S(1)}, f32[8,2,8,128]{3,2,1,0:T(8,128)S(1)}, u32[]{:S(2)}, u32[]{:S(2)}) collective-permute-start(f32[8,2,8,128]{3,2,1,0:T(8,128)S(1)} %get-tuple-element.21), channel_id=1, source_target_pairs={{0,24},{8,16},{16,8},{24,0},{1,25},{9,17},{17,9},{25,1},{2,26},{10... | collective-permute-start | bytes 196616 | tf_op jit(solution)/shard_map/ppermute | solution.py:826
  38.6 10.8 %collective-permute-start.12 = (f32[8,8,128]{2,1,0:T(8,128)S(1)}, f32[8,8,128]{2,1,0:T(8,128)S(1)}, u32[]{:S(2)}, u32[]{:S(2)}) collective-permute-start(f32[8,8,128]{2,1,0:T(8,128)S(1)} %get-tuple-element.25), channel_id=1, source_target_pairs={{0,8},{8,0},{16,24},{24,16},{1,9},{9,1},{17,25},{25,17},{2,10},{10... | collective-permute-start | bytes 98312 | tf_op jit(solution)/shard_map/ppermute | solution.py:826
  40.2 9.2 %collective-permute-start.13 = (f32[8,8,128]{2,1,0:T(8,128)S(1)}, f32[8,8,128]{2,1,0:T(8,128)S(1)}, u32[]{:S(2)}, u32[]{:S(2)}) collective-permute-start(f32[8,8,128]{2,1,0:T(8,128)S(1)} %get-tuple-element.26), channel_id=1, source_target_pairs={{0,16},{8,24},{16,0},{24,8},{1,17},{9,25},{17,1},{25,9},{2,18},{10... | collective-permute-start | bytes 98312 | tf_op jit(solution)/shard_map/ppermute | solution.py:826
  42.9 6.6 %collective-permute-start.14 = (f32[8,8,128]{2,1,0:T(8,128)S(1)}, f32[8,8,128]{2,1,0:T(8,128)S(1)}, u32[]{:S(2)}, u32[]{:S(2)}) collective-permute-start(f32[8,8,128]{2,1,0:T(8,128)S(1)} %get-tuple-element.27), channel_id=1, source_target_pairs={{0,24},{8,16},{16,8},{24,0},{1,25},{9,17},{17,9},{25,1},{2,26},{10... | collective-permute-start | bytes 98312 | tf_op jit(solution)/shard_map/ppermute | solution.py:826
  49.6 6.1 %collective-permute-start.21 = (f32[18,8,128]{2,1,0:T(8,128)S(1)}, f32[18,8,128]{2,1,0:T(8,128)S(1)}, u32[]{:S(2)}, u32[]{:S(2)}) collective-permute-start(f32[18,8,128]{2,1,0:T(8,128)S(1)} %get-tuple-element.36), channel_id=1, source_target_pairs={{0,6},{1,7},{2,4},{3,5},{4,2},{5,3},{6,0},{7,1},{8,14},{9,15},{10,... | collective-permute-start | bytes 221192 | tf_op jit(solution)/shard_map/ppermute | solution.py:820
  50.2 5.6 %collective-permute-start.20 = (f32[18,8,128]{2,1,0:T(8,128)S(1)}, f32[18,8,128]{2,1,0:T(8,128)S(1)}, u32[]{:S(2)}, u32[]{:S(2)}) collective-permute-start(f32[18,8,128]{2,1,0:T(8,128)S(1)} %get-tuple-element.37), channel_id=1, source_target_pairs={{0,7},{1,6},{2,5},{3,4},{4,3},{5,2},{6,1},{7,0},{8,15},{9,14},{10,... | collective-permute-start | bytes 221192 | tf_op jit(solution)/shard_map/ppermute | solution.py:820
  50.4 6.7 %collective-permute-start.19 = (f32[18,8,128]{2,1,0:T(8,128)S(1)}, f32[18,8,128]{2,1,0:T(8,128)S(1)}, u32[]{:S(2)}, u32[]{:S(2)}) collective-permute-start(f32[18,8,128]{2,1,0:T(8,128)S(1)} %get-tuple-element.38), channel_id=1, source_target_pairs={{0,2},{1,3},{2,0},{3,1},{4,6},{5,7},{6,4},{7,5},{8,10},{9,11},{10,... | collective-permute-start | bytes 221192 | tf_op jit(solution)/shard_map/ppermute | solution.py:820
  51.2 6.3 %collective-permute-start.18 = (f32[18,8,128]{2,1,0:T(8,128)S(1)}, f32[18,8,128]{2,1,0:T(8,128)S(1)}, u32[]{:S(2)}, u32[]{:S(2)}) collective-permute-start(f32[18,8,128]{2,1,0:T(8,128)S(1)} %get-tuple-element.39), channel_id=1, source_target_pairs={{0,4},{1,5},{2,6},{3,7},{4,0},{5,1},{6,2},{7,3},{8,12},{9,13},{10,... | collective-permute-start | bytes 221192 | tf_op jit(solution)/shard_map/ppermute | solution.py:820
  53.4 4.2 %collective-permute-start.17 = (f32[18,8,128]{2,1,0:T(8,128)S(1)}, f32[18,8,128]{2,1,0:T(8,128)S(1)}, u32[]{:S(2)}, u32[]{:S(2)}) collective-permute-start(f32[18,8,128]{2,1,0:T(8,128)S(1)} %get-tuple-element.40), channel_id=1, source_target_pairs={{0,3},{1,2},{2,1},{3,0},{4,7},{5,6},{6,5},{7,4},{8,11},{9,10},{10,... | collective-permute-start | bytes 221192 | tf_op jit(solution)/shard_map/ppermute | solution.py:820
  55.7 3.9 %collective-permute-start.16 = (f32[18,8,128]{2,1,0:T(8,128)S(1)}, f32[18,8,128]{2,1,0:T(8,128)S(1)}, u32[]{:S(2)}, u32[]{:S(2)}) collective-permute-start(f32[18,8,128]{2,1,0:T(8,128)S(1)} %get-tuple-element.41), channel_id=1, source_target_pairs={{0,5},{1,4},{2,7},{3,6},{4,1},{5,0},{6,3},{7,2},{8,13},{9,12},{10,... | collective-permute-start | bytes 221192 | tf_op jit(solution)/shard_map/ppermute | solution.py:820
  55.7 3.9 %collective-permute-start.15 = (f32[18,8,128]{2,1,0:T(8,128)S(1)}, f32[18,8,128]{2,1,0:T(8,128)S(1)}, u32[]{:S(2)}, u32[]{:S(2)}) collective-permute-start(f32[18,8,128]{2,1,0:T(8,128)S(1)} %get-tuple-element.42), channel_id=1, source_target_pairs={{0,1},{1,0},{2,3},{3,2},{4,5},{5,4},{6,7},{7,6},{8,9},{9,8},{10,11... | collective-permute-start | bytes 221192 | tf_op jit(solution)/shard_map/ppermute | solution.py:820

commit v7 on v6

--- a/solution.py
+++ b/solution.py
@@ -629,6 +629,20 @@
     lax.fori_loop(0, slab.sub, one, 0, unroll=unroll)
 
 
+def one_ahead(slab, arrive, collide, held):
+    def bring(tile):
+        for number, value in enumerate(arrive(tile)):
+            held[number] = value
+
+    def body(tile):
+        values = [held[number] for number in range(held.shape[0])]
+        bring(lax.rem(tile + 1, slab.sub))
+        collide(tile, values)
+
+    bring(jnp.int32(0))
+    over_tiles(slab, body)
+
+
 def over_steps(count, body):
     def one(number, _):
         body(number)
@@ -640,9 +654,9 @@
 def first_window(slab, rates_hbm, state, *refs):
     heat_parts, refs = refs[: slab.grp], refs[slab.grp :]
     flow_out, keep_out, heat_outs = refs[0], refs[1], refs[2 : 2 + slab.grp]
-    (rates_ref, sem, speed, heat_tiles, flow_post, heat_post, heat_a, heat_b, held, came_heat) = refs[
-        2 + slab.grp :
-    ]
+    (rates_ref, sem, speed, heat_tiles, flow_post, heat_post, heat_a, heat_b, held, came_heat, ahead) = (
+        refs[2 + slab.grp :]
+    )
     rates_copy = pltpu.make_async_copy(rates_hbm, rates_ref, sem)
     rates_copy.start()
     make_heat_tiles(slab, heat_parts, came_heat, heat_tiles)
@@ -665,25 +679,27 @@
 
     over_tiles(slab, begin)
 
+    def arrive(tile, source):
+        flow = stream_flow(slab, flow_post.at[source], tile)
+        return flow + stream(slab, heat_post.at[source], tile, HEAT_OFFSETS)
+
     def step(number):
         source = lax.rem(number, 2)
 
-        def go_on(tile):
-            flow = stream_flow(slab, flow_post.at[source], tile)
+        def go_on(tile, values):
+            flow, heat = values[:27], values[27:]
             solid = state[SOLID_AT, tile] != 0.0
             collide_flow(rates_ref, flow, keep_out[0, tile], solid, flow_post.at[1 - source], tile)
-            heat = stream(slab, heat_post.at[source], tile, HEAT_OFFSETS)
             omega = heat_tiles[7, tile]
             collide_heat(heat, omega, speeds_of(tile), heat_post.at[1 - source], tile)
 
-        over_tiles(slab, go_on)
+        one_ahead(slab, lambda tile: arrive(tile, source), go_on, ahead)
 
     over_steps(STEPS - 1, step)
     source = (STEPS - 1) % 2
 
-    def next_window(tile):
-        flow = stream_flow(slab, flow_post.at[source], tile)
-        heat = stream(slab, heat_post.at[source], tile, HEAT_OFFSETS)
+    def next_window(tile, values):
+        flow, heat = values[:27], values[27:]
         solid = state[SOLID_AT, tile] != 0.0
         speeds = [
             jnp.where(solid, 0.0, each) for each in flow_speed_tile(flow, keep_out[0, tile])
@@ -695,7 +711,7 @@
         collide_flow(rates_ref, flow, force, solid, flow_out, tile)
         collide_heat(heat, heat_tiles[7, tile], speeds, heat_a, tile)
 
-    over_tiles(slab, next_window)
+    one_ahead(slab, lambda tile: arrive(tile, source), next_window, ahead)
     here, there = heat_a, heat_b
     for _ in range(STEPS - 1):
 
@@ -719,7 +735,7 @@
         heat_outs[step_number][...] = held[jnp.bitwise_xor(mine, step_number)]
 
 
-def last_window(slab, rates_hbm, came, flow_in, keep_ref, sent, rates_ref, sem, flow_post):
+def last_window(slab, rates_hbm, came, flow_in, keep_ref, sent, rates_ref, sem, flow_post, ahead):
     rates_copy = pltpu.make_async_copy(rates_hbm, rates_ref, sem)
     rates_copy.start()
 
@@ -733,12 +749,11 @@
     def step(number):
         source = lax.rem(number, 2)
 
-        def go_on(tile):
-            flow = stream_flow(slab, flow_post.at[source], tile)
+        def go_on(tile, flow):
             solid = keep_ref[1, tile] != 0.0
             collide_flow(rates_ref, flow, keep_ref[0, tile], solid, flow_post.at[1 - source], tile)
 
-        over_tiles(slab, go_on)
+        one_ahead(slab, lambda tile: stream_flow(slab, flow_post.at[source], tile), go_on, ahead)
 
     over_steps(STEPS - 1, step)
 
@@ -871,7 +886,7 @@
         scalars
         + [(3,) + plane, (8,) + plane, (2, 27) + plane, (2, 7) + plane]
         + [(7,) + plane] * 2
-        + [(slab.grp,) + plane, (slab.grp,) + heat_shape],
+        + [(slab.grp,) + plane, (slab.grp,) + heat_shape, (34,) + tile],
         in_hbm=1,
     )
     parts = across_planes(slab, parts)
@@ -881,7 +896,7 @@
         slab,
         [rates, came, flow, keep],
         [last_shape],
-        scalars + [(2, 27) + plane],
+        scalars + [(2, 27) + plane, (27,) + tile],
         in_hbm=1,
     )
     (sent,) = local_call(

time: 62.1 us -> 61.1 us (0.984)
  Pallas kernels: 20.8 us -> 19.8 us
    pallas_call x7, Pallas kernels: 20.8 us -> 19.8 us  [local_call(): pl.pallas_call(kernel, out_shape=[jax.ShapeDtypeStruct(shape, F32) for sh...]
  transfers between devices with their start and end apart: 22 -> 22, of which waited for: 11 -> 11; matrix products, arithmetic and copies ran while one was open for 0% -> 0% of each run, Pallas kernels for 11% -> 10%
where the time goes in v7:
time: 61.1 us; the launch traced here: 60.9 us
  starting transfers between devices  26.6 us (44%)
  Pallas kernels  19.8 us (32%)
  waiting for transfers between devices  13.7 us (22%)
  between operations  0.73 us (1%)
    pallas_call x7, Pallas kernels, local_call(): pl.pallas_call(kernel, out_shape=[jax.ShapeDtypeStruct(shape, F32) for sh...  19.8 us
    ppermute x14, starting transfers between devices, across_plane(): came[step] = lax.ppermute(sent[step], ('gx', 'gy'), pairs)  13.6 us
    ppermute x14, waiting for transfers between devices, across_plane(): came[step] = lax.ppermute(sent[step], ('gx', 'gy'), pairs)  10.3 us
    ppermute x6, starting transfers between devices, across_planes(): lax.ppermute(parts[step], 'grp', [(i, i ^ step) for i in range(slab.grp)])  9.39 us
    ppermute x1, starting transfers between devices, exchange(): from_above = lax.ppermute(low, RING, [(b, a) for a, b in upward])  3.43 us
    ppermute x6, waiting for transfers between devices, across_planes(): lax.ppermute(parts[step], 'grp', [(i, i ^ step) for i in range(slab.grp)])  2.46 us
  transfers between devices with their start and end apart: 22, of which 11 were waited for; matrix products, arithmetic and copies ran while one was open for 0% of the time, Pallas kernels for 10%

profile of v7, /device:TPU:0, one launch (start us, length us, event | category | flops | bytes accessed | tf_op | source)
XLA Modules:
  0.0 60.9 jit_solution(5317454047114361463)
XLA Ops:
  0.6 2.5 %shard_map.86 = f32[8,24,8,128]{3,2,1,0:T(8,128)S(1)} custom-call(f32[4]{0:T(128)} %refs_0_.3, f32[27,4,8,128]{3,2,1,0:T(8,128)} %refs_1_.1, f32[3,4,8,128]{3,2,1,0:T(8,128)} %refs_2_.1, s32[4,8,128]{2,1,0:T(8,128)} %refs_3_.1, f32[7,1,8,512]{3,2,1,0:T(8,128)} %refs_4_.1, s32[1,8,512]{2,1,0:T(8,128)} %refs_5_.1), custom_call_target="tpu_custom_call" | custom-call | tf_op jit(solution)/shard_map/pallas_call | solution.py:796
  3.2 0.1 slice_bitcast_fusion
  3.2 4.0 %collective-permute-start.6 = (f32[24,8,128]{2,1,0:T(8,128)S(1)}, f32[24,8,128]{2,1,0:T(8,128)S(1)}, u32[]{:S(2)}, u32[]{:S(2)}) collective-permute-start(f32[24,8,128]{2,1,0:T(8,128)S(1)} %get-tuple-element.28), channel_id=1, source_target_pairs={{0,6},{1,7},{2,4},{3,5},{4,2},{5,3},{6,0},{7,1},{8,14},{9,15},{10,... | collective-permute-start | bytes 294920 | tf_op jit(solution)/shard_map/ppermute | solution.py:835
  7.2 0.0 collective-permute-start.5
  7.2 1.1 %collective-permute-start.4 = (f32[24,8,128]{2,1,0:T(8,128)S(1)}, f32[24,8,128]{2,1,0:T(8,128)S(1)}, u32[]{:S(2)}, u32[]{:S(2)}) collective-permute-start(f32[24,8,128]{2,1,0:T(8,128)S(1)} %get-tuple-element.30), channel_id=1, source_target_pairs={{0,2},{1,3},{2,0},{3,1},{4,6},{5,7},{6,4},{7,5},{8,10},{9,11},{10,... | collective-permute-start | bytes 294920 | tf_op jit(solution)/shard_map/ppermute | solution.py:835
  8.3 1.5 %collective-permute-start.3 = (f32[24,8,128]{2,1,0:T(8,128)S(1)}, f32[24,8,128]{2,1,0:T(8,128)S(1)}, u32[]{:S(2)}, u32[]{:S(2)}) collective-permute-start(f32[24,8,128]{2,1,0:T(8,128)S(1)} %get-tuple-element.31), channel_id=1, source_target_pairs={{0,4},{1,5},{2,6},{3,7},{4,0},{5,1},{6,2},{7,3},{8,12},{9,13},{10,... | collective-permute-start | bytes 294920 | tf_op jit(solution)/shard_map/ppermute | solution.py:835
  9.8 0.6 collective-permute-start.2
  10.4 0.0 collective-permute-done.6.refs_7_
  10.4 0.6 collective-permute-start.1
  11.0 2.2 %collective-permute-done.5.refs_6_ = f32[24,8,128]{2,1,0:T(8,128)S(1)} collective-permute-done((f32[24,8,128]{2,1,0:T(8,128)S(1)}, f32[24,8,128]{2,1,0:T(8,128)S(1)}, u32[]{:S(2)}, u32[]{:S(2)}) %collective-permute-start.5) | collective-permute-done | bytes 98336 | tf_op jit(solution)/shard_map/ppermute | solution.py:835
  13.2 0.0 collective-permute-start
  13.2 1.6 %collective-permute-done.4.refs_5_ = f32[24,8,128]{2,1,0:T(8,128)S(1)} collective-permute-done((f32[24,8,128]{2,1,0:T(8,128)S(1)}, f32[24,8,128]{2,1,0:T(8,128)S(1)}, u32[]{:S(2)}, u32[]{:S(2)}) %collective-permute-start.4) | collective-permute-done | bytes 98336 | tf_op jit(solution)/shard_map/ppermute | solution.py:835
  14.7 0.3 collective-permute-done.3.refs_4_
  15.0 1.4 %collective-permute-done.2.refs_3_ = f32[24,8,128]{2,1,0:T(8,128)S(1)} collective-permute-done((f32[24,8,128]{2,1,0:T(8,128)S(1)}, f32[24,8,128]{2,1,0:T(8,128)S(1)}, u32[]{:S(2)}, u32[]{:S(2)}) %collective-permute-start.2) | collective-permute-done | bytes 98336 | tf_op jit(solution)/shard_map/ppermute | solution.py:835
  16.4 0.7 %collective-permute-done.1.refs_2_ = f32[24,8,128]{2,1,0:T(8,128)S(1)} collective-permute-done((f32[24,8,128]{2,1,0:T(8,128)S(1)}, f32[24,8,128]{2,1,0:T(8,128)S(1)}, u32[]{:S(2)}, u32[]{:S(2)}) %collective-permute-start.1) | collective-permute-done | bytes 98336 | tf_op jit(solution)/shard_map/ppermute | solution.py:835
  17.1 0.0 collective-permute-done.refs_1_
  17.1 0.5 shard_map.87
  17.6 0.2 collective-permute-start.7
  17.8 3.4 %collective-permute-start.8 = (f32[4,16,8,128]{3,2,1,0:T(8,128)S(1)}, f32[4,16,8,128]{3,2,1,0:T(8,128)S(1)}, u32[]{:S(2)}, u32[]{:S(2)}) collective-permute-start(f32[4,16,8,128]{3,2,1,0:T(8,128)S(1)} %get-tuple-element.17), channel_id=1, source_target_pairs={{0,25},{1,0},{2,1},{3,2},{7,3},{6,7},{5,6},{4,5},{13,4},{12,13},{8... | collective-permute-start | bytes 786440 | tf_op jit(solution)/shard_map/ppermute | solution.py:827
  21.2 0.1 collective-permute-start.9
  21.3 2.6 %collective-permute-start.10 = (f32[8,2,8,128]{3,2,1,0:T(8,128)S(1)}, f32[8,2,8,128]{3,2,1,0:T(8,128)S(1)}, u32[]{:S(2)}, u32[]{:S(2)}) collective-permute-start(f32[8,2,8,128]{3,2,1,0:T(8,128)S(1)} %get-tuple-element.20), channel_id=1, source_target_pairs={{0,16},{8,24},{16,0},{24,8},{1,17},{9,25},{17,1},{25,9},{2,18},{10... | collective-permute-start | bytes 196616 | tf_op jit(solution)/shard_map/ppermute | solution.py:841
  23.8 1.7 %collective-permute-start.11 = (f32[8,2,8,128]{3,2,1,0:T(8,128)S(1)}, f32[8,2,8,128]{3,2,1,0:T(8,128)S(1)}, u32[]{:S(2)}, u32[]{:S(2)}) collective-permute-start(f32[8,2,8,128]{3,2,1,0:T(8,128)S(1)} %get-tuple-element.21), channel_id=1, source_target_pairs={{0,24},{8,16},{16,8},{24,0},{1,25},{9,17},{17,9},{25,1},{2,26},{10... | collective-permute-start | bytes 196616 | tf_op jit(solution)/shard_map/ppermute | solution.py:841
  25.6 0.0 collective-permute-done.7.refs_1_
  25.6 1.0 %collective-permute-done.8.refs_2_ = f32[4,16,8,128]{3,2,1,0:T(8,128)S(1)} collective-permute-done((f32[4,16,8,128]{3,2,1,0:T(8,128)S(1)}, f32[4,16,8,128]{3,2,1,0:T(8,128)S(1)}, u32[]{:S(2)}, u32[]{:S(2)}) %collective-permute-start.8) | collective-permute-done | bytes 262176 | tf_op jit(solution)/shard_map/ppermute | solution.py:827
  26.6 1.0 %shard_map.88.refs_1_ = f32[32,8,8,128]{3,2,1,0:T(8,128)S(1)} custom-call(f32[8,24,8,128]{3,2,1,0:T(8,128)S(1)} %get-tuple-element.15.refs_0_.refs_1_, f32[4,16,8,128]{3,2,1,0:T(8,128)S(1)} %collective-permute-done.7.refs_1_, f32[4,16,8,128]{3,2,1,0:T(8,128)S(1)} %collective-permute-done.8.refs_2_), custom_call_target="tpu_custom_call" | custom-call | tf_op jit(solution)/shard_map/pallas_call | solution.py:796
  27.5 0.0 collective-permute-done.9.refs_3_
  27.5 2.4 %collective-permute-done.10.refs_4_ = f32[8,2,8,128]{3,2,1,0:T(8,128)S(1)} collective-permute-done((f32[8,2,8,128]{3,2,1,0:T(8,128)S(1)}, f32[8,2,8,128]{3,2,1,0:T(8,128)S(1)}, u32[]{:S(2)}, u32[]{:S(2)}) %collective-permute-start.10) | collective-permute-done | bytes 65568 | tf_op jit(solution)/shard_map/ppermute | solution.py:841
  30.0 0.0 collective-permute-done.11.refs_5_
  30.0 8.1 %shard_map.89 = (f32[27,8,8,128]{3,2,1,0:T(8,128)S(1)}, f32[2,8,8,128]{3,2,1,0:T(8,128)S(1)}, f32[8,8,128]{2,1,0:T(8,128)S(1)}, f32[8,8,128]{2,1,0:T(8,128)S(1)}...) custom-call(f32[27]{0:T(128)} %refs_0_.5, f32[32,8,8,128]{3,2,1,0:T(8,128)S(1)} %shard_map.88.refs_1_, ...), custom_call_target="tpu_custom_call" | custom-call | tf_op jit(solution)/shard_map/pallas_call | solution.py:796
  38.1 1.6 %collective-permute-start.12 = (f32[8,8,128]{2,1,0:T(8,128)S(1)}, f32[8,8,128]{2,1,0:T(8,128)S(1)}, u32[]{:S(2)}, u32[]{:S(2)}) collective-permute-start(f32[8,8,128]{2,1,0:T(8,128)S(1)} %get-tuple-element.25), channel_id=1, source_target_pairs={{0,8},{8,0},{16,24},{24,16},{1,9},{9,1},{17,25},{25,17},{2,10},{10... | collective-permute-start | bytes 98312 | tf_op jit(solution)/shard_map/ppermute | solution.py:841
  39.8 2.7 %collective-permute-start.13 = (f32[8,8,128]{2,1,0:T(8,128)S(1)}, f32[8,8,128]{2,1,0:T(8,128)S(1)}, u32[]{:S(2)}, u32[]{:S(2)}) collective-permute-start(f32[8,8,128]{2,1,0:T(8,128)S(1)} %get-tuple-element.26), channel_id=1, source_target_pairs={{0,16},{8,24},{16,0},{24,8},{1,17},{9,25},{17,1},{25,9},{2,18},{10... | collective-permute-start | bytes 98312 | tf_op jit(solution)/shard_map/ppermute | solution.py:841
  42.5 0.7 %collective-permute-start.14 = (f32[8,8,128]{2,1,0:T(8,128)S(1)}, f32[8,8,128]{2,1,0:T(8,128)S(1)}, u32[]{:S(2)}, u32[]{:S(2)}) collective-permute-start(f32[8,8,128]{2,1,0:T(8,128)S(1)} %get-tuple-element.27), channel_id=1, source_target_pairs={{0,24},{8,16},{16,8},{24,0},{1,25},{9,17},{17,9},{25,1},{2,26},{10... | collective-permute-start | bytes 98312 | tf_op jit(solution)/shard_map/ppermute | solution.py:841
  43.1 5.3 %shard_map.90.refs_0_ = f32[8,18,8,128]{3,2,1,0:T(8,128)S(1)} custom-call(f32[27]{0:T(128)} %refs_0_.5, f32[8,24,8,128]{3,2,1,0:T(8,128)S(1)} %get-tuple-element.15.refs_0_.refs_1_, f32[27,8,8,128]{3,2,1,0:T(8,128)S(1)} %get-tuple-element.22.refs_2_, f32[2,8,8,128]{3,2,1,0:T(8,128)S(1)} %get-tuple-element.23.refs_3_), custom_call_target="tpu_custom_call" | custom-call | tf_op jit(solution)/shard_map/pallas_call | solution.py:796
  48.4 0.0 collective-permute-done.12.refs_2_
  48.4 0.0 collective-permute-done.13.refs_3_
  48.4 0.0 collective-permute-done.14.refs_4_
  48.4 0.1 shard_map.91
  48.6 0.6 collective-permute-start.21
  49.1 0.2 collective-permute-start.20
  49.4 0.8 %collective-permute-start.19 = (f32[18,8,128]{2,1,0:T(8,128)S(1)}, f32[18,8,128]{2,1,0:T(8,128)S(1)}, u32[]{:S(2)}, u32[]{:S(2)}) collective-permute-start(f32[18,8,128]{2,1,0:T(8,128)S(1)} %get-tuple-element.38), channel_id=1, source_target_pairs={{0,2},{1,3},{2,0},{3,1},{4,6},{5,7},{6,4},{7,5},{8,10},{9,11},{10,... | collective-permute-start | bytes 221192 | tf_op jit(solution)/shard_map/ppermute | solution.py:835
  50.2 2.2 %collective-permute-start.18 = (f32[18,8,128]{2,1,0:T(8,128)S(1)}, f32[18,8,128]{2,1,0:T(8,128)S(1)}, u32[]{:S(2)}, u32[]{:S(2)}) collective-permute-start(f32[18,8,128]{2,1,0:T(8,128)S(1)} %get-tuple-element.39), channel_id=1, source_target_pairs={{0,4},{1,5},{2,6},{3,7},{4,0},{5,1},{6,2},{7,3},{8,12},{9,13},{10,... | collective-permute-start | bytes 221192 | tf_op jit(solution)/shard_map/ppermute | solution.py:835
  52.4 0.6 %collective-permute-start.17 = (f32[18,8,128]{2,1,0:T(8,128)S(1)}, f32[18,8,128]{2,1,0:T(8,128)S(1)}, u32[]{:S(2)}, u32[]{:S(2)}) collective-permute-start(f32[18,8,128]{2,1,0:T(8,128)S(1)} %get-tuple-element.40), channel_id=1, source_target_pairs={{0,3},{1,2},{2,1},{3,0},{4,7},{5,6},{6,5},{7,4},{8,11},{9,10},{10,... | collective-permute-start | bytes 221192 | tf_op jit(solution)/shard_map/ppermute | solution.py:835
  53.0 1.6 %collective-permute-done.21.refs_7_ = f32[18,8,128]{2,1,0:T(8,128)S(1)} collective-permute-done((f32[18,8,128]{2,1,0:T(8,128)S(1)}, f32[18,8,128]{2,1,0:T(8,128)S(1)}, u32[]{:S(2)}, u32[]{:S(2)}) %collective-permute-start.21) | collective-permute-done | bytes 73760 | tf_op jit(solution)/shard_map/ppermute | solution.py:835
  54.7 0.0 collective-permute-start.16
  54.7 0.0 collective-permute-done.20.refs_6_
  54.7 1.4 %collective-permute-start.15 = (f32[18,8,128]{2,1,0:T(8,128)S(1)}, f32[18,8,128]{2,1,0:T(8,128)S(1)}, u32[]{:S(2)}, u32[]{:S(2)}) collective-permute-start(f32[18,8,128]{2,1,0:T(8,128)S(1)} %get-tuple-element.42), channel_id=1, source_target_pairs={{0,1},{1,0},{2,3},{3,2},{4,5},{5,4},{6,7},{7,6},{8,9},{9,8},{10,11... | collective-permute-start | bytes 221192 | tf_op jit(solution)/shard_map/ppermute | solution.py:835
  56.1 0.0 collective-permute-done.19.refs_5_
  56.1 0.4 collective-permute-done.18.refs_4_
  56.5 0.1 collective-permute-done.17.refs_3_
  56.6 2.0 %collective-permute-done.16.refs_2_ = f32[18,8,128]{2,1,0:T(8,128)S(1)} collective-permute-done((f32[18,8,128]{2,1,0:T(8,128)S(1)}, f32[18,8,128]{2,1,0:T(8,128)S(1)}, u32[]{:S(2)}, u32[]{:S(2)}) %collective-permute-start.16) | collective-permute-done | bytes 73760 | tf_op jit(solution)/shard_map/ppermute | solution.py:835
  58.5 0.0 collective-permute-done.15.refs_1_
  58.5 2.3 %shard_map.92 = (f32[27,4,8,128]{3,2,1,0:T(8,128)}, f32[7,1,8,512]{3,2,1,0:T(8,128)}) custom-call(f32[18,8,128]{2,1,0:T(8,128)S(1)} %get-tuple-element.43.refs_0_, f32[18,8,128]{2,1,0:T(8,128)S(1)} %collective-permute-done.15.refs_1_, f32[18,8,128]{2,1,0:T(8,128)S(1)} %collective-permute-done.16.refs_2_, f32[18,8,128]{2,1,0:T(8,128)S(1)} %collective-permute-done.17.refs_3_, ...), custom_call_target="tpu_custom_call" | custom-call | tf_op jit(solution)/shard_map/pallas_call | solution.py:796
  (1 shorter events, 0.0 us)
Async XLA Ops:
  3.2 7.2 %collective-permute-start.6 = (f32[24,8,128]{2,1,0:T(8,128)S(1)}, f32[24,8,128]{2,1,0:T(8,128)S(1)}, u32[]{:S(2)}, u32[]{:S(2)}) collective-permute-start(f32[24,8,128]{2,1,0:T(8,128)S(1)} %get-tuple-element.28), channel_id=1, source_target_pairs={{0,6},{1,7},{2,4},{3,5},{4,2},{5,3},{6,0},{7,1},{8,14},{9,15},{10,... | collective-permute-start | bytes 294920 | tf_op jit(solution)/shard_map/ppermute | solution.py:835
  7.2 6.0 %collective-permute-start.5 = (f32[24,8,128]{2,1,0:T(8,128)S(1)}, f32[24,8,128]{2,1,0:T(8,128)S(1)}, u32[]{:S(2)}, u32[]{:S(2)}) collective-permute-start(f32[24,8,128]{2,1,0:T(8,128)S(1)} %get-tuple-element.29), channel_id=1, source_target_pairs={{0,7},{1,6},{2,5},{3,4},{4,3},{5,2},{6,1},{7,0},{8,15},{9,14},{10,... | collective-permute-start | bytes 294920 | tf_op jit(solution)/shard_map/ppermute | solution.py:835
  7.2 7.5 %collective-permute-start.4 = (f32[24,8,128]{2,1,0:T(8,128)S(1)}, f32[24,8,128]{2,1,0:T(8,128)S(1)}, u32[]{:S(2)}, u32[]{:S(2)}) collective-permute-start(f32[24,8,128]{2,1,0:T(8,128)S(1)} %get-tuple-element.30), channel_id=1, source_target_pairs={{0,2},{1,3},{2,0},{3,1},{4,6},{5,7},{6,4},{7,5},{8,10},{9,11},{10,... | collective-permute-start | bytes 294920 | tf_op jit(solution)/shard_map/ppermute | solution.py:835
  8.3 6.7 %collective-permute-start.3 = (f32[24,8,128]{2,1,0:T(8,128)S(1)}, f32[24,8,128]{2,1,0:T(8,128)S(1)}, u32[]{:S(2)}, u32[]{:S(2)}) collective-permute-start(f32[24,8,128]{2,1,0:T(8,128)S(1)} %get-tuple-element.31), channel_id=1, source_target_pairs={{0,4},{1,5},{2,6},{3,7},{4,0},{5,1},{6,2},{7,3},{8,12},{9,13},{10,... | collective-permute-start | bytes 294920 | tf_op jit(solution)/shard_map/ppermute | solution.py:835
  9.8 6.6 %collective-permute-start.2 = (f32[24,8,128]{2,1,0:T(8,128)S(1)}, f32[24,8,128]{2,1,0:T(8,128)S(1)}, u32[]{:S(2)}, u32[]{:S(2)}) collective-permute-start(f32[24,8,128]{2,1,0:T(8,128)S(1)} %get-tuple-element.32), channel_id=1, source_target_pairs={{0,3},{1,2},{2,1},{3,0},{4,7},{5,6},{6,5},{7,4},{8,11},{9,10},{10,... | collective-permute-start | bytes 294920 | tf_op jit(solution)/shard_map/ppermute | solution.py:835
  10.4 6.7 %collective-permute-start.1 = (f32[24,8,128]{2,1,0:T(8,128)S(1)}, f32[24,8,128]{2,1,0:T(8,128)S(1)}, u32[]{:S(2)}, u32[]{:S(2)}) collective-permute-start(f32[24,8,128]{2,1,0:T(8,128)S(1)} %get-tuple-element.33), channel_id=1, source_target_pairs={{0,5},{1,4},{2,7},{3,6},{4,1},{5,0},{6,3},{7,2},{8,13},{9,12},{10,... | collective-permute-start | bytes 294920 | tf_op jit(solution)/shard_map/ppermute | solution.py:835
  13.2 3.9 %collective-permute-start = (f32[24,8,128]{2,1,0:T(8,128)S(1)}, f32[24,8,128]{2,1,0:T(8,128)S(1)}, u32[]{:S(2)}, u32[]{:S(2)}) collective-permute-start(f32[24,8,128]{2,1,0:T(8,128)S(1)} %get-tuple-element.34), channel_id=1, source_target_pairs={{0,1},{1,0},{2,3},{3,2},{4,5},{5,4},{6,7},{7,6},{8,9},{9,8},{10,11... | collective-permute-start | bytes 294920 | tf_op jit(solution)/shard_map/ppermute | solution.py:835
  17.6 8.0 %collective-permute-start.7 = (f32[4,16,8,128]{3,2,1,0:T(8,128)S(1)}, f32[4,16,8,128]{3,2,1,0:T(8,128)S(1)}, u32[]{:S(2)}, u32[]{:S(2)}) collective-permute-start(f32[4,16,8,128]{3,2,1,0:T(8,128)S(1)} %get-tuple-element.16), channel_id=1, source_target_pairs={{25,0},{0,1},{1,2},{2,3},{3,7},{7,6},{6,5},{5,4},{4,13},{13,12},{1... | collective-permute-start | bytes 786440 | tf_op jit(solution)/shard_map/ppermute | solution.py:826
  17.8 8.8 %collective-permute-start.8 = (f32[4,16,8,128]{3,2,1,0:T(8,128)S(1)}, f32[4,16,8,128]{3,2,1,0:T(8,128)S(1)}, u32[]{:S(2)}, u32[]{:S(2)}) collective-permute-start(f32[4,16,8,128]{3,2,1,0:T(8,128)S(1)} %get-tuple-element.17), channel_id=1, source_target_pairs={{0,25},{1,0},{2,1},{3,2},{7,3},{6,7},{5,6},{4,5},{13,4},{12,13},{8... | collective-permute-start | bytes 786440 | tf_op jit(solution)/shard_map/ppermute | solution.py:827
  21.2 6.4 %collective-permute-start.9 = (f32[8,2,8,128]{3,2,1,0:T(8,128)S(1)}, f32[8,2,8,128]{3,2,1,0:T(8,128)S(1)}, u32[]{:S(2)}, u32[]{:S(2)}) collective-permute-start(f32[8,2,8,128]{3,2,1,0:T(8,128)S(1)} %get-tuple-element.19), channel_id=1, source_target_pairs={{0,8},{8,0},{16,24},{24,16},{1,9},{9,1},{17,25},{25,17},{2,10},{10... | collective-permute-start | bytes 196616 | tf_op jit(solution)/shard_map/ppermute | solution.py:841
  21.3 8.7 %collective-permute-start.10 = (f32[8,2,8,128]{3,2,1,0:T(8,128)S(1)}, f32[8,2,8,128]{3,2,1,0:T(8,128)S(1)}, u32[]{:S(2)}, u32[]{:S(2)}) collective-permute-start(f32[8,2,8,128]{3,2,1,0:T(8,128)S(1)} %get-tuple-element.20), channel_id=1, source_target_pairs={{0,16},{8,24},{16,0},{24,8},{1,17},{9,25},{17,1},{25,9},{2,18},{10... | collective-permute-start | bytes 196616 | tf_op jit(solution)/shard_map/ppermute | solution.py:841
  23.8 6.1 %collective-permute-start.11 = (f32[8,2,8,128]{3,2,1,0:T(8,128)S(1)}, f32[8,2,8,128]{3,2,1,0:T(8,128)S(1)}, u32[]{:S(2)}, u32[]{:S(2)}) collective-permute-start(f32[8,2,8,128]{3,2,1,0:T(8,128)S(1)} %get-tuple-element.21), channel_id=1, source_target_pairs={{0,24},{8,16},{16,8},{24,0},{1,25},{9,17},{17,9},{25,1},{2,26},{10... | collective-permute-start | bytes 196616 | tf_op jit(solution)/shard_map/ppermute | solution.py:841
  38.1 10.3 %collective-permute-start.12 = (f32[8,8,128]{2,1,0:T(8,128)S(1)}, f32[8,8,128]{2,1,0:T(8,128)S(1)}, u32[]{:S(2)}, u32[]{:S(2)}) collective-permute-start(f32[8,8,128]{2,1,0:T(8,128)S(1)} %get-tuple-element.25), channel_id=1, source_target_pairs={{0,8},{8,0},{16,24},{24,16},{1,9},{9,1},{17,25},{25,17},{2,10},{10... | collective-permute-start | bytes 98312 | tf_op jit(solution)/shard_map/ppermute | solution.py:841
  39.8 8.7 %collective-permute-start.13 = (f32[8,8,128]{2,1,0:T(8,128)S(1)}, f32[8,8,128]{2,1,0:T(8,128)S(1)}, u32[]{:S(2)}, u32[]{:S(2)}) collective-permute-start(f32[8,8,128]{2,1,0:T(8,128)S(1)} %get-tuple-element.26), channel_id=1, source_target_pairs={{0,16},{8,24},{16,0},{24,8},{1,17},{9,25},{17,1},{25,9},{2,18},{10... | collective-permute-start | bytes 98312 | tf_op jit(solution)/shard_map/ppermute | solution.py:841
  42.5 6.0 %collective-permute-start.14 = (f32[8,8,128]{2,1,0:T(8,128)S(1)}, f32[8,8,128]{2,1,0:T(8,128)S(1)}, u32[]{:S(2)}, u32[]{:S(2)}) collective-permute-start(f32[8,8,128]{2,1,0:T(8,128)S(1)} %get-tuple-element.27), channel_id=1, source_target_pairs={{0,24},{8,16},{16,8},{24,0},{1,25},{9,17},{17,9},{25,1},{2,26},{10... | collective-permute-start | bytes 98312 | tf_op jit(solution)/shard_map/ppermute | solution.py:841
  48.6 6.1 %collective-permute-start.21 = (f32[18,8,128]{2,1,0:T(8,128)S(1)}, f32[18,8,128]{2,1,0:T(8,128)S(1)}, u32[]{:S(2)}, u32[]{:S(2)}) collective-permute-start(f32[18,8,128]{2,1,0:T(8,128)S(1)} %get-tuple-element.36), channel_id=1, source_target_pairs={{0,6},{1,7},{2,4},{3,5},{4,2},{5,3},{6,0},{7,1},{8,14},{9,15},{10,... | collective-permute-start | bytes 221192 | tf_op jit(solution)/shard_map/ppermute | solution.py:835
  49.1 5.6 %collective-permute-start.20 = (f32[18,8,128]{2,1,0:T(8,128)S(1)}, f32[18,8,128]{2,1,0:T(8,128)S(1)}, u32[]{:S(2)}, u32[]{:S(2)}) collective-permute-start(f32[18,8,128]{2,1,0:T(8,128)S(1)} %get-tuple-element.37), channel_id=1, source_target_pairs={{0,7},{1,6},{2,5},{3,4},{4,3},{5,2},{6,1},{7,0},{8,15},{9,14},{10,... | collective-permute-start | bytes 221192 | tf_op jit(solution)/shard_map/ppermute | solution.py:835
  49.4 6.7 %collective-permute-start.19 = (f32[18,8,128]{2,1,0:T(8,128)S(1)}, f32[18,8,128]{2,1,0:T(8,128)S(1)}, u32[]{:S(2)}, u32[]{:S(2)}) collective-permute-start(f32[18,8,128]{2,1,0:T(8,128)S(1)} %get-tuple-element.38), channel_id=1, source_target_pairs={{0,2},{1,3},{2,0},{3,1},{4,6},{5,7},{6,4},{7,5},{8,10},{9,11},{10,... | collective-permute-start | bytes 221192 | tf_op jit(solution)/shard_map/ppermute | solution.py:835
  50.2 6.3 %collective-permute-start.18 = (f32[18,8,128]{2,1,0:T(8,128)S(1)}, f32[18,8,128]{2,1,0:T(8,128)S(1)}, u32[]{:S(2)}, u32[]{:S(2)}) collective-permute-start(f32[18,8,128]{2,1,0:T(8,128)S(1)} %get-tuple-element.39), channel_id=1, source_target_pairs={{0,4},{1,5},{2,6},{3,7},{4,0},{5,1},{6,2},{7,3},{8,12},{9,13},{10,... | collective-permute-start | bytes 221192 | tf_op jit(solution)/shard_map/ppermute | solution.py:835
  52.4 4.2 %collective-permute-start.17 = (f32[18,8,128]{2,1,0:T(8,128)S(1)}, f32[18,8,128]{2,1,0:T(8,128)S(1)}, u32[]{:S(2)}, u32[]{:S(2)}) collective-permute-start(f32[18,8,128]{2,1,0:T(8,128)S(1)} %get-tuple-element.40), channel_id=1, source_target_pairs={{0,3},{1,2},{2,1},{3,0},{4,7},{5,6},{6,5},{7,4},{8,11},{9,10},{10,... | collective-permute-start | bytes 221192 | tf_op jit(solution)/shard_map/ppermute | solution.py:835
  54.7 3.9 %collective-permute-start.16 = (f32[18,8,128]{2,1,0:T(8,128)S(1)}, f32[18,8,128]{2,1,0:T(8,128)S(1)}, u32[]{:S(2)}, u32[]{:S(2)}) collective-permute-start(f32[18,8,128]{2,1,0:T(8,128)S(1)} %get-tuple-element.41), channel_id=1, source_target_pairs={{0,5},{1,4},{2,7},{3,6},{4,1},{5,0},{6,3},{7,2},{8,13},{9,12},{10,... | collective-permute-start | bytes 221192 | tf_op jit(solution)/shard_map/ppermute | solution.py:835
  54.7 3.9 %collective-permute-start.15 = (f32[18,8,128]{2,1,0:T(8,128)S(1)}, f32[18,8,128]{2,1,0:T(8,128)S(1)}, u32[]{:S(2)}, u32[]{:S(2)}) collective-permute-start(f32[18,8,128]{2,1,0:T(8,128)S(1)} %get-tuple-element.42), channel_id=1, source_target_pairs={{0,1},{1,0},{2,3},{3,2},{4,5},{5,4},{6,7},{7,6},{8,9},{9,8},{10,11... | collective-permute-start | bytes 221192 | tf_op jit(solution)/shard_map/ppermute | solution.py:835

commit v8 on v7

--- a/solution.py
+++ b/solution.py
@@ -501,62 +501,59 @@
         for n in range(27):
             if n // stride % 3 == 0:
                 a, b, c = values[n], values[n + stride], values[n + 2 * stride]
-                even, odd = 0.5 * c, 0.5 * b
-                out[n], out[n + stride], out[n + 2 * stride] = even - odd, a - c, even + odd
+                out[n], out[n + stride], out[n + 2 * stride] = c - b, (a - c) - c, c + b
         values = out
     return values
 
 
-def collide_tile(values, force, rate, solid):
+CONSERVED = (0, 1, 3, 9)
+
+
+def powers_of(n):
+    return (n // 9, n // 3 % 3, n % 3)
+
+
+def weigh_rates(rates_ref, keep_ref, blend_ref):
+    for n in range(27):
+        if n not in CONSERVED:
+            powers = powers_of(n)
+            half = 0.5 ** sum(power > 0 for power in powers)
+            keep_ref[n] = (1.0 - rates_ref[n]) * half
+            blend_ref[n] = rates_ref[n] * (half * (1.0 / 3.0) ** powers.count(2))
+
+
+def collide_tile(values, force, shares, solid):
+    keep_ref, blend_ref = shares
     moments = forward3(values)
     density = moments[0]
-    jx, jy, jz = moments[9], moments[3], moments[1] + 0.5 * force
+    flux = (moments[9], moments[3], moments[1] + 0.5 * force)
     inverse = 1.0 / density
-    flux = (jx, jy, jz)
     u = tuple(j * inverse for j in flux)
-    third = 1.0 / 3.0
-    base = {0: density}
-    for k in (1, 2, 3):
-        base[k] = density * third**k
-    squares = [flux[d] * u[d] for d in range(3)]
-    square_at = {}
-    scaled = {}
-
-    def scale(key, value, count):
-        if count == 0:
-            return value
-        if (key, count) not in scaled:
-            scaled[key, count] = value * third**count
-        return scaled[key, count]
-
-    cross = {(0, 1): jx * u[1], (0, 2): jx * u[2], (1, 2): jy * u[2]}
+    triple = 3.0 * inverse
+    squares = [j * (j * triple) for j in flux]
+    cross = {(0, 1): flux[0] * u[1], (0, 2): flux[0] * u[2], (1, 2): flux[1] * u[2]}
+    level_of = {}
     out = [None] * 27
     for n in range(27):
-        powers = (n // 9, n // 3 % 3, n % 3)
-        if n in (0, 3, 9):
-            out[n] = moments[n]
-            continue
-        if n == 1:
-            out[n] = moments[n] + force
+        powers = powers_of(n)
+        if n in CONSERVED:
+            value = moments[n] + force if n == 1 else moments[n]
+            out[n] = value if n == 0 else 0.5 * value
             continue
         odd = tuple(d for d in range(3) if powers[d] == 1)
         even = tuple(d for d in range(3) if powers[d] == 2)
-        count = len(even)
+        out[n] = keep_ref[n] * moments[n]
         if len(odd) == 3:
-            out[n] = moments[n] - rate(n) * moments[n]
             continue
         if len(odd) == 0:
-            if even not in square_at:
-                total = squares[even[0]]
-                for d in even[1:]:
-                    total = total + squares[d]
-                square_at[even] = base[count] + (total * (3.0 * third**count) if count > 1 else total)
-            level = square_at[even]
+            if even not in level_of:
+                level_of[even] = level_of.get(even[:-1], density) + squares[even[-1]]
+            level = level_of[even]
         elif len(odd) == 1:
-            level = scale(odd, flux[odd[0]], count)
+            level = flux[odd[0]]
         else:
-            level = scale(odd, cross[odd], count)
-        out[n] = moments[n] - rate(n) * (moments[n] - level)
+            level = cross[odd]
+        out[n] = out[n] + blend_ref[n] * level
     out[26] = jnp.where(solid, jnp.nan, out[26])
     return backward3(out)
 
@@ -564,8 +561,8 @@
 HEAT_OFFSETS = [(0, 0, 0), (1, 0, 0), (-1, 0, 0), (0, 1, 0), (0, -1, 0), (0, 0, 1), (0, 0, -1)]
 
 
-def collide_flow(rates_ref, flow, force, solid, target, tile):
-    for n, value in enumerate(collide_tile(flow, force, lambda n: rates_ref[n], solid)):
+def collide_flow(shares, flow, force, solid, target, tile):
+    for n, value in enumerate(collide_tile(flow, force, shares, solid)):
         target[n, tile] = value
 
 
@@ -654,13 +651,14 @@
 def first_window(slab, rates_hbm, state, *refs):
     heat_parts, refs = refs[: slab.grp], refs[slab.grp :]
     flow_out, keep_out, heat_outs = refs[0], refs[1], refs[2 : 2 + slab.grp]
-    (rates_ref, sem, speed, heat_tiles, flow_post, heat_post, heat_a, heat_b, held, came_heat, ahead) = (
+    (rates_ref, sem, speed, heat_tiles, flow_post, heat_post, heat_a, heat_b, held, came_heat, ahead, *shares) = (
         refs[2 + slab.grp :]
     )
     rates_copy = pltpu.make_async_copy(rates_hbm, rates_ref, sem)
     rates_copy.start()
     make_heat_tiles(slab, heat_parts, came_heat, heat_tiles)
     rates_copy.wait()
+    weigh_rates(rates_ref, *shares)
 
     def speeds_of(tile):
         return [speed[d, tile] for d in range(3)]
@@ -674,7 +672,7 @@
         keep_out[0, tile] = force
         keep_out[1, tile] = solid
         flow = [state[n, tile] for n in range(27)]
-        collide_flow(rates_ref, flow, force, solid != 0.0, flow_post.at[0], tile)
+        collide_flow(shares, flow, force, solid != 0.0, flow_post.at[0], tile)
         collide_heat(heat, heat_tiles[7, tile], speeds_of(tile), heat_post.at[0], tile)
 
     over_tiles(slab, begin)
@@ -689,7 +687,7 @@
         def go_on(tile, values):
             flow, heat = values[:27], values[27:]
             solid = state[SOLID_AT, tile] != 0.0
-            collide_flow(rates_ref, flow, keep_out[0, tile], solid, flow_post.at[1 - source], tile)
+            collide_flow(shares, flow, keep_out[0, tile], solid, flow_post.at[1 - source], tile)
             omega = heat_tiles[7, tile]
             collide_heat(heat, omega, speeds_of(tile), heat_post.at[1 - source], tile)
 
@@ -708,7 +706,7 @@
             speed[d, tile] = speeds[d]
         force = heat_force(heat)
         keep_out[0, tile] = force
-        collide_flow(rates_ref, flow, force, solid, flow_out, tile)
+        collide_flow(shares, flow, force, solid, flow_out, tile)
         collide_heat(heat, heat_tiles[7, tile], speeds, heat_a, tile)
 
     one_ahead(slab, lambda tile: arrive(tile, source), next_window, ahead)
@@ -735,7 +733,8 @@
         heat_outs[step_number][...] = held[jnp.bitwise_xor(mine, step_number)]
 
 
-def last_window(slab, rates_hbm, came, flow_in, keep_ref, sent, rates_ref, sem, flow_post, ahead):
+def last_window(slab, rates_hbm, came, flow_in, keep_ref, sent, *refs):
+    rates_ref, sem, flow_post, ahead, *shares = refs
     rates_copy = pltpu.make_async_copy(rates_hbm, rates_ref, sem)
     rates_copy.start()
 
@@ -745,23 +744,23 @@
 
     lax.fori_loop(0, 27, copy, 0, unroll=3)
     rates_copy.wait()
+    weigh_rates(rates_ref, *shares)
 
     def step(number):
         source = lax.rem(number, 2)
 
         def go_on(tile, flow):
             solid = keep_ref[1, tile] != 0.0
-            collide_flow(rates_ref, flow, keep_ref[0, tile], solid, flow_post.at[1 - source], tile)
+            collide_flow(shares, flow, keep_ref[0, tile], solid, flow_post.at[1 - source], tile)
 
         one_ahead(slab, lambda tile: stream_flow(slab, flow_post.at[source], tile), go_on, ahead)
 
     over_steps(STEPS - 1, step)
 
-    def end(tile):
-        flow = stream_flow(slab, flow_post.at[(STEPS - 1) % 2], tile)
-        pack_out(slab, flow, came, tile, sent)
-
-    over_tiles(slab, end)
+    def arrive(tile):
+        return stream_flow(slab, flow_post.at[(STEPS - 1) % 2], tile)
+
+    one_ahead(slab, arrive, lambda tile, flow: pack_out(slab, flow, came, tile, sent), ahead)
 
 
 def heat_force(heat):
@@ -878,6 +877,7 @@
     parts = across_planes(slab, parts)
     (state,) = local_call(make_tiles, slab, [came, below, above], [(2 * IN_PAIRS,) + plane])
     scalars = [pltpu.SMEM(rates.shape, F32), pltpu.SemaphoreType.DMA]
+    shares = [pltpu.SMEM(rates.shape, F32)] * 2
     flow, keep, *parts = local_call(
         first_window,
         slab,
@@ -886,7 +886,8 @@
         scalars
         + [(3,) + plane, (8,) + plane, (2, 27) + plane, (2, 7) + plane]
         + [(7,) + plane] * 2
-        + [(slab.grp,) + plane, (slab.grp,) + heat_shape, (34,) + tile],
+        + [(slab.grp,) + plane, (slab.grp,) + heat_shape, (34,) + tile]
+        + shares,
         in_hbm=1,
     )
     parts = across_planes(slab, parts)
@@ -896,7 +897,7 @@
         slab,
         [rates, came, flow, keep],
         [last_shape],
-        scalars + [(2, 27) + plane, (27,) + tile],
+        scalars + [(2, 27) + plane, (27,) + tile] + shares,
         in_hbm=1,
     )
     (sent,) = local_call(

time: 61.1 us -> 61 us (level)
  no operation moved by 1% of the time
where the time goes in v8:
time: 61 us; the launch traced here: 60.8 us
  starting transfers between devices  26.6 us (44%)
  Pallas kernels  19.7 us (32%)
  waiting for transfers between devices  13.7 us (22%)
  between operations  0.73 us (1%)
    pallas_call x7, Pallas kernels, local_call(): pl.pallas_call(kernel, out_shape=[jax.ShapeDtypeStruct(shape, F32) for sh...  19.7 us
    ppermute x14, starting transfers between devices, across_plane(): came[step] = lax.ppermute(sent[step], ('gx', 'gy'), pairs)  13.6 us
    ppermute x14, waiting for transfers between devices, across_plane(): came[step] = lax.ppermute(sent[step], ('gx', 'gy'), pairs)  10.3 us
    ppermute x6, starting transfers between devices, across_planes(): lax.ppermute(parts[step], 'grp', [(i, i ^ step) for i in range(slab.grp)])  9.39 us
    ppermute x1, starting transfers between devices, exchange(): from_above = lax.ppermute(low, RING, [(b, a) for a, b in upward])  3.43 us
    ppermute x6, waiting for transfers between devices, across_planes(): lax.ppermute(parts[step], 'grp', [(i, i ^ step) for i in range(slab.grp)])  2.46 us
  transfers between devices with their start and end apart: 22, of which 11 were waited for; matrix products, arithmetic and copies ran while one was open for 0% of the time, Pallas kernels for 10%

profile of v8, /device:TPU:0, one launch (start us, length us, event | category | flops | bytes accessed | tf_op | source)
XLA Modules:
  0.0 60.8 jit_solution(820929759813295961)
XLA Ops:
  0.6 2.5 %shard_map.86 = f32[8,24,8,128]{3,2,1,0:T(8,128)S(1)} custom-call(f32[4]{0:T(128)} %refs_0_.3, f32[27,4,8,128]{3,2,1,0:T(8,128)} %refs_1_.1, f32[3,4,8,128]{3,2,1,0:T(8,128)} %refs_2_.1, s32[4,8,128]{2,1,0:T(8,128)} %refs_3_.1, f32[7,1,8,512]{3,2,1,0:T(8,128)} %refs_4_.1, s32[1,8,512]{2,1,0:T(8,128)} %refs_5_.1), custom_call_target="tpu_custom_call" | custom-call | tf_op jit(solution)/shard_map/pallas_call | solution.py:795
  3.2 0.1 slice_bitcast_fusion
  3.2 4.0 %collective-permute-start.6 = (f32[24,8,128]{2,1,0:T(8,128)S(1)}, f32[24,8,128]{2,1,0:T(8,128)S(1)}, u32[]{:S(2)}, u32[]{:S(2)}) collective-permute-start(f32[24,8,128]{2,1,0:T(8,128)S(1)} %get-tuple-element.28), channel_id=1, source_target_pairs={{0,6},{1,7},{2,4},{3,5},{4,2},{5,3},{6,0},{7,1},{8,14},{9,15},{10,... | collective-permute-start | bytes 294920 | tf_op jit(solution)/shard_map/ppermute | solution.py:834
  7.2 0.0 collective-permute-start.5
  7.2 1.1 %collective-permute-start.4 = (f32[24,8,128]{2,1,0:T(8,128)S(1)}, f32[24,8,128]{2,1,0:T(8,128)S(1)}, u32[]{:S(2)}, u32[]{:S(2)}) collective-permute-start(f32[24,8,128]{2,1,0:T(8,128)S(1)} %get-tuple-element.30), channel_id=1, source_target_pairs={{0,2},{1,3},{2,0},{3,1},{4,6},{5,7},{6,4},{7,5},{8,10},{9,11},{10,... | collective-permute-start | bytes 294920 | tf_op jit(solution)/shard_map/ppermute | solution.py:834
  8.3 1.5 %collective-permute-start.3 = (f32[24,8,128]{2,1,0:T(8,128)S(1)}, f32[24,8,128]{2,1,0:T(8,128)S(1)}, u32[]{:S(2)}, u32[]{:S(2)}) collective-permute-start(f32[24,8,128]{2,1,0:T(8,128)S(1)} %get-tuple-element.31), channel_id=1, source_target_pairs={{0,4},{1,5},{2,6},{3,7},{4,0},{5,1},{6,2},{7,3},{8,12},{9,13},{10,... | collective-permute-start | bytes 294920 | tf_op jit(solution)/shard_map/ppermute | solution.py:834
  9.8 0.6 collective-permute-start.2
  10.4 0.0 collective-permute-done.6.refs_7_
  10.4 0.6 collective-permute-start.1
  11.0 2.2 %collective-permute-done.5.refs_6_ = f32[24,8,128]{2,1,0:T(8,128)S(1)} collective-permute-done((f32[24,8,128]{2,1,0:T(8,128)S(1)}, f32[24,8,128]{2,1,0:T(8,128)S(1)}, u32[]{:S(2)}, u32[]{:S(2)}) %collective-permute-start.5) | collective-permute-done | bytes 98336 | tf_op jit(solution)/shard_map/ppermute | solution.py:834
  13.2 0.0 collective-permute-start
  13.2 1.6 %collective-permute-done.4.refs_5_ = f32[24,8,128]{2,1,0:T(8,128)S(1)} collective-permute-done((f32[24,8,128]{2,1,0:T(8,128)S(1)}, f32[24,8,128]{2,1,0:T(8,128)S(1)}, u32[]{:S(2)}, u32[]{:S(2)}) %collective-permute-start.4) | collective-permute-done | bytes 98336 | tf_op jit(solution)/shard_map/ppermute | solution.py:834
  14.7 0.3 collective-permute-done.3.refs_4_
  15.0 1.4 %collective-permute-done.2.refs_3_ = f32[24,8,128]{2,1,0:T(8,128)S(1)} collective-permute-done((f32[24,8,128]{2,1,0:T(8,128)S(1)}, f32[24,8,128]{2,1,0:T(8,128)S(1)}, u32[]{:S(2)}, u32[]{:S(2)}) %collective-permute-start.2) | collective-permute-done | bytes 98336 | tf_op jit(solution)/shard_map/ppermute | solution.py:834
  16.4 0.7 %collective-permute-done.1.refs_2_ = f32[24,8,128]{2,1,0:T(8,128)S(1)} collective-permute-done((f32[24,8,128]{2,1,0:T(8,128)S(1)}, f32[24,8,128]{2,1,0:T(8,128)S(1)}, u32[]{:S(2)}, u32[]{:S(2)}) %collective-permute-start.1) | collective-permute-done | bytes 98336 | tf_op jit(solution)/shard_map/ppermute | solution.py:834
  17.1 0.0 collective-permute-done.refs_1_
  17.1 0.5 shard_map.87
  17.6 0.2 collective-permute-start.7
  17.8 3.4 %collective-permute-start.8 = (f32[4,16,8,128]{3,2,1,0:T(8,128)S(1)}, f32[4,16,8,128]{3,2,1,0:T(8,128)S(1)}, u32[]{:S(2)}, u32[]{:S(2)}) collective-permute-start(f32[4,16,8,128]{3,2,1,0:T(8,128)S(1)} %get-tuple-element.17), channel_id=1, source_target_pairs={{0,25},{1,0},{2,1},{3,2},{7,3},{6,7},{5,6},{4,5},{13,4},{12,13},{8... | collective-permute-start | bytes 786440 | tf_op jit(solution)/shard_map/ppermute | solution.py:826
  21.2 0.1 collective-permute-start.9
  21.3 2.6 %collective-permute-start.10 = (f32[8,2,8,128]{3,2,1,0:T(8,128)S(1)}, f32[8,2,8,128]{3,2,1,0:T(8,128)S(1)}, u32[]{:S(2)}, u32[]{:S(2)}) collective-permute-start(f32[8,2,8,128]{3,2,1,0:T(8,128)S(1)} %get-tuple-element.20), channel_id=1, source_target_pairs={{0,16},{8,24},{16,0},{24,8},{1,17},{9,25},{17,1},{25,9},{2,18},{10... | collective-permute-start | bytes 196616 | tf_op jit(solution)/shard_map/ppermute | solution.py:840
  23.8 1.7 %collective-permute-start.11 = (f32[8,2,8,128]{3,2,1,0:T(8,128)S(1)}, f32[8,2,8,128]{3,2,1,0:T(8,128)S(1)}, u32[]{:S(2)}, u32[]{:S(2)}) collective-permute-start(f32[8,2,8,128]{3,2,1,0:T(8,128)S(1)} %get-tuple-element.21), channel_id=1, source_target_pairs={{0,24},{8,16},{16,8},{24,0},{1,25},{9,17},{17,9},{25,1},{2,26},{10... | collective-permute-start | bytes 196616 | tf_op jit(solution)/shard_map/ppermute | solution.py:840
  25.6 0.0 collective-permute-done.7.refs_1_
  25.6 1.0 %collective-permute-done.8.refs_2_ = f32[4,16,8,128]{3,2,1,0:T(8,128)S(1)} collective-permute-done((f32[4,16,8,128]{3,2,1,0:T(8,128)S(1)}, f32[4,16,8,128]{3,2,1,0:T(8,128)S(1)}, u32[]{:S(2)}, u32[]{:S(2)}) %collective-permute-start.8) | collective-permute-done | bytes 262176 | tf_op jit(solution)/shard_map/ppermute | solution.py:826
  26.6 1.0 %shard_map.88.refs_1_ = f32[32,8,8,128]{3,2,1,0:T(8,128)S(1)} custom-call(f32[8,24,8,128]{3,2,1,0:T(8,128)S(1)} %get-tuple-element.15.refs_0_.refs_1_, f32[4,16,8,128]{3,2,1,0:T(8,128)S(1)} %collective-permute-done.7.refs_1_, f32[4,16,8,128]{3,2,1,0:T(8,128)S(1)} %collective-permute-done.8.refs_2_), custom_call_target="tpu_custom_call" | custom-call | tf_op jit(solution)/shard_map/pallas_call | solution.py:795
  27.5 0.0 collective-permute-done.9.refs_3_
  27.5 2.4 %collective-permute-done.10.refs_4_ = f32[8,2,8,128]{3,2,1,0:T(8,128)S(1)} collective-permute-done((f32[8,2,8,128]{3,2,1,0:T(8,128)S(1)}, f32[8,2,8,128]{3,2,1,0:T(8,128)S(1)}, u32[]{:S(2)}, u32[]{:S(2)}) %collective-permute-start.10) | collective-permute-done | bytes 65568 | tf_op jit(solution)/shard_map/ppermute | solution.py:840
  30.0 0.0 collective-permute-done.11.refs_5_
  30.0 8.1 %shard_map.89 = (f32[27,8,8,128]{3,2,1,0:T(8,128)S(1)}, f32[2,8,8,128]{3,2,1,0:T(8,128)S(1)}, f32[8,8,128]{2,1,0:T(8,128)S(1)}, f32[8,8,128]{2,1,0:T(8,128)S(1)}...) custom-call(f32[27]{0:T(128)} %refs_0_.5, f32[32,8,8,128]{3,2,1,0:T(8,128)S(1)} %shard_map.88.refs_1_, ...), custom_call_target="tpu_custom_call" | custom-call | tf_op jit(solution)/shard_map/pallas_call | solution.py:795
  38.2 1.6 %collective-permute-start.12 = (f32[8,8,128]{2,1,0:T(8,128)S(1)}, f32[8,8,128]{2,1,0:T(8,128)S(1)}, u32[]{:S(2)}, u32[]{:S(2)}) collective-permute-start(f32[8,8,128]{2,1,0:T(8,128)S(1)} %get-tuple-element.25), channel_id=1, source_target_pairs={{0,8},{8,0},{16,24},{24,16},{1,9},{9,1},{17,25},{25,17},{2,10},{10... | collective-permute-start | bytes 98312 | tf_op jit(solution)/shard_map/ppermute | solution.py:840
  39.8 2.7 %collective-permute-start.13 = (f32[8,8,128]{2,1,0:T(8,128)S(1)}, f32[8,8,128]{2,1,0:T(8,128)S(1)}, u32[]{:S(2)}, u32[]{:S(2)}) collective-permute-start(f32[8,8,128]{2,1,0:T(8,128)S(1)} %get-tuple-element.26), channel_id=1, source_target_pairs={{0,16},{8,24},{16,0},{24,8},{1,17},{9,25},{17,1},{25,9},{2,18},{10... | collective-permute-start | bytes 98312 | tf_op jit(solution)/shard_map/ppermute | solution.py:840
  42.5 0.7 %collective-permute-start.14 = (f32[8,8,128]{2,1,0:T(8,128)S(1)}, f32[8,8,128]{2,1,0:T(8,128)S(1)}, u32[]{:S(2)}, u32[]{:S(2)}) collective-permute-start(f32[8,8,128]{2,1,0:T(8,128)S(1)} %get-tuple-element.27), channel_id=1, source_target_pairs={{0,24},{8,16},{16,8},{24,0},{1,25},{9,17},{17,9},{25,1},{2,26},{10... | collective-permute-start | bytes 98312 | tf_op jit(solution)/shard_map/ppermute | solution.py:840
  43.2 5.2 %shard_map.90.refs_0_ = f32[8,18,8,128]{3,2,1,0:T(8,128)S(1)} custom-call(f32[27]{0:T(128)} %refs_0_.5, f32[8,24,8,128]{3,2,1,0:T(8,128)S(1)} %get-tuple-element.15.refs_0_.refs_1_, f32[27,8,8,128]{3,2,1,0:T(8,128)S(1)} %get-tuple-element.22.refs_2_, f32[2,8,8,128]{3,2,1,0:T(8,128)S(1)} %get-tuple-element.23.refs_3_), custom_call_target="tpu_custom_call" | custom-call | tf_op jit(solution)/shard_map/pallas_call | solution.py:795
  48.4 0.0 collective-permute-done.12.refs_2_
  48.4 0.0 collective-permute-done.13.refs_3_
  48.4 0.0 collective-permute-done.14.refs_4_
  48.4 0.1 shard_map.91
  48.5 0.6 collective-permute-start.21
  49.1 0.2 collective-permute-start.20
  49.3 0.8 %collective-permute-start.19 = (f32[18,8,128]{2,1,0:T(8,128)S(1)}, f32[18,8,128]{2,1,0:T(8,128)S(1)}, u32[]{:S(2)}, u32[]{:S(2)}) collective-permute-start(f32[18,8,128]{2,1,0:T(8,128)S(1)} %get-tuple-element.38), channel_id=1, source_target_pairs={{0,2},{1,3},{2,0},{3,1},{4,6},{5,7},{6,4},{7,5},{8,10},{9,11},{10,... | collective-permute-start | bytes 221192 | tf_op jit(solution)/shard_map/ppermute | solution.py:834
  50.1 2.2 %collective-permute-start.18 = (f32[18,8,128]{2,1,0:T(8,128)S(1)}, f32[18,8,128]{2,1,0:T(8,128)S(1)}, u32[]{:S(2)}, u32[]{:S(2)}) collective-permute-start(f32[18,8,128]{2,1,0:T(8,128)S(1)} %get-tuple-element.39), channel_id=1, source_target_pairs={{0,4},{1,5},{2,6},{3,7},{4,0},{5,1},{6,2},{7,3},{8,12},{9,13},{10,... | collective-permute-start | bytes 221192 | tf_op jit(solution)/shard_map/ppermute | solution.py:834
  52.3 0.6 %collective-permute-start.17 = (f32[18,8,128]{2,1,0:T(8,128)S(1)}, f32[18,8,128]{2,1,0:T(8,128)S(1)}, u32[]{:S(2)}, u32[]{:S(2)}) collective-permute-start(f32[18,8,128]{2,1,0:T(8,128)S(1)} %get-tuple-element.40), channel_id=1, source_target_pairs={{0,3},{1,2},{2,1},{3,0},{4,7},{5,6},{6,5},{7,4},{8,11},{9,10},{10,... | collective-permute-start | bytes 221192 | tf_op jit(solution)/shard_map/ppermute | solution.py:834
  53.0 1.6 %collective-permute-done.21.refs_7_ = f32[18,8,128]{2,1,0:T(8,128)S(1)} collective-permute-done((f32[18,8,128]{2,1,0:T(8,128)S(1)}, f32[18,8,128]{2,1,0:T(8,128)S(1)}, u32[]{:S(2)}, u32[]{:S(2)}) %collective-permute-start.21) | collective-permute-done | bytes 73760 | tf_op jit(solution)/shard_map/ppermute | solution.py:834
  54.6 0.0 collective-permute-start.16
  54.6 0.0 collective-permute-done.20.refs_6_
  54.6 1.4 %collective-permute-start.15 = (f32[18,8,128]{2,1,0:T(8,128)S(1)}, f32[18,8,128]{2,1,0:T(8,128)S(1)}, u32[]{:S(2)}, u32[]{:S(2)}) collective-permute-start(f32[18,8,128]{2,1,0:T(8,128)S(1)} %get-tuple-element.42), channel_id=1, source_target_pairs={{0,1},{1,0},{2,3},{3,2},{4,5},{5,4},{6,7},{7,6},{8,9},{9,8},{10,11... | collective-permute-start | bytes 221192 | tf_op jit(solution)/shard_map/ppermute | solution.py:834
  56.0 0.0 collective-permute-done.19.refs_5_
  56.0 0.4 collective-permute-done.18.refs_4_
  56.4 0.1 collective-permute-done.17.refs_3_
  56.5 2.0 %collective-permute-done.16.refs_2_ = f32[18,8,128]{2,1,0:T(8,128)S(1)} collective-permute-done((f32[18,8,128]{2,1,0:T(8,128)S(1)}, f32[18,8,128]{2,1,0:T(8,128)S(1)}, u32[]{:S(2)}, u32[]{:S(2)}) %collective-permute-start.16) | collective-permute-done | bytes 73760 | tf_op jit(solution)/shard_map/ppermute | solution.py:834
  58.5 0.0 collective-permute-done.15.refs_1_
  58.5 2.3 %shard_map.92 = (f32[27,4,8,128]{3,2,1,0:T(8,128)}, f32[7,1,8,512]{3,2,1,0:T(8,128)}) custom-call(f32[18,8,128]{2,1,0:T(8,128)S(1)} %get-tuple-element.43.refs_0_, f32[18,8,128]{2,1,0:T(8,128)S(1)} %collective-permute-done.15.refs_1_, f32[18,8,128]{2,1,0:T(8,128)S(1)} %collective-permute-done.16.refs_2_, f32[18,8,128]{2,1,0:T(8,128)S(1)} %collective-permute-done.17.refs_3_, ...), custom_call_target="tpu_custom_call" | custom-call | tf_op jit(solution)/shard_map/pallas_call | solution.py:795
  (1 shorter events, 0.0 us)
Async XLA Ops:
  3.2 7.2 %collective-permute-start.6 = (f32[24,8,128]{2,1,0:T(8,128)S(1)}, f32[24,8,128]{2,1,0:T(8,128)S(1)}, u32[]{:S(2)}, u32[]{:S(2)}) collective-permute-start(f32[24,8,128]{2,1,0:T(8,128)S(1)} %get-tuple-element.28), channel_id=1, source_target_pairs={{0,6},{1,7},{2,4},{3,5},{4,2},{5,3},{6,0},{7,1},{8,14},{9,15},{10,... | collective-permute-start | bytes 294920 | tf_op jit(solution)/shard_map/ppermute | solution.py:834
  7.2 6.0 %collective-permute-start.5 = (f32[24,8,128]{2,1,0:T(8,128)S(1)}, f32[24,8,128]{2,1,0:T(8,128)S(1)}, u32[]{:S(2)}, u32[]{:S(2)}) collective-permute-start(f32[24,8,128]{2,1,0:T(8,128)S(1)} %get-tuple-element.29), channel_id=1, source_target_pairs={{0,7},{1,6},{2,5},{3,4},{4,3},{5,2},{6,1},{7,0},{8,15},{9,14},{10,... | collective-permute-start | bytes 294920 | tf_op jit(solution)/shard_map/ppermute | solution.py:834
  7.2 7.5 %collective-permute-start.4 = (f32[24,8,128]{2,1,0:T(8,128)S(1)}, f32[24,8,128]{2,1,0:T(8,128)S(1)}, u32[]{:S(2)}, u32[]{:S(2)}) collective-permute-start(f32[24,8,128]{2,1,0:T(8,128)S(1)} %get-tuple-element.30), channel_id=1, source_target_pairs={{0,2},{1,3},{2,0},{3,1},{4,6},{5,7},{6,4},{7,5},{8,10},{9,11},{10,... | collective-permute-start | bytes 294920 | tf_op jit(solution)/shard_map/ppermute | solution.py:834
  8.3 6.7 %collective-permute-start.3 = (f32[24,8,128]{2,1,0:T(8,128)S(1)}, f32[24,8,128]{2,1,0:T(8,128)S(1)}, u32[]{:S(2)}, u32[]{:S(2)}) collective-permute-start(f32[24,8,128]{2,1,0:T(8,128)S(1)} %get-tuple-element.31), channel_id=1, source_target_pairs={{0,4},{1,5},{2,6},{3,7},{4,0},{5,1},{6,2},{7,3},{8,12},{9,13},{10,... | collective-permute-start | bytes 294920 | tf_op jit(solution)/shard_map/ppermute | solution.py:834
  9.8 6.6 %collective-permute-start.2 = (f32[24,8,128]{2,1,0:T(8,128)S(1)}, f32[24,8,128]{2,1,0:T(8,128)S(1)}, u32[]{:S(2)}, u32[]{:S(2)}) collective-permute-start(f32[24,8,128]{2,1,0:T(8,128)S(1)} %get-tuple-element.32), channel_id=1, source_target_pairs={{0,3},{1,2},{2,1},{3,0},{4,7},{5,6},{6,5},{7,4},{8,11},{9,10},{10,... | collective-permute-start | bytes 294920 | tf_op jit(solution)/shard_map/ppermute | solution.py:834
  10.4 6.7 %collective-permute-start.1 = (f32[24,8,128]{2,1,0:T(8,128)S(1)}, f32[24,8,128]{2,1,0:T(8,128)S(1)}, u32[]{:S(2)}, u32[]{:S(2)}) collective-permute-start(f32[24,8,128]{2,1,0:T(8,128)S(1)} %get-tuple-element.33), channel_id=1, source_target_pairs={{0,5},{1,4},{2,7},{3,6},{4,1},{5,0},{6,3},{7,2},{8,13},{9,12},{10,... | collective-permute-start | bytes 294920 | tf_op jit(solution)/shard_map/ppermute | solution.py:834
  13.2 3.9 %collective-permute-start = (f32[24,8,128]{2,1,0:T(8,128)S(1)}, f32[24,8,128]{2,1,0:T(8,128)S(1)}, u32[]{:S(2)}, u32[]{:S(2)}) collective-permute-start(f32[24,8,128]{2,1,0:T(8,128)S(1)} %get-tuple-element.34), channel_id=1, source_target_pairs={{0,1},{1,0},{2,3},{3,2},{4,5},{5,4},{6,7},{7,6},{8,9},{9,8},{10,11... | collective-permute-start | bytes 294920 | tf_op jit(solution)/shard_map/ppermute | solution.py:834
  17.6 8.0 %collective-permute-start.7 = (f32[4,16,8,128]{3,2,1,0:T(8,128)S(1)}, f32[4,16,8,128]{3,2,1,0:T(8,128)S(1)}, u32[]{:S(2)}, u32[]{:S(2)}) collective-permute-start(f32[4,16,8,128]{3,2,1,0:T(8,128)S(1)} %get-tuple-element.16), channel_id=1, source_target_pairs={{25,0},{0,1},{1,2},{2,3},{3,7},{7,6},{6,5},{5,4},{4,13},{13,12},{1... | collective-permute-start | bytes 786440 | tf_op jit(solution)/shard_map/ppermute | solution.py:825
  17.8 8.8 %collective-permute-start.8 = (f32[4,16,8,128]{3,2,1,0:T(8,128)S(1)}, f32[4,16,8,128]{3,2,1,0:T(8,128)S(1)}, u32[]{:S(2)}, u32[]{:S(2)}) collective-permute-start(f32[4,16,8,128]{3,2,1,0:T(8,128)S(1)} %get-tuple-element.17), channel_id=1, source_target_pairs={{0,25},{1,0},{2,1},{3,2},{7,3},{6,7},{5,6},{4,5},{13,4},{12,13},{8... | collective-permute-start | bytes 786440 | tf_op jit(solution)/shard_map/ppermute | solution.py:826
  21.2 6.4 %collective-permute-start.9 = (f32[8,2,8,128]{3,2,1,0:T(8,128)S(1)}, f32[8,2,8,128]{3,2,1,0:T(8,128)S(1)}, u32[]{:S(2)}, u32[]{:S(2)}) collective-permute-start(f32[8,2,8,128]{3,2,1,0:T(8,128)S(1)} %get-tuple-element.19), channel_id=1, source_target_pairs={{0,8},{8,0},{16,24},{24,16},{1,9},{9,1},{17,25},{25,17},{2,10},{10... | collective-permute-start | bytes 196616 | tf_op jit(solution)/shard_map/ppermute | solution.py:840
  21.3 8.7 %collective-permute-start.10 = (f32[8,2,8,128]{3,2,1,0:T(8,128)S(1)}, f32[8,2,8,128]{3,2,1,0:T(8,128)S(1)}, u32[]{:S(2)}, u32[]{:S(2)}) collective-permute-start(f32[8,2,8,128]{3,2,1,0:T(8,128)S(1)} %get-tuple-element.20), channel_id=1, source_target_pairs={{0,16},{8,24},{16,0},{24,8},{1,17},{9,25},{17,1},{25,9},{2,18},{10... | collective-permute-start | bytes 196616 | tf_op jit(solution)/shard_map/ppermute | solution.py:840
  23.8 6.1 %collective-permute-start.11 = (f32[8,2,8,128]{3,2,1,0:T(8,128)S(1)}, f32[8,2,8,128]{3,2,1,0:T(8,128)S(1)}, u32[]{:S(2)}, u32[]{:S(2)}) collective-permute-start(f32[8,2,8,128]{3,2,1,0:T(8,128)S(1)} %get-tuple-element.21), channel_id=1, source_target_pairs={{0,24},{8,16},{16,8},{24,0},{1,25},{9,17},{17,9},{25,1},{2,26},{10... | collective-permute-start | bytes 196616 | tf_op jit(solution)/shard_map/ppermute | solution.py:840
  38.2 10.2 %collective-permute-start.12 = (f32[8,8,128]{2,1,0:T(8,128)S(1)}, f32[8,8,128]{2,1,0:T(8,128)S(1)}, u32[]{:S(2)}, u32[]{:S(2)}) collective-permute-start(f32[8,8,128]{2,1,0:T(8,128)S(1)} %get-tuple-element.25), channel_id=1, source_target_pairs={{0,8},{8,0},{16,24},{24,16},{1,9},{9,1},{17,25},{25,17},{2,10},{10... | collective-permute-start | bytes 98312 | tf_op jit(solution)/shard_map/ppermute | solution.py:840
  39.8 8.6 %collective-permute-start.13 = (f32[8,8,128]{2,1,0:T(8,128)S(1)}, f32[8,8,128]{2,1,0:T(8,128)S(1)}, u32[]{:S(2)}, u32[]{:S(2)}) collective-permute-start(f32[8,8,128]{2,1,0:T(8,128)S(1)} %get-tuple-element.26), channel_id=1, source_target_pairs={{0,16},{8,24},{16,0},{24,8},{1,17},{9,25},{17,1},{25,9},{2,18},{10... | collective-permute-start | bytes 98312 | tf_op jit(solution)/shard_map/ppermute | solution.py:840
  42.5 5.9 %collective-permute-start.14 = (f32[8,8,128]{2,1,0:T(8,128)S(1)}, f32[8,8,128]{2,1,0:T(8,128)S(1)}, u32[]{:S(2)}, u32[]{:S(2)}) collective-permute-start(f32[8,8,128]{2,1,0:T(8,128)S(1)} %get-tuple-element.27), channel_id=1, source_target_pairs={{0,24},{8,16},{16,8},{24,0},{1,25},{9,17},{17,9},{25,1},{2,26},{10... | collective-permute-start | bytes 98312 | tf_op jit(solution)/shard_map/ppermute | solution.py:840
  48.5 6.1 %collective-permute-start.21 = (f32[18,8,128]{2,1,0:T(8,128)S(1)}, f32[18,8,128]{2,1,0:T(8,128)S(1)}, u32[]{:S(2)}, u32[]{:S(2)}) collective-permute-start(f32[18,8,128]{2,1,0:T(8,128)S(1)} %get-tuple-element.36), channel_id=1, source_target_pairs={{0,6},{1,7},{2,4},{3,5},{4,2},{5,3},{6,0},{7,1},{8,14},{9,15},{10,... | collective-permute-start | bytes 221192 | tf_op jit(solution)/shard_map/ppermute | solution.py:834
  49.1 5.6 %collective-permute-start.20 = (f32[18,8,128]{2,1,0:T(8,128)S(1)}, f32[18,8,128]{2,1,0:T(8,128)S(1)}, u32[]{:S(2)}, u32[]{:S(2)}) collective-permute-start(f32[18,8,128]{2,1,0:T(8,128)S(1)} %get-tuple-element.37), channel_id=1, source_target_pairs={{0,7},{1,6},{2,5},{3,4},{4,3},{5,2},{6,1},{7,0},{8,15},{9,14},{10,... | collective-permute-start | bytes 221192 | tf_op jit(solution)/shard_map/ppermute | solution.py:834
  49.3 6.7 %collective-permute-start.19 = (f32[18,8,128]{2,1,0:T(8,128)S(1)}, f32[18,8,128]{2,1,0:T(8,128)S(1)}, u32[]{:S(2)}, u32[]{:S(2)}) collective-permute-start(f32[18,8,128]{2,1,0:T(8,128)S(1)} %get-tuple-element.38), channel_id=1, source_target_pairs={{0,2},{1,3},{2,0},{3,1},{4,6},{5,7},{6,4},{7,5},{8,10},{9,11},{10,... | collective-permute-start | bytes 221192 | tf_op jit(solution)/shard_map/ppermute | solution.py:834
  50.1 6.3 %collective-permute-start.18 = (f32[18,8,128]{2,1,0:T(8,128)S(1)}, f32[18,8,128]{2,1,0:T(8,128)S(1)}, u32[]{:S(2)}, u32[]{:S(2)}) collective-permute-start(f32[18,8,128]{2,1,0:T(8,128)S(1)} %get-tuple-element.39), channel_id=1, source_target_pairs={{0,4},{1,5},{2,6},{3,7},{4,0},{5,1},{6,2},{7,3},{8,12},{9,13},{10,... | collective-permute-start | bytes 221192 | tf_op jit(solution)/shard_map/ppermute | solution.py:834
  52.3 4.2 %collective-permute-start.17 = (f32[18,8,128]{2,1,0:T(8,128)S(1)}, f32[18,8,128]{2,1,0:T(8,128)S(1)}, u32[]{:S(2)}, u32[]{:S(2)}) collective-permute-start(f32[18,8,128]{2,1,0:T(8,128)S(1)} %get-tuple-element.40), channel_id=1, source_target_pairs={{0,3},{1,2},{2,1},{3,0},{4,7},{5,6},{6,5},{7,4},{8,11},{9,10},{10,... | collective-permute-start | bytes 221192 | tf_op jit(solution)/shard_map/ppermute | solution.py:834
  54.6 3.9 %collective-permute-start.16 = (f32[18,8,128]{2,1,0:T(8,128)S(1)}, f32[18,8,128]{2,1,0:T(8,128)S(1)}, u32[]{:S(2)}, u32[]{:S(2)}) collective-permute-start(f32[18,8,128]{2,1,0:T(8,128)S(1)} %get-tuple-element.41), channel_id=1, source_target_pairs={{0,5},{1,4},{2,7},{3,6},{4,1},{5,0},{6,3},{7,2},{8,13},{9,12},{10,... | collective-permute-start | bytes 221192 | tf_op jit(solution)/shard_map/ppermute | solution.py:834
  54.6 3.9 %collective-permute-start.15 = (f32[18,8,128]{2,1,0:T(8,128)S(1)}, f32[18,8,128]{2,1,0:T(8,128)S(1)}, u32[]{:S(2)}, u32[]{:S(2)}) collective-permute-start(f32[18,8,128]{2,1,0:T(8,128)S(1)} %get-tuple-element.42), channel_id=1, source_target_pairs={{0,1},{1,0},{2,3},{3,2},{4,5},{5,4},{6,7},{7,6},{8,9},{9,8},{10,11... | collective-permute-start | bytes 221192 | tf_op jit(solution)/shard_map/ppermute | solution.py:834

commit v9 on v7

--- a/solution.py
+++ b/solution.py
@@ -262,6 +262,9 @@
             jnp.bitwise_xor(self.round_plane(lax.rem(begin + place, self.sub)), mine)
             for place in range(self.sub)
         ]
+
+    def planes_far_first(self):
+        return [0] + list(range(self.grp - 1, 0, -1))
 
     def place_in_plane(self):
         return lax.axis_index("gx") * self.gy + lax.axis_index("gy")
@@ -395,7 +398,7 @@
 
 def make_heat_tiles(slab, parts, held, heat_tiles):
     mine = lax.axis_index("grp")
-    for step, part in enumerate(parts):
+    for step, part in zip(slab.planes_far_first(), parts):
         held[jnp.bitwise_xor(mine, step)] = part[...]
     first = in_first_half(slab)
     for tile in range(slab.sub):
@@ -757,11 +760,10 @@
 
     over_steps(STEPS - 1, step)
 
-    def end(tile):
-        flow = stream_flow(slab, flow_post.at[(STEPS - 1) % 2], tile)
-        pack_out(slab, flow, came, tile, sent)
-
-    over_tiles(slab, end)
+    def arrive(tile):
+        return stream_flow(slab, flow_post.at[(STEPS - 1) % 2], tile)
+
+    one_ahead(slab, arrive, lambda tile, flow: pack_out(slab, flow, came, tile, sent), ahead)
 
 
 def heat_force(heat):
@@ -881,7 +883,7 @@
     flow, keep, *parts = local_call(
         first_window,
         slab,
-        [rates, state] + parts,
+        [rates, state] + [parts[step] for step in slab.planes_far_first()],
         [(27,) + plane, (2,) + plane] + [plane] * slab.grp,
         scalars
         + [(3,) + plane, (8,) + plane, (2, 27) + plane, (2, 7) + plane]

time: 61.1 us -> 61.1 us (level)
  waiting for transfers between devices: 13.7 us -> 14.8 us
  starting transfers between devices: 26.6 us -> 25.7 us
  transfers between devices with their start and end apart: 22 -> 22, of which waited for: 11 -> 13; matrix products, arithmetic and copies ran while one was open for 0% -> 0% of each run, Pallas kernels for 10% -> 10%
where the time goes in v9:
time: 61.1 us; the launch traced here: 61 us
  starting transfers between devices  25.7 us (42%)
  Pallas kernels  19.6 us (32%)
  waiting for transfers between devices  14.8 us (24%)
  between operations  0.73 us (1%)
    pallas_call x7, Pallas kernels, local_call(): pl.pallas_call(kernel, out_shape=[jax.ShapeDtypeStruct(shape, F32) for sh...  19.6 us
    ppermute x14, starting transfers between devices, across_plane(): came[step] = lax.ppermute(sent[step], ('gx', 'gy'), pairs)  13.3 us
    ppermute x14, waiting for transfers between devices, across_plane(): came[step] = lax.ppermute(sent[step], ('gx', 'gy'), pairs)  10.6 us
    ppermute x6, starting transfers between devices, across_planes(): lax.ppermute(parts[step], 'grp', [(i, i ^ step) for i in range(slab.grp)])  8.84 us
    ppermute x1, starting transfers between devices, exchange(): from_above = lax.ppermute(low, RING, [(b, a) for a, b in upward])  3.43 us
    ppermute x6, waiting for transfers between devices, across_planes(): lax.ppermute(parts[step], 'grp', [(i, i ^ step) for i in range(slab.grp)])  2.79 us
    ppermute x1, waiting for transfers between devices, exchange(): from_above = lax.ppermute(low, RING, [(b, a) for a, b in upward])  1.37 us
  transfers between devices with their start and end apart: 22, of which 13 were waited for; matrix products, arithmetic and copies ran while one was open for 0% of the time, Pallas kernels for 10%

profile of v9, /device:TPU:0, one launch (start us, length us, event | category | flops | bytes accessed | tf_op | source)
XLA Modules:
  0.0 61.0 jit_solution(12226787051765925338)
XLA Ops:
  0.6 2.5 %shard_map.86 = f32[8,24,8,128]{3,2,1,0:T(8,128)S(1)} custom-call(f32[4]{0:T(128)} %refs_0_.3, f32[27,4,8,128]{3,2,1,0:T(8,128)} %refs_1_.1, f32[3,4,8,128]{3,2,1,0:T(8,128)} %refs_2_.1, s32[4,8,128]{2,1,0:T(8,128)} %refs_3_.1, f32[7,1,8,512]{3,2,1,0:T(8,128)} %refs_4_.1, s32[1,8,512]{2,1,0:T(8,128)} %refs_5_.1), custom_call_target="tpu_custom_call" | custom-call | tf_op jit(solution)/shard_map/pallas_call | solution.py:798
  3.2 0.1 slice_bitcast_fusion
  3.2 4.0 %collective-permute-start.6 = (f32[24,8,128]{2,1,0:T(8,128)S(1)}, f32[24,8,128]{2,1,0:T(8,128)S(1)}, u32[]{:S(2)}, u32[]{:S(2)}) collective-permute-start(f32[24,8,128]{2,1,0:T(8,128)S(1)} %get-tuple-element.28), channel_id=1, source_target_pairs={{0,6},{1,7},{2,4},{3,5},{4,2},{5,3},{6,0},{7,1},{8,14},{9,15},{10,... | collective-permute-start | bytes 294920 | tf_op jit(solution)/shard_map/ppermute | solution.py:837
  7.2 0.0 collective-permute-start.5
  7.2 1.1 %collective-permute-start.4 = (f32[24,8,128]{2,1,0:T(8,128)S(1)}, f32[24,8,128]{2,1,0:T(8,128)S(1)}, u32[]{:S(2)}, u32[]{:S(2)}) collective-permute-start(f32[24,8,128]{2,1,0:T(8,128)S(1)} %get-tuple-element.30), channel_id=1, source_target_pairs={{0,2},{1,3},{2,0},{3,1},{4,6},{5,7},{6,4},{7,5},{8,10},{9,11},{10,... | collective-permute-start | bytes 294920 | tf_op jit(solution)/shard_map/ppermute | solution.py:837
  8.3 1.5 %collective-permute-start.3 = (f32[24,8,128]{2,1,0:T(8,128)S(1)}, f32[24,8,128]{2,1,0:T(8,128)S(1)}, u32[]{:S(2)}, u32[]{:S(2)}) collective-permute-start(f32[24,8,128]{2,1,0:T(8,128)S(1)} %get-tuple-element.31), channel_id=1, source_target_pairs={{0,4},{1,5},{2,6},{3,7},{4,0},{5,1},{6,2},{7,3},{8,12},{9,13},{10,... | collective-permute-start | bytes 294920 | tf_op jit(solution)/shard_map/ppermute | solution.py:837
  9.8 0.6 collective-permute-start.2
  10.4 0.0 collective-permute-done.6.refs_7_
  10.4 0.6 collective-permute-start.1
  11.0 2.2 %collective-permute-done.5.refs_6_ = f32[24,8,128]{2,1,0:T(8,128)S(1)} collective-permute-done((f32[24,8,128]{2,1,0:T(8,128)S(1)}, f32[24,8,128]{2,1,0:T(8,128)S(1)}, u32[]{:S(2)}, u32[]{:S(2)}) %collective-permute-start.5) | collective-permute-done | bytes 98336 | tf_op jit(solution)/shard_map/ppermute | solution.py:837
  13.2 0.0 collective-permute-start
  13.2 1.6 %collective-permute-done.4.refs_5_ = f32[24,8,128]{2,1,0:T(8,128)S(1)} collective-permute-done((f32[24,8,128]{2,1,0:T(8,128)S(1)}, f32[24,8,128]{2,1,0:T(8,128)S(1)}, u32[]{:S(2)}, u32[]{:S(2)}) %collective-permute-start.4) | collective-permute-done | bytes 98336 | tf_op jit(solution)/shard_map/ppermute | solution.py:837
  14.7 0.3 collective-permute-done.3.refs_4_
  15.0 1.4 %collective-permute-done.2.refs_3_ = f32[24,8,128]{2,1,0:T(8,128)S(1)} collective-permute-done((f32[24,8,128]{2,1,0:T(8,128)S(1)}, f32[24,8,128]{2,1,0:T(8,128)S(1)}, u32[]{:S(2)}, u32[]{:S(2)}) %collective-permute-start.2) | collective-permute-done | bytes 98336 | tf_op jit(solution)/shard_map/ppermute | solution.py:837
  16.4 0.7 %collective-permute-done.1.refs_2_ = f32[24,8,128]{2,1,0:T(8,128)S(1)} collective-permute-done((f32[24,8,128]{2,1,0:T(8,128)S(1)}, f32[24,8,128]{2,1,0:T(8,128)S(1)}, u32[]{:S(2)}, u32[]{:S(2)}) %collective-permute-start.1) | collective-permute-done | bytes 98336 | tf_op jit(solution)/shard_map/ppermute | solution.py:837
  17.1 0.0 collective-permute-done.refs_1_
  17.1 0.5 shard_map.87
  17.6 0.2 collective-permute-start.7
  17.8 3.4 %collective-permute-start.8 = (f32[4,16,8,128]{3,2,1,0:T(8,128)S(1)}, f32[4,16,8,128]{3,2,1,0:T(8,128)S(1)}, u32[]{:S(2)}, u32[]{:S(2)}) collective-permute-start(f32[4,16,8,128]{3,2,1,0:T(8,128)S(1)} %get-tuple-element.17), channel_id=1, source_target_pairs={{0,25},{1,0},{2,1},{3,2},{7,3},{6,7},{5,6},{4,5},{13,4},{12,13},{8... | collective-permute-start | bytes 786440 | tf_op jit(solution)/shard_map/ppermute | solution.py:829
  21.2 2.1 %collective-permute-start.9 = (f32[8,2,8,128]{3,2,1,0:T(8,128)S(1)}, f32[8,2,8,128]{3,2,1,0:T(8,128)S(1)}, u32[]{:S(2)}, u32[]{:S(2)}) collective-permute-start(f32[8,2,8,128]{3,2,1,0:T(8,128)S(1)} %get-tuple-element.19), channel_id=1, source_target_pairs={{0,24},{8,16},{16,8},{24,0},{1,25},{9,17},{17,9},{25,1},{2,26},{10... | collective-permute-start | bytes 196616 | tf_op jit(solution)/shard_map/ppermute | solution.py:843
  23.3 0.0 collective-permute-start.10
  23.3 2.3 %collective-permute-start.11 = (f32[8,2,8,128]{3,2,1,0:T(8,128)S(1)}, f32[8,2,8,128]{3,2,1,0:T(8,128)S(1)}, u32[]{:S(2)}, u32[]{:S(2)}) collective-permute-start(f32[8,2,8,128]{3,2,1,0:T(8,128)S(1)} %get-tuple-element.21), channel_id=1, source_target_pairs={{0,8},{8,0},{16,24},{24,16},{1,9},{9,1},{17,25},{25,17},{2,10},{10... | collective-permute-start | bytes 196616 | tf_op jit(solution)/shard_map/ppermute | solution.py:843
  25.6 0.0 collective-permute-done.7.refs_1_
  25.6 1.4 %collective-permute-done.8.refs_2_ = f32[4,16,8,128]{3,2,1,0:T(8,128)S(1)} collective-permute-done((f32[4,16,8,128]{3,2,1,0:T(8,128)S(1)}, f32[4,16,8,128]{3,2,1,0:T(8,128)S(1)}, u32[]{:S(2)}, u32[]{:S(2)}) %collective-permute-start.8) | collective-permute-done | bytes 262176 | tf_op jit(solution)/shard_map/ppermute | solution.py:829
  27.0 1.0 %shard_map.88.refs_1_ = f32[32,8,8,128]{3,2,1,0:T(8,128)S(1)} custom-call(f32[8,24,8,128]{3,2,1,0:T(8,128)S(1)} %get-tuple-element.15.refs_0_.refs_1_, f32[4,16,8,128]{3,2,1,0:T(8,128)S(1)} %collective-permute-done.7.refs_1_, f32[4,16,8,128]{3,2,1,0:T(8,128)S(1)} %collective-permute-done.8.refs_2_), custom_call_target="tpu_custom_call" | custom-call | tf_op jit(solution)/shard_map/pallas_call | solution.py:798
  27.9 0.1 collective-permute-done.9.refs_3_
  28.0 2.7 %collective-permute-done.10.refs_4_ = f32[8,2,8,128]{3,2,1,0:T(8,128)S(1)} collective-permute-done((f32[8,2,8,128]{3,2,1,0:T(8,128)S(1)}, f32[8,2,8,128]{3,2,1,0:T(8,128)S(1)}, u32[]{:S(2)}, u32[]{:S(2)}) %collective-permute-start.10) | collective-permute-done | bytes 65568 | tf_op jit(solution)/shard_map/ppermute | solution.py:843
  30.7 0.0 collective-permute-done.11.refs_5_
  30.7 8.1 %shard_map.89 = (f32[27,8,8,128]{3,2,1,0:T(8,128)S(1)}, f32[2,8,8,128]{3,2,1,0:T(8,128)S(1)}, f32[8,8,128]{2,1,0:T(8,128)S(1)}, f32[8,8,128]{2,1,0:T(8,128)S(1)}...) custom-call(f32[27]{0:T(128)} %refs_0_.5, f32[32,8,8,128]{3,2,1,0:T(8,128)S(1)} %shard_map.88.refs_1_, ...), custom_call_target="tpu_custom_call" | custom-call | tf_op jit(solution)/shard_map/pallas_call | solution.py:798
  38.9 0.9 %collective-permute-start.12 = (f32[8,8,128]{2,1,0:T(8,128)S(1)}, f32[8,8,128]{2,1,0:T(8,128)S(1)}, u32[]{:S(2)}, u32[]{:S(2)}) collective-permute-start(f32[8,8,128]{2,1,0:T(8,128)S(1)} %get-tuple-element.25), channel_id=1, source_target_pairs={{0,8},{8,0},{16,24},{24,16},{1,9},{9,1},{17,25},{25,17},{2,10},{10... | collective-permute-start | bytes 98312 | tf_op jit(solution)/shard_map/ppermute | solution.py:843
  39.8 2.4 %collective-permute-start.13 = (f32[8,8,128]{2,1,0:T(8,128)S(1)}, f32[8,8,128]{2,1,0:T(8,128)S(1)}, u32[]{:S(2)}, u32[]{:S(2)}) collective-permute-start(f32[8,8,128]{2,1,0:T(8,128)S(1)} %get-tuple-element.26), channel_id=1, source_target_pairs={{0,16},{8,24},{16,0},{24,8},{1,17},{9,25},{17,1},{25,9},{2,18},{10... | collective-permute-start | bytes 98312 | tf_op jit(solution)/shard_map/ppermute | solution.py:843
  42.2 1.1 %collective-permute-start.14 = (f32[8,8,128]{2,1,0:T(8,128)S(1)}, f32[8,8,128]{2,1,0:T(8,128)S(1)}, u32[]{:S(2)}, u32[]{:S(2)}) collective-permute-start(f32[8,8,128]{2,1,0:T(8,128)S(1)} %get-tuple-element.27), channel_id=1, source_target_pairs={{0,24},{8,16},{16,8},{24,0},{1,25},{9,17},{17,9},{25,1},{2,26},{10... | collective-permute-start | bytes 98312 | tf_op jit(solution)/shard_map/ppermute | solution.py:843
  43.3 5.1 %shard_map.90.refs_0_ = f32[8,18,8,128]{3,2,1,0:T(8,128)S(1)} custom-call(f32[27]{0:T(128)} %refs_0_.5, f32[8,24,8,128]{3,2,1,0:T(8,128)S(1)} %get-tuple-element.15.refs_0_.refs_1_, f32[27,8,8,128]{3,2,1,0:T(8,128)S(1)} %get-tuple-element.22.refs_2_, f32[2,8,8,128]{3,2,1,0:T(8,128)S(1)} %get-tuple-element.23.refs_3_), custom_call_target="tpu_custom_call" | custom-call | tf_op jit(solution)/shard_map/pallas_call | solution.py:798
  48.4 0.0 collective-permute-done.12.refs_2_
  48.4 0.0 collective-permute-done.13.refs_3_
  48.4 0.0 collective-permute-done.14.refs_4_
  48.5 0.1 shard_map.91
  48.6 0.8 %collective-permute-start.21 = (f32[18,8,128]{2,1,0:T(8,128)S(1)}, f32[18,8,128]{2,1,0:T(8,128)S(1)}, u32[]{:S(2)}, u32[]{:S(2)}) collective-permute-start(f32[18,8,128]{2,1,0:T(8,128)S(1)} %get-tuple-element.36), channel_id=1, source_target_pairs={{0,6},{1,7},{2,4},{3,5},{4,2},{5,3},{6,0},{7,1},{8,14},{9,15},{10,... | collective-permute-start | bytes 221192 | tf_op jit(solution)/shard_map/ppermute | solution.py:837
  49.3 0.6 collective-permute-start.20
  49.9 0.0 collective-permute-start.19
  49.9 3.0 %collective-permute-start.18 = (f32[18,8,128]{2,1,0:T(8,128)S(1)}, f32[18,8,128]{2,1,0:T(8,128)S(1)}, u32[]{:S(2)}, u32[]{:S(2)}) collective-permute-start(f32[18,8,128]{2,1,0:T(8,128)S(1)} %get-tuple-element.39), channel_id=1, source_target_pairs={{0,4},{1,5},{2,6},{3,7},{4,0},{5,1},{6,2},{7,3},{8,12},{9,13},{10,... | collective-permute-start | bytes 221192 | tf_op jit(solution)/shard_map/ppermute | solution.py:837
  52.9 0.1 collective-permute-start.17
  53.0 1.5 %collective-permute-done.21.refs_7_ = f32[18,8,128]{2,1,0:T(8,128)S(1)} collective-permute-done((f32[18,8,128]{2,1,0:T(8,128)S(1)}, f32[18,8,128]{2,1,0:T(8,128)S(1)}, u32[]{:S(2)}, u32[]{:S(2)}) %collective-permute-start.21) | collective-permute-done | bytes 73760 | tf_op jit(solution)/shard_map/ppermute | solution.py:837
  54.6 0.0 collective-permute-start.16
  54.6 0.3 collective-permute-done.20.refs_6_
  54.9 1.1 %collective-permute-start.15 = (f32[18,8,128]{2,1,0:T(8,128)S(1)}, f32[18,8,128]{2,1,0:T(8,128)S(1)}, u32[]{:S(2)}, u32[]{:S(2)}) collective-permute-start(f32[18,8,128]{2,1,0:T(8,128)S(1)} %get-tuple-element.42), channel_id=1, source_target_pairs={{0,1},{1,0},{2,3},{3,2},{4,5},{5,4},{6,7},{7,6},{8,9},{9,8},{10,11... | collective-permute-start | bytes 221192 | tf_op jit(solution)/shard_map/ppermute | solution.py:837
  56.0 0.0 collective-permute-done.19.refs_5_
  56.0 1.1 %collective-permute-done.18.refs_4_ = f32[18,8,128]{2,1,0:T(8,128)S(1)} collective-permute-done((f32[18,8,128]{2,1,0:T(8,128)S(1)}, f32[18,8,128]{2,1,0:T(8,128)S(1)}, u32[]{:S(2)}, u32[]{:S(2)}) %collective-permute-start.18) | collective-permute-done | bytes 73760 | tf_op jit(solution)/shard_map/ppermute | solution.py:837
  57.1 0.1 collective-permute-done.17.refs_3_
  57.1 1.5 %collective-permute-done.16.refs_2_ = f32[18,8,128]{2,1,0:T(8,128)S(1)} collective-permute-done((f32[18,8,128]{2,1,0:T(8,128)S(1)}, f32[18,8,128]{2,1,0:T(8,128)S(1)}, u32[]{:S(2)}, u32[]{:S(2)}) %collective-permute-start.16) | collective-permute-done | bytes 73760 | tf_op jit(solution)/shard_map/ppermute | solution.py:837
  58.6 0.0 collective-permute-done.15.refs_1_
  58.6 2.3 %shard_map.92 = (f32[27,4,8,128]{3,2,1,0:T(8,128)}, f32[7,1,8,512]{3,2,1,0:T(8,128)}) custom-call(f32[18,8,128]{2,1,0:T(8,128)S(1)} %get-tuple-element.43.refs_0_, f32[18,8,128]{2,1,0:T(8,128)S(1)} %collective-permute-done.15.refs_1_, f32[18,8,128]{2,1,0:T(8,128)S(1)} %collective-permute-done.16.refs_2_, f32[18,8,128]{2,1,0:T(8,128)S(1)} %collective-permute-done.17.refs_3_, ...), custom_call_target="tpu_custom_call" | custom-call | tf_op jit(solution)/shard_map/pallas_call | solution.py:798
  (1 shorter events, 0.0 us)
Async XLA Ops:
  3.2 7.2 %collective-permute-start.6 = (f32[24,8,128]{2,1,0:T(8,128)S(1)}, f32[24,8,128]{2,1,0:T(8,128)S(1)}, u32[]{:S(2)}, u32[]{:S(2)}) collective-permute-start(f32[24,8,128]{2,1,0:T(8,128)S(1)} %get-tuple-element.28), channel_id=1, source_target_pairs={{0,6},{1,7},{2,4},{3,5},{4,2},{5,3},{6,0},{7,1},{8,14},{9,15},{10,... | collective-permute-start | bytes 294920 | tf_op jit(solution)/shard_map/ppermute | solution.py:837
  7.2 6.0 %collective-permute-start.5 = (f32[24,8,128]{2,1,0:T(8,128)S(1)}, f32[24,8,128]{2,1,0:T(8,128)S(1)}, u32[]{:S(2)}, u32[]{:S(2)}) collective-permute-start(f32[24,8,128]{2,1,0:T(8,128)S(1)} %get-tuple-element.29), channel_id=1, source_target_pairs={{0,7},{1,6},{2,5},{3,4},{4,3},{5,2},{6,1},{7,0},{8,15},{9,14},{10,... | collective-permute-start | bytes 294920 | tf_op jit(solution)/shard_map/ppermute | solution.py:837
  7.2 7.5 %collective-permute-start.4 = (f32[24,8,128]{2,1,0:T(8,128)S(1)}, f32[24,8,128]{2,1,0:T(8,128)S(1)}, u32[]{:S(2)}, u32[]{:S(2)}) collective-permute-start(f32[24,8,128]{2,1,0:T(8,128)S(1)} %get-tuple-element.30), channel_id=1, source_target_pairs={{0,2},{1,3},{2,0},{3,1},{4,6},{5,7},{6,4},{7,5},{8,10},{9,11},{10,... | collective-permute-start | bytes 294920 | tf_op jit(solution)/shard_map/ppermute | solution.py:837
  8.3 6.7 %collective-permute-start.3 = (f32[24,8,128]{2,1,0:T(8,128)S(1)}, f32[24,8,128]{2,1,0:T(8,128)S(1)}, u32[]{:S(2)}, u32[]{:S(2)}) collective-permute-start(f32[24,8,128]{2,1,0:T(8,128)S(1)} %get-tuple-element.31), channel_id=1, source_target_pairs={{0,4},{1,5},{2,6},{3,7},{4,0},{5,1},{6,2},{7,3},{8,12},{9,13},{10,... | collective-permute-start | bytes 294920 | tf_op jit(solution)/shard_map/ppermute | solution.py:837
  9.8 6.6 %collective-permute-start.2 = (f32[24,8,128]{2,1,0:T(8,128)S(1)}, f32[24,8,128]{2,1,0:T(8,128)S(1)}, u32[]{:S(2)}, u32[]{:S(2)}) collective-permute-start(f32[24,8,128]{2,1,0:T(8,128)S(1)} %get-tuple-element.32), channel_id=1, source_target_pairs={{0,3},{1,2},{2,1},{3,0},{4,7},{5,6},{6,5},{7,4},{8,11},{9,10},{10,... | collective-permute-start | bytes 294920 | tf_op jit(solution)/shard_map/ppermute | solution.py:837
  10.4 6.7 %collective-permute-start.1 = (f32[24,8,128]{2,1,0:T(8,128)S(1)}, f32[24,8,128]{2,1,0:T(8,128)S(1)}, u32[]{:S(2)}, u32[]{:S(2)}) collective-permute-start(f32[24,8,128]{2,1,0:T(8,128)S(1)} %get-tuple-element.33), channel_id=1, source_target_pairs={{0,5},{1,4},{2,7},{3,6},{4,1},{5,0},{6,3},{7,2},{8,13},{9,12},{10,... | collective-permute-start | bytes 294920 | tf_op jit(solution)/shard_map/ppermute | solution.py:837
  13.2 3.9 %collective-permute-start = (f32[24,8,128]{2,1,0:T(8,128)S(1)}, f32[24,8,128]{2,1,0:T(8,128)S(1)}, u32[]{:S(2)}, u32[]{:S(2)}) collective-permute-start(f32[24,8,128]{2,1,0:T(8,128)S(1)} %get-tuple-element.34), channel_id=1, source_target_pairs={{0,1},{1,0},{2,3},{3,2},{4,5},{5,4},{6,7},{7,6},{8,9},{9,8},{10,11... | collective-permute-start | bytes 294920 | tf_op jit(solution)/shard_map/ppermute | solution.py:837
  17.6 8.0 %collective-permute-start.7 = (f32[4,16,8,128]{3,2,1,0:T(8,128)S(1)}, f32[4,16,8,128]{3,2,1,0:T(8,128)S(1)}, u32[]{:S(2)}, u32[]{:S(2)}) collective-permute-start(f32[4,16,8,128]{3,2,1,0:T(8,128)S(1)} %get-tuple-element.16), channel_id=1, source_target_pairs={{25,0},{0,1},{1,2},{2,3},{3,7},{7,6},{6,5},{5,4},{4,13},{13,12},{1... | collective-permute-start | bytes 786440 | tf_op jit(solution)/shard_map/ppermute | solution.py:828
  17.8 9.2 %collective-permute-start.8 = (f32[4,16,8,128]{3,2,1,0:T(8,128)S(1)}, f32[4,16,8,128]{3,2,1,0:T(8,128)S(1)}, u32[]{:S(2)}, u32[]{:S(2)}) collective-permute-start(f32[4,16,8,128]{3,2,1,0:T(8,128)S(1)} %get-tuple-element.17), channel_id=1, source_target_pairs={{0,25},{1,0},{2,1},{3,2},{7,3},{6,7},{5,6},{4,5},{13,4},{12,13},{8... | collective-permute-start | bytes 786440 | tf_op jit(solution)/shard_map/ppermute | solution.py:829
  21.2 6.9 %collective-permute-start.9 = (f32[8,2,8,128]{3,2,1,0:T(8,128)S(1)}, f32[8,2,8,128]{3,2,1,0:T(8,128)S(1)}, u32[]{:S(2)}, u32[]{:S(2)}) collective-permute-start(f32[8,2,8,128]{3,2,1,0:T(8,128)S(1)} %get-tuple-element.19), channel_id=1, source_target_pairs={{0,24},{8,16},{16,8},{24,0},{1,25},{9,17},{17,9},{25,1},{2,26},{10... | collective-permute-start | bytes 196616 | tf_op jit(solution)/shard_map/ppermute | solution.py:843
  23.3 7.4 %collective-permute-start.10 = (f32[8,2,8,128]{3,2,1,0:T(8,128)S(1)}, f32[8,2,8,128]{3,2,1,0:T(8,128)S(1)}, u32[]{:S(2)}, u32[]{:S(2)}) collective-permute-start(f32[8,2,8,128]{3,2,1,0:T(8,128)S(1)} %get-tuple-element.20), channel_id=1, source_target_pairs={{0,16},{8,24},{16,0},{24,8},{1,17},{9,25},{17,1},{25,9},{2,18},{10... | collective-permute-start | bytes 196616 | tf_op jit(solution)/shard_map/ppermute | solution.py:843
  23.3 7.4 %collective-permute-start.11 = (f32[8,2,8,128]{3,2,1,0:T(8,128)S(1)}, f32[8,2,8,128]{3,2,1,0:T(8,128)S(1)}, u32[]{:S(2)}, u32[]{:S(2)}) collective-permute-start(f32[8,2,8,128]{3,2,1,0:T(8,128)S(1)} %get-tuple-element.21), channel_id=1, source_target_pairs={{0,8},{8,0},{16,24},{24,16},{1,9},{9,1},{17,25},{25,17},{2,10},{10... | collective-permute-start | bytes 196616 | tf_op jit(solution)/shard_map/ppermute | solution.py:843
  38.9 9.6 %collective-permute-start.12 = (f32[8,8,128]{2,1,0:T(8,128)S(1)}, f32[8,8,128]{2,1,0:T(8,128)S(1)}, u32[]{:S(2)}, u32[]{:S(2)}) collective-permute-start(f32[8,8,128]{2,1,0:T(8,128)S(1)} %get-tuple-element.25), channel_id=1, source_target_pairs={{0,8},{8,0},{16,24},{24,16},{1,9},{9,1},{17,25},{25,17},{2,10},{10... | collective-permute-start | bytes 98312 | tf_op jit(solution)/shard_map/ppermute | solution.py:843
  39.8 8.7 %collective-permute-start.13 = (f32[8,8,128]{2,1,0:T(8,128)S(1)}, f32[8,8,128]{2,1,0:T(8,128)S(1)}, u32[]{:S(2)}, u32[]{:S(2)}) collective-permute-start(f32[8,8,128]{2,1,0:T(8,128)S(1)} %get-tuple-element.26), channel_id=1, source_target_pairs={{0,16},{8,24},{16,0},{24,8},{1,17},{9,25},{17,1},{25,9},{2,18},{10... | collective-permute-start | bytes 98312 | tf_op jit(solution)/shard_map/ppermute | solution.py:843
  42.2 6.3 %collective-permute-start.14 = (f32[8,8,128]{2,1,0:T(8,128)S(1)}, f32[8,8,128]{2,1,0:T(8,128)S(1)}, u32[]{:S(2)}, u32[]{:S(2)}) collective-permute-start(f32[8,8,128]{2,1,0:T(8,128)S(1)} %get-tuple-element.27), channel_id=1, source_target_pairs={{0,24},{8,16},{16,8},{24,0},{1,25},{9,17},{17,9},{25,1},{2,26},{10... | collective-permute-start | bytes 98312 | tf_op jit(solution)/shard_map/ppermute | solution.py:843
  48.6 6.0 %collective-permute-start.21 = (f32[18,8,128]{2,1,0:T(8,128)S(1)}, f32[18,8,128]{2,1,0:T(8,128)S(1)}, u32[]{:S(2)}, u32[]{:S(2)}) collective-permute-start(f32[18,8,128]{2,1,0:T(8,128)S(1)} %get-tuple-element.36), channel_id=1, source_target_pairs={{0,6},{1,7},{2,4},{3,5},{4,2},{5,3},{6,0},{7,1},{8,14},{9,15},{10,... | collective-permute-start | bytes 221192 | tf_op jit(solution)/shard_map/ppermute | solution.py:837
  49.3 5.5 %collective-permute-start.20 = (f32[18,8,128]{2,1,0:T(8,128)S(1)}, f32[18,8,128]{2,1,0:T(8,128)S(1)}, u32[]{:S(2)}, u32[]{:S(2)}) collective-permute-start(f32[18,8,128]{2,1,0:T(8,128)S(1)} %get-tuple-element.37), channel_id=1, source_target_pairs={{0,7},{1,6},{2,5},{3,4},{4,3},{5,2},{6,1},{7,0},{8,15},{9,14},{10,... | collective-permute-start | bytes 221192 | tf_op jit(solution)/shard_map/ppermute | solution.py:837
  49.9 6.1 %collective-permute-start.19 = (f32[18,8,128]{2,1,0:T(8,128)S(1)}, f32[18,8,128]{2,1,0:T(8,128)S(1)}, u32[]{:S(2)}, u32[]{:S(2)}) collective-permute-start(f32[18,8,128]{2,1,0:T(8,128)S(1)} %get-tuple-element.38), channel_id=1, source_target_pairs={{0,2},{1,3},{2,0},{3,1},{4,6},{5,7},{6,4},{7,5},{8,10},{9,11},{10,... | collective-permute-start | bytes 221192 | tf_op jit(solution)/shard_map/ppermute | solution.py:837
  49.9 7.1 %collective-permute-start.18 = (f32[18,8,128]{2,1,0:T(8,128)S(1)}, f32[18,8,128]{2,1,0:T(8,128)S(1)}, u32[]{:S(2)}, u32[]{:S(2)}) collective-permute-start(f32[18,8,128]{2,1,0:T(8,128)S(1)} %get-tuple-element.39), channel_id=1, source_target_pairs={{0,4},{1,5},{2,6},{3,7},{4,0},{5,1},{6,2},{7,3},{8,12},{9,13},{10,... | collective-permute-start | bytes 221192 | tf_op jit(solution)/shard_map/ppermute | solution.py:837
  52.9 4.2 %collective-permute-start.17 = (f32[18,8,128]{2,1,0:T(8,128)S(1)}, f32[18,8,128]{2,1,0:T(8,128)S(1)}, u32[]{:S(2)}, u32[]{:S(2)}) collective-permute-start(f32[18,8,128]{2,1,0:T(8,128)S(1)} %get-tuple-element.40), channel_id=1, source_target_pairs={{0,3},{1,2},{2,1},{3,0},{4,7},{5,6},{6,5},{7,4},{8,11},{9,10},{10,... | collective-permute-start | bytes 221192 | tf_op jit(solution)/shard_map/ppermute | solution.py:837
  54.6 4.0 %collective-permute-start.16 = (f32[18,8,128]{2,1,0:T(8,128)S(1)}, f32[18,8,128]{2,1,0:T(8,128)S(1)}, u32[]{:S(2)}, u32[]{:S(2)}) collective-permute-start(f32[18,8,128]{2,1,0:T(8,128)S(1)} %get-tuple-element.41), channel_id=1, source_target_pairs={{0,5},{1,4},{2,7},{3,6},{4,1},{5,0},{6,3},{7,2},{8,13},{9,12},{10,... | collective-permute-start | bytes 221192 | tf_op jit(solution)/shard_map/ppermute | solution.py:837
  54.9 3.8 %collective-permute-start.15 = (f32[18,8,128]{2,1,0:T(8,128)S(1)}, f32[18,8,128]{2,1,0:T(8,128)S(1)}, u32[]{:S(2)}, u32[]{:S(2)}) collective-permute-start(f32[18,8,128]{2,1,0:T(8,128)S(1)} %get-tuple-element.42), channel_id=1, source_target_pairs={{0,1},{1,0},{2,3},{3,2},{4,5},{5,4},{6,7},{7,6},{8,9},{9,8},{10,11... | collective-permute-start | bytes 221192 | tf_op jit(solution)/shard_map/ppermute | solution.py:837

commit v10 on v9

--- a/solution.py
+++ b/solution.py
@@ -738,32 +738,25 @@
         heat_outs[step_number][...] = held[jnp.bitwise_xor(mine, step_number)]
 
 
-def last_window(slab, rates_hbm, came, flow_in, keep_ref, sent, rates_ref, sem, flow_post, ahead):
-    rates_copy = pltpu.make_async_copy(rates_hbm, rates_ref, sem)
-    rates_copy.start()
-
-    def copy(n, _):
-        flow_post[0, n] = flow_in[n]
-        return 0
-
-    lax.fori_loop(0, 27, copy, 0, unroll=3)
-    rates_copy.wait()
-
-    def step(number):
-        source = lax.rem(number, 2)
-
-        def go_on(tile, flow):
+def last_window(slab, rates_hbm, came, flow_in, keep_ref, sent, *refs):
+    rates_ref, sem, flow_a, flow_b, ahead = refs
+    fetch = pltpu.make_async_copy(rates_hbm, rates_ref, sem)
+    fetch.start()
+    fetch.wait()
+    source, target, spare = flow_in, flow_a, flow_b
+    for _ in range(STEPS - 1):
+
+        def go_on(tile, flow, target=target):
             solid = keep_ref[1, tile] != 0.0
-            collide_flow(rates_ref, flow, keep_ref[0, tile], solid, flow_post.at[1 - source], tile)
-
-        one_ahead(slab, lambda tile: stream_flow(slab, flow_post.at[source], tile), go_on, ahead)
-
-    over_steps(STEPS - 1, step)
-
-    def arrive(tile):
-        return stream_flow(slab, flow_post.at[(STEPS - 1) % 2], tile)
-
-    one_ahead(slab, arrive, lambda tile, flow: pack_out(slab, flow, came, tile, sent), ahead)
+            collide_flow(rates_ref, flow, keep_ref[0, tile], solid, target, tile)
+
+        one_ahead(slab, lambda tile, source=source: stream_flow(slab, source, tile), go_on, ahead)
+        source, target, spare = target, spare, target
+
+    def end(tile, flow):
+        pack_out(slab, flow, came, tile, sent)
+
+    one_ahead(slab, lambda tile: stream_flow(slab, source, tile), end, ahead)
 
 
 def heat_force(heat):
@@ -898,7 +891,7 @@
         slab,
         [rates, came, flow, keep],
         [last_shape],
-        scalars + [(2, 27) + plane, (27,) + tile],
+        scalars + [(27,) + plane, (27,) + plane, (27,) + tile],
         in_hbm=1,
     )
     (sent,) = local_call(

time: 61.1 us -> 61.1 us (level)
  no operation moved by 1% of the time
where the time goes in v10:
time: 61.1 us; the launch traced here: 61 us
  starting transfers between devices  25.7 us (42%)
  Pallas kernels  19.6 us (32%)
  waiting for transfers between devices  14.8 us (24%)
  between operations  0.73 us (1%)
    pallas_call x7, Pallas kernels, local_call(): pl.pallas_call(kernel, out_shape=[jax.ShapeDtypeStruct(shape, F32) for sh...  19.6 us
    ppermute x14, starting transfers between devices, across_plane(): came[step] = lax.ppermute(sent[step], ('gx', 'gy'), pairs)  13.3 us
    ppermute x14, waiting for transfers between devices, across_plane(): came[step] = lax.ppermute(sent[step], ('gx', 'gy'), pairs)  10.7 us
    ppermute x6, starting transfers between devices, across_planes(): lax.ppermute(parts[step], 'grp', [(i, i ^ step) for i in range(slab.grp)])  8.84 us
    ppermute x1, starting transfers between devices, exchange(): from_above = lax.ppermute(low, RING, [(b, a) for a, b in upward])  3.43 us
    ppermute x6, waiting for transfers between devices, across_planes(): lax.ppermute(parts[step], 'grp', [(i, i ^ step) for i in range(slab.grp)])  2.79 us
    ppermute x1, waiting for transfers between devices, exchange(): from_above = lax.ppermute(low, RING, [(b, a) for a, b in upward])  1.37 us
  transfers between devices with their start and end apart: 22, of which 13 were waited for; matrix products, arithmetic and copies ran while one was open for 0% of the time, Pallas kernels for 10%

profile of v10, /device:TPU:0, one launch (start us, length us, event | category | flops | bytes accessed | tf_op | source)
XLA Modules:
  0.0 61.0 jit_solution(1334681987240098938)
XLA Ops:
  0.6 2.5 %shard_map.86 = f32[8,24,8,128]{3,2,1,0:T(8,128)S(1)} custom-call(f32[4]{0:T(128)} %refs_0_.3, f32[27,4,8,128]{3,2,1,0:T(8,128)} %refs_1_.1, f32[3,4,8,128]{3,2,1,0:T(8,128)} %refs_2_.1, s32[4,8,128]{2,1,0:T(8,128)} %refs_3_.1, f32[7,1,8,512]{3,2,1,0:T(8,128)} %refs_4_.1, s32[1,8,512]{2,1,0:T(8,128)} %refs_5_.1), custom_call_target="tpu_custom_call" | custom-call | tf_op jit(solution)/shard_map/pallas_call | solution.py:791
  3.2 0.1 slice_bitcast_fusion
  3.2 4.0 %collective-permute-start.6 = (f32[24,8,128]{2,1,0:T(8,128)S(1)}, f32[24,8,128]{2,1,0:T(8,128)S(1)}, u32[]{:S(2)}, u32[]{:S(2)}) collective-permute-start(f32[24,8,128]{2,1,0:T(8,128)S(1)} %get-tuple-element.28), channel_id=1, source_target_pairs={{0,6},{1,7},{2,4},{3,5},{4,2},{5,3},{6,0},{7,1},{8,14},{9,15},{10,... | collective-permute-start | bytes 294920 | tf_op jit(solution)/shard_map/ppermute | solution.py:830
  7.2 0.0 collective-permute-start.5
  7.2 1.1 %collective-permute-start.4 = (f32[24,8,128]{2,1,0:T(8,128)S(1)}, f32[24,8,128]{2,1,0:T(8,128)S(1)}, u32[]{:S(2)}, u32[]{:S(2)}) collective-permute-start(f32[24,8,128]{2,1,0:T(8,128)S(1)} %get-tuple-element.30), channel_id=1, source_target_pairs={{0,2},{1,3},{2,0},{3,1},{4,6},{5,7},{6,4},{7,5},{8,10},{9,11},{10,... | collective-permute-start | bytes 294920 | tf_op jit(solution)/shard_map/ppermute | solution.py:830
  8.3 1.5 %collective-permute-start.3 = (f32[24,8,128]{2,1,0:T(8,128)S(1)}, f32[24,8,128]{2,1,0:T(8,128)S(1)}, u32[]{:S(2)}, u32[]{:S(2)}) collective-permute-start(f32[24,8,128]{2,1,0:T(8,128)S(1)} %get-tuple-element.31), channel_id=1, source_target_pairs={{0,4},{1,5},{2,6},{3,7},{4,0},{5,1},{6,2},{7,3},{8,12},{9,13},{10,... | collective-permute-start | bytes 294920 | tf_op jit(solution)/shard_map/ppermute | solution.py:830
  9.8 0.6 collective-permute-start.2
  10.4 0.0 collective-permute-done.6.refs_7_
  10.4 0.6 collective-permute-start.1
  11.0 2.2 %collective-permute-done.5.refs_6_ = f32[24,8,128]{2,1,0:T(8,128)S(1)} collective-permute-done((f32[24,8,128]{2,1,0:T(8,128)S(1)}, f32[24,8,128]{2,1,0:T(8,128)S(1)}, u32[]{:S(2)}, u32[]{:S(2)}) %collective-permute-start.5) | collective-permute-done | bytes 98336 | tf_op jit(solution)/shard_map/ppermute | solution.py:830
  13.2 0.0 collective-permute-start
  13.2 1.6 %collective-permute-done.4.refs_5_ = f32[24,8,128]{2,1,0:T(8,128)S(1)} collective-permute-done((f32[24,8,128]{2,1,0:T(8,128)S(1)}, f32[24,8,128]{2,1,0:T(8,128)S(1)}, u32[]{:S(2)}, u32[]{:S(2)}) %collective-permute-start.4) | collective-permute-done | bytes 98336 | tf_op jit(solution)/shard_map/ppermute | solution.py:830
  14.7 0.3 collective-permute-done.3.refs_4_
  15.0 1.4 %collective-permute-done.2.refs_3_ = f32[24,8,128]{2,1,0:T(8,128)S(1)} collective-permute-done((f32[24,8,128]{2,1,0:T(8,128)S(1)}, f32[24,8,128]{2,1,0:T(8,128)S(1)}, u32[]{:S(2)}, u32[]{:S(2)}) %collective-permute-start.2) | collective-permute-done | bytes 98336 | tf_op jit(solution)/shard_map/ppermute | solution.py:830
  16.4 0.7 %collective-permute-done.1.refs_2_ = f32[24,8,128]{2,1,0:T(8,128)S(1)} collective-permute-done((f32[24,8,128]{2,1,0:T(8,128)S(1)}, f32[24,8,128]{2,1,0:T(8,128)S(1)}, u32[]{:S(2)}, u32[]{:S(2)}) %collective-permute-start.1) | collective-permute-done | bytes 98336 | tf_op jit(solution)/shard_map/ppermute | solution.py:830
  17.1 0.0 collective-permute-done.refs_1_
  17.1 0.5 shard_map.87
  17.6 0.2 collective-permute-start.7
  17.8 3.4 %collective-permute-start.8 = (f32[4,16,8,128]{3,2,1,0:T(8,128)S(1)}, f32[4,16,8,128]{3,2,1,0:T(8,128)S(1)}, u32[]{:S(2)}, u32[]{:S(2)}) collective-permute-start(f32[4,16,8,128]{3,2,1,0:T(8,128)S(1)} %get-tuple-element.17), channel_id=1, source_target_pairs={{0,25},{1,0},{2,1},{3,2},{7,3},{6,7},{5,6},{4,5},{13,4},{12,13},{8... | collective-permute-start | bytes 786440 | tf_op jit(solution)/shard_map/ppermute | solution.py:822
  21.2 2.1 %collective-permute-start.9 = (f32[8,2,8,128]{3,2,1,0:T(8,128)S(1)}, f32[8,2,8,128]{3,2,1,0:T(8,128)S(1)}, u32[]{:S(2)}, u32[]{:S(2)}) collective-permute-start(f32[8,2,8,128]{3,2,1,0:T(8,128)S(1)} %get-tuple-element.19), channel_id=1, source_target_pairs={{0,24},{8,16},{16,8},{24,0},{1,25},{9,17},{17,9},{25,1},{2,26},{10... | collective-permute-start | bytes 196616 | tf_op jit(solution)/shard_map/ppermute | solution.py:836
  23.3 0.0 collective-permute-start.10
  23.3 2.3 %collective-permute-start.11 = (f32[8,2,8,128]{3,2,1,0:T(8,128)S(1)}, f32[8,2,8,128]{3,2,1,0:T(8,128)S(1)}, u32[]{:S(2)}, u32[]{:S(2)}) collective-permute-start(f32[8,2,8,128]{3,2,1,0:T(8,128)S(1)} %get-tuple-element.21), channel_id=1, source_target_pairs={{0,8},{8,0},{16,24},{24,16},{1,9},{9,1},{17,25},{25,17},{2,10},{10... | collective-permute-start | bytes 196616 | tf_op jit(solution)/shard_map/ppermute | solution.py:836
  25.6 0.0 collective-permute-done.7.refs_1_
  25.6 1.4 %collective-permute-done.8.refs_2_ = f32[4,16,8,128]{3,2,1,0:T(8,128)S(1)} collective-permute-done((f32[4,16,8,128]{3,2,1,0:T(8,128)S(1)}, f32[4,16,8,128]{3,2,1,0:T(8,128)S(1)}, u32[]{:S(2)}, u32[]{:S(2)}) %collective-permute-start.8) | collective-permute-done | bytes 262176 | tf_op jit(solution)/shard_map/ppermute | solution.py:822
  27.0 1.0 %shard_map.88.refs_1_ = f32[32,8,8,128]{3,2,1,0:T(8,128)S(1)} custom-call(f32[8,24,8,128]{3,2,1,0:T(8,128)S(1)} %get-tuple-element.15.refs_0_.refs_1_, f32[4,16,8,128]{3,2,1,0:T(8,128)S(1)} %collective-permute-done.7.refs_1_, f32[4,16,8,128]{3,2,1,0:T(8,128)S(1)} %collective-permute-done.8.refs_2_), custom_call_target="tpu_custom_call" | custom-call | tf_op jit(solution)/shard_map/pallas_call | solution.py:791
  27.9 0.1 collective-permute-done.9.refs_3_
  28.0 2.7 %collective-permute-done.10.refs_4_ = f32[8,2,8,128]{3,2,1,0:T(8,128)S(1)} collective-permute-done((f32[8,2,8,128]{3,2,1,0:T(8,128)S(1)}, f32[8,2,8,128]{3,2,1,0:T(8,128)S(1)}, u32[]{:S(2)}, u32[]{:S(2)}) %collective-permute-start.10) | collective-permute-done | bytes 65568 | tf_op jit(solution)/shard_map/ppermute | solution.py:836
  30.7 0.0 collective-permute-done.11.refs_5_
  30.7 8.1 %shard_map.89 = (f32[27,8,8,128]{3,2,1,0:T(8,128)S(1)}, f32[2,8,8,128]{3,2,1,0:T(8,128)S(1)}, f32[8,8,128]{2,1,0:T(8,128)S(1)}, f32[8,8,128]{2,1,0:T(8,128)S(1)}...) custom-call(f32[27]{0:T(128)} %refs_0_.5, f32[32,8,8,128]{3,2,1,0:T(8,128)S(1)} %shard_map.88.refs_1_, ...), custom_call_target="tpu_custom_call" | custom-call | tf_op jit(solution)/shard_map/pallas_call | solution.py:791
  38.9 0.9 %collective-permute-start.12 = (f32[8,8,128]{2,1,0:T(8,128)S(1)}, f32[8,8,128]{2,1,0:T(8,128)S(1)}, u32[]{:S(2)}, u32[]{:S(2)}) collective-permute-start(f32[8,8,128]{2,1,0:T(8,128)S(1)} %get-tuple-element.25), channel_id=1, source_target_pairs={{0,8},{8,0},{16,24},{24,16},{1,9},{9,1},{17,25},{25,17},{2,10},{10... | collective-permute-start | bytes 98312 | tf_op jit(solution)/shard_map/ppermute | solution.py:836
  39.8 2.4 %collective-permute-start.13 = (f32[8,8,128]{2,1,0:T(8,128)S(1)}, f32[8,8,128]{2,1,0:T(8,128)S(1)}, u32[]{:S(2)}, u32[]{:S(2)}) collective-permute-start(f32[8,8,128]{2,1,0:T(8,128)S(1)} %get-tuple-element.26), channel_id=1, source_target_pairs={{0,16},{8,24},{16,0},{24,8},{1,17},{9,25},{17,1},{25,9},{2,18},{10... | collective-permute-start | bytes 98312 | tf_op jit(solution)/shard_map/ppermute | solution.py:836
  42.2 1.1 %collective-permute-start.14 = (f32[8,8,128]{2,1,0:T(8,128)S(1)}, f32[8,8,128]{2,1,0:T(8,128)S(1)}, u32[]{:S(2)}, u32[]{:S(2)}) collective-permute-start(f32[8,8,128]{2,1,0:T(8,128)S(1)} %get-tuple-element.27), channel_id=1, source_target_pairs={{0,24},{8,16},{16,8},{24,0},{1,25},{9,17},{17,9},{25,1},{2,26},{10... | collective-permute-start | bytes 98312 | tf_op jit(solution)/shard_map/ppermute | solution.py:836
  43.3 5.1 %shard_map.90.refs_0_ = f32[8,18,8,128]{3,2,1,0:T(8,128)S(1)} custom-call(f32[27]{0:T(128)} %refs_0_.5, f32[8,24,8,128]{3,2,1,0:T(8,128)S(1)} %get-tuple-element.15.refs_0_.refs_1_, f32[27,8,8,128]{3,2,1,0:T(8,128)S(1)} %get-tuple-element.22.refs_2_, f32[2,8,8,128]{3,2,1,0:T(8,128)S(1)} %get-tuple-element.23.refs_3_), custom_call_target="tpu_custom_call" | custom-call | tf_op jit(solution)/shard_map/pallas_call | solution.py:791
  48.4 0.0 collective-permute-done.12.refs_2_
  48.4 0.0 collective-permute-done.13.refs_3_
  48.4 0.0 collective-permute-done.14.refs_4_
  48.4 0.1 shard_map.91
  48.6 0.8 %collective-permute-start.21 = (f32[18,8,128]{2,1,0:T(8,128)S(1)}, f32[18,8,128]{2,1,0:T(8,128)S(1)}, u32[]{:S(2)}, u32[]{:S(2)}) collective-permute-start(f32[18,8,128]{2,1,0:T(8,128)S(1)} %get-tuple-element.36), channel_id=1, source_target_pairs={{0,6},{1,7},{2,4},{3,5},{4,2},{5,3},{6,0},{7,1},{8,14},{9,15},{10,... | collective-permute-start | bytes 221192 | tf_op jit(solution)/shard_map/ppermute | solution.py:830
  49.3 0.6 collective-permute-start.20
  49.9 0.0 collective-permute-start.19
  49.9 3.0 %collective-permute-start.18 = (f32[18,8,128]{2,1,0:T(8,128)S(1)}, f32[18,8,128]{2,1,0:T(8,128)S(1)}, u32[]{:S(2)}, u32[]{:S(2)}) collective-permute-start(f32[18,8,128]{2,1,0:T(8,128)S(1)} %get-tuple-element.39), channel_id=1, source_target_pairs={{0,4},{1,5},{2,6},{3,7},{4,0},{5,1},{6,2},{7,3},{8,12},{9,13},{10,... | collective-permute-start | bytes 221192 | tf_op jit(solution)/shard_map/ppermute | solution.py:830
  52.9 0.1 collective-permute-start.17
  53.0 1.5 %collective-permute-done.21.refs_7_ = f32[18,8,128]{2,1,0:T(8,128)S(1)} collective-permute-done((f32[18,8,128]{2,1,0:T(8,128)S(1)}, f32[18,8,128]{2,1,0:T(8,128)S(1)}, u32[]{:S(2)}, u32[]{:S(2)}) %collective-permute-start.21) | collective-permute-done | bytes 73760 | tf_op jit(solution)/shard_map/ppermute | solution.py:830
  54.6 0.0 collective-permute-start.16
  54.6 0.3 collective-permute-done.20.refs_6_
  54.9 1.1 %collective-permute-start.15 = (f32[18,8,128]{2,1,0:T(8,128)S(1)}, f32[18,8,128]{2,1,0:T(8,128)S(1)}, u32[]{:S(2)}, u32[]{:S(2)}) collective-permute-start(f32[18,8,128]{2,1,0:T(8,128)S(1)} %get-tuple-element.42), channel_id=1, source_target_pairs={{0,1},{1,0},{2,3},{3,2},{4,5},{5,4},{6,7},{7,6},{8,9},{9,8},{10,11... | collective-permute-start | bytes 221192 | tf_op jit(solution)/shard_map/ppermute | solution.py:830
  55.9 0.0 collective-permute-done.19.refs_5_
  55.9 1.1 %collective-permute-done.18.refs_4_ = f32[18,8,128]{2,1,0:T(8,128)S(1)} collective-permute-done((f32[18,8,128]{2,1,0:T(8,128)S(1)}, f32[18,8,128]{2,1,0:T(8,128)S(1)}, u32[]{:S(2)}, u32[]{:S(2)}) %collective-permute-start.18) | collective-permute-done | bytes 73760 | tf_op jit(solution)/shard_map/ppermute | solution.py:830
  57.0 0.1 collective-permute-done.17.refs_3_
  57.1 1.5 %collective-permute-done.16.refs_2_ = f32[18,8,128]{2,1,0:T(8,128)S(1)} collective-permute-done((f32[18,8,128]{2,1,0:T(8,128)S(1)}, f32[18,8,128]{2,1,0:T(8,128)S(1)}, u32[]{:S(2)}, u32[]{:S(2)}) %collective-permute-start.16) | collective-permute-done | bytes 73760 | tf_op jit(solution)/shard_map/ppermute | solution.py:830
  58.6 0.0 collective-permute-done.15.refs_1_
  58.6 2.3 %shard_map.92 = (f32[27,4,8,128]{3,2,1,0:T(8,128)}, f32[7,1,8,512]{3,2,1,0:T(8,128)}) custom-call(f32[18,8,128]{2,1,0:T(8,128)S(1)} %get-tuple-element.43.refs_0_, f32[18,8,128]{2,1,0:T(8,128)S(1)} %collective-permute-done.15.refs_1_, f32[18,8,128]{2,1,0:T(8,128)S(1)} %collective-permute-done.16.refs_2_, f32[18,8,128]{2,1,0:T(8,128)S(1)} %collective-permute-done.17.refs_3_, ...), custom_call_target="tpu_custom_call" | custom-call | tf_op jit(solution)/shard_map/pallas_call | solution.py:791
  (1 shorter events, 0.0 us)
Async XLA Ops:
  3.2 7.2 %collective-permute-start.6 = (f32[24,8,128]{2,1,0:T(8,128)S(1)}, f32[24,8,128]{2,1,0:T(8,128)S(1)}, u32[]{:S(2)}, u32[]{:S(2)}) collective-permute-start(f32[24,8,128]{2,1,0:T(8,128)S(1)} %get-tuple-element.28), channel_id=1, source_target_pairs={{0,6},{1,7},{2,4},{3,5},{4,2},{5,3},{6,0},{7,1},{8,14},{9,15},{10,... | collective-permute-start | bytes 294920 | tf_op jit(solution)/shard_map/ppermute | solution.py:830
  7.2 6.0 %collective-permute-start.5 = (f32[24,8,128]{2,1,0:T(8,128)S(1)}, f32[24,8,128]{2,1,0:T(8,128)S(1)}, u32[]{:S(2)}, u32[]{:S(2)}) collective-permute-start(f32[24,8,128]{2,1,0:T(8,128)S(1)} %get-tuple-element.29), channel_id=1, source_target_pairs={{0,7},{1,6},{2,5},{3,4},{4,3},{5,2},{6,1},{7,0},{8,15},{9,14},{10,... | collective-permute-start | bytes 294920 | tf_op jit(solution)/shard_map/ppermute | solution.py:830
  7.2 7.5 %collective-permute-start.4 = (f32[24,8,128]{2,1,0:T(8,128)S(1)}, f32[24,8,128]{2,1,0:T(8,128)S(1)}, u32[]{:S(2)}, u32[]{:S(2)}) collective-permute-start(f32[24,8,128]{2,1,0:T(8,128)S(1)} %get-tuple-element.30), channel_id=1, source_target_pairs={{0,2},{1,3},{2,0},{3,1},{4,6},{5,7},{6,4},{7,5},{8,10},{9,11},{10,... | collective-permute-start | bytes 294920 | tf_op jit(solution)/shard_map/ppermute | solution.py:830
  8.3 6.7 %collective-permute-start.3 = (f32[24,8,128]{2,1,0:T(8,128)S(1)}, f32[24,8,128]{2,1,0:T(8,128)S(1)}, u32[]{:S(2)}, u32[]{:S(2)}) collective-permute-start(f32[24,8,128]{2,1,0:T(8,128)S(1)} %get-tuple-element.31), channel_id=1, source_target_pairs={{0,4},{1,5},{2,6},{3,7},{4,0},{5,1},{6,2},{7,3},{8,12},{9,13},{10,... | collective-permute-start | bytes 294920 | tf_op jit(solution)/shard_map/ppermute | solution.py:830
  9.8 6.6 %collective-permute-start.2 = (f32[24,8,128]{2,1,0:T(8,128)S(1)}, f32[24,8,128]{2,1,0:T(8,128)S(1)}, u32[]{:S(2)}, u32[]{:S(2)}) collective-permute-start(f32[24,8,128]{2,1,0:T(8,128)S(1)} %get-tuple-element.32), channel_id=1, source_target_pairs={{0,3},{1,2},{2,1},{3,0},{4,7},{5,6},{6,5},{7,4},{8,11},{9,10},{10,... | collective-permute-start | bytes 294920 | tf_op jit(solution)/shard_map/ppermute | solution.py:830
  10.4 6.7 %collective-permute-start.1 = (f32[24,8,128]{2,1,0:T(8,128)S(1)}, f32[24,8,128]{2,1,0:T(8,128)S(1)}, u32[]{:S(2)}, u32[]{:S(2)}) collective-permute-start(f32[24,8,128]{2,1,0:T(8,128)S(1)} %get-tuple-element.33), channel_id=1, source_target_pairs={{0,5},{1,4},{2,7},{3,6},{4,1},{5,0},{6,3},{7,2},{8,13},{9,12},{10,... | collective-permute-start | bytes 294920 | tf_op jit(solution)/shard_map/ppermute | solution.py:830
  13.2 3.9 %collective-permute-start = (f32[24,8,128]{2,1,0:T(8,128)S(1)}, f32[24,8,128]{2,1,0:T(8,128)S(1)}, u32[]{:S(2)}, u32[]{:S(2)}) collective-permute-start(f32[24,8,128]{2,1,0:T(8,128)S(1)} %get-tuple-element.34), channel_id=1, source_target_pairs={{0,1},{1,0},{2,3},{3,2},{4,5},{5,4},{6,7},{7,6},{8,9},{9,8},{10,11... | collective-permute-start | bytes 294920 | tf_op jit(solution)/shard_map/ppermute | solution.py:830
  17.6 8.0 %collective-permute-start.7 = (f32[4,16,8,128]{3,2,1,0:T(8,128)S(1)}, f32[4,16,8,128]{3,2,1,0:T(8,128)S(1)}, u32[]{:S(2)}, u32[]{:S(2)}) collective-permute-start(f32[4,16,8,128]{3,2,1,0:T(8,128)S(1)} %get-tuple-element.16), channel_id=1, source_target_pairs={{25,0},{0,1},{1,2},{2,3},{3,7},{7,6},{6,5},{5,4},{4,13},{13,12},{1... | collective-permute-start | bytes 786440 | tf_op jit(solution)/shard_map/ppermute | solution.py:821
  17.8 9.2 %collective-permute-start.8 = (f32[4,16,8,128]{3,2,1,0:T(8,128)S(1)}, f32[4,16,8,128]{3,2,1,0:T(8,128)S(1)}, u32[]{:S(2)}, u32[]{:S(2)}) collective-permute-start(f32[4,16,8,128]{3,2,1,0:T(8,128)S(1)} %get-tuple-element.17), channel_id=1, source_target_pairs={{0,25},{1,0},{2,1},{3,2},{7,3},{6,7},{5,6},{4,5},{13,4},{12,13},{8... | collective-permute-start | bytes 786440 | tf_op jit(solution)/shard_map/ppermute | solution.py:822
  21.2 6.9 %collective-permute-start.9 = (f32[8,2,8,128]{3,2,1,0:T(8,128)S(1)}, f32[8,2,8,128]{3,2,1,0:T(8,128)S(1)}, u32[]{:S(2)}, u32[]{:S(2)}) collective-permute-start(f32[8,2,8,128]{3,2,1,0:T(8,128)S(1)} %get-tuple-element.19), channel_id=1, source_target_pairs={{0,24},{8,16},{16,8},{24,0},{1,25},{9,17},{17,9},{25,1},{2,26},{10... | collective-permute-start | bytes 196616 | tf_op jit(solution)/shard_map/ppermute | solution.py:836
  23.3 7.4 %collective-permute-start.10 = (f32[8,2,8,128]{3,2,1,0:T(8,128)S(1)}, f32[8,2,8,128]{3,2,1,0:T(8,128)S(1)}, u32[]{:S(2)}, u32[]{:S(2)}) collective-permute-start(f32[8,2,8,128]{3,2,1,0:T(8,128)S(1)} %get-tuple-element.20), channel_id=1, source_target_pairs={{0,16},{8,24},{16,0},{24,8},{1,17},{9,25},{17,1},{25,9},{2,18},{10... | collective-permute-start | bytes 196616 | tf_op jit(solution)/shard_map/ppermute | solution.py:836
  23.3 7.4 %collective-permute-start.11 = (f32[8,2,8,128]{3,2,1,0:T(8,128)S(1)}, f32[8,2,8,128]{3,2,1,0:T(8,128)S(1)}, u32[]{:S(2)}, u32[]{:S(2)}) collective-permute-start(f32[8,2,8,128]{3,2,1,0:T(8,128)S(1)} %get-tuple-element.21), channel_id=1, source_target_pairs={{0,8},{8,0},{16,24},{24,16},{1,9},{9,1},{17,25},{25,17},{2,10},{10... | collective-permute-start | bytes 196616 | tf_op jit(solution)/shard_map/ppermute | solution.py:836
  38.9 9.5 %collective-permute-start.12 = (f32[8,8,128]{2,1,0:T(8,128)S(1)}, f32[8,8,128]{2,1,0:T(8,128)S(1)}, u32[]{:S(2)}, u32[]{:S(2)}) collective-permute-start(f32[8,8,128]{2,1,0:T(8,128)S(1)} %get-tuple-element.25), channel_id=1, source_target_pairs={{0,8},{8,0},{16,24},{24,16},{1,9},{9,1},{17,25},{25,17},{2,10},{10... | collective-permute-start | bytes 98312 | tf_op jit(solution)/shard_map/ppermute | solution.py:836
  39.8 8.7 %collective-permute-start.13 = (f32[8,8,128]{2,1,0:T(8,128)S(1)}, f32[8,8,128]{2,1,0:T(8,128)S(1)}, u32[]{:S(2)}, u32[]{:S(2)}) collective-permute-start(f32[8,8,128]{2,1,0:T(8,128)S(1)} %get-tuple-element.26), channel_id=1, source_target_pairs={{0,16},{8,24},{16,0},{24,8},{1,17},{9,25},{17,1},{25,9},{2,18},{10... | collective-permute-start | bytes 98312 | tf_op jit(solution)/shard_map/ppermute | solution.py:836
  42.2 6.2 %collective-permute-start.14 = (f32[8,8,128]{2,1,0:T(8,128)S(1)}, f32[8,8,128]{2,1,0:T(8,128)S(1)}, u32[]{:S(2)}, u32[]{:S(2)}) collective-permute-start(f32[8,8,128]{2,1,0:T(8,128)S(1)} %get-tuple-element.27), channel_id=1, source_target_pairs={{0,24},{8,16},{16,8},{24,0},{1,25},{9,17},{17,9},{25,1},{2,26},{10... | collective-permute-start | bytes 98312 | tf_op jit(solution)/shard_map/ppermute | solution.py:836
  48.6 6.0 %collective-permute-start.21 = (f32[18,8,128]{2,1,0:T(8,128)S(1)}, f32[18,8,128]{2,1,0:T(8,128)S(1)}, u32[]{:S(2)}, u32[]{:S(2)}) collective-permute-start(f32[18,8,128]{2,1,0:T(8,128)S(1)} %get-tuple-element.36), channel_id=1, source_target_pairs={{0,6},{1,7},{2,4},{3,5},{4,2},{5,3},{6,0},{7,1},{8,14},{9,15},{10,... | collective-permute-start | bytes 221192 | tf_op jit(solution)/shard_map/ppermute | solution.py:830
  49.3 5.5 %collective-permute-start.20 = (f32[18,8,128]{2,1,0:T(8,128)S(1)}, f32[18,8,128]{2,1,0:T(8,128)S(1)}, u32[]{:S(2)}, u32[]{:S(2)}) collective-permute-start(f32[18,8,128]{2,1,0:T(8,128)S(1)} %get-tuple-element.37), channel_id=1, source_target_pairs={{0,7},{1,6},{2,5},{3,4},{4,3},{5,2},{6,1},{7,0},{8,15},{9,14},{10,... | collective-permute-start | bytes 221192 | tf_op jit(solution)/shard_map/ppermute | solution.py:830
  49.9 6.0 %collective-permute-start.19 = (f32[18,8,128]{2,1,0:T(8,128)S(1)}, f32[18,8,128]{2,1,0:T(8,128)S(1)}, u32[]{:S(2)}, u32[]{:S(2)}) collective-permute-start(f32[18,8,128]{2,1,0:T(8,128)S(1)} %get-tuple-element.38), channel_id=1, source_target_pairs={{0,2},{1,3},{2,0},{3,1},{4,6},{5,7},{6,4},{7,5},{8,10},{9,11},{10,... | collective-permute-start | bytes 221192 | tf_op jit(solution)/shard_map/ppermute | solution.py:830
  49.9 7.1 %collective-permute-start.18 = (f32[18,8,128]{2,1,0:T(8,128)S(1)}, f32[18,8,128]{2,1,0:T(8,128)S(1)}, u32[]{:S(2)}, u32[]{:S(2)}) collective-permute-start(f32[18,8,128]{2,1,0:T(8,128)S(1)} %get-tuple-element.39), channel_id=1, source_target_pairs={{0,4},{1,5},{2,6},{3,7},{4,0},{5,1},{6,2},{7,3},{8,12},{9,13},{10,... | collective-permute-start | bytes 221192 | tf_op jit(solution)/shard_map/ppermute | solution.py:830
  52.9 4.2 %collective-permute-start.17 = (f32[18,8,128]{2,1,0:T(8,128)S(1)}, f32[18,8,128]{2,1,0:T(8,128)S(1)}, u32[]{:S(2)}, u32[]{:S(2)}) collective-permute-start(f32[18,8,128]{2,1,0:T(8,128)S(1)} %get-tuple-element.40), channel_id=1, source_target_pairs={{0,3},{1,2},{2,1},{3,0},{4,7},{5,6},{6,5},{7,4},{8,11},{9,10},{10,... | collective-permute-start | bytes 221192 | tf_op jit(solution)/shard_map/ppermute | solution.py:830
  54.6 4.1 %collective-permute-start.16 = (f32[18,8,128]{2,1,0:T(8,128)S(1)}, f32[18,8,128]{2,1,0:T(8,128)S(1)}, u32[]{:S(2)}, u32[]{:S(2)}) collective-permute-start(f32[18,8,128]{2,1,0:T(8,128)S(1)} %get-tuple-element.41), channel_id=1, source_target_pairs={{0,5},{1,4},{2,7},{3,6},{4,1},{5,0},{6,3},{7,2},{8,13},{9,12},{10,... | collective-permute-start | bytes 221192 | tf_op jit(solution)/shard_map/ppermute | solution.py:830
  54.9 3.8 %collective-permute-start.15 = (f32[18,8,128]{2,1,0:T(8,128)S(1)}, f32[18,8,128]{2,1,0:T(8,128)S(1)}, u32[]{:S(2)}, u32[]{:S(2)}) collective-permute-start(f32[18,8,128]{2,1,0:T(8,128)S(1)} %get-tuple-element.42), channel_id=1, source_target_pairs={{0,1},{1,0},{2,3},{3,2},{4,5},{5,4},{6,7},{7,6},{8,9},{9,8},{10,11... | collective-permute-start | bytes 221192 | tf_op jit(solution)/shard_map/ppermute | solution.py:830
